TPU v7x, 32 devices: a whole 2x2x4 slice. The times are simulated.
32 devices in a mesh: fsdp: 4 (over y, x), ctx: 4 (over z), tp: 2 (over core).
Axes of the slice: x: 2, y: 2, z: 4, core: 2. Of those that a mesh axis runs over, the one named last changes fastest.
Arguments:
- block_input: bfloat16 [4, 2048, 1536], P('fsdp', 'ctx'), may hold values from -6 to 6
- out_cotangent: bfloat16 [4, 2048, 1536], P('fsdp', 'ctx'), may hold values from -6 to 6
- block_ids: int32 [4, 2048], P('fsdp'), may hold values from 0 to 12, never falling along the last dimension, each value on 1 to 256 neighbouring positions
- expert_routes: int32 [4, 2048, 8], P('fsdp', 'ctx'), may hold values from 0 to 15, all different within a row; in each aligned block of 512 rows (0 to 511, 512 to 1023, ..., all dimensions but the last counted through in order) at most 384 rows name the same one
- norm_gains: float32 [2, 1536], P(None, 'fsdp'), may hold values from 0.5 to 1.5
- gains_first: float32 [2, 1536], P(None, 'fsdp'), may hold values from -128 to 128
- gains_second: float32 [2, 1536], P(None, 'fsdp'), may hold values from 1638.4 to 6553.6
- joint_weight: float32 [1536, 2560], P('fsdp', 'tp'), may hold values from -0.15625 to 0.15625
- joint_first: float32 [1536, 2560], P('fsdp', 'tp'), may hold values from -128 to 128
- joint_second: float32 [1536, 2560], P('fsdp', 'tp'), may hold values from 1720.32 to 6881.28
- output_weight: float32 [1536, 1536], P('fsdp', 'tp'), may hold values from -1.75 to 1.75
- output_first: float32 [1536, 1536], P('fsdp', 'tp'), may hold values from -6 to 6
- output_second: float32 [1536, 1536], P('fsdp', 'tp'), may hold values from 13.9264 to 55.7056
- router_weight: float32 [1536, 16], P('fsdp'), may hold values from -0.078125 to 0.078125
- router_first: float32 [1536, 16], P('fsdp'), may hold values from -448 to 448
- router_second: float32 [1536, 16], P('fsdp'), may hold values from 21708.8 to 86016
- expert_weight: float32 [1536, 16, 3, 512], P('fsdp', None, None, 'tp')
- expert_first: float32 [1536, 16, 3, 512], P('fsdp', None, None, 'tp')
- expert_second: float32 [1536, 16, 3, 512], P('fsdp', None, None, 'tp')
Outputs:
- block_output: bfloat16 [4, 2048, 1536], P('fsdp', 'ctx')
- input_grad: float32 [4, 2048, 1536], P('fsdp', 'ctx')
- gains_master: float32 [2, 1536], P(None, 'fsdp')
- gains_moment: float32 [2, 1536], P(None, 'fsdp')
- gains_square: float32 [2, 1536], P(None, 'fsdp')
- gains_rounded: bfloat16 [2, 1536], P(None, 'fsdp')
- joint_master: float32 [1536, 2560], P('fsdp', 'tp')
- joint_moment: float32 [1536, 2560], P('fsdp', 'tp')
- joint_square: float32 [1536, 2560], P('fsdp', 'tp')
- joint_rounded: bfloat16 [1536, 2560], P('fsdp', 'tp')
- output_master: float32 [1536, 1536], P('fsdp', 'tp')
- output_moment: float32 [1536, 1536], P('fsdp', 'tp')
- output_square: float32 [1536, 1536], P('fsdp', 'tp')
- output_rounded: bfloat16 [1536, 1536], P('fsdp', 'tp')
- router_master: float32 [1536, 16], P('fsdp')
- router_moment: float32 [1536, 16], P('fsdp')
- router_square: float32 [1536, 16], P('fsdp')
- router_rounded: bfloat16 [1536, 16], P('fsdp')
- expert_master: float32 [1536, 16, 3, 512], P('fsdp', None, None, 'tp')
- expert_moment: float32 [1536, 16, 3, 512], P('fsdp', None, None, 'tp')
- expert_square: float32 [1536, 16, 2, 512], P('fsdp', None, None, 'tp')
- down_square: float32 [1536, 16, 512], P('fsdp', None, 'tp')
- expert_rounded: bfloat16 [1536, 16, 3, 512], P('fsdp', None, None, 'tp')
Inputs may be any that keep to these rules, and one draw needn't show every extreme that they name: `block_ids`: within a sequence the ids never fall along the positions, each id holds 1 to 256 positions, and one holds exactly 256. `expert_routes`: each row names 8 different experts. In each aligned block of 512 rows (the rows of one device) no expert is named by more than 384 rows, and in some blocks one expert is named by exactly 384.
All inputs are finite; a program needn't handle non-finite values.
Results may differ from a plain program's by a relative error of at most 0.025.
Values may be sent and summed in bfloat16 or wider, within the bound.
A program may use at most 448 MiB of HBM per device.

v0:
```python
import math

import jax
import jax.numpy as jnp
from jax import lax
from jax.sharding import PartitionSpec as P

QUERY_HEADS = 24
KEY_VALUE_HEADS = 8
HEAD_SIZE = 64
TOPK = 8
E = 16
STEP = 10
CAP = 384


def inverse_rms(rows):
    return lax.rsqrt(jnp.mean(rows * rows, axis=-1, keepdims=True) + 1e-06)


def rotary_tables(positions):
    halves = jnp.arange(HEAD_SIZE // 2).astype(jnp.float32)
    frequency = jnp.exp(halves * (-2.0 * math.log(10000.0) / HEAD_SIZE))
    angles = positions[:, None] * frequency[None, :]
    return (jnp.cos(angles), jnp.sin(angles))


def rotate(vectors, cosine, sine_part, inverse):
    trailing = (1,) * (vectors.ndim - 2)
    cos_rows = cosine.reshape((cosine.shape[0],) + trailing + (cosine.shape[1],))
    sin_rows = sine_part.reshape((sine_part.shape[0],) + trailing + (sine_part.shape[1],))
    middle = vectors.shape[-1] // 2
    leading = vectors[..., :middle]
    ending = vectors[..., middle:]
    if inverse:
        return jnp.concatenate(
            [leading * cos_rows + ending * sin_rows, ending * cos_rows - leading * sin_rows],
            axis=-1,
        )
    return jnp.concatenate(
        [leading * cos_rows - ending * sin_rows, ending * cos_rows + leading * sin_rows], axis=-1
    )


def slot_tables(route_rows):
    flat_routes = route_rows.reshape(-1)
    member = (flat_routes[:, None] == jnp.arange(E, dtype=jnp.int32)[None, :]).astype(jnp.int32)
    rank_rows = jnp.sum((jnp.cumsum(member, axis=0) - 1) * member, axis=1)
    slot_ids = flat_routes * CAP + rank_rows
    entry_ids = jnp.arange(flat_routes.shape[0], dtype=jnp.int32)
    owners = (
        jnp.full((E * CAP,), route_rows.shape[0], jnp.int32).at[slot_ids].set(entry_ids // TOPK)
    )
    entries = jnp.full((E * CAP,), flat_routes.shape[0], jnp.int32).at[slot_ids].set(entry_ids)
    return (slot_ids.reshape(route_rows.shape), owners, entries)


def block_scores(query_rows, key_part):
    return jnp.einsum(
        "qhgd,khd->hgqk", query_rows, key_part, preferred_element_type=jnp.float32
    ) * (1.0 / math.sqrt(HEAD_SIZE))


def adamw(master, first_moment, second_moment, gradient, rate, decay):
    moment_new = 0.9 * first_moment + 0.1 * gradient
    square_new = 0.95 * second_moment + 0.05 * gradient * gradient
    corrected = moment_new / (1.0 - 0.9**STEP) / (jnp.sqrt(square_new / (1.0 - 0.95**STEP)) + 1e-08)
    master_new = master - rate * (corrected + decay * master)
    return (master_new, moment_new, square_new, master_new.astype(jnp.bfloat16))


def local(
    block_input,
    out_cotangent,
    block_ids,
    expert_routes,
    norm_gains,
    gains_first,
    gains_second,
    joint_weight,
    joint_first,
    joint_second,
    output_weight,
    output_first,
    output_second,
    router_weight,
    router_first,
    router_second,
    expert_weight,
    expert_first,
    expert_second,
):
    tokens = block_input[0].astype(jnp.float32)
    cotangent = out_cotangent[0].astype(jnp.float32)
    id_rows = block_ids[0]
    route_rows = expert_routes[0]
    tok_count = tokens.shape[0]
    width = tokens.shape[1]
    seq_length = id_rows.shape[0]
    heads_per_group = QUERY_HEADS // KEY_VALUE_HEADS
    ctx_place = lax.axis_index("ctx")
    start_row = ctx_place * tok_count
    gain_rows, joint_full, output_full, router_full = (
        lax.all_gather(norm_gains.astype(jnp.bfloat16), "fsdp", axis=1, tiled=True),
        lax.all_gather(joint_weight.astype(jnp.bfloat16), "fsdp", axis=0, tiled=True),
        lax.all_gather(output_weight.astype(jnp.bfloat16), "fsdp", axis=0, tiled=True),
        lax.all_gather(router_weight.astype(jnp.bfloat16), "fsdp", axis=0, tiled=True),
    )
    gain_first = gain_rows[0].astype(jnp.float32)
    gain_second = gain_rows[1].astype(jnp.float32)
    inv_first = inverse_rms(tokens)
    normed_first = (tokens * inv_first * gain_first).astype(jnp.bfloat16)
    combined_rows = jnp.dot(normed_first, joint_full, preferred_element_type=jnp.float32)
    kv_local = joint_full.shape[1] // ((heads_per_group + 2) * HEAD_SIZE)
    grouped_queries = combined_rows.reshape(tok_count, kv_local, heads_per_group + 2, HEAD_SIZE)
    positions = (start_row + jnp.arange(tok_count, dtype=jnp.int32)).astype(jnp.float32)
    cosine, sine_part = rotary_tables(positions)
    query_rows = rotate(grouped_queries[:, :, :heads_per_group], cosine, sine_part, False).astype(
        jnp.bfloat16
    )
    key_rows = rotate(grouped_queries[:, :, heads_per_group], cosine, sine_part, False).astype(
        jnp.bfloat16
    )
    value_rows = grouped_queries[:, :, heads_per_group + 1].astype(jnp.bfloat16)
    all_keys, all_values = (
        lax.all_gather(key_rows, "ctx", axis=0, tiled=True),
        lax.all_gather(value_rows, "ctx", axis=0, tiled=True),
    )
    query_ids = lax.dynamic_slice_in_dim(id_rows, start_row, tok_count, 0)
    key_block = min(seq_length, 512)
    block_starts = jnp.arange(seq_length // key_block, dtype=jnp.int32) * key_block
    stat_shape = (kv_local, heads_per_group, tok_count)

    def key_slices(row_start):
        key_part = lax.dynamic_slice_in_dim(all_keys, row_start, key_block, 0)
        value_part = lax.dynamic_slice_in_dim(all_values, row_start, key_block, 0)
        visible = (
            query_ids[:, None]
            >= lax.dynamic_slice_in_dim(id_rows, row_start, key_block, 0)[None, :]
        )
        return (key_part, value_part, visible)

    def max_pass(carried, row_start):
        row_max, row_total = carried
        key_part, value_part, visible = key_slices(row_start)
        scores = jnp.where(visible, block_scores(query_rows, key_part), -1e30)
        new_max = jnp.maximum(row_max, jnp.max(scores, axis=-1))
        exponent = jnp.where(visible, jnp.exp(scores - new_max[..., None]), 0.0)
        row_total = row_total * jnp.exp(row_max - new_max) + jnp.sum(exponent, axis=-1)
        return ((new_max, row_total), None)

    (row_max, row_total), unused = lax.scan(
        max_pass,
        (jnp.full(stat_shape, -1e30, jnp.float32), jnp.zeros(stat_shape, jnp.float32)),
        block_starts,
    )
    log_total = row_max + jnp.log(row_total)

    def probabilities(key_part, visible):
        return jnp.where(
            visible, jnp.exp(block_scores(query_rows, key_part) - log_total[..., None]), 0.0
        )

    def value_pass(running, row_start):
        key_part, value_part, visible = key_slices(row_start)
        weights_low = probabilities(key_part, visible).astype(jnp.bfloat16)
        return (
            running
            + jnp.einsum(
                "hgqk,khd->qhgd", weights_low, value_part, preferred_element_type=jnp.float32
            ),
            None,
        )

    attended, unused = lax.scan(
        value_pass,
        jnp.zeros((tok_count, kv_local, heads_per_group, HEAD_SIZE), jnp.float32),
        block_starts,
    )
    attended_low = attended.reshape(tok_count, -1).astype(jnp.bfloat16)
    attn_sum = lax.psum(
        jnp.einsum("tj,dj->td", attended_low, output_full, preferred_element_type=jnp.float32), "tp"
    )
    residual = tokens + attn_sum
    inv_second = inverse_rms(residual)
    normed_second = (residual * inv_second * gain_second).astype(jnp.bfloat16)
    logits = jnp.dot(normed_second, router_full, preferred_element_type=jnp.float32)
    member = (route_rows[:, :, None] == jnp.arange(E, dtype=jnp.int32)[None, None, :]).astype(
        jnp.float32
    )
    chosen = jnp.sum(member * logits[:, None, :], axis=2)
    exponent = jnp.exp(chosen - jnp.max(chosen, axis=1, keepdims=True))
    gates = exponent / jnp.sum(exponent, axis=1, keepdims=True)
    slot_ids, owners, entries = slot_tables(route_rows)
    padded_rows = jnp.concatenate([normed_second, jnp.zeros((1, width), jnp.bfloat16)], axis=0)
    dispatched = padded_rows[owners].reshape(E, CAP, width)
    expert_low = expert_weight.astype(jnp.bfloat16)
    piece_rows = lax.all_gather(expert_low, "fsdp", axis=0, tiled=True)
    gate_sums = jnp.einsum(
        "ecd,dejf->ecjf", dispatched, piece_rows[:, :, 0:2], preferred_element_type=jnp.float32
    )
    stored = piece_rows[:, :, 2:3]
    folded = (gate_sums, stored)
    gate_up, stored = folded
    down_low = stored[:, :, -1]
    gate_part = gate_up[:, :, 0]
    up_part = gate_up[:, :, 1]
    sigmoid_gate = jax.nn.sigmoid(gate_part)
    hidden = (gate_part * sigmoid_gate * up_part).astype(jnp.bfloat16)
    expert_out = jnp.einsum(
        "ecf,def->ecd", hidden, down_low, preferred_element_type=jnp.float32
    ).reshape(E * CAP, width)
    picked = expert_out[slot_ids]
    moe_part = jnp.sum(gates[:, :, None] * picked, axis=1)
    gate_part_grads = jnp.sum(picked * cotangent[:, None, :], axis=2)
    moe_sum, gate_grads = (
        lax.psum(moe_part.astype(jnp.bfloat16), "tp").astype(jnp.float32),
        lax.psum(gate_part_grads.astype(jnp.bfloat16), "tp").astype(jnp.float32),
    )
    block_output = (residual + moe_sum).astype(jnp.bfloat16)[None]
    chosen_grads = gates * (gate_grads - jnp.sum(gates * gate_grads, axis=1, keepdims=True))
    logit_grads = jnp.sum(chosen_grads[:, :, None] * member, axis=1).astype(jnp.bfloat16)
    gate_slots = jnp.concatenate([gates.reshape(-1), jnp.zeros((1,), jnp.float32)])[entries]
    cot_slots = jnp.concatenate([out_cotangent[0], jnp.zeros((1, width), jnp.bfloat16)], axis=0)[
        owners
    ]
    out_grads = (
        (gate_slots[:, None] * cot_slots.astype(jnp.float32))
        .astype(jnp.bfloat16)
        .reshape(E, CAP, width)
    )
    hidden_grads = jnp.einsum(
        "ecd,def->ecf", out_grads, down_low, preferred_element_type=jnp.float32
    )
    pre_grads = jnp.stack(
        [
            hidden_grads * up_part * sigmoid_gate * (1.0 + gate_part * (1.0 - sigmoid_gate)),
            hidden_grads * gate_part * sigmoid_gate,
        ],
        axis=2,
    ).astype(jnp.bfloat16)
    piece_rows = lax.all_gather(expert_low[:, :, 0:2], "fsdp", axis=0, tiled=True)
    slot_piece = jnp.einsum(
        "ecjf,dejf->ecd", pre_grads, piece_rows, preferred_element_type=jnp.float32
    )
    slot_input = slot_piece.reshape(E * CAP, piece_rows.shape[0])
    moe_input_part = jnp.sum(slot_input[slot_ids], axis=1)
    moe_input = lax.psum(moe_input_part.astype(jnp.bfloat16), "tp").astype(jnp.float32)
    norm_second_grads = moe_input + jnp.einsum(
        "te,de->td", logit_grads, router_full, preferred_element_type=jnp.float32
    )
    scaled_second = gain_second * norm_second_grads
    cube_second = inv_second * inv_second * inv_second / width
    residual_grads = (
        cotangent
        + inv_second * scaled_second
        - residual * cube_second * jnp.sum(scaled_second * residual, axis=1, keepdims=True)
    )
    gain_second_grad = jnp.sum(norm_second_grads * residual * inv_second, axis=0)
    residual_low = residual_grads.astype(jnp.bfloat16)
    attended_grads = jnp.dot(residual_low, output_full, preferred_element_type=jnp.float32).astype(
        jnp.bfloat16
    )
    attended_grads = attended_grads.reshape(tok_count, kv_local, heads_per_group, HEAD_SIZE)

    def delta_pass(running, row_start):
        key_part, value_part, visible = key_slices(row_start)
        weights_full = probabilities(key_part, visible)
        prob_grads = jnp.einsum(
            "qhgd,khd->hgqk", attended_grads, value_part, preferred_element_type=jnp.float32
        )
        return (running + jnp.sum(weights_full * prob_grads, axis=-1), None)

    delta_rows, unused = lax.scan(delta_pass, jnp.zeros(stat_shape, jnp.float32), block_starts)

    def grad_pass(carried, row_start):
        query_acc, key_acc, value_acc = carried
        key_part, value_part, visible = key_slices(row_start)
        weights_full = probabilities(key_part, visible)
        prob_grads = jnp.einsum(
            "qhgd,khd->hgqk", attended_grads, value_part, preferred_element_type=jnp.float32
        )
        score_grads = (weights_full * (prob_grads - delta_rows[..., None])).astype(jnp.bfloat16)
        query_acc = query_acc + jnp.einsum(
            "hgqk,khd->qhgd", score_grads, key_part, preferred_element_type=jnp.float32
        )
        key_part_grads = jnp.einsum(
            "hgqk,qhgd->khd", score_grads, query_rows, preferred_element_type=jnp.float32
        )
        value_part_grads = jnp.einsum(
            "hgqk,qhgd->khd",
            weights_full.astype(jnp.bfloat16),
            attended_grads,
            preferred_element_type=jnp.float32,
        )
        key_acc = lax.dynamic_update_slice_in_dim(key_acc, key_part_grads, row_start, 0)
        value_acc = lax.dynamic_update_slice_in_dim(value_acc, value_part_grads, row_start, 0)
        return ((query_acc, key_acc, value_acc), None)

    kv_shape = (seq_length, kv_local, HEAD_SIZE)
    (query_grads, key_all, value_all), unused = lax.scan(
        grad_pass,
        (
            jnp.zeros((tok_count, kv_local, heads_per_group, HEAD_SIZE), jnp.float32),
            jnp.zeros(kv_shape, jnp.float32),
            jnp.zeros(kv_shape, jnp.float32),
        ),
        block_starts,
    )
    key_grads, value_grads = (
        lax.psum_scatter(
            key_all.astype(jnp.bfloat16), "ctx", scatter_dimension=0, tiled=True
        ).astype(jnp.float32),
        lax.psum_scatter(
            value_all.astype(jnp.bfloat16), "ctx", scatter_dimension=0, tiled=True
        ).astype(jnp.float32),
    )
    scale_factor = 1.0 / math.sqrt(HEAD_SIZE)
    query_back = rotate(query_grads * scale_factor, cosine, sine_part, True)
    key_back = rotate(key_grads * scale_factor, cosine, sine_part, True)
    joint_grads = jnp.concatenate(
        [query_back, key_back[:, :, None], value_grads[:, :, None]], axis=2
    )
    joint_grads = joint_grads.reshape(tok_count, -1).astype(jnp.bfloat16)
    norm_first_grads = lax.psum(
        jnp.einsum("tc,dc->td", joint_grads, joint_full, preferred_element_type=jnp.float32).astype(
            jnp.bfloat16
        ),
        "tp",
    ).astype(jnp.float32)
    scaled_first = gain_first * norm_first_grads
    cube_first = inv_first * inv_first * inv_first / width
    input_rows = (
        residual_grads
        + inv_first * scaled_first
        - tokens * cube_first * jnp.sum(scaled_first * tokens, axis=1, keepdims=True)
    )
    gain_first_grad = jnp.sum(norm_first_grads * tokens * inv_first, axis=0)
    joint_term = jnp.einsum(
        "td,tc->dc", normed_first, joint_grads, preferred_element_type=jnp.float32
    )
    output_term = jnp.einsum(
        "td,tj->dj", residual_low, attended_low, preferred_element_type=jnp.float32
    )
    router_term = jnp.einsum(
        "td,te->de", normed_second, logit_grads, preferred_element_type=jnp.float32
    )
    gains_term = jnp.stack([gain_first_grad, gain_second_grad])
    gains_part, joint_part, output_part, router_part = (
        lax.psum_scatter(
            gains_term.astype(jnp.bfloat16), "fsdp", scatter_dimension=1, tiled=True
        ).astype(jnp.float32),
        lax.psum_scatter(
            joint_term.astype(jnp.bfloat16), "fsdp", scatter_dimension=0, tiled=True
        ).astype(jnp.float32),
        lax.psum_scatter(
            output_term.astype(jnp.bfloat16), "fsdp", scatter_dimension=0, tiled=True
        ).astype(jnp.float32),
        lax.psum_scatter(
            router_term.astype(jnp.bfloat16), "fsdp", scatter_dimension=0, tiled=True
        ).astype(jnp.float32),
    )
    up_term = jnp.einsum(
        "ecd,ecjf->dejf", dispatched, pre_grads, preferred_element_type=jnp.float32
    )
    down_term = jnp.einsum("ecd,ecf->def", out_grads, hidden, preferred_element_type=jnp.float32)
    expert_part = lax.psum_scatter(
        jnp.concatenate([up_term, down_term[:, :, None]], axis=2).astype(jnp.bfloat16),
        "fsdp",
        scatter_dimension=0,
        tiled=True,
    )
    gains_sum, joint_sum, output_sum, router_sum, expert_sum = (
        lax.psum(gains_part.astype(jnp.bfloat16), "ctx").astype(jnp.float32),
        lax.psum(joint_part.astype(jnp.bfloat16), "ctx").astype(jnp.float32),
        lax.psum(output_part.astype(jnp.bfloat16), "ctx").astype(jnp.float32),
        lax.psum(router_part.astype(jnp.bfloat16), "ctx").astype(jnp.float32),
        lax.psum(expert_part, "ctx").astype(jnp.float32),
    )
    gains_new = adamw(norm_gains, gains_first, gains_second, gains_sum, 0.6, 0.0)
    joint_new = adamw(joint_weight, joint_first, joint_second, joint_sum, 0.03, 0.1)
    output_new = adamw(output_weight, output_first, output_second, output_sum, 0.25, 0.1)
    router_new = adamw(router_weight, router_first, router_second, router_sum, 0.015, 0.1)
    expert_rate = jnp.array([0.03, 0.03, 0.25], jnp.float32).reshape(1, 1, 3, 1)
    expert_new = adamw(expert_weight, expert_first, expert_second, expert_sum, expert_rate, 0.1)
    return (
        block_output,
        input_rows[None],
        gains_new[0],
        gains_new[1],
        gains_new[2],
        gains_new[3],
        joint_new[0],
        joint_new[1],
        joint_new[2],
        joint_new[3],
        output_new[0],
        output_new[1],
        output_new[2],
        output_new[3],
        router_new[0],
        router_new[1],
        router_new[2],
        router_new[3],
        expert_new[0],
        expert_new[1],
        expert_new[2][:, :, 0:2],
        expert_new[2][:, :, 2],
        expert_new[3],
    )


def solution(mesh):
    return jax.shard_map(
        local,
        mesh=mesh,
        in_specs=(
            P("fsdp", "ctx", None),
            P("fsdp", "ctx", None),
            P("fsdp", None),
            P("fsdp", "ctx", None),
            P(None, "fsdp"),
            P(None, "fsdp"),
            P(None, "fsdp"),
            P("fsdp", "tp"),
            P("fsdp", "tp"),
            P("fsdp", "tp"),
            P("fsdp", "tp"),
            P("fsdp", "tp"),
            P("fsdp", "tp"),
            P("fsdp", None),
            P("fsdp", None),
            P("fsdp", None),
            P("fsdp", None, None, "tp"),
            P("fsdp", None, None, "tp"),
            P("fsdp", None, None, "tp"),
        ),
        out_specs=(
            P("fsdp", "ctx", None),
            P("fsdp", "ctx", None),
            P(None, "fsdp"),
            P(None, "fsdp"),
            P(None, "fsdp"),
            P(None, "fsdp"),
            P("fsdp", "tp"),
            P("fsdp", "tp"),
            P("fsdp", "tp"),
            P("fsdp", "tp"),
            P("fsdp", "tp"),
            P("fsdp", "tp"),
            P("fsdp", "tp"),
            P("fsdp", "tp"),
            P("fsdp", None),
            P("fsdp", None),
            P("fsdp", None),
            P("fsdp", None),
            P("fsdp", None, None, "tp"),
            P("fsdp", None, None, "tp"),
            P("fsdp", None, None, "tp"),
            P("fsdp", None, "tp"),
            P("fsdp", None, None, "tp"),
        ),
        check_vma=False,
    )
```

profile of v0, /device:TPU:0, one launch (start us, length us, event | category | flops | bytes accessed | tf_op | source)
XLA Modules:
  0.0 2337.9 jit_solution(17381949320576614093)
XLA Ops:
  10.1 9.5 all_gather.24
  21.0 42.7 %all-gather.8.cloned.1.call-done = bf16[1536,1280]{1,0:T(8,128)(2,1)} async-done(((bf16[384,1280]{1,0:T(8,128)(2,1)}), bf16[1536,1280]{1,0:T(8,128)(2,1)}) %all-gather.8.cloned.1.call-update) | async-done | bytes 3932176 | tf_op jit(solution)/shard_map/all_gather | solution.py:105
  82.4 22.5 all-gather.10.cloned.1.call-done
  104.9 72.1 %while.50 = (s32[]{:T(128)}, f32[4,3,512]{2,1,0:T(4,128)S(1)}, f32[4,3,512]{2,1,0:T(4,128)S(1)}, s32[512]{0:T(512)S(1)}, s32[4]{0:T(128)S(1)}, /*index=5*/s32[20...) while((s32[]{:T(128)}, f32[4,3,512]{2,1,0:T(4,128)S(1)}, ...), condition=%wide.region_4.5_spmd.clone, body=%wide.region_1.4_spmd.clone.sunk | while | flops 428111872 | bytes 27328684 | solution.py:152
  108.4 7.9 fusion.211
  116.3 6.6 select_reduce_fusion.4
  126.5 7.9 fusion.211
  134.4 6.5 select_reduce_fusion.4
  144.5 7.9 fusion.211
  152.4 6.5 select_reduce_fusion.4
  162.6 7.9 fusion.211
  170.4 6.5 select_reduce_fusion.4
  177.1 39.5 %while.51 = (s32[]{:T(128)}, f32[512,4,3,64]{0,3,2,1:T(8,128)}, s32[4]{0:T(128)S(1)}, bf16[2048,4,64]{0,2,1:T(8,128)(2,1)}, s32[512]{0:T(512)S(1)}, /*index=5*/s...) while((s32[]{:T(128)}, f32[512,4,3,64]{0,3,2,1:T(8,128)}, ...), condition=%wide.region_6.7_spmd.clone, body=%wide.region_5.6_spmd.clone.sunk | while | flops 818937856 | bytes 5015216 | solution.py:175
  190.1 6.5 bitcast_add_fusion.5
  200.1 6.5 bitcast_add_fusion.5
  224.9 14.2 copy.209
  239.2 6.5 slice.112
  253.1 15.5 scatter_custom_fusion
  268.7 15.5 scatter_custom_fusion.1
  285.8 28.0 %gather_fusion.3 = bf16[6144,1536]{1,0:T(8,128)(2,1)} fusion(bf16[513,1536]{1,0:T(8,128)(2,1)S(1)} %concatenate.34, s32[6144]{0:T(1024)S(1)} %fusion.115), kind=kCustom, calls=%fused_computation.3 | custom fusion | bytes 37773312 | tf_op jit(solution)/shard_map/gather | solution.py:224
  313.8 8.9 all_gather.29
  332.8 34.5 %gather_fusion.2 = f32[6144]{0:T(1024)S(1)} fusion(f32[4097]{0:T(1024)S(1)} %pad_maximum_fusion.4, s32[6144]{0:T(1024)S(1)} %fusion.116), kind=kCustom, calls=%fused_computation.2 | custom fusion | bytes 73728 | tf_op jit(solution)/shard_map/gather | solution.py:223
  367.4 28.0 %gather_fusion = bf16[6144,1536]{1,0:T(8,128)(2,1)} fusion(bf16[513,1536]{1,0:T(8,128)(2,1)S(1)} %concatenate.32, s32[6144]{0:T(1024)S(1)} %fusion.115), kind=kCustom, calls=%fused_computation | custom fusion | bytes 37773312 | tf_op jit(solution)/shard_map/gather | solution.py:196
  395.4 188.8 %all-gather.14.cloned.1.call-done = bf16[1536,16,3,256]{3,0,2,1:T(8,128)(2,1)} async-done(((bf16[384,16,3,256]{3,0,2,1:T(8,128)(2,1)}), bf16[1536,16,3,256]{3,0,2,1:T(8,128)(2,1)}) %all-gather.14.cloned.1.call-update) | async-done | bytes 37748752 | tf_op jit(solution)/shard_map/all_gather | solution.py:198
  584.2 26.5 %fusion.60 = f32[16,384,2,256]{3,1,2,0:T(8,128)} fusion(bf16[16,384,1536,1]{2,1,3,0:T(8,128)(2,1)} %bitcast.356, bf16[1536,16,3,256]{3,0,2,1:T(8,128)(2,1)} %all-gather.14.cloned.1.call-done), kind=kOutput, calls=%fused_computation.77 | convolution fusion | flops 9663676416 | bytes 56623104 | tf_op jit(solution)/shard_map/ecd,dejf->ecjf/dot_general | solution.py:199
  610.6 20.5 fusion.97
  631.1 183.4 %all-gather.16.cloned.1.call-done = bf16[1536,16,2,256]{3,0,2,1:T(8,128)(2,1)} async-done(((bf16[384,16,2,256]{3,0,2,1:T(8,128)(2,1)}), bf16[1536,16,2,256]{3,0,2,1:T(8,128)(2,1)}) %all-gather.16.cloned.1.call-update) | async-done | bytes 25165840 | tf_op jit(solution)/shard_map/all_gather | solution.py:242
  814.5 25.9 %fusion.64 = f32[16,384,1536,1]{2,1,0,3:T(8,128)} fusion(bf16[1536,16,2,256]{3,0,2,1:T(8,128)(2,1)} %all-gather.16.cloned.1.call-done, bf16[16,384,1,256]{3,1,0,2:T(8,128)(2,1)} %get-tuple-element.649, bf16[16,384,1,256]{3,1,0,2:T(8,128)(2,1)} %get-tuple-element.648), kind=kOutput, calls=%fused_computation.84 | convolution fusion | flops 9666822144 | bytes 69206016 | tf_op jit(solution)/shard_map/ecjf,dejf->ecd/dot_general | solution.py:243
  840.3 39.0 %gather_fusion.4 = f32[4096,1536]{1,0:T(8,128)} fusion(f32[6144,1536]{1,0:T(8,128)} %bitcast.351, s32[4096]{0:T(1024)S(1)} %broadcast_clamp_fusion), kind=kCustom, calls=%fused_computation.4 | custom fusion | bytes 50348032 | tf_op jit(solution)/shard_map/gather | solution.py:247
  879.3 14.3 bitcast_reduce_fusion
  893.7 24.0 %fusion.75 = f32[16,384,1536]{2,1,0:T(8,128)} fusion(bf16[16,384,256]{2,1,0:T(8,128)(2,1)S(1)} %get-tuple-element.650, bf16[1536,16,3,256]{3,0,2,1:T(8,128)(2,1)} %all-gather.14.cloned.1.call-done), kind=kOutput, calls=%fused_computation.96 | convolution fusion | flops 4831838208 | bytes 53477376 | tf_op jit(solution)/shard_map/ecf,def->ecd/dot_general | solution.py:210
  917.7 39.1 %gather_fusion.1 = f32[4096,1536]{1,0:T(8,128)} fusion(f32[6144,1536]{1,0:T(8,128)} %bitcast.350, s32[4096]{0:T(1024)S(1)} %broadcast_clamp_fusion), kind=kCustom, calls=%fused_computation.1 | custom fusion | bytes 50348032 | tf_op jit(solution)/shard_map/gather | solution.py:213
  956.9 16.5 fusion.62
  985.4 39.6 %while.52 = (s32[]{:T(128)}, f32[4,3,512]{2,1,0:T(4,128)S(1)}, s32[512]{0:T(512)S(1)}, s32[4]{0:T(128)S(1)}, s32[2048]{0:T(1024)S(1)}, /*index=5*/bf16[2048,4,64...) while((s32[]{:T(128)}, f32[4,3,512]{2,1,0:T(4,128)S(1)}, ...), condition=%wide.region_28.29_spmd.clone, body=%wide.region_26.28_spmd.clone.sunk | while | flops 821303296 | bytes 31064284 | solution.py:274
  1027.3 152.2 %while.53 = (s32[]{:T(128)}, f32[512,4,3,64]{0,3,2,1:T(8,128)S(1)}, bf16[2048,4,64]{0,2,1:T(8,128)(2,1)}, bf16[2048,4,64]{0,2,1:T(8,128)(2,1)}, s32[4]{0:T(128)S...) while((s32[]{:T(128)}, f32[512,4,3,64]{0,3,2,1:T(8,128)S(1)}, ...), condition=%wide.region_30.31_spmd.clone, body=%wide.region_29.30_spmd.clone.sunk | while | flops 2045771776 | bytes 145834320 | solution.py:301
  1036.6 6.8 fusion.234
  1054.1 8.1 fusion.235
  1075.0 6.8 fusion.234
  1092.5 8.1 fusion.235
  1113.3 6.8 fusion.234
  1130.8 8.1 fusion.235
  1151.6 6.8 fusion.234
  1168.6 8.1 fusion.235
  1180.2 24.0 %convert_bitcast_fusion = bf16[1536,16,2,256]{0,3,2,1:T(8,128)(2,1)} fusion(bf16[16,384,1536,1]{2,1,3,0:T(8,128)(2,1)} %bitcast.357, bf16[16,384,1,256]{3,1,0,2:T(8,128)(2,1)} %get-tuple-element.649, bf16[16,384,1,256]{3,1,0,2:T(8,128)(2,1)} %get-tuple-element.648), kind=kOutput, calls=%fused_computation.86 | convolution fusion | flops 9679405056 | bytes 50331648 | tf_op jit(solution)/shard_map/ecd,ecjf->dejf/dot_general | solution.py:363
  1208.0 27.5 %reduce-scatter.16.cloned.1.call-done = bf16[512,4,64]{0,2,1:T(8,128)(2,1)} async-done(((bf16[2048,4,64]{0,2,1:T(8,128)(2,1)}), bf16[512,4,64]{0,2,1:T(8,128)(2,1)}) %reduce-scatter.16.cloned.1.call-update) | async-done | bytes 262160 | tf_op jit(solution)/shard_map/reduce_scatter | solution.py:314
  1244.5 14.6 fusion.76
  1259.0 26.9 %pad_maximum_fusion = bf16[1536,16,3,256]{0,3,2,1:T(8,128)(2,1)} fusion(bf16[1536,16,1,256]{0,3,2,1:T(8,128)(2,1)} %fusion.76, bf16[1536,16,2,256]{0,3,2,1:T(8,128)(2,1)} %convert_bitcast_fusion), kind=kLoop, calls=%fused_computation.73 | loop fusion | flops 18874368 | bytes 75497472 | tf_op jit(solution)/shard_map/concatenate | solution.py:368
  1285.9 48.7 %copy.198 = bf16[1536,12288]{1,0:T(8,128)(2,1)} copy(bf16[1536,12288]{0,1:T(8,128)(2,1)} %bitcast.352) | data formatting | bytes 75497472
  1351.0 304.2 %reduce-scatter.26.cloned.1.call-done = bf16[384,12288]{1,0:T(8,128)(2,1)} async-done(((bf16[1536,12288]{1,0:T(8,128)(2,1)}), bf16[384,12288]{1,0:T(8,128)(2,1)}) %reduce-scatter.26.cloned.1.call-update) | async-done | bytes 9437200
  1655.2 12.6 copy.199
  1667.8 28.4 %reduce-scatter.20.cloned.1.call-done = bf16[384,768]{1,0:T(8,128)(2,1)} async-done(((bf16[1536,768]{1,0:T(8,128)(2,1)}), bf16[384,768]{1,0:T(8,128)(2,1)}) %reduce-scatter.20.cloned.1.call-update) | async-done | bytes 589840 | tf_op jit(solution)/shard_map/reduce_scatter | solution.py:356
  1696.2 54.0 %reduce-scatter.18.cloned.1.call-done = bf16[384,1280]{1,0:T(8,128)(2,1)} async-done(((bf16[1536,1280]{1,0:T(8,128)(2,1)}), bf16[384,1280]{1,0:T(8,128)(2,1)}) %reduce-scatter.18.cloned.1.call-update) | async-done | bytes 983056 | tf_op jit(solution)/shard_map/reduce_scatter | solution.py:353
  1750.3 18.7 copy.168
  1769.0 18.7 copy.163
  1787.7 18.9 copy.166
  1815.2 20.6 all-reduce.2
  1837.0 349.1 %all-reduce.14.cloned.1.call-done = (bf16[384,1280]{1,0:T(8,128)(2,1)}, bf16[384,768]{1,0:T(8,128)(2,1)}, bf16[384,16,3,256]{0,3,2,1:T(8,128)(2,1)}) async-done(((bf16[384,1280]{1,0:T(8,128)(2,1)}, bf16[384,768]{1,0:T(8,128)(2,1)}, bf16[384,16,3,256]{0,3,2,1:T(8,128)(2,1)}), (bf16[384,1280]{1,0:T(8,128)(2,1)}, bf16[384,768]{1,0:T(8,128)(2,1)}, ...) | async-done | bytes 11010064 | tf_op jit(solution)/shard_map/psum | solution.py:375
  2186.1 42.8 %fusion.136 = (bf16[384,16,3,256]{0,3,2,1:T(8,128)(2,1)}, f32[384,16,3,256]{0,3,2,1:T(8,128)}, f32[384,16,3,256]{0,3,2,1:T(8,128)}, f32[384,16,3,256]{0,3,2,1:T(8,128)}) fusion(f32[384,16,3,256]{0,3,2,1:T(8,128)} %copy.168, f32[3]{0:T(128)S(1)} %copy-done.78, bf16[384,16,3,256]{0,3,2,1:T(8,128)(2,1)} %get-tuple-element.621, f32[384,16,3,256]{0,3,2,1:T(8,128)} %copy.163, ...), kind=kLoop, calls=%fused_computation.243 | loop fusion | flops 80216064 | bytes 132120592 | tf_op jit(solution)/shard_map/convert_element_type | solution.py:69
  2229.0 10.5 slice.117
  2245.6 19.0 copy.171
  2264.6 18.9 copy.169
  2283.5 18.9 copy.170
  2302.4 6.6 copy.172
  2309.0 13.3 copy.173
  (429 shorter events, 259.7 us)
Async XLA Ops:
  7.2 12.4 copy-start.11
  7.2 56.5 %all-gather.8.cloned.1.call-start = ((), (), s32[]{:S(2)}) async-start(), calls=%async_computation.7 | async-start | bytes 4915200 | tf_op jit(solution)/shard_map/all_gather | solution.py:105
  10.0 94.9 %all-gather.10.cloned.1.call-start = ((), (), s32[]{:S(2)}) async-start(), calls=%async_computation.8 | async-start | bytes 1310720 | tf_op jit(solution)/shard_map/all_gather | solution.py:126
  19.7 50.3 %copy-start.57 = (f32[1536]{0:T(1024)}, f32[1536]{0:T(1024)S(1)}, u32[]{:S(2)}) copy-start(f32[1536]{0:T(1024)S(1)} %get-tuple-element.536) | copy-start | bytes 18436
  19.7 309.6 %copy-start.53 = (f32[1536]{0:T(1024)}, f32[1536]{0:T(1024)S(1)}, u32[]{:S(2)}) copy-start(f32[1536]{0:T(1024)S(1)} %get-tuple-element.535) | copy-start | bytes 18436
  20.7 49.3 %copy-start.69 = (f32[512]{0:T(512)}, f32[512]{0:T(512)S(1)}, u32[]{:S(2)}) copy-start(f32[512]{0:T(512)S(1)} %get-tuple-element.662) | copy-start | bytes 6148
  21.0 59.7 %copy-start.27 = (f32[512,32]{0,1:T(8,128)}, f32[512,32]{0,1:T(8,128)S(1)}, u32[]{:S(2)}) copy-start(f32[512,32]{0,1:T(8,128)S(1)} %get-tuple-element.659) | copy-start | bytes 196612
  21.0 59.7 %copy-start.29 = (f32[512,32]{0,1:T(8,128)}, f32[512,32]{0,1:T(8,128)S(1)}, u32[]{:S(2)}) copy-start(f32[512,32]{0,1:T(8,128)S(1)} %get-tuple-element.660) | copy-start | bytes 196612
  76.8 100.3 %all-gather.18.cloned.1.call-start = ((), (), s32[]{:S(2)}) async-start(), calls=%async_computation.18 | async-start | bytes 1310720 | tf_op jit(solution)/shard_map/all_gather | solution.py:127
  78.7 140.6 %all-gather.12.cloned.1.call-start = ((), (), s32[]{:S(2)}) async-start(), calls=%async_computation.9 | async-start | bytes 2949120 | tf_op jit(solution)/shard_map/all_gather | solution.py:106
  79.6 246.6 %all-reduce.10.cloned.1.call-start = ((), (), s32[]{:S(2)}) async-start(), calls=%async_computation.10 | async-start | bytes 6291456 | tf_op jit(solution)/shard_map/psum | solution.py:181
  216.6 7.7 copy-start.1
  216.6 7.7 copy-start.36
  216.6 7.7 copy-start.61
  216.6 7.7 copy-start.80
  224.4 359.8 %all-gather.14.cloned.1.call-start = ((), (), s32[]{:S(2)}) async-start(), calls=%async_computation.11 | async-start | bytes 47185920 | tf_op jit(solution)/shard_map/all_gather | solution.py:198
  239.1 575.4 %all-gather.16.cloned.1.call-start = ((), (), s32[]{:S(2)}) async-start(), calls=%async_computation.12 | async-start | bytes 31457280 | tf_op jit(solution)/shard_map/all_gather | solution.py:242
  245.7 731.3 %all-reduce.12.cloned.1.call-start = ((), (), s32[]{:S(2)}) async-start(), calls=%async_computation.13 | async-start | bytes 3145728 | tf_op jit(solution)/shard_map/psum | solution.py:248
  322.6 7.9 copy-start.44
  330.6 36.7 %copy-start.9 = (bf16[512,1536]{1,0:T(8,128)(2,1)}, bf16[512,1536]{1,0:T(8,128)(2,1)S(1)}, u32[]{:S(2)}) copy-start(bf16[512,1536]{1,0:T(8,128)(2,1)S(1)} %multiply_convert_fusion.3) | copy-start | bytes 4718596
  367.3 243.3 %copy-start.47 = (f32[16,384]{1,0:T(8,128)}, f32[16,384]{1,0:T(8,128)S(1)}, u32[]{:S(2)}) copy-start(f32[16,384]{1,0:T(8,128)S(1)} %mul.685) | copy-start | bytes 73732
  631.1 262.6 %copy-start.14 = (bf16[16,384,256]{2,1,0:T(8,128)(2,1)}, bf16[16,384,256]{2,1,0:T(8,128)(2,1)S(1)}, u32[]{:S(2)}) copy-start(bf16[16,384,256]{2,1,0:T(8,128)(2,1)S(1)} %get-tuple-element.650) | copy-start | bytes 9437188
  893.6 313.2 %reduce-scatter.14.cloned.1.call-start = ((), (), s32[]{:S(2)}) async-start(), calls=%async_computation.14 | async-start | bytes 1310720 | tf_op jit(solution)/shard_map/reduce_scatter | solution.py:311
  917.7 39.1 %copy-start.25 = (f32[512,8]{1,0:T(8,128)S(1)}, f32[512,8]{1,0:T(8,128)}, u32[]{:S(2)}) copy-start(f32[512,8]{1,0:T(8,128)} %copy-done.24) | copy-start | bytes 49156
  956.8 20.0 copy-start.43
  956.8 20.0 copy-start.60
  956.8 20.0 copy-start.64
  956.8 20.1 copy-start.52
  956.8 20.2 copy-start.5
  956.9 20.2 copy-start.45
  956.9 20.1 copy-start.54
  956.9 20.1 copy-start.66
  985.4 41.9 %copy-start.7 = (f32[512,4,3,64]{0,3,2,1:T(8,128)S(1)}, f32[512,4,3,64]{0,3,2,1:T(8,128)}, u32[]{:S(2)}) copy-start(f32[512,4,3,64]{0,3,2,1:T(8,128)} %custom-call.4) | copy-start | bytes 4718596
  1029.8 6.8 copy-start.40
  1068.1 6.8 copy-start.40
  1106.5 6.8 copy-start.40
  1144.8 6.8 copy-start.40
  1179.5 55.9 %reduce-scatter.16.cloned.1.call-start = ((), (), s32[]{:S(2)}) async-start(), calls=%async_computation.15 | async-start | bytes 1310720 | tf_op jit(solution)/shard_map/reduce_scatter | solution.py:314
  1180.1 167.2 %all-reduce.16.cloned.1.call-start = ((), (), s32[]{:S(2)}) async-start(), calls=%async_computation.23 | async-start | bytes 6291456 | tf_op jit(solution)/shard_map/psum | solution.py:217
  1236.5 6.0 copy-start.31
  1236.6 6.1 copy-start.48
  1242.6 412.6 %reduce-scatter.26.cloned.1.call-start = ((), (), s32[]{:S(2)}) async-start(), calls=%async_computation.21 | async-start | bytes 47185920
  1334.7 5.5 copy-start.12
  1334.7 5.5 copy-start.32
  1334.7 5.5 copy-start.58
  1334.7 361.5 %reduce-scatter.20.cloned.1.call-start = ((), (), s32[]{:S(2)}) async-start(), calls=%async_computation.17 | async-start | bytes 2949120 | tf_op jit(solution)/shard_map/reduce_scatter | solution.py:356
  1340.1 410.2 %reduce-scatter.18.cloned.1.call-start = ((), (), s32[]{:S(2)}) async-start(), calls=%async_computation.16 | async-start | bytes 4915200 | tf_op jit(solution)/shard_map/reduce_scatter | solution.py:353
  1344.6 462.1 %reduce-scatter.24.cloned.1.call-start = ((), (), s32[]{:S(2)}) async-start(), calls=%async_computation.20 | async-start | bytes 491520
  1347.2 466.9 %reduce-scatter.22.cloned.1.call-start = ((), (), s32[]{:S(2)}) async-start(), calls=%async_computation.19 | async-start | bytes 491520
  1350.9 835.2 %all-reduce.14.cloned.1.call-start = ((), (), s32[]{:S(2)}) async-start(), calls=%async_computation.22 | async-start | bytes 22020096 | tf_op jit(solution)/shard_map/psum | solution.py:375
  1787.7 19.9 copy-start.6
  1811.5 24.2 %copy-start.73 = (f32[2,384]{1,0:T(2,128)S(1)}, f32[2,384]{1,0:T(2,128)}, u32[]{:S(2)}) copy-start(f32[2,384]{1,0:T(2,128)} %param.32) | copy-start | bytes 9220
  1811.5 24.2 %copy-start.76 = (f32[2,384]{1,0:T(2,128)S(1)}, f32[2,384]{1,0:T(2,128)}, u32[]{:S(2)}) copy-start(f32[2,384]{1,0:T(2,128)} %param.33) | copy-start | bytes 9220
  1811.5 24.2 %copy-start.77 = (f32[2,384]{1,0:T(2,128)S(1)}, f32[2,384]{1,0:T(2,128)}, u32[]{:S(2)}) copy-start(f32[2,384]{1,0:T(2,128)} %param.34) | copy-start | bytes 9220
  1811.5 24.9 %copy-start.56 = (f32[384,16]{0,1:T(8,128)S(1)}, f32[384,16]{0,1:T(8,128)}, u32[]{:S(2)}) copy-start(f32[384,16]{0,1:T(8,128)} %param.41) | copy-start | bytes 73732
  1811.5 24.9 %copy-start.67 = (f32[384,16]{0,1:T(8,128)S(1)}, f32[384,16]{0,1:T(8,128)}, u32[]{:S(2)}) copy-start(f32[384,16]{0,1:T(8,128)} %param.42) | copy-start | bytes 73732
  1811.5 24.8 %copy-start.68 = (f32[384,16]{0,1:T(8,128)S(1)}, f32[384,16]{0,1:T(8,128)}, u32[]{:S(2)}) copy-start(f32[384,16]{0,1:T(8,128)} %param.43) | copy-start | bytes 73732
  1811.6 374.6 %copy-start.78 = (f32[3]{0:T(128)S(1)}, f32[3]{0:T(128)}, u32[]{:S(2)}) copy-start(f32[3]{0:T(128)} %constant.123.clone) | copy-start | bytes 40
  2309.0 13.3 copy-start.19
  2309.0 13.3 copy-start.35
  2322.3 6.2 copy-start.23
  2322.3 6.2 copy-start.33
  2322.3 6.2 copy-start.34
  2322.3 6.2 copy-start.41
  (50 other events, 142.2 us)
Sparse Core Ops, SparseCore 0:
  10.5 53.2 all-gather.7
  76.9 27.9 all-gather.9
  107.0 27.4 all-gather.17
  136.8 36.9 all-gather.11
  224.5 22.6 all-reduce.9
  249.7 334.4 all-gather.13
  586.8 227.6 all-gather.15
  893.8 20.4 all-reduce.11
  1179.7 27.1 reduce-scatter.13
  1209.7 25.7 reduce-scatter.15
  1242.7 21.8 all-reduce.15
  1334.8 320.3 reduce-scatter.25
  1658.8 37.3 reduce-scatter.19
  1699.7 50.5 reduce-scatter.17
  1753.5 24.4 reduce-scatter.23
  1781.2 24.4 reduce-scatter.21
  1808.9 377.2 all-reduce.13
where the time goes:
time: 2350 us; the launch traced here: 2340 us
  waiting for transfers between devices  1200 us (51%)
  local copies, waits for them, and re-layouts  524 us (22%)
  matrix products  345 us (15%)
  other arithmetic  175 us (7%)
  blocking collectives  41.5 us (2%)
  loops' own time  32.2 us (1%)
    psum x1, waiting for transfers between devices, local(): lax.psum(joint_part.astype(jnp.bfloat16), 'ctx').astype(jnp.float32)  349 us
    unnamed x20, waiting for transfers between devices  305 us
    unnamed x170, local copies, waits for them, and re-layouts  223 us
    all_gather x1, waiting for transfers between devices, local(): piece_rows = lax.all_gather(expert_low, 'fsdp', axis=0, tiled=True)  189 us
    all_gather x1, waiting for transfers between devices, local(): lax.all_gather(expert_low[:, :, 0:2], 'fsdp', axis=0, tiled=True)  183 us
    reduce_scatter x1, waiting for transfers between devices, local(): lax.psum_scatter(joint_term.astype(jnp.bfloat16), 'fsdp', scatter_dimensi...  54 us
    convert_element_type x5, other arithmetic, adamw(): return (master_new, moment_new, square_new, master_new.astype(jnp.bfloat16))  52.9 us
    dot_general x12, matrix products, block_scores(): jnp.einsum('qhgd,khd->hgqk', query_rows, key_part, preferred_element_type...  47 us
  transfers between devices with their start and end apart: 17, of which 10 were waited for; matrix products, arithmetic and copies ran while one was open for 26% of the time, Pallas kernels for 0%

commit v1 on v0

v1 whole, which is shorter than its diff:
```python
import functools
import math

import jax
import jax.numpy as jnp
from jax import lax
from jax.experimental import pallas as pl
from jax.experimental.pallas import tpu as pltpu
from jax.sharding import PartitionSpec as P

QUERY_HEADS = 24
KEY_VALUE_HEADS = 8
HEAD_SIZE = 64
GROUP = QUERY_HEADS // KEY_VALUE_HEADS
E = 16
STEP = 10
SPAN = 256
LANES = 128
BF = jnp.bfloat16
F32 = jnp.float32
NT = (((1,), (1,)), ((), ()))
TN = (((0,), (0,)), ((), ()))
VMEM_LIMIT = 58 * 1024 * 1024


def params(**more):
    return pltpu.CompilerParams(vmem_limit_bytes=VMEM_LIMIT, **more)


def inverse_rms(rows):
    return lax.rsqrt(jnp.mean(rows * rows, axis=-1, keepdims=True) + 1e-06)


def half_turn(x, inverse):
    lane = lax.broadcasted_iota(jnp.int32, x.shape, 1)
    first = (lane % HEAD_SIZE) < HEAD_SIZE // 2
    later = pltpu.roll(x, LANES - HEAD_SIZE // 2, 1)
    sooner = pltpu.roll(x, HEAD_SIZE // 2, 1)
    return jnp.where(first, later, -sooner) if inverse else jnp.where(first, -later, sooner)


def project_kernel(x_ref, gain_ref, w_ref, cos_ref, sin_ref, n_ref, q_ref, k_ref, v_ref):
    x = x_ref[...].astype(F32)
    n = (x * inverse_rms(x) * gain_ref[...]).astype(BF)
    n_ref[...] = n
    c = jnp.dot(n, w_ref[:, LANES:], preferred_element_type=F32)
    cos, sin = cos_ref[...], sin_ref[...]
    a = c[:, :LANES]
    b = c[:, LANES : 2 * LANES]
    a = a * cos + half_turn(a, False) * sin
    b = b * cos + half_turn(b, False) * sin
    scale = 1.0 / math.sqrt(HEAD_SIZE)
    a = a.astype(BF) * jnp.asarray(scale, BF)
    q_ref[0] = a[:, :HEAD_SIZE]
    q_ref[1] = a[:, HEAD_SIZE:]
    b = b.astype(BF)
    q_ref[2] = b[:, :HEAD_SIZE] * jnp.asarray(scale, BF)
    k_ref[...] = b[:, HEAD_SIZE:]
    v_ref[...] = c[:, 2 * LANES :].astype(BF)


def project(x, gain, w, cos, sin):
    rows, width = x.shape
    tile = 512
    row = lambda n: pl.BlockSpec((tile, n), lambda i: (i, 0))
    whole = lambda s: pl.BlockSpec(s, lambda i: (0, 0))
    return pl.pallas_call(
        project_kernel,
        grid=(rows // tile,),
        in_specs=[row(width), whole(gain.shape), whole(w.shape), row(LANES), row(LANES)],
        out_specs=[
            row(width),
            pl.BlockSpec((GROUP, tile, HEAD_SIZE), lambda i: (0, i, 0)),
            row(HEAD_SIZE),
            row(HEAD_SIZE),
        ],
        out_shape=[
            jax.ShapeDtypeStruct((rows, width), BF),
            jax.ShapeDtypeStruct((GROUP, rows, HEAD_SIZE), BF),
            jax.ShapeDtypeStruct((rows, HEAD_SIZE), BF),
            jax.ShapeDtypeStruct((rows, HEAD_SIZE), BF),
        ],
        compiler_params=params(),
        cost_estimate=pl.CostEstimate(
            flops=2 * rows * width * w.shape[1], bytes_accessed=rows * width * 4, transcendentals=0
        ),
    )(x, gain, w, cos, sin)


def to_row(column, eye):
    return jnp.sum(jnp.where(eye, column, 0.0), axis=0, keepdims=True)


def to_column(row, eye):
    return jnp.sum(jnp.where(eye, row, 0.0), axis=1, keepdims=True)


def identity_mask():
    return lax.broadcasted_iota(jnp.int32, (SPAN, SPAN), 0) == lax.broadcasted_iota(
        jnp.int32, (SPAN, SPAN), 1
    )


def attend_kernel(idc_ref, idr_ref, q_ref, k_ref, v_ref, o_ref, lse_ref, s_ref, m_ref, l_ref, a_ref):
    i = pl.program_id(0)
    blocks = pl.num_programs(0)
    q = q_ref[...].reshape(GROUP * SPAN, HEAD_SIZE)
    m_ref[...] = jnp.full(m_ref.shape, -1e30, F32)
    l_ref[...] = jnp.zeros(l_ref.shape, F32)
    a_ref[...] = jnp.zeros(a_ref.shape, F32)

    def place(block):
        return pl.ds(pl.multiple_of(block * SPAN, SPAN), SPAN)

    def score(block, masked):
        at = place(block)
        s = lax.dot_general(k_ref[at, :], q, NT, preferred_element_type=F32)
        if masked:
            seen = (idc_ref[at, :] <= idr_ref[...]).astype(F32)
            s = jnp.where(jnp.concatenate([seen] * GROUP, axis=1) > 0.5, s, -1e30)
        s_ref[at, :] = s
        m_ref[...] = jnp.maximum(m_ref[...], jnp.max(s, axis=0, keepdims=True))

    def weigh(block):
        at = place(block)
        p = jnp.exp(s_ref[at, :] - m_ref[...])
        l_ref[...] += jnp.sum(p, axis=0, keepdims=True)
        a_ref[...] += lax.dot_general(p.astype(BF), v_ref[at, :], TN, preferred_element_type=F32)

    def open_score(block, carried):
        score(block, False)
        return carried

    def open_weigh(block, carried):
        weigh(block)
        return carried

    lax.fori_loop(0, i, open_score, 0)
    score(i, True)

    @pl.when(i + 1 < blocks)
    def _():
        score(i + 1, True)

    lax.fori_loop(0, jnp.minimum(i + 2, blocks), open_weigh, 0)

    total = l_ref[...]
    lse = m_ref[...] + jnp.log(total)
    eye = identity_mask()
    for g in range(GROUP):
        part = slice(g * SPAN, (g + 1) * SPAN)
        out = a_ref[part, :] / to_column(total[:, part], eye)
        o_ref[:, g * HEAD_SIZE : (g + 1) * HEAD_SIZE] = out.astype(BF)
        lse_ref[g] = lse[:, part]


def attend(id_column, id_row, q, k, v):
    rows = k.shape[0]
    whole = lambda s: pl.BlockSpec(s, lambda i: (0,) * len(s))
    return pl.pallas_call(
        attend_kernel,
        grid=(rows // SPAN,),
        in_specs=[
            whole(id_column.shape),
            pl.BlockSpec((1, SPAN), lambda i: (0, i)),
            pl.BlockSpec((GROUP, SPAN, HEAD_SIZE), lambda i: (0, i, 0)),
            whole(k.shape),
            whole(v.shape),
        ],
        out_specs=[
            pl.BlockSpec((SPAN, GROUP * HEAD_SIZE), lambda i: (i, 0)),
            pl.BlockSpec((GROUP, 1, SPAN), lambda i: (0, 0, i)),
        ],
        out_shape=[
            jax.ShapeDtypeStruct((rows, GROUP * HEAD_SIZE), BF),
            jax.ShapeDtypeStruct((GROUP, 1, rows), F32),
        ],
        scratch_shapes=[
            pltpu.VMEM((rows, GROUP * SPAN), F32),
            pltpu.VMEM((1, GROUP * SPAN), F32),
            pltpu.VMEM((1, GROUP * SPAN), F32),
            pltpu.VMEM((GROUP * SPAN, HEAD_SIZE), F32),
        ],
        compiler_params=params(),
        cost_estimate=pl.CostEstimate(
            flops=20 * 1000**3, bytes_accessed=6 * rows * 256, transcendentals=rows * rows
        ),
    )(id_column, id_row, q, k, v)


def attend_back_kernel(
    idc_ref, idr_ref, q_ref, k_ref, v_ref, o_ref, do_ref, lse_ref, dq_ref, dk_ref, dv_ref, a_ref
):
    i = pl.program_id(0)
    blocks = pl.num_programs(0)

    @pl.when(i == 0)
    def _():
        dk_ref[...] = jnp.zeros(dk_ref.shape, F32)
        dv_ref[...] = jnp.zeros(dv_ref.shape, F32)

    q = q_ref[...].reshape(GROUP * SPAN, HEAD_SIZE)
    eye = identity_mask()
    grads, deltas = [], []
    for g in range(GROUP):
        lanes = slice(g * HEAD_SIZE, (g + 1) * HEAD_SIZE)
        part = do_ref[:, lanes]
        grads.append(part)
        product = part.astype(F32) * o_ref[:, lanes].astype(F32)
        deltas.append(to_row(jnp.sum(product, axis=1, keepdims=True), eye))
    do = jnp.concatenate(grads, axis=0)
    delta = jnp.concatenate(deltas, axis=1)
    lse = jnp.concatenate([lse_ref[g] for g in range(GROUP)], axis=1)
    a_ref[...] = jnp.zeros(a_ref.shape, F32)

    def step(block, masked):
        at = pl.ds(pl.multiple_of(block * SPAN, SPAN), SPAN)
        k = k_ref[at, :]
        s = lax.dot_general(k, q, NT, preferred_element_type=F32)
        p = jnp.exp(s - lse)
        if masked:
            seen = idc_ref[at, :] <= idr_ref[...]
            p = jnp.where(jnp.concatenate([seen.astype(F32)] * GROUP, axis=1) > 0.5, p, 0.0)
        dp = lax.dot_general(v_ref[at, :], do, NT, preferred_element_type=F32)
        ds = (p * (dp - delta)).astype(BF)
        dv_ref[at, :] += jnp.dot(p.astype(BF), do, preferred_element_type=F32)
        dk_ref[at, :] += jnp.dot(ds, q, preferred_element_type=F32)
        a_ref[...] += lax.dot_general(ds, k, TN, preferred_element_type=F32)

    def open_step(block, carried):
        step(block, False)
        return carried

    lax.fori_loop(0, i, open_step, 0)
    step(i, True)

    @pl.when(i + 1 < blocks)
    def _():
        step(i + 1, True)

    dq_ref[...] = a_ref[...].reshape(GROUP, SPAN, HEAD_SIZE) * (1.0 / math.sqrt(HEAD_SIZE))


def attend_back(id_column, id_row, q, k, v, o, do, lse):
    rows = k.shape[0]
    whole = lambda s: pl.BlockSpec(s, lambda i: (0,) * len(s))
    heads = pl.BlockSpec((GROUP, SPAN, HEAD_SIZE), lambda i: (0, i, 0))
    flat = pl.BlockSpec((SPAN, GROUP * HEAD_SIZE), lambda i: (i, 0))
    return pl.pallas_call(
        attend_back_kernel,
        grid=(rows // SPAN,),
        in_specs=[
            whole(id_column.shape),
            pl.BlockSpec((1, SPAN), lambda i: (0, i)),
            heads,
            whole(k.shape),
            whole(v.shape),
            flat,
            flat,
            pl.BlockSpec((GROUP, 1, SPAN), lambda i: (0, 0, i)),
        ],
        out_specs=[heads, whole(k.shape), whole(v.shape)],
        out_shape=[
            jax.ShapeDtypeStruct((GROUP, rows, HEAD_SIZE), F32),
            jax.ShapeDtypeStruct(k.shape, F32),
            jax.ShapeDtypeStruct(v.shape, F32),
        ],
        scratch_shapes=[pltpu.VMEM((GROUP * SPAN, HEAD_SIZE), F32)],
        compiler_params=params(),
        cost_estimate=pl.CostEstimate(
            flops=40 * 1000**3, bytes_accessed=12 * rows * 256, transcendentals=rows * rows
        ),
    )(id_column, id_row, q, k, v, o, do, lse)


def turn_back_kernel(dq_ref, dk_ref, dv_ref, cos_ref, sin_ref, out_ref):
    cos, sin = cos_ref[...], sin_ref[...]
    a = jnp.concatenate([dq_ref[0], dq_ref[1]], axis=1)
    b = jnp.concatenate([dq_ref[2], dk_ref[...]], axis=1)
    out_ref[:, :LANES] = (a * cos + half_turn(a, True) * sin).astype(BF)
    out_ref[:, LANES : 2 * LANES] = (b * cos + half_turn(b, True) * sin).astype(BF)
    out_ref[:, 2 * LANES :] = dv_ref[...].astype(BF)


def turn_back(dq, dk, dv, cos, sin):
    rows = dk.shape[0]
    tile = 512
    row = lambda n: pl.BlockSpec((tile, n), lambda i: (i, 0))
    columns = (GROUP + 2) * HEAD_SIZE
    return pl.pallas_call(
        turn_back_kernel,
        grid=(rows // tile,),
        in_specs=[
            pl.BlockSpec((GROUP, tile, HEAD_SIZE), lambda i: (0, i, 0)),
            row(HEAD_SIZE),
            row(HEAD_SIZE),
            row(LANES),
            row(LANES),
        ],
        out_specs=row(columns),
        out_shape=jax.ShapeDtypeStruct((rows, columns), BF),
        compiler_params=params(),
    )(dq, dk, dv, cos, sin)


def expert_kernel(count, at_ref, x_ref, c_ref, r_ref, w_ref, pre_ref, wh_ref, out_ref, grad_ref):
    width = x_ref.shape[1]
    hidden_columns = wh_ref.shape[1]
    units = hidden_columns // count
    x = x_ref[...]
    cot = c_ref[:, :width]
    named = c_ref[:, width:].astype(F32) > 0.5
    logits = jnp.where(named, jnp.dot(x, r_ref[...], preferred_element_type=F32), -1e30)
    top = jnp.max(logits, axis=1, keepdims=True)
    exponent = jnp.where(named, jnp.exp(logits - top), 0.0)
    gates = exponent / jnp.sum(exponent, axis=1, keepdims=True)
    lane = lax.broadcasted_iota(jnp.int32, gates.shape, 1)
    first = at_ref[0]
    found = jnp.zeros(gates.shape, F32)
    for e in range(count):
        cols = slice(e * units, (e + 1) * units)
        up_cols = slice(hidden_columns + e * units, hidden_columns + (e + 1) * units)
        down_cols = slice(2 * hidden_columns + e * units, 2 * hidden_columns + (e + 1) * units)
        mine = lane == first + e
        gate_here = jnp.sum(jnp.where(mine, gates, 0.0), axis=1, keepdims=True)
        g = jnp.dot(x, w_ref[:, cols], preferred_element_type=F32)
        u = jnp.dot(x, w_ref[:, up_cols], preferred_element_type=F32)
        hg = jnp.dot(cot, w_ref[:, down_cols], preferred_element_type=F32)
        s = 1.0 / (1.0 + jnp.exp(-g))
        gs = g * s
        h = (gs * u).astype(BF).astype(F32)
        found = found + jnp.where(mine, jnp.sum(h * hg, axis=1, keepdims=True), 0.0)
        wh_ref[:, cols] = (h * gate_here).astype(BF)
        hg = hg * gate_here
        pre_ref[:, cols] = (hg * u * s * (1.0 + g * (1.0 - s))).astype(BF)
        pre_ref[:, up_cols] = (hg * gs).astype(BF)
    grad_ref[:, width:] = found.astype(BF)
    grad_ref[:, :width] = lax.dot_general(
        pre_ref[...], w_ref[:, : 2 * hidden_columns], NT, preferred_element_type=F32
    ).astype(BF)
    out_ref[...] = lax.dot_general(
        wh_ref[...], w_ref[:, 2 * hidden_columns :], NT, preferred_element_type=F32
    ).astype(BF)


def experts(first, x, c, router, w, count):
    rows, width = x.shape
    tile = 256
    hidden_columns = w.shape[1] // 3
    row = lambda n: pl.BlockSpec((tile, n), lambda i: (i, 0))
    whole = lambda s: pl.BlockSpec(s, lambda i: (0, 0), pipeline_mode=pl.Buffered(1))
    return pl.pallas_call(
        functools.partial(expert_kernel, count),
        grid=(rows // tile,),
        in_specs=[
            pl.BlockSpec(memory_space=pltpu.SMEM),
            row(width),
            row(c.shape[1]),
            whole(router.shape),
            whole(w.shape),
        ],
        out_specs=[row(2 * hidden_columns), row(hidden_columns), row(width), row(c.shape[1])],
        out_shape=[
            jax.ShapeDtypeStruct((rows, 2 * hidden_columns), BF),
            jax.ShapeDtypeStruct((rows, hidden_columns), BF),
            jax.ShapeDtypeStruct((rows, width), BF),
            jax.ShapeDtypeStruct((rows, c.shape[1]), BF),
        ],
        compiler_params=params(),
        cost_estimate=pl.CostEstimate(
            flops=4 * rows * width * w.shape[1],
            bytes_accessed=2 * w.size + rows * 20000,
            transcendentals=rows * hidden_columns,
        ),
    )(first, x, c, router, w)


def adamw(master, first_moment, second_moment, gradient, rate, decay):
    moment_new = 0.9 * first_moment + 0.1 * gradient
    square_new = 0.95 * second_moment + 0.05 * gradient * gradient
    corrected = moment_new / (1.0 - 0.9**STEP) / (jnp.sqrt(square_new / (1.0 - 0.95**STEP)) + 1e-08)
    master_new = master - rate * (corrected + decay * master)
    return (master_new, moment_new, square_new, master_new.astype(BF))


def expert_adamw_kernel(rate, parts, chained, joined, *refs):
    p_ref, f_ref, s_ref, g_ref = refs[:4]
    master_ref, moment_ref, rounded_ref, square_ref = refs[-4:]
    each = E // parts
    pack = max(1, 8 // each)
    for at in range(0, parts, pack):
        rows = slice(at * each, (at + pack) * each)
        grad = jnp.concatenate([g_ref[k].astype(F32) for k in range(at, at + pack)], axis=1)
        new = adamw(p_ref[:, 0, rows], f_ref[:, 0, rows], s_ref[:, 0, rows], grad, rate, 0.1)
        master_ref[:, 0, rows] = new[0]
        moment_ref[:, 0, rows] = new[1]
        rounded_ref[:, 0, rows] = new[3]
        if joined:
            square_ref[:, rows, 0] = refs[4][:, rows]
            square_ref[:, rows, 1] = new[2]
        else:
            square_ref[:, rows] = new[2]


def expert_adamw(slot, rate, weight, first, second, gradient, earlier, joined=None):
    rows, _, count, units = weight.shape
    parts = gradient.shape[0]
    tile = next(t for t in (32, 16, 8) if rows % t == 0)
    here = pl.BlockSpec((tile, 1, count, units), lambda i: (i, slot, 0, 0))
    plain = pl.BlockSpec((tile, count, units), lambda i: (i, 0, 0))
    pair = pl.BlockSpec((tile, count, 2, units), lambda i: (i, 0, 0, 0))
    shape = jax.ShapeDtypeStruct(weight.shape, F32)
    chained = len(earlier)
    more = [] if joined is None else [joined]
    square = (rows, count, units) if joined is None else (rows, count, 2, units)
    return pl.pallas_call(
        functools.partial(expert_adamw_kernel, rate, parts, chained, joined is not None),
        grid=(rows // tile,),
        in_specs=[here, here, here]
        + [pl.BlockSpec((parts, tile, count // parts, units), lambda i: (0, i, 0, 0))]
        + [plain] * len(more)
        + [pl.BlockSpec(memory_space=pl.ANY)] * chained,
        out_specs=[here, here, here, plain if joined is None else pair],
        out_shape=[
            shape,
            shape,
            jax.ShapeDtypeStruct(weight.shape, BF),
            jax.ShapeDtypeStruct(square, F32),
        ],
        input_output_aliases={4 + len(more) + k: k for k in range(chained)},
        compiler_params=params(),
        cost_estimate=pl.CostEstimate(
            flops=20 * rows * count * units,
            bytes_accessed=28 * rows * count * units,
            transcendentals=rows * count * units,
        ),
    )(weight, first, second, gradient, *more, *earlier)


def local(
    sizes,
    block_input,
    out_cotangent,
    block_ids,
    expert_routes,
    norm_gains,
    gains_first,
    gains_second,
    joint_weight,
    joint_first,
    joint_second,
    output_weight,
    output_first,
    output_second,
    router_weight,
    router_first,
    router_second,
    expert_weight,
    expert_first,
    expert_second,
):
    n_fsdp, n_ctx, n_tp = sizes
    z = lax.axis_index("ctx")
    t = lax.axis_index("tp")
    f = lax.axis_index("fsdp")
    tokens_low = block_input[0]
    cot_low = out_cotangent[0]
    count, width = tokens_low.shape
    half = count // n_tp
    length = n_ctx * count
    tokens = tokens_low.astype(F32)
    cotangent = cot_low.astype(F32)
    own_rows = width // n_fsdp
    each = E // n_ctx

    barrier = lax.optimization_barrier

    def beyond(x, m):
        return lax.ppermute(x, "ctx", [(i, i ^ m) for i in range(n_ctx)])

    def swap(x):
        return lax.ppermute(x, "tp", [(0, 1), (1, 0)])

    def across(x, m):
        return lax.ppermute(x, "fsdp", [(i, i ^ m) for i in range(n_fsdp)])

    def mine(x):
        return lax.dynamic_slice_in_dim(x, t * half, half, 0)

    def other(x):
        return lax.dynamic_slice_in_dim(x, (1 - t) * half, half, 0)

    def in_order(a, b):
        return jnp.where(t == 0, jnp.concatenate([a, b], 0), jnp.concatenate([b, a], 0))

    def put(buffer, x, row):
        return lax.dynamic_update_slice_in_dim(buffer, x, row, 0)

    def take(x, row, rows):
        return lax.dynamic_slice_in_dim(x, row, rows, 0)

    def gather_fsdp(x):
        if n_fsdp != 4:
            full = lax.all_gather(x, "fsdp", axis=0, tiled=True)
            return full, full
        rows = x.shape[0]
        cut = rows // 2
        a, b = across(x, 1), across(x, 2)
        c, d = across(a[:cut], 2), across(b[cut:], 1)
        full = jnp.zeros((n_fsdp * rows, x.shape[1]), x.dtype)
        full = put(full, x, f * rows)
        full = put(full, a, (f ^ 1) * rows)
        full = put(full, b, (f ^ 2) * rows)
        full = put(full, c, (f ^ 3) * rows)
        return put(full, d, (f ^ 3) * rows + cut), c

    def scatter_fsdp(x, axis):
        if n_fsdp != 4:
            return lax.psum_scatter(x, "fsdp", scatter_dimension=axis, tiled=True)
        piece = lambda k: lax.dynamic_slice_in_dim(x, k * own_rows, own_rows, axis)
        total = piece(f).astype(F32)
        for m in (3, 1, 2):
            total = total + across(piece(f ^ m), m).astype(F32)
        return total.astype(BF)

    def spread(x):
        one, two = beyond(x, 1), beyond(x, 2)
        return {1: one, 2: two, 3: beyond(two, 1)}

    joint_columns = joint_weight.shape[1]
    group_columns = (GROUP + 2) * HEAD_SIZE
    joint_low = joint_weight.astype(BF)
    first_pack = jnp.concatenate(
        [
            router_weight.astype(BF),
            norm_gains.T.astype(BF),
            jnp.zeros((own_rows, LANES - E - 2), BF),
            lax.dynamic_slice_in_dim(joint_low, z * group_columns, group_columns, 1),
        ],
        axis=1,
    )
    first_full, first_came = gather_fsdp(first_pack)
    small_full = first_full[:, :LANES]
    router_full = small_full[:, :E]
    router_wide = jnp.where(jnp.arange(LANES)[None, :] < E, small_full, jnp.zeros((), BF))
    gain_first = small_full[:, E].astype(F32)[None, :]
    gain_second = small_full[:, E + 1].astype(F32)[None, :]

    tokens_came = spread(mine(tokens_low))
    sequence = put(jnp.zeros((length, width), BF), tokens_low, z * count)
    for m in (1, 2, 3):
        base = (z ^ m) * count
        sequence = put(sequence, tokens_came[m], base + t * half)
        sequence = put(sequence, swap(tokens_came[m]), base + (1 - t) * half)

    slots_first = jnp.transpose(expert_weight, (0, 2, 1, 3))
    units = expert_weight.shape[3]
    output_low, _ = barrier((output_weight.astype(BF), first_came))
    output_full, output_came = gather_fsdp(output_low)
    expert_part = (
        lax.dynamic_slice_in_dim(slots_first, z * each, each, 2)
        .astype(BF)
        .reshape(own_rows, 3 * each * units)
    )
    expert_part, _ = barrier((expert_part, output_came))
    expert_full = lax.all_gather(expert_part, "fsdp", axis=0, tiled=True)
    joint_late, _ = barrier((joint_low, expert_full))
    joint_full, _ = gather_fsdp(joint_late)
    output_turned = barrier(output_full.T)
    joint_turned = barrier(joint_full.T)

    route_rows = expert_routes[0]
    member = jnp.sum(
        (route_rows[:, :, None] == jnp.arange(LANES, dtype=jnp.int32)[None, None, :]).astype(F32),
        axis=1,
    )
    cot_pack = jnp.concatenate([cot_low, member.astype(BF)], axis=1)
    cot_half, _ = barrier((mine(cot_pack), tokens_came[3]))
    cot_came = spread(cot_half)

    positions = jnp.arange(length, dtype=jnp.int32).astype(F32)
    lanes = jnp.arange(LANES, dtype=jnp.int32) % (HEAD_SIZE // 2)
    frequency = jnp.exp(lanes.astype(F32) * (-2.0 * math.log(10000.0) / HEAD_SIZE))
    angles = positions[:, None] * frequency[None, :]
    cosine, sine = jnp.cos(angles), jnp.sin(angles)
    id_row = block_ids
    id_column = block_ids.reshape(length, 1)
    normed_all, queries, keys, values = project(sequence, gain_first, first_full, cosine, sine)
    attended_all, lse = attend(id_column, id_row, queries, keys, values)
    head_columns = GROUP * HEAD_SIZE

    def to_positions(x):
        parts = [take(x, (z ^ m) * count, count) for m in range(n_ctx)]
        return [parts[0]] + [beyond(parts[m], m) for m in range(1, n_ctx)]

    def by_heads(turned, columns):
        return [take(turned, (z ^ m) * columns, columns) for m in range(n_ctx)]

    output_by = by_heads(output_turned, head_columns)
    attended = to_positions(attended_all)
    attn_part = sum(
        jnp.dot(a, w, preferred_element_type=F32) for a, w in zip(attended, output_by)
    )
    attn_part, cot_came = barrier((attn_part, cot_came))
    residual = tokens + (attn_part + swap(attn_part))
    inv_second = inverse_rms(residual)
    normed_second = (residual * inv_second * gain_second).astype(BF)

    normed_half = mine(normed_second)
    came = spread(normed_half)
    first_expert = jnp.reshape(z * each, (1,)).astype(jnp.int32)
    x_chunks, cot_chunks, pre_chunks, hidden_chunks, outs = {}, {}, {}, {}, {}
    grad_sum = None
    for m in range(n_ctx):
        if m == 0:
            x_chunks[0] = jnp.concatenate([normed_half, other(normed_second)], axis=0)
            cot_chunks[0] = jnp.concatenate([mine(cot_pack), other(cot_pack)], axis=0)
        else:
            got, pre_chunks[m - 1] = barrier((came[m], pre_chunks[m - 1]))
            x_chunks[m] = jnp.concatenate([got, swap(got)], axis=0)
            cot_chunks[m] = jnp.concatenate([cot_came[m], swap(cot_came[m])], axis=0)
        pre_chunks[m], hidden_chunks[m], out_part, grad_part = experts(
            first_expert, x_chunks[m], cot_chunks[m], router_wide, expert_full, each
        )
        grad_here = grad_part[:half].astype(F32) + swap(grad_part[half:]).astype(F32)
        outs[m] = out_part[:half].astype(F32) + swap(out_part[half:]).astype(F32)
        if m == 0:
            grad_sum = grad_here
        else:
            grad_sum = grad_sum + beyond(grad_here.astype(BF), m).astype(F32)
    grad_low = grad_sum.astype(BF)
    grad_rows = in_order(grad_low, swap(grad_low)).astype(F32)
    moe_input = grad_rows[:, :width]
    gate_grads = grad_rows[:, width : width + E]

    x_all = jnp.concatenate([x_chunks[m] for m in range(n_ctx)], axis=0)
    cot_all = jnp.concatenate([cot_chunks[m][:, :width] for m in range(n_ctx)], axis=0)
    pre_all = jnp.concatenate([pre_chunks[m] for m in range(n_ctx)], axis=0)
    hidden_all = jnp.concatenate([hidden_chunks[m] for m in range(n_ctx)], axis=0)
    wide = each * units
    terms = {
        2: lax.dot_general(cot_all, hidden_all, TN, preferred_element_type=F32),
        0: lax.dot_general(x_all, pre_all[:, :wide], TN, preferred_element_type=F32),
        1: lax.dot_general(x_all, pre_all[:, wide:], TN, preferred_element_type=F32),
    }
    expert_sums = {}
    for j in (2, 0, 1):
        owned = scatter_fsdp(terms[j].astype(BF), 0).reshape(own_rows, each, units)
        expert_sums[j] = lax.all_gather(owned, "ctx", axis=0, tiled=False)

    named = member[:, :E]
    logits = jnp.dot(normed_second, router_full, preferred_element_type=F32)
    masked = jnp.where(named > 0.5, logits, -1e30)
    exponent = jnp.where(
        named > 0.5, jnp.exp(masked - jnp.max(masked, axis=1, keepdims=True)), 0.0
    )
    gates = exponent / jnp.sum(exponent, axis=1, keepdims=True)
    logit_grads = (
        gates * (gate_grads - jnp.sum(gates * gate_grads, axis=1, keepdims=True))
    ).astype(BF)
    norm_second_grads = moe_input + lax.dot_general(
        logit_grads, router_full, NT, preferred_element_type=F32
    )
    scaled_second = gain_second * norm_second_grads
    cube_second = inv_second * inv_second * inv_second / width
    residual_grads = (
        cotangent
        + inv_second * scaled_second
        - residual * cube_second * jnp.sum(scaled_second * residual, axis=1, keepdims=True)
    )
    gain_second_grad = jnp.sum(norm_second_grads * residual * inv_second, axis=0, keepdims=True)
    residual_low = residual_grads.astype(BF)

    attended_grads_all = jnp.zeros((length, head_columns), BF)
    for m in range(n_ctx):
        part = lax.dot_general(
            residual_low, output_by[m], NT, preferred_element_type=F32
        ).astype(BF)
        got = part if m == 0 else beyond(part, m)
        attended_grads_all = put(attended_grads_all, got, (z ^ m) * count)
    dq, dk, dv = attend_back(
        id_column, id_row, queries, keys, values, attended_all, attended_grads_all, lse
    )
    joint_grads_all = turn_back(dq, dk, dv, cosine, sine)
    joint_grads = to_positions(joint_grads_all)
    first_part = sum(
        jnp.dot(g, w, preferred_element_type=F32)
        for g, w in zip(joint_grads, by_heads(joint_turned, group_columns))
    ).astype(BF)
    norm_first_grads = first_part.astype(F32) + swap(first_part).astype(F32)
    inv_first = inverse_rms(tokens)
    scaled_first = gain_first * norm_first_grads
    cube_first = inv_first * inv_first * inv_first / width
    input_rows = (
        residual_grads
        + inv_first * scaled_first
        - tokens * cube_first * jnp.sum(scaled_first * tokens, axis=1, keepdims=True)
    )
    gain_first_grad = jnp.sum(norm_first_grads * tokens * inv_first, axis=0, keepdims=True)

    late = [outs[m].astype(BF) for m in range(1, n_ctx)]
    late, attended_grads_all = barrier((late, attended_grads_all))
    moe_two = late[1].astype(F32) + beyond(late[2], 1).astype(F32)
    moe_sum = (
        outs[0] + beyond(late[0], 1).astype(F32) + beyond(moe_two.astype(BF), 2).astype(F32)
    )
    moe_low = moe_sum.astype(BF)
    moe_rows = in_order(moe_low, swap(moe_low)).astype(F32)
    block_output = (residual + moe_rows).astype(BF)[None]

    joint_term = lax.dot_general(joint_grads_all, normed_all, TN, preferred_element_type=F32)
    joint_owned = scatter_fsdp(joint_term.astype(BF), 1)
    joint_sum = jnp.zeros((n_ctx * group_columns, own_rows), BF)
    for m, got in {0: joint_owned, **spread(joint_owned)}.items():
        joint_sum = put(joint_sum, got, (z ^ m) * group_columns)
    joint_sum = joint_sum.T.astype(F32)

    def summed_over_ctx(owned):
        part = owned.shape[0] // n_ctx
        total = take(owned, z * part, part).astype(F32)
        for m in range(1, n_ctx):
            total = total + beyond(take(owned, (z ^ m) * part, part), m).astype(F32)
        total = total.astype(BF)
        full = put(jnp.zeros(owned.shape, BF), total, z * part)
        for m, got in spread(total).items():
            full = put(full, got, (z ^ m) * part)
        return full

    output_columns = output_weight.shape[1]
    rest_term = jnp.zeros((output_columns + 64, width), BF)
    for m in range(n_ctx):
        term = lax.dot_general(attended[m], residual_low, TN, preferred_element_type=F32)
        rest_term = put(rest_term, term.astype(BF), (z ^ m) * head_columns)
    router_term = lax.dot_general(logit_grads, normed_second, TN, preferred_element_type=F32)
    few_rows = jnp.concatenate(
        [router_term, gain_second_grad, jnp.zeros((64 - E - 1, width), F32)], axis=0
    )
    rest_term = put(rest_term, few_rows.astype(BF), output_columns)
    rest_full = summed_over_ctx(scatter_fsdp(rest_term, 1))
    output_sum = rest_full[:output_columns].T.astype(F32)
    router_sum = rest_full[output_columns : output_columns + E].T.astype(F32)
    last_term = jnp.concatenate([gain_first_grad, jnp.zeros((15, width), F32)], axis=0)
    last_owned = scatter_fsdp(last_term.astype(BF), 1)
    last_sum = last_owned.astype(F32)
    for m in range(1, n_ctx):
        last_sum = last_sum + beyond(last_owned, m).astype(F32)
    gains_sum = jnp.concatenate(
        [
            last_sum[:1],
            rest_full[output_columns + E : output_columns + E + 1].astype(F32),
        ],
        axis=0,
    )

    gains_new = adamw(norm_gains, gains_first, gains_second, gains_sum, 0.6, 0.0)
    joint_new = adamw(joint_weight, joint_first, joint_second, joint_sum, 0.03, 0.1)
    output_new = adamw(output_weight, output_first, output_second, output_sum, 0.25, 0.1)
    router_new = adamw(router_weight, router_first, router_second, router_sum, 0.015, 0.1)

    first_view = jnp.transpose(expert_first, (0, 2, 1, 3))
    second_view = jnp.transpose(expert_second, (0, 2, 1, 3))
    made = ()
    squares = {}
    for j in (2, 0, 1):
        *made, squares[j] = expert_adamw(
            j,
            0.25 if j == 2 else 0.03,
            slots_first,
            first_view,
            second_view,
            expert_sums[j],
            tuple(made),
            squares[0] if j == 1 else None,
        )
    back = lambda x: jnp.transpose(x, (0, 2, 1, 3))
    return (
        block_output,
        input_rows[None],
        *gains_new,
        *joint_new,
        *output_new,
        *router_new,
        back(made[0]),
        back(made[1]),
        squares[1],
        squares[2],
        back(made[2]),
    )


def solution(mesh):
    rows = P("fsdp", "ctx", None)
    gains = P(None, "fsdp")
    matrix = P("fsdp", "tp")
    router = P("fsdp", None)
    expert = P("fsdp", None, None, "tp")
    sizes = (mesh.shape["fsdp"], mesh.shape["ctx"], mesh.shape["tp"])
    return jax.shard_map(
        functools.partial(local, sizes),
        mesh=mesh,
        in_specs=(rows, rows, P("fsdp", None), rows)
        + (gains,) * 3
        + (matrix,) * 6
        + (router,) * 3
        + (expert,) * 3,
        out_specs=(rows, rows)
        + (gains,) * 4
        + (matrix,) * 8
        + (router,) * 4
        + (expert, expert, expert, P("fsdp", None, "tp"), expert),
        check_vma=False,
    )
```

time: 2350 us -> 1050 us (0.45)
  waiting for transfers between devices: 1200 us -> 309 us
  local copies, waits for them, and re-layouts: 524 us -> 175 us
  matrix products: 345 us -> 69.3 us
  Pallas kernels: 0 us -> 217 us
  starting transfers between devices: 1.73 us -> 162 us
  other arithmetic: 175 us -> 90.5 us
  blocking collectives: 41.5 us -> 0 us
  loops' own time: 32.2 us -> 0 us
    all_gather x6 -> x4, waiting for transfers between devices: 437 us -> 0.01 us  [the longest x3 0.01 us: local(): expert_sums[j] = lax.all_gather(owned, 'ctx', axis=0, tiled=False)]
    psum x4 -> x0, waiting for transfers between devices: 349 us -> none  [the longest x1 349 us: local(): lax.psum(joint_part.astype(jnp.bfloat16), 'ctx').astype(jnp.float32)]
    ppermute x0 -> x87, waiting for transfers between devices: none -> 309 us  [the longest x36 218 us: beyond(): return lax.ppermute(x, 'ctx', [(i, i ^ m) for i in range(n_ctx)])]
    unnamed x20 -> x4, waiting for transfers between devices: 305 us -> 0.07 us
    dot_general x51 -> x23, matrix products: 345 us -> 69.3 us  [the longest x1 12.4 us: local(): lax.dot_general(cot_all, hidden_all, TN, preferred_element_type=F32)]
    pallas_call x0 -> x11, Pallas kernels: none -> 217 us  [the longest x4 66.1 us: experts(): pl.pallas_call(functools.partial(expert_kernel, count), grid=(rows // til...]
    unnamed x170 -> x198, local copies, waits for them, and re-layouts: 223 us -> 51 us
    gather x5 -> x0, local copies, waits for them, and re-layouts: 168 us -> none  [the longest x1 39.1 us: local(): picked = expert_out[slot_ids]]
  transfers between devices with their start and end apart: 17 -> 91, of which waited for: 10 -> 27; matrix products, arithmetic and copies ran while one was open for 26% -> 30% of each run, Pallas kernels for 0% -> 18%
where the time goes in v1:
time: 1050 us; the launch traced here: 1040 us
  waiting for transfers between devices  309 us (29%)
  Pallas kernels  217 us (21%)
  local copies, waits for them, and re-layouts  175 us (17%)
  starting transfers between devices  162 us (15%)
  other arithmetic  90.5 us (9%)
  matrix products  69.3 us (7%)
  between operations  15.5 us (1%)
    ppermute x36, waiting for transfers between devices, beyond(): return lax.ppermute(x, 'ctx', [(i, i ^ m) for i in range(n_ctx)])  218 us
    ppermute x36, starting transfers between devices, beyond(): return lax.ppermute(x, 'ctx', [(i, i ^ m) for i in range(n_ctx)])  123 us
    ppermute x30, waiting for transfers between devices, across(): return lax.ppermute(x, 'fsdp', [(i, i ^ m) for i in range(n_fsdp)])  90.1 us
    pallas_call x4, Pallas kernels, experts(): pl.pallas_call(functools.partial(expert_kernel, count), grid=(rows // til...  66.1 us
    pallas_call x3, Pallas kernels, expert_adamw(): pl.pallas_call(functools.partial(expert_adamw_kernel, rate, parts, chaine...  65.9 us
    unnamed x198, local copies, waits for them, and re-layouts  51 us
    dynamic_update_slice x32, local copies, waits for them, and re-layouts, put(): return lax.dynamic_update_slice_in_dim(buffer, x, row, 0)  40.2 us
    pallas_call x1, Pallas kernels, attend_back(): pl.pallas_call(attend_back_kernel, grid=(rows // SPAN,), in_specs=[whole(...  37.2 us
  transfers between devices with their start and end apart: 91, of which 27 were waited for; matrix products, arithmetic and copies ran while one was open for 30% of the time, Pallas kernels for 18%

profile of v1, /device:TPU:0, one launch (start us, length us, event | category | flops | bytes accessed | tf_op | source)
XLA Modules:
  0.0 1037.5 jit_solution(2450208261877605392)
XLA Ops:
  13.2 2.9 collective-permute-start.6
  16.1 9.3 collective-permute-done.6
  28.1 4.2 collective-permute-done.8
  33.7 12.2 %collective-permute-done.10 = bf16[384,768]{1,0:T(8,128)(2,1)S(1)} collective-permute-done((bf16[384,768]{1,0:T(8,128)(2,1)S(1)}, bf16[384,768]{1,0:T(8,128)(2,1)S(1)}, u32[]{:S(2)}, u32[]{:S(2)}) %collective-permute-start.10) | collective-permute-done | bytes 589856 | tf_op jit(solution)/shard_map/ppermute | solution.py:485
  47.9 4.6 fusion.45
  52.5 2.9 reshape.139
  63.4 5.5 multiply_sine_fusion
  69.0 3.1 broadcast_in_dim.77
  73.3 2.9 convert_reduce_fusion
  86.4 6.0 collective-permute-done.2
  99.4 8.6 collective-permute-done.11
  110.9 3.3 collective-permute-start.18
  120.0 9.9 shard_map.362
  130.0 32.1 %shard_map.363 = (bf16[2048,192]{1,0:T(8,128)(2,1)}, f32[3,1,2048]{2,1,0:T(1,128)}) custom-call(s32[2048,1]{1,0:T(8,128)} %copy.154.idc_ref, s32[1,2048]{1,0:T(1,128)} %idr_ref.3, bf16[3,2048,64]{2,1,0:T(8,128)(2,1)} %get-tuple-element.77.q_ref, bf16[2048,64]{1,0:T(8,128)(2,1)} %get-tuple-element.78.k_ref, bf16[2048,64]{1,0:T(8,128)(2,1)} %get-tuple-element.79.v_ref), custom_call_target="tpu_custom_call" | custom-call | flops 20000000000 | bytes 3145728 | tf_op jit(solution)/shard_map/pallas_call | solution.py:160
  165.7 3.9 collective-permute-start.16
  169.6 8.4 collective-permute-done.14
  181.2 20.4 %collective-permute-done.16 = bf16[512,192]{1,0:T(8,128)(2,1)S(1)} collective-permute-done((bf16[512,192]{1,0:T(8,128)(2,1)S(1)}, bf16[512,192]{1,0:T(8,128)(2,1)S(1)}, u32[]{:S(2)}, u32[]{:S(2)}) %collective-permute-start.16) | collective-permute-done | bytes 196640 | tf_op jit(solution)/shard_map/ppermute | solution.py:479
  203.1 16.8 %collective-permute-done.19 = bf16[256,1664]{1,0:T(8,128)(2,1)} collective-permute-done((bf16[256,1664]{1,0:T(8,128)(2,1)}, bf16[256,1664]{1,0:T(8,128)(2,1)}, u32[]{:S(2)}, u32[]{:S(2)}) %collective-permute-start.19) | collective-permute-done | bytes 852000 | tf_op jit(solution)/shard_map/ppermute | solution.py:479
  240.5 2.9 multiply_reduce_fusion.2
  250.5 16.8 %shard_map.364 = (bf16[512,2048]{1,0:T(8,128)(2,1)}, bf16[512,1024]{1,0:T(8,128)(2,1)}, bf16[512,1536]{1,0:T(8,128)(2,1)}, bf16[512,1664]{1,0:T(8,128)(2,1)}) custom-call(s32[1]{0:T(128)} %bitcast.7.at_ref, bf16[512,1536]{1,0:T(8,128)(2,1)} %pad_maximum_fusion.1.x_ref, bf16[512,1664]{1,0:T(8,128)(2,1)} %pad_maximum_fusion.c_ref, ...), custom_call_target="tpu_custom_call" | custom-call | flops 9663676416 | bytes 19677184 | tf_op jit(solution)/shard_map/pallas_call | solution.py:352
  279.7 16.4 %shard_map.365 = (bf16[512,2048]{1,0:T(8,128)(2,1)}, bf16[512,1024]{1,0:T(8,128)(2,1)}, bf16[512,1536]{1,0:T(8,128)(2,1)}, bf16[512,1664]{1,0:T(8,128)(2,1)}) custom-call(s32[1]{0:T(128)} %bitcast.7.at_ref, bf16[512,1536]{1,0:T(8,128)(2,1)} %pad_maximum_fusion.2.x_ref, bf16[512,1664]{1,0:T(8,128)(2,1)} %copy-done.28, ...), custom_call_target="tpu_custom_call" | custom-call | flops 9663676416 | bytes 19677184 | tf_op jit(solution)/shard_map/pallas_call | solution.py:352
  296.1 18.3 %collective-permute-done.26 = bf16[256,1536]{1,0:T(8,128)(2,1)} collective-permute-done((bf16[256,1536]{1,0:T(8,128)(2,1)}, bf16[256,1536]{1,0:T(8,128)(2,1)}, u32[]{:S(2)}, u32[]{:S(2)}) %collective-permute-start.26) | collective-permute-done | bytes 786464 | tf_op jit(solution)/shard_map/ppermute | solution.py:479
  328.7 16.5 %shard_map.366 = (bf16[512,2048]{1,0:T(8,128)(2,1)}, bf16[512,1024]{1,0:T(8,128)(2,1)}, bf16[512,1536]{1,0:T(8,128)(2,1)}, bf16[512,1664]{1,0:T(8,128)(2,1)}) custom-call(s32[1]{0:T(128)} %bitcast.7.at_ref, bf16[512,1536]{1,0:T(8,128)(2,1)} %pad_maximum_fusion.3.x_ref, bf16[512,1664]{1,0:T(8,128)(2,1)} %copy-done.26, ...), custom_call_target="tpu_custom_call" | custom-call | flops 9663676416 | bytes 19677184 | tf_op jit(solution)/shard_map/pallas_call | solution.py:352
  350.1 3.4 copy-done.70
  354.7 16.5 %shard_map.367 = (bf16[512,2048]{1,0:T(8,128)(2,1)}, bf16[512,1024]{1,0:T(8,128)(2,1)}, bf16[512,1536]{1,0:T(8,128)(2,1)}, bf16[512,1664]{1,0:T(8,128)(2,1)}) custom-call(s32[1]{0:T(128)} %bitcast.7.at_ref, bf16[512,1536]{1,0:T(8,128)(2,1)} %pad_maximum_fusion.4.x_ref, bf16[512,1664]{1,0:T(8,128)(2,1)} %copy-done.29, ...), custom_call_target="tpu_custom_call" | custom-call | flops 9663676416 | bytes 19677184 | tf_op jit(solution)/shard_map/pallas_call | solution.py:352
  371.2 12.4 %fusion.25 = bf16[1536,1024]{0,1:T(8,128)(2,1)} fusion(bf16[512,1024]{1,0:T(8,128)(2,1)} %get-tuple-element.118, bf16[512,1024]{1,0:T(8,128)(2,1)} %get-tuple-element.117, bf16[512,1024]{1,0:T(8,128)(2,1)} %get-tuple-element.116, bf16[512,1024]{1,0:T(8,128)(2,1)} %get-tuple-element.115, bf16[512,1536]{1,0:T(8,128)(2,1)} %slice.185, ...), kind=kOutput, calls=%fused_computation.27 | convolution fusion | flops 6485966848 | bytes 13631488 | tf_op jit(solution)/shard_map/dot_general | solution.py:642
  402.8 4.2 collective-permute-done.84
  408.5 14.8 %collective-permute-done.86 = bf16[384,1024]{0,1:T(8,128)(2,1)S(1)} collective-permute-done((bf16[384,1024]{0,1:T(8,128)(2,1)S(1)}, bf16[384,1024]{0,1:T(8,128)(2,1)S(1)}, u32[]{:S(2)}, u32[]{:S(2)}) %collective-permute-start.86) | collective-permute-done | bytes 786464 | tf_op jit(solution)/shard_map/ppermute | solution.py:485
  437.5 10.5 %fusion.22 = bf16[1536,1024]{0,1:T(8,128)(2,1)S(1)} fusion(bf16[2048,1536]{1,0:T(8,128)(2,1)} %constant_dynamic-update-slice_fusion.6, bf16[2048,2048]{1,0:T(8,128)(2,1)} %constant_dynamic-update-slice_fusion.14), kind=kOutput, calls=%fused_computation.26 | convolution fusion | flops 6444023808 | bytes 13631488 | tf_op jit(solution)/shard_map/dot_general | solution.py:643
  461.4 8.5 collective-permute-done.81
  469.8 15.1 %collective-permute-done.83 = bf16[384,1024]{0,1:T(8,128)(2,1)S(1)} collective-permute-done((bf16[384,1024]{0,1:T(8,128)(2,1)S(1)}, bf16[384,1024]{0,1:T(8,128)(2,1)S(1)}, u32[]{:S(2)}, u32[]{:S(2)}) %collective-permute-start.83) | collective-permute-done | bytes 786464 | tf_op jit(solution)/shard_map/ppermute | solution.py:485
  498.4 10.6 %fusion.19 = bf16[1536,1024]{0,1:T(8,128)(2,1)S(1)} fusion(bf16[2048,1536]{1,0:T(8,128)(2,1)} %constant_dynamic-update-slice_fusion.6, bf16[2048,2048]{1,0:T(8,128)(2,1)} %constant_dynamic-update-slice_fusion.14), kind=kOutput, calls=%fused_computation.25 | convolution fusion | flops 6444023808 | bytes 13631488 | tf_op jit(solution)/shard_map/dot_general | solution.py:644
  510.3 43.8 %collective-permute-done.36 = bf16[256,1664]{1,0:T(8,128)(2,1)S(1)} collective-permute-done((bf16[256,1664]{1,0:T(8,128)(2,1)S(1)}, bf16[256,1664]{1,0:T(8,128)(2,1)S(1)}, u32[]{:S(2)}, u32[]{:S(2)}) %collective-permute-start.36) | collective-permute-done | bytes 852000 | tf_op jit(solution)/shard_map/ppermute | solution.py:479
  555.3 28.9 %collective-permute-done.38 = bf16[256,1664]{1,0:T(8,128)(2,1)S(1)} collective-permute-done((bf16[256,1664]{1,0:T(8,128)(2,1)S(1)}, bf16[256,1664]{1,0:T(8,128)(2,1)S(1)}, u32[]{:S(2)}, u32[]{:S(2)}) %collective-permute-start.38) | collective-permute-done | bytes 852000 | tf_op jit(solution)/shard_map/ppermute | solution.py:479
  584.2 12.2 %collective-permute-done.40 = bf16[256,1664]{1,0:T(8,128)(2,1)S(1)} collective-permute-done((bf16[256,1664]{1,0:T(8,128)(2,1)S(1)}, bf16[256,1664]{1,0:T(8,128)(2,1)S(1)}, u32[]{:S(2)}, u32[]{:S(2)}) %collective-permute-start.40) | collective-permute-done | bytes 852000 | tf_op jit(solution)/shard_map/ppermute | solution.py:479
  601.8 12.5 %collective-permute-done.79 = bf16[384,1024]{0,1:T(8,128)(2,1)S(1)} collective-permute-done((bf16[384,1024]{0,1:T(8,128)(2,1)S(1)}, bf16[384,1024]{0,1:T(8,128)(2,1)S(1)}, u32[]{:S(2)}, u32[]{:S(2)}) %collective-permute-start.79) | collective-permute-done | bytes 786464 | tf_op jit(solution)/shard_map/ppermute | solution.py:485
  626.9 4.6 fusion.117
  634.8 26.2 %collective-permute-start.42 = (bf16[512,192]{1,0:T(8,128)(2,1)S(1)}, bf16[512,192]{1,0:T(8,128)(2,1)}, u32[]{:S(2)}, u32[]{:S(2)}) collective-permute-start(bf16[512,192]{1,0:T(8,128)(2,1)S(1)} %copy.158), channel_id=1, source_target_pairs={{0,2},{2,0},{4,6},{6,4},{1,3},{3,1},{5,7},{7,5},{8,10},{10,8},{12,... | collective-permute-start | bytes 589832 | tf_op jit(solution)/shard_map/ppermute | solution.py:479
  674.7 8.9 collective-permute-done.42
  684.6 9.6 collective-permute-done.43
  697.0 37.2 %shard_map.368 = (f32[3,2048,64]{2,1,0:T(8,128)}, f32[2048,64]{1,0:T(8,128)}, f32[2048,64]{1,0:T(8,128)}) custom-call(s32[2048,1]{1,0:T(8,128)} %copy.154.idc_ref, s32[1,2048]{1,0:T(1,128)} %idr_ref.3, bf16[3,2048,64]{2,1,0:T(8,128)(2,1)} %get-tuple-element.77.q_ref, bf16[2048,64]{1,0:T(8,128)(2,1)} %get-tuple-element.78.k_ref, ...), custom_call_target="tpu_custom_call" | custom-call | flops 40000000000 | bytes 6291456 | tf_op jit(solution)/shard_map/pallas_call | solution.py:249
  734.2 5.6 shard_map.369
  739.7 5.6 convolution_convert_fusion
  750.0 20.7 %collective-permute-start.53 = (bf16[512,320]{1,0:T(8,128)(2,1)}, bf16[512,320]{1,0:T(8,128)(2,1)}, u32[]{:S(2)}, u32[]{:S(2)}) collective-permute-start(bf16[512,320]{1,0:T(8,128)(2,1)} %get-tuple-element.297), channel_id=1, source_target_pairs={{0,2},{2,0},{4,6},{6,4},{1,3},{3,1},{5,7},{7,5},{8,10},{10,8},{12,... | collective-permute-start | bytes 983048 | tf_op jit(solution)/shard_map/ppermute | solution.py:479
  777.8 3.9 dynamic_update_slice.152
  781.7 16.3 %collective-permute-start.54 = (bf16[512,320]{1,0:T(8,128)(2,1)}, bf16[512,320]{1,0:T(8,128)(2,1)S(1)}, u32[]{:S(2)}, u32[]{:S(2)}) collective-permute-start(bf16[512,320]{1,0:T(8,128)(2,1)} %get-tuple-element.295), channel_id=1, source_target_pairs={{0,4},{2,6},{4,0},{6,2},{1,5},{3,7},{5,1},{7,3},{8,12},{10,14},{12... | collective-permute-start | bytes 983048 | tf_op jit(solution)/shard_map/ppermute | solution.py:479
  800.6 10.1 collective-permute-start.76
  815.9 4.2 collective-permute-start.75
  822.9 4.2 collective-permute-start.68
  835.0 5.0 dynamic_update_slice.153
  841.8 4.2 dynamic_update_slice.154
  850.3 5.5 collective-permute-start.70
  856.9 3.7 dynamic_update_slice.155
  860.6 6.7 fusion.112
  867.4 22.6 %collective-permute-done.69 = bf16[208,384]{1,0:T(8,128)(2,1)S(1)} collective-permute-done((bf16[208,384]{1,0:T(8,128)(2,1)S(1)}, bf16[208,384]{1,0:T(8,128)(2,1)S(1)}, u32[]{:S(2)}, u32[]{:S(2)}) %collective-permute-start.69) | collective-permute-done | bytes 159776 | tf_op jit(solution)/shard_map/ppermute | solution.py:479
  890.0 3.8 collective-permute-start.71
  917.0 16.3 %collective-permute-done.47 = bf16[256,1536]{1,0:T(8,128)(2,1)} collective-permute-done((bf16[256,1536]{1,0:T(8,128)(2,1)}, bf16[256,1536]{1,0:T(8,128)(2,1)}, u32[]{:S(2)}, u32[]{:S(2)}) %collective-permute-start.47) | collective-permute-done | bytes 786464 | tf_op jit(solution)/shard_map/ppermute | solution.py:479
  939.9 4.3 fusion.35
  946.7 6.0 copy.173.refs_3_
  952.7 6.2 copy.174.refs_3_
  958.9 20.2 %shard_map.370 = (f32[384,3,16,256]{3,2,1,0:T(8,128)}, f32[384,3,16,256]{3,2,1,0:T(8,128)}, bf16[384,3,16,256]{3,2,1,0:T(8,128)(2,1)}, f32[384,16,256]{2,1,0:T(8,128)}) custom-call(f32[384,3,16,256]{3,2,1,0:T(8,128)} %bitcast.80, f32[384,3,16,256]{3,2,1,0:T(8,128)} %bitcast.83, f32[384,3,16,256]{3,2,1,0:T(8,128)} %bitcast.86, ...), custom_call_target="tpu_custom_call" | custom-call | flops 31457280 | bytes 44040192 | tf_op jit(solution)/shard_map/pallas_call | solution.py:416
  979.1 20.3 %shard_map.371 = (f32[384,3,16,256]{3,2,1,0:T(8,128)}, f32[384,3,16,256]{3,2,1,0:T(8,128)}, bf16[384,3,16,256]{3,2,1,0:T(8,128)(2,1)}, f32[384,16,256]{2,1,0:T(8,128)}) custom-call(f32[384,3,16,256]{3,2,1,0:T(8,128)} %bitcast.81, f32[384,3,16,256]{3,2,1,0:T(8,128)} %bitcast.84, ...), custom_call_target="tpu_custom_call", output_to_operand_aliasing={{0}: (4, {}), {1}: (5, {}), {2}: (6, {})} | custom-call | flops 31457280 | bytes 44040192 | tf_op jit(solution)/shard_map/pallas_call | solution.py:416
  999.4 6.0 copy.175.refs_3_
  1005.4 25.4 %shard_map.372 = (f32[384,3,16,256]{3,2,1,0:T(8,128)}, f32[384,3,16,256]{3,2,1,0:T(8,128)}, bf16[384,3,16,256]{3,2,1,0:T(8,128)(2,1)}, f32[384,16,2,256]{3,2,1,0:T(2,128)}) custom-call(f32[384,3,16,256]{3,2,1,0:T(8,128)} %bitcast.82, f32[384,3,16,256]{3,2,1,0:T(8,128)} %bitcast.85, ...), custom_call_target="tpu_custom_call", output_to_operand_aliasing={{0}: (5, {}), {1}: (6, {}), {2}: (7, {})} | custom-call | flops 31457280 | bytes 44040192 | tf_op jit(solution)/shard_map/pallas_call | solution.py:416
  (509 shorter events, 287.2 us)
Async XLA Ops:
  7.2 243.3 %all-gather.5.cloned.1.call-start = ((), (), s32[]{:S(2)}) async-start(), calls=%async_computation | async-start | bytes 11796480 | tf_op jit(solution)/shard_map/all_gather | solution.py:566
  55.5 891.2 %all-gather.11.cloned.1.call-start = ((), (), s32[]{:S(2)}) async-start(), calls=%async_computation.3 | async-start | bytes 3932160 | tf_op jit(solution)/shard_map/all_gather | solution.py:649
  57.9 34.5 %collective-permute-start.2 = (bf16[256,1536]{1,0:T(8,128)(2,1)}, bf16[256,1536]{1,0:T(8,128)(2,1)}, u32[]{:S(2)}, u32[]{:S(2)}) collective-permute-start(bf16[256,1536]{1,0:T(8,128)(2,1)} %dynamic-slice_bitcast_fusion), channel_id=1, source_target_pairs={{0,4},{2,6},{4,0},{6,2},{1,5},{3,7},{5,1},{7,3},{8,12},{10,14},{12... | collective-permute-start | bytes 2359304 | tf_op jit(solution)/shard_map/ppermute | solution.py:479
  60.5 32.4 %collective-permute-start = (bf16[256,1536]{1,0:T(8,128)(2,1)}, bf16[256,1536]{1,0:T(8,128)(2,1)}, u32[]{:S(2)}, u32[]{:S(2)}) collective-permute-start(bf16[256,1536]{1,0:T(8,128)(2,1)} %dynamic-slice_bitcast_fusion), channel_id=1, source_target_pairs={{0,2},{2,0},{4,6},{6,4},{1,3},{3,1},{5,7},{7,5},{8,10},{10,8},{12,... | collective-permute-start | bytes 2359304 | tf_op jit(solution)/shard_map/ppermute | solution.py:479
  84.1 23.8 %collective-permute-start.11 = (bf16[384,768]{1,0:T(8,128)(2,1)S(1)}, bf16[384,768]{1,0:T(8,128)(2,1)S(1)}, u32[]{:S(2)}, u32[]{:S(2)}) collective-permute-start(bf16[384,768]{1,0:T(8,128)(2,1)S(1)} %copy-done.41), channel_id=1, source_target_pairs={{0,16},{8,24},{16,0},{24,8},{1,17},{9,25},{17,1},{25,9},{2,18},{10... | collective-permute-start | bytes 1769480 | tf_op jit(solution)/shard_map/ppermute | solution.py:485
  92.9 21.3 %collective-permute-start.1 = (bf16[256,1536]{1,0:T(8,128)(2,1)}, bf16[256,1536]{1,0:T(8,128)(2,1)S(1)}, u32[]{:S(2)}, u32[]{:S(2)}) collective-permute-start(bf16[256,1536]{1,0:T(8,128)(2,1)} %collective-permute-done), channel_id=1, source_target_pairs={{0,1},{1,0},{2,3},{3,2},{4,5},{5,4},{6,7},{7,6},{8,9},{9,8},{10,11... | collective-permute-start | bytes 2359304 | tf_op jit(solution)/shard_map/ppermute | solution.py:482
  108.0 57.1 %collective-permute-start.13 = (bf16[192,768]{1,0:T(8,128)(2,1)S(1)}, bf16[192,768]{1,0:T(8,128)(2,1)S(1)}, u32[]{:S(2)}, u32[]{:S(2)}) collective-permute-start(bf16[192,768]{1,0:T(8,128)(2,1)S(1)} %slice.163), channel_id=1, source_target_pairs={{0,8},{8,0},{16,24},{24,16},{1,9},{9,1},{17,25},{25,17},{2,10},{10... | collective-permute-start | bytes 884744 | tf_op jit(solution)/shard_map/ppermute | solution.py:485
  110.9 58.7 %collective-permute-start.18 = (bf16[256,1664]{1,0:T(8,128)(2,1)}, bf16[256,1664]{1,0:T(8,128)(2,1)}, u32[]{:S(2)}, u32[]{:S(2)}) collective-permute-start(bf16[256,1664]{1,0:T(8,128)(2,1)} %get-tuple-element.82), channel_id=1, source_target_pairs={{0,4},{2,6},{4,0},{6,2},{1,5},{3,7},{5,1},{7,3},{8,12},{10,14},{12... | collective-permute-start | bytes 2555912 | tf_op jit(solution)/shard_map/ppermute | solution.py:479
  165.2 38.0 %collective-permute-start.17 = (bf16[256,1664]{1,0:T(8,128)(2,1)}, bf16[256,1664]{1,0:T(8,128)(2,1)}, u32[]{:S(2)}, u32[]{:S(2)}) collective-permute-start(bf16[256,1664]{1,0:T(8,128)(2,1)} %get-tuple-element.82), channel_id=1, source_target_pairs={{0,2},{2,0},{4,6},{6,4},{1,3},{3,1},{5,7},{7,5},{8,10},{10,8},{12,... | collective-permute-start | bytes 2555912 | tf_op jit(solution)/shard_map/ppermute | solution.py:479
  165.5 36.8 %collective-permute-start.15 = (bf16[512,192]{1,0:T(8,128)(2,1)S(1)}, bf16[512,192]{1,0:T(8,128)(2,1)S(1)}, u32[]{:S(2)}, u32[]{:S(2)}) collective-permute-start(bf16[512,192]{1,0:T(8,128)(2,1)S(1)} %get-tuple-element.298), channel_id=1, source_target_pairs={{0,4},{2,6},{4,0},{6,2},{1,5},{3,7},{5,1},{7,3},{8,12},{10,14},{12... | collective-permute-start | bytes 589832 | tf_op jit(solution)/shard_map/ppermute | solution.py:479
  165.7 35.8 %collective-permute-start.16 = (bf16[512,192]{1,0:T(8,128)(2,1)S(1)}, bf16[512,192]{1,0:T(8,128)(2,1)S(1)}, u32[]{:S(2)}, u32[]{:S(2)}) collective-permute-start(bf16[512,192]{1,0:T(8,128)(2,1)S(1)} %get-tuple-element.299), channel_id=1, source_target_pairs={{0,6},{2,4},{4,2},{6,0},{1,7},{3,5},{5,3},{7,1},{8,14},{10,12},{12... | collective-permute-start | bytes 589832 | tf_op jit(solution)/shard_map/ppermute | solution.py:479
  169.6 50.3 %collective-permute-start.19 = (bf16[256,1664]{1,0:T(8,128)(2,1)}, bf16[256,1664]{1,0:T(8,128)(2,1)}, u32[]{:S(2)}, u32[]{:S(2)}) collective-permute-start(bf16[256,1664]{1,0:T(8,128)(2,1)} %collective-permute-done.18), channel_id=1, source_target_pairs={{0,2},{2,0},{4,6},{6,4},{1,3},{3,1},{5,7},{7,5},{8,10},{10,8},{12,... | collective-permute-start | bytes 2555912 | tf_op jit(solution)/shard_map/ppermute | solution.py:479
  235.2 33.4 %collective-permute-start.24 = (bf16[256,1664]{1,0:T(8,128)(2,1)}, bf16[256,1664]{1,0:T(8,128)(2,1)}, u32[]{:S(2)}, u32[]{:S(2)}) collective-permute-start(bf16[256,1664]{1,0:T(8,128)(2,1)} %collective-permute-done.17), channel_id=1, source_target_pairs={{0,1},{1,0},{2,3},{3,2},{4,5},{5,4},{6,7},{7,6},{8,9},{9,8},{10,11... | collective-permute-start | bytes 2555912 | tf_op jit(solution)/shard_map/ppermute | solution.py:482
  235.7 35.7 %collective-permute-start.28 = (bf16[256,1664]{1,0:T(8,128)(2,1)}, bf16[256,1664]{1,0:T(8,128)(2,1)}, u32[]{:S(2)}, u32[]{:S(2)}) collective-permute-start(bf16[256,1664]{1,0:T(8,128)(2,1)} %collective-permute-done.18), channel_id=1, source_target_pairs={{0,1},{1,0},{2,3},{3,2},{4,5},{5,4},{6,7},{7,6},{8,9},{9,8},{10,11... | collective-permute-start | bytes 2555912 | tf_op jit(solution)/shard_map/ppermute | solution.py:482
  235.7 38.4 %collective-permute-start.32 = (bf16[256,1664]{1,0:T(8,128)(2,1)}, bf16[256,1664]{1,0:T(8,128)(2,1)}, u32[]{:S(2)}, u32[]{:S(2)}) collective-permute-start(bf16[256,1664]{1,0:T(8,128)(2,1)} %collective-permute-done.19), channel_id=1, source_target_pairs={{0,1},{1,0},{2,3},{3,2},{4,5},{5,4},{6,7},{7,6},{8,9},{9,8},{10,11... | collective-permute-start | bytes 2555912 | tf_op jit(solution)/shard_map/ppermute | solution.py:482
  245.4 21.9 %collective-permute-start.22 = (bf16[256,1536]{1,0:T(8,128)(2,1)}, bf16[256,1536]{1,0:T(8,128)(2,1)}, u32[]{:S(2)}, u32[]{:S(2)}) collective-permute-start(bf16[256,1536]{1,0:T(8,128)(2,1)} %get-tuple-element.255), channel_id=1, source_target_pairs={{0,2},{2,0},{4,6},{6,4},{1,3},{3,1},{5,7},{7,5},{8,10},{10,8},{12,... | collective-permute-start | bytes 2359304 | tf_op jit(solution)/shard_map/ppermute | solution.py:479
  276.7 37.7 %collective-permute-start.26 = (bf16[256,1536]{1,0:T(8,128)(2,1)}, bf16[256,1536]{1,0:T(8,128)(2,1)}, u32[]{:S(2)}, u32[]{:S(2)}) collective-permute-start(bf16[256,1536]{1,0:T(8,128)(2,1)} %get-tuple-element.255), channel_id=1, source_target_pairs={{0,4},{2,6},{4,0},{6,2},{1,5},{3,7},{5,1},{7,3},{8,12},{10,14},{12... | collective-permute-start | bytes 2359304 | tf_op jit(solution)/shard_map/ppermute | solution.py:479
  317.0 28.2 %collective-permute-start.30 = (bf16[256,1536]{1,0:T(8,128)(2,1)}, bf16[256,1536]{1,0:T(8,128)(2,1)S(1)}, u32[]{:S(2)}, u32[]{:S(2)}) collective-permute-start(bf16[256,1536]{1,0:T(8,128)(2,1)} %collective-permute-done.26), channel_id=1, source_target_pairs={{0,2},{2,0},{4,6},{6,4},{1,3},{3,1},{5,7},{7,5},{8,10},{10,8},{12,... | collective-permute-start | bytes 2359304 | tf_op jit(solution)/shard_map/ppermute | solution.py:479
  317.0 77.1 %collective-permute-start.50 = (bf16[384,1280]{1,0:T(8,128)(2,1)S(1)}, bf16[384,1280]{1,0:T(8,128)(2,1)}, u32[]{:S(2)}, u32[]{:S(2)}) collective-permute-start(bf16[384,1280]{1,0:T(8,128)(2,1)S(1)} %copy-done.18), channel_id=1, source_target_pairs={{0,16},{8,24},{16,0},{24,8},{1,17},{9,25},{17,1},{25,9},{2,18},{10... | collective-permute-start | bytes 2949128 | tf_op jit(solution)/shard_map/ppermute | solution.py:485
  317.6 78.4 %collective-permute-start.49 = (bf16[384,1280]{1,0:T(8,128)(2,1)S(1)}, bf16[384,1280]{1,0:T(8,128)(2,1)}, u32[]{:S(2)}, u32[]{:S(2)}) collective-permute-start(bf16[384,1280]{1,0:T(8,128)(2,1)S(1)} %copy-done.18), channel_id=1, source_target_pairs={{0,8},{8,0},{16,24},{24,16},{1,9},{9,1},{17,25},{25,17},{2,10},{10... | collective-permute-start | bytes 2949128 | tf_op jit(solution)/shard_map/ppermute | solution.py:485
  385.6 21.4 %collective-permute-start.84 = (bf16[384,1024]{0,1:T(8,128)(2,1)S(1)}, bf16[384,1024]{0,1:T(8,128)(2,1)S(1)}, u32[]{:S(2)}, u32[]{:S(2)}) collective-permute-start(bf16[384,1024]{0,1:T(8,128)(2,1)S(1)} %get-tuple-element.280), channel_id=1, source_target_pairs={{0,24},{8,16},{16,8},{24,0},{1,25},{9,17},{17,9},{25,1},{2,26},{10... | collective-permute-start | bytes 2359304 | tf_op jit(solution)/shard_map/ppermute | solution.py:485
  387.2 36.1 %collective-permute-start.86 = (bf16[384,1024]{0,1:T(8,128)(2,1)S(1)}, bf16[384,1024]{0,1:T(8,128)(2,1)S(1)}, u32[]{:S(2)}, u32[]{:S(2)}) collective-permute-start(bf16[384,1024]{0,1:T(8,128)(2,1)S(1)} %get-tuple-element.281), channel_id=1, source_target_pairs={{0,16},{8,24},{16,0},{24,8},{1,17},{9,25},{17,1},{25,9},{2,18},{10... | collective-permute-start | bytes 2359304 | tf_op jit(solution)/shard_map/ppermute | solution.py:485
  387.7 36.2 %collective-permute-start.85 = (bf16[384,1024]{0,1:T(8,128)(2,1)S(1)}, bf16[384,1024]{0,1:T(8,128)(2,1)S(1)}, u32[]{:S(2)}, u32[]{:S(2)}) collective-permute-start(bf16[384,1024]{0,1:T(8,128)(2,1)S(1)} %get-tuple-element.282), channel_id=1, source_target_pairs={{0,8},{8,0},{16,24},{24,16},{1,9},{9,1},{17,25},{25,17},{2,10},{10... | collective-permute-start | bytes 2359304 | tf_op jit(solution)/shard_map/ppermute | solution.py:485
  394.1 62.6 %collective-permute-start.25 = (bf16[256,1536]{1,0:T(8,128)(2,1)}, bf16[256,1536]{1,0:T(8,128)(2,1)}, u32[]{:S(2)}, u32[]{:S(2)}) collective-permute-start(bf16[256,1536]{1,0:T(8,128)(2,1)} %slice.130), channel_id=1, source_target_pairs={{0,1},{1,0},{2,3},{3,2},{4,5},{5,4},{6,7},{7,6},{8,9},{9,8},{10,11... | collective-permute-start | bytes 2359304 | tf_op jit(solution)/shard_map/ppermute | solution.py:482
  396.0 57.8 %collective-permute-start.52 = (bf16[192,1280]{1,0:T(8,128)(2,1)}, bf16[192,1280]{1,0:T(8,128)(2,1)}, u32[]{:S(2)}, u32[]{:S(2)}) collective-permute-start(bf16[192,1280]{1,0:T(8,128)(2,1)} %slice.171), channel_id=1, source_target_pairs={{0,8},{8,0},{16,24},{24,16},{1,9},{9,1},{17,25},{25,17},{2,10},{10... | collective-permute-start | bytes 1474568 | tf_op jit(solution)/shard_map/ppermute | solution.py:485
  407.0 43.4 %collective-permute-start.51 = (bf16[192,1280]{1,0:T(8,128)(2,1)}, bf16[192,1280]{1,0:T(8,128)(2,1)}, u32[]{:S(2)}, u32[]{:S(2)}) collective-permute-start(bf16[192,1280]{1,0:T(8,128)(2,1)} %slice.170), channel_id=1, source_target_pairs={{0,16},{8,24},{16,0},{24,8},{1,17},{9,25},{17,1},{25,9},{2,18},{10... | collective-permute-start | bytes 1474568 | tf_op jit(solution)/shard_map/ppermute | solution.py:485
  428.7 524.0 %all-gather.9.cloned.1.call-start = ((), (), s32[]{:S(2)}) async-start(), calls=%async_computation.2 | async-start | bytes 3932160 | tf_op jit(solution)/shard_map/all_gather | solution.py:649
  448.3 21.5 %collective-permute-start.81 = (bf16[384,1024]{0,1:T(8,128)(2,1)S(1)}, bf16[384,1024]{0,1:T(8,128)(2,1)S(1)}, u32[]{:S(2)}, u32[]{:S(2)}) collective-permute-start(bf16[384,1024]{0,1:T(8,128)(2,1)S(1)} %get-tuple-element.283), channel_id=1, source_target_pairs={{0,24},{8,16},{16,8},{24,0},{1,25},{9,17},{17,9},{25,1},{2,26},{10... | collective-permute-start | bytes 2359304 | tf_op jit(solution)/shard_map/ppermute | solution.py:485
  449.3 35.6 %collective-permute-start.83 = (bf16[384,1024]{0,1:T(8,128)(2,1)S(1)}, bf16[384,1024]{0,1:T(8,128)(2,1)S(1)}, u32[]{:S(2)}, u32[]{:S(2)}) collective-permute-start(bf16[384,1024]{0,1:T(8,128)(2,1)S(1)} %get-tuple-element.284), channel_id=1, source_target_pairs={{0,16},{8,24},{16,0},{24,8},{1,17},{9,25},{17,1},{25,9},{2,18},{10... | collective-permute-start | bytes 2359304 | tf_op jit(solution)/shard_map/ppermute | solution.py:485
  450.4 34.7 %collective-permute-start.82 = (bf16[384,1024]{0,1:T(8,128)(2,1)S(1)}, bf16[384,1024]{0,1:T(8,128)(2,1)S(1)}, u32[]{:S(2)}, u32[]{:S(2)}) collective-permute-start(bf16[384,1024]{0,1:T(8,128)(2,1)S(1)} %get-tuple-element.285), channel_id=1, source_target_pairs={{0,8},{8,0},{16,24},{24,16},{1,9},{9,1},{17,25},{25,17},{2,10},{10... | collective-permute-start | bytes 2359304 | tf_op jit(solution)/shard_map/ppermute | solution.py:485
  453.7 35.5 %collective-permute-start.35 = (bf16[256,1664]{1,0:T(8,128)(2,1)}, bf16[256,1664]{1,0:T(8,128)(2,1)}, u32[]{:S(2)}, u32[]{:S(2)}) collective-permute-start(bf16[256,1664]{1,0:T(8,128)(2,1)} %slice.138), channel_id=1, source_target_pairs={{0,1},{1,0},{2,3},{3,2},{4,5},{5,4},{6,7},{7,6},{8,9},{9,8},{10,11... | collective-permute-start | bytes 2555912 | tf_op jit(solution)/shard_map/ppermute | solution.py:482
  456.7 36.4 %collective-permute-start.37 = (bf16[256,1664]{1,0:T(8,128)(2,1)}, bf16[256,1664]{1,0:T(8,128)(2,1)}, u32[]{:S(2)}, u32[]{:S(2)}) collective-permute-start(bf16[256,1664]{1,0:T(8,128)(2,1)} %slice.140), channel_id=1, source_target_pairs={{0,1},{1,0},{2,3},{3,2},{4,5},{5,4},{6,7},{7,6},{8,9},{9,8},{10,11... | collective-permute-start | bytes 2555912 | tf_op jit(solution)/shard_map/ppermute | solution.py:482
  469.8 40.4 %collective-permute-start.34 = (bf16[256,1664]{1,0:T(8,128)(2,1)}, bf16[256,1664]{1,0:T(8,128)(2,1)}, u32[]{:S(2)}, u32[]{:S(2)}) collective-permute-start(bf16[256,1664]{1,0:T(8,128)(2,1)} %slice.136), channel_id=1, source_target_pairs={{0,1},{1,0},{2,3},{3,2},{4,5},{5,4},{6,7},{7,6},{8,9},{9,8},{10,11... | collective-permute-start | bytes 2555912 | tf_op jit(solution)/shard_map/ppermute | solution.py:482
  485.0 114.6 %collective-permute-start.29 = (bf16[256,1536]{1,0:T(8,128)(2,1)}, bf16[256,1536]{1,0:T(8,128)(2,1)}, u32[]{:S(2)}, u32[]{:S(2)}) collective-permute-start(bf16[256,1536]{1,0:T(8,128)(2,1)} %slice.132), channel_id=1, source_target_pairs={{0,1},{1,0},{2,3},{3,2},{4,5},{5,4},{6,7},{7,6},{8,9},{9,8},{10,11... | collective-permute-start | bytes 2359304 | tf_op jit(solution)/shard_map/ppermute | solution.py:482
  489.1 510.2 %all-gather.7.cloned.1.call-start = ((), (), s32[]{:S(2)}) async-start(), calls=%async_computation.1 | async-start | bytes 3932160 | tf_op jit(solution)/shard_map/all_gather | solution.py:649
  491.0 63.2 %collective-permute-start.36 = (bf16[256,1664]{1,0:T(8,128)(2,1)S(1)}, bf16[256,1664]{1,0:T(8,128)(2,1)S(1)}, u32[]{:S(2)}, u32[]{:S(2)}) collective-permute-start(bf16[256,1664]{1,0:T(8,128)(2,1)S(1)} %add_convert_fusion.4), channel_id=1, source_target_pairs={{0,2},{2,0},{4,6},{6,4},{1,3},{3,1},{5,7},{7,5},{8,10},{10,8},{12,... | collective-permute-start | bytes 2555912 | tf_op jit(solution)/shard_map/ppermute | solution.py:479
  494.5 89.8 %collective-permute-start.38 = (bf16[256,1664]{1,0:T(8,128)(2,1)S(1)}, bf16[256,1664]{1,0:T(8,128)(2,1)S(1)}, u32[]{:S(2)}, u32[]{:S(2)}) collective-permute-start(bf16[256,1664]{1,0:T(8,128)(2,1)S(1)} %add_convert_fusion.3), channel_id=1, source_target_pairs={{0,4},{2,6},{4,0},{6,2},{1,5},{3,7},{5,1},{7,3},{8,12},{10,14},{12... | collective-permute-start | bytes 2555912 | tf_op jit(solution)/shard_map/ppermute | solution.py:479
  495.9 100.5 %collective-permute-start.40 = (bf16[256,1664]{1,0:T(8,128)(2,1)S(1)}, bf16[256,1664]{1,0:T(8,128)(2,1)S(1)}, u32[]{:S(2)}, u32[]{:S(2)}) collective-permute-start(bf16[256,1664]{1,0:T(8,128)(2,1)S(1)} %add_convert_fusion.2), channel_id=1, source_target_pairs={{0,6},{2,4},{4,2},{6,0},{1,7},{3,5},{5,3},{7,1},{8,14},{10,12},{12... | collective-permute-start | bytes 2555912 | tf_op jit(solution)/shard_map/ppermute | solution.py:479
  510.2 107.6 %collective-permute-start.33 = (bf16[256,1536]{1,0:T(8,128)(2,1)}, bf16[256,1536]{1,0:T(8,128)(2,1)}, u32[]{:S(2)}, u32[]{:S(2)}) collective-permute-start(bf16[256,1536]{1,0:T(8,128)(2,1)} %slice.134), channel_id=1, source_target_pairs={{0,1},{1,0},{2,3},{3,2},{4,5},{5,4},{6,7},{7,6},{8,9},{9,8},{10,11... | collective-permute-start | bytes 2359304 | tf_op jit(solution)/shard_map/ppermute | solution.py:482
  554.2 47.6 %collective-permute-start.78 = (bf16[384,1024]{0,1:T(8,128)(2,1)S(1)}, bf16[384,1024]{0,1:T(8,128)(2,1)S(1)}, u32[]{:S(2)}, u32[]{:S(2)}) collective-permute-start(bf16[384,1024]{0,1:T(8,128)(2,1)S(1)} %get-tuple-element.286), channel_id=1, source_target_pairs={{0,24},{8,16},{16,8},{24,0},{1,25},{9,17},{17,9},{25,1},{2,26},{10... | collective-permute-start | bytes 2359304 | tf_op jit(solution)/shard_map/ppermute | solution.py:485
  634.8 48.8 %collective-permute-start.42 = (bf16[512,192]{1,0:T(8,128)(2,1)S(1)}, bf16[512,192]{1,0:T(8,128)(2,1)}, u32[]{:S(2)}, u32[]{:S(2)}) collective-permute-start(bf16[512,192]{1,0:T(8,128)(2,1)S(1)} %copy.158), channel_id=1, source_target_pairs={{0,2},{2,0},{4,6},{6,4},{1,3},{3,1},{5,7},{7,5},{8,10},{10,8},{12,... | collective-permute-start | bytes 589832 | tf_op jit(solution)/shard_map/ppermute | solution.py:479
  661.1 33.1 %collective-permute-start.43 = (bf16[512,192]{1,0:T(8,128)(2,1)S(1)}, bf16[512,192]{1,0:T(8,128)(2,1)S(1)}, u32[]{:S(2)}, u32[]{:S(2)}) collective-permute-start(bf16[512,192]{1,0:T(8,128)(2,1)S(1)} %copy.159), channel_id=1, source_target_pairs={{0,4},{2,6},{4,0},{6,2},{1,5},{3,7},{5,1},{7,3},{8,12},{10,14},{12... | collective-permute-start | bytes 589832 | tf_op jit(solution)/shard_map/ppermute | solution.py:479
  661.1 34.9 %collective-permute-start.44 = (bf16[512,192]{1,0:T(8,128)(2,1)S(1)}, bf16[512,192]{1,0:T(8,128)(2,1)S(1)}, u32[]{:S(2)}, u32[]{:S(2)}) collective-permute-start(bf16[512,192]{1,0:T(8,128)(2,1)S(1)} %copy.160), channel_id=1, source_target_pairs={{0,6},{2,4},{4,2},{6,0},{1,7},{3,5},{5,3},{7,1},{8,14},{10,12},{12... | collective-permute-start | bytes 589832 | tf_op jit(solution)/shard_map/ppermute | solution.py:479
  745.4 30.1 %collective-permute-start.72 = (bf16[320,384]{1,0:T(8,128)(2,1)S(1)}, bf16[320,384]{1,0:T(8,128)(2,1)S(1)}, u32[]{:S(2)}, u32[]{:S(2)}) collective-permute-start(bf16[320,384]{1,0:T(8,128)(2,1)S(1)} %get-tuple-element.301), channel_id=1, source_target_pairs={{0,24},{8,16},{16,8},{24,0},{1,25},{9,17},{17,9},{25,1},{2,26},{10... | collective-permute-start | bytes 737288 | tf_op jit(solution)/shard_map/ppermute | solution.py:485
  746.9 29.1 %collective-permute-start.74 = (bf16[320,384]{1,0:T(8,128)(2,1)S(1)}, bf16[320,384]{1,0:T(8,128)(2,1)S(1)}, u32[]{:S(2)}, u32[]{:S(2)}) collective-permute-start(bf16[320,384]{1,0:T(8,128)(2,1)S(1)} %get-tuple-element.302), channel_id=1, source_target_pairs={{0,16},{8,24},{16,0},{24,8},{1,17},{9,25},{17,1},{25,9},{2,18},{10... | collective-permute-start | bytes 737288 | tf_op jit(solution)/shard_map/ppermute | solution.py:485
  748.4 28.5 %collective-permute-start.73 = (bf16[320,384]{1,0:T(8,128)(2,1)S(1)}, bf16[320,384]{1,0:T(8,128)(2,1)S(1)}, u32[]{:S(2)}, u32[]{:S(2)}) collective-permute-start(bf16[320,384]{1,0:T(8,128)(2,1)S(1)} %get-tuple-element.303), channel_id=1, source_target_pairs={{0,8},{8,0},{16,24},{24,16},{1,9},{9,1},{17,25},{25,17},{2,10},{10... | collective-permute-start | bytes 737288 | tf_op jit(solution)/shard_map/ppermute | solution.py:485
  750.0 31.8 %collective-permute-start.53 = (bf16[512,320]{1,0:T(8,128)(2,1)}, bf16[512,320]{1,0:T(8,128)(2,1)}, u32[]{:S(2)}, u32[]{:S(2)}) collective-permute-start(bf16[512,320]{1,0:T(8,128)(2,1)} %get-tuple-element.297), channel_id=1, source_target_pairs={{0,2},{2,0},{4,6},{6,4},{1,3},{3,1},{5,7},{7,5},{8,10},{10,8},{12,... | collective-permute-start | bytes 983048 | tf_op jit(solution)/shard_map/ppermute | solution.py:479
  773.4 42.5 %collective-permute-start.63 = (bf16[832,384]{1,0:T(8,128)(2,1)}, bf16[832,384]{1,0:T(8,128)(2,1)}, u32[]{:S(2)}, u32[]{:S(2)}) collective-permute-start(bf16[832,384]{1,0:T(8,128)(2,1)} %get-tuple-element.289), channel_id=1, source_target_pairs={{0,24},{8,16},{16,8},{24,0},{1,25},{9,17},{17,9},{25,1},{2,26},{10... | collective-permute-start | bytes 1916936 | tf_op jit(solution)/shard_map/ppermute | solution.py:485
  775.5 44.5 %collective-permute-start.65 = (bf16[832,384]{1,0:T(8,128)(2,1)}, bf16[832,384]{1,0:T(8,128)(2,1)}, u32[]{:S(2)}, u32[]{:S(2)}) collective-permute-start(bf16[832,384]{1,0:T(8,128)(2,1)} %get-tuple-element.290), channel_id=1, source_target_pairs={{0,16},{8,24},{16,0},{24,8},{1,17},{9,25},{17,1},{25,9},{2,18},{10... | collective-permute-start | bytes 1916936 | tf_op jit(solution)/shard_map/ppermute | solution.py:485
  776.0 44.1 %collective-permute-start.64 = (bf16[832,384]{1,0:T(8,128)(2,1)}, bf16[832,384]{1,0:T(8,128)(2,1)}, u32[]{:S(2)}, u32[]{:S(2)}) collective-permute-start(bf16[832,384]{1,0:T(8,128)(2,1)} %get-tuple-element.291), channel_id=1, source_target_pairs={{0,8},{8,0},{16,24},{24,16},{1,9},{9,1},{17,25},{25,17},{2,10},{10... | collective-permute-start | bytes 1916936 | tf_op jit(solution)/shard_map/ppermute | solution.py:485
  776.9 23.7 %collective-permute-start.55 = (bf16[512,320]{1,0:T(8,128)(2,1)S(1)}, bf16[512,320]{1,0:T(8,128)(2,1)}, u32[]{:S(2)}, u32[]{:S(2)}) collective-permute-start(bf16[512,320]{1,0:T(8,128)(2,1)S(1)} %get-tuple-element.296), channel_id=1, source_target_pairs={{0,6},{2,4},{4,2},{6,0},{1,7},{3,5},{5,3},{7,1},{8,14},{10,12},{12... | collective-permute-start | bytes 983048 | tf_op jit(solution)/shard_map/ppermute | solution.py:479
  781.7 45.4 %collective-permute-start.54 = (bf16[512,320]{1,0:T(8,128)(2,1)}, bf16[512,320]{1,0:T(8,128)(2,1)S(1)}, u32[]{:S(2)}, u32[]{:S(2)}) collective-permute-start(bf16[512,320]{1,0:T(8,128)(2,1)} %get-tuple-element.295), channel_id=1, source_target_pairs={{0,4},{2,6},{4,0},{6,2},{1,5},{3,7},{5,1},{7,3},{8,12},{10,14},{12... | collective-permute-start | bytes 983048 | tf_op jit(solution)/shard_map/ppermute | solution.py:479
  800.6 27.7 %collective-permute-start.76 = (bf16[320,384]{1,0:T(8,128)(2,1)S(1)}, bf16[320,384]{1,0:T(8,128)(2,1)}, u32[]{:S(2)}, u32[]{:S(2)}) collective-permute-start(bf16[320,384]{1,0:T(8,128)(2,1)S(1)} %add_convert_fusion.14), channel_id=1, source_target_pairs={{0,4},{2,6},{4,0},{6,2},{1,5},{3,7},{5,1},{7,3},{8,12},{10,14},{12... | collective-permute-start | bytes 737288 | tf_op jit(solution)/shard_map/ppermute | solution.py:479
  822.9 23.1 %collective-permute-start.66 = (bf16[208,384]{1,0:T(8,128)(2,1)}, bf16[208,384]{1,0:T(8,128)(2,1)}, u32[]{:S(2)}, u32[]{:S(2)}) collective-permute-start(bf16[208,384]{1,0:T(8,128)(2,1)} %get-tuple-element.304), channel_id=1, source_target_pairs={{0,2},{2,0},{4,6},{6,4},{1,3},{3,1},{5,7},{7,5},{8,10},{10,8},{12,... | collective-permute-start | bytes 479240 | tf_op jit(solution)/shard_map/ppermute | solution.py:479
  822.9 23.3 %collective-permute-start.68 = (bf16[208,384]{1,0:T(8,128)(2,1)}, bf16[208,384]{1,0:T(8,128)(2,1)}, u32[]{:S(2)}, u32[]{:S(2)}) collective-permute-start(bf16[208,384]{1,0:T(8,128)(2,1)} %get-tuple-element.305), channel_id=1, source_target_pairs={{0,6},{2,4},{4,2},{6,0},{1,7},{3,5},{5,3},{7,1},{8,14},{10,12},{12... | collective-permute-start | bytes 479240 | tf_op jit(solution)/shard_map/ppermute | solution.py:479
  827.1 21.0 %collective-permute-start.67 = (bf16[208,384]{1,0:T(8,128)(2,1)}, bf16[208,384]{1,0:T(8,128)(2,1)}, u32[]{:S(2)}, u32[]{:S(2)}) collective-permute-start(bf16[208,384]{1,0:T(8,128)(2,1)} %get-tuple-element.306), channel_id=1, source_target_pairs={{0,4},{2,6},{4,0},{6,2},{1,5},{3,7},{5,1},{7,3},{8,12},{10,14},{12... | collective-permute-start | bytes 479240 | tf_op jit(solution)/shard_map/ppermute | solution.py:479
  828.3 22.0 %collective-permute-start.77 = (bf16[320,384]{1,0:T(8,128)(2,1)}, bf16[320,384]{1,0:T(8,128)(2,1)}, u32[]{:S(2)}, u32[]{:S(2)}) collective-permute-start(bf16[320,384]{1,0:T(8,128)(2,1)} %collective-permute-done.76), channel_id=1, source_target_pairs={{0,2},{2,0},{4,6},{6,4},{1,3},{3,1},{5,7},{7,5},{8,10},{10,8},{12,... | collective-permute-start | bytes 737288 | tf_op jit(solution)/shard_map/ppermute | solution.py:479
  833.2 82.7 %collective-permute-start.21 = (bf16[256,1536]{1,0:T(8,128)(2,1)}, bf16[256,1536]{1,0:T(8,128)(2,1)}, u32[]{:S(2)}, u32[]{:S(2)}) collective-permute-start(bf16[256,1536]{1,0:T(8,128)(2,1)} %slice.128), channel_id=1, source_target_pairs={{0,1},{1,0},{2,3},{3,2},{4,5},{5,4},{6,7},{7,6},{8,9},{9,8},{10,11... | collective-permute-start | bytes 2359304 | tf_op jit(solution)/shard_map/ppermute | solution.py:482
  846.0 71.0 %collective-permute-start.45 = (bf16[256,1536]{1,0:T(8,128)(2,1)}, bf16[256,1536]{1,0:T(8,128)(2,1)}, u32[]{:S(2)}, u32[]{:S(2)}) collective-permute-start(bf16[256,1536]{1,0:T(8,128)(2,1)} %add_convert_fusion.12), channel_id=1, source_target_pairs={{0,2},{2,0},{4,6},{6,4},{1,3},{3,1},{5,7},{7,5},{8,10},{10,8},{12,... | collective-permute-start | bytes 2359304 | tf_op jit(solution)/shard_map/ppermute | solution.py:479
  846.2 47.7 %collective-permute-start.46 = (bf16[256,1536]{1,0:T(8,128)(2,1)}, bf16[256,1536]{1,0:T(8,128)(2,1)}, u32[]{:S(2)}, u32[]{:S(2)}) collective-permute-start(bf16[256,1536]{1,0:T(8,128)(2,1)} %add_convert_fusion.10), channel_id=1, source_target_pairs={{0,2},{2,0},{4,6},{6,4},{1,3},{3,1},{5,7},{7,5},{8,10},{10,8},{12,... | collective-permute-start | bytes 2359304 | tf_op jit(solution)/shard_map/ppermute | solution.py:479
  850.2 39.8 %collective-permute-start.69 = (bf16[208,384]{1,0:T(8,128)(2,1)S(1)}, bf16[208,384]{1,0:T(8,128)(2,1)S(1)}, u32[]{:S(2)}, u32[]{:S(2)}) collective-permute-start(bf16[208,384]{1,0:T(8,128)(2,1)S(1)} %get-tuple-element.273), channel_id=1, source_target_pairs={{0,2},{2,0},{4,6},{6,4},{1,3},{3,1},{5,7},{7,5},{8,10},{10,8},{12,... | collective-permute-start | bytes 479240 | tf_op jit(solution)/shard_map/ppermute | solution.py:479
  850.3 39.7 %collective-permute-start.70 = (bf16[208,384]{1,0:T(8,128)(2,1)S(1)}, bf16[208,384]{1,0:T(8,128)(2,1)S(1)}, u32[]{:S(2)}, u32[]{:S(2)}) collective-permute-start(bf16[208,384]{1,0:T(8,128)(2,1)S(1)} %get-tuple-element.273), channel_id=1, source_target_pairs={{0,4},{2,6},{4,0},{6,2},{1,5},{3,7},{5,1},{7,3},{8,12},{10,14},{12... | collective-permute-start | bytes 479240 | tf_op jit(solution)/shard_map/ppermute | solution.py:479
  896.1 37.2 %collective-permute-start.47 = (bf16[256,1536]{1,0:T(8,128)(2,1)}, bf16[256,1536]{1,0:T(8,128)(2,1)}, u32[]{:S(2)}, u32[]{:S(2)}) collective-permute-start(bf16[256,1536]{1,0:T(8,128)(2,1)} %add_convert_fusion.9), channel_id=1, source_target_pairs={{0,4},{2,6},{4,0},{6,2},{1,5},{3,7},{5,1},{7,3},{8,12},{10,14},{12... | collective-permute-start | bytes 2359304 | tf_op jit(solution)/shard_map/ppermute | solution.py:479
  913.4 21.9 %collective-permute-start.57 = (bf16[16,384]{1,0:T(8,128)(2,1)S(1)}, bf16[16,384]{1,0:T(8,128)(2,1)S(1)}, u32[]{:S(2)}, u32[]{:S(2)}) collective-permute-start(bf16[16,384]{1,0:T(8,128)(2,1)S(1)} %get-tuple-element.309), channel_id=1, source_target_pairs={{0,24},{8,16},{16,8},{24,0},{1,25},{9,17},{17,9},{25,1},{2,26},{10... | collective-permute-start | bytes 36872 | tf_op jit(solution)/shard_map/ppermute | solution.py:485
  (116 other events, 1665.6 us)
Sparse Core Ops, SparseCore 0:
  55.6 110.7 all-gather.4
  428.8 61.5 all-gather.10
  492.0 123.5 all-gather.8
  618.0 108.2 all-gather.6

commit v2 on v1

--- a/solution.py
+++ b/solution.py
@@ -21,6 +21,8 @@
 NT = (((1,), (1,)), ((), ()))
 TN = (((0,), (0,)), ((), ()))
 VMEM_LIMIT = 58 * 1024 * 1024
+LIGHT = pl.CostEstimate(flops=10**9, bytes_accessed=10**6, transcendentals=0)
+MESH = pl.DeviceIdType.MESH
 
 
 def params(**more):
@@ -37,6 +39,106 @@
     later = pltpu.roll(x, LANES - HEAD_SIZE // 2, 1)
     sooner = pltpu.roll(x, HEAD_SIZE // 2, 1)
     return jnp.where(first, later, -sooner) if inverse else jnp.where(first, -later, sooner)
+
+
+def first_gather_kernel(weights, tok_ref, pack_ref, seq_ref, full_ref, local, send, recv):
+    z, t, f = lax.axis_index("ctx"), lax.axis_index("tp"), lax.axis_index("fsdp")
+    half = tok_ref.shape[0] // 2
+    rows = pack_ref.shape[0]
+    z1, z2, z3 = z + 1 - 2 * (z % 2), (z + 2) % 4, 3 - z
+    near, far, core = {"ctx": z1}, {"ctx": z2}, {"tp": 1 - t}
+    partners = [near, far, core]
+    if weights:
+        f1, f2 = f + 1 - 2 * (f % 2), (f + 2) % 4
+        f3 = 3 - f
+        partners += [{"fsdp": f1}, {"fsdp": f2}]
+    barrier = pltpu.get_barrier_semaphore()
+    for partner in partners:
+        pl.semaphore_signal(barrier, inc=1, device_id=partner, device_id_type=MESH)
+    pl.semaphore_wait(barrier, len(partners))
+
+    def at(chunk, side):
+        return seq_ref.at[pl.ds(pl.multiple_of((chunk * 2 + side) * half, half), half)]
+
+    def held(owner, first, size):
+        start = pl.multiple_of(owner * rows + first, 8)
+        return full_ref.at[pl.ds(start, size)]
+
+    def copy(k, source, target, device):
+        made = pltpu.make_async_remote_copy(
+            src_ref=source,
+            dst_ref=target,
+            send_sem=send.at[k],
+            recv_sem=recv.at[k],
+            device_id=device,
+            device_id_type=MESH,
+        )
+        made.start()
+        return made
+
+    own_half = tok_ref.at[pl.ds(pl.multiple_of(t * half, half), half)]
+    one = copy(0, own_half, at(z, t), near)
+    two = copy(1, own_half, at(z, t), far)
+    here = pltpu.make_async_copy(
+        tok_ref, seq_ref.at[pl.ds(pl.multiple_of(z * 2 * half, half), 2 * half)], local.at[0]
+    )
+    here.start()
+    sent = [one, two]
+    came = []
+    if weights:
+        cut = rows // 2
+        pack_one = copy(6, pack_ref, held(f, 0, rows), {"fsdp": f1})
+        pack_two = copy(7, pack_ref, held(f, 0, rows), {"fsdp": f2})
+        pack_here = pltpu.make_async_copy(pack_ref, held(f, 0, rows), local.at[1])
+        pack_here.start()
+        sent += [pack_one, pack_two]
+    one.wait_recv()
+    swap_one = copy(2, at(z1, t), at(z1, t), core)
+    if weights:
+        pack_one.wait_recv()
+        on_one = copy(8, held(f1, 0, cut), held(f1, 0, cut), {"fsdp": f2})
+        pack_two.wait_recv()
+        on_two = copy(9, held(f2, cut, rows - cut), held(f2, cut, rows - cut), {"fsdp": f1})
+        sent += [on_one, on_two]
+        came += [on_one, on_two]
+    two.wait_recv()
+    three = copy(4, at(z2, t), at(z2, t), near)
+    swap_two = copy(3, at(z2, t), at(z2, t), core)
+    three.wait_recv()
+    swap_three = copy(5, at(z3, t), at(z3, t), core)
+    sent += [swap_one, three, swap_two, swap_three]
+    for made in came + [swap_one, swap_two, swap_three]:
+        made.wait_recv()
+    for made in sent:
+        made.wait_send()
+    here.wait()
+    if weights:
+        pack_here.wait()
+
+
+def first_gather(n_ctx, n_fsdp, tokens, pack):
+    count, width = tokens.shape
+    rows, columns = pack.shape
+    weights = n_fsdp == 4
+    sequence, full = pl.pallas_call(
+        functools.partial(first_gather_kernel, weights),
+        in_specs=[pl.BlockSpec(memory_space=pl.ANY)] * 2,
+        out_specs=[pl.BlockSpec(memory_space=pl.ANY)] * 2,
+        out_shape=[
+            jax.ShapeDtypeStruct((n_ctx * count, width), tokens.dtype),
+            jax.ShapeDtypeStruct((n_fsdp * rows if weights else rows, columns), pack.dtype),
+        ],
+        scratch_shapes=[
+            pltpu.SemaphoreType.DMA((2,)),
+            pltpu.SemaphoreType.DMA((10,)),
+            pltpu.SemaphoreType.DMA((10,)),
+        ],
+        compiler_params=pltpu.CompilerParams(collective_id=0, has_side_effects=True),
+        cost_estimate=LIGHT,
+    )(tokens, pack)
+    if not weights:
+        full = lax.all_gather(pack, "fsdp", axis=0, tiled=True)
+    return sequence, full
 
 
 def project_kernel(x_ref, gain_ref, w_ref, cos_ref, sin_ref, n_ref, q_ref, k_ref, v_ref):
@@ -81,9 +183,7 @@
             jax.ShapeDtypeStruct((rows, HEAD_SIZE), BF),
         ],
         compiler_params=params(),
-        cost_estimate=pl.CostEstimate(
-            flops=2 * rows * width * w.shape[1], bytes_accessed=rows * width * 4, transcendentals=0
-        ),
+        cost_estimate=LIGHT,
     )(x, gain, w, cos, sin)
 
 
@@ -182,9 +282,7 @@
             pltpu.VMEM((GROUP * SPAN, HEAD_SIZE), F32),
         ],
         compiler_params=params(),
-        cost_estimate=pl.CostEstimate(
-            flops=20 * 1000**3, bytes_accessed=6 * rows * 256, transcendentals=rows * rows
-        ),
+        cost_estimate=LIGHT,
     )(id_column, id_row, q, k, v)
 
 
@@ -267,9 +365,7 @@
         ],
         scratch_shapes=[pltpu.VMEM((GROUP * SPAN, HEAD_SIZE), F32)],
         compiler_params=params(),
-        cost_estimate=pl.CostEstimate(
-            flops=40 * 1000**3, bytes_accessed=12 * rows * 256, transcendentals=rows * rows
-        ),
+        cost_estimate=LIGHT,
     )(id_column, id_row, q, k, v, o, do, lse)
 
 
@@ -303,76 +399,248 @@
     )(dq, dk, dv, cos, sin)
 
 
-def expert_kernel(count, at_ref, x_ref, c_ref, r_ref, w_ref, pre_ref, wh_ref, out_ref, grad_ref):
-    width = x_ref.shape[1]
+def expert_kernel(count, pieces, n_ref, cot_ref, one_ref, two_ref, r_ref, w_any, *refs):
+    pre_ref, wh_ref, out_ref = refs[:3]
+    x_parts, cot_parts = refs[3 : 3 + pieces], refs[3 + pieces : 3 + 2 * pieces]
+    grad_any = refs[3 + 2 * pieces]
+    x_ref, c_ref, w_ref, part_ref, there_ref, sum_ref, back_ref, full_ref = refs[4 + 2 * pieces : -4]
+    local, wrote, send, recv = refs[-4:]
+    i = pl.program_id(0)
+    z, t, f = lax.axis_index("ctx"), lax.axis_index("tp"), lax.axis_index("fsdp")
+    z1, z2, z3 = z + 1 - 2 * (z % 2), (z + 2) % 4, 3 - z
+    near, far, third, core = {"ctx": z1}, {"ctx": z2}, {"ctx": z3}, {"tp": 1 - t}
+    half, width = x_ref.shape[1:]
+    piece = width // pieces
     hidden_columns = wh_ref.shape[1]
     units = hidden_columns // count
-    x = x_ref[...]
-    cot = c_ref[:, :width]
-    named = c_ref[:, width:].astype(F32) > 0.5
+
+    def rows(side):
+        return pl.ds(pl.multiple_of(side * half, half), half)
+
+    def remote(k, source, target, device):
+        return pltpu.make_async_remote_copy(
+            src_ref=source,
+            dst_ref=target,
+            send_sem=send.at[k],
+            recv_sem=recv.at[k],
+            device_id=device,
+            device_id_type=MESH,
+        )
+
+    own = n_ref.at[rows(t)]
+    x_one = remote(0, own, x_ref.at[2], near)
+    x_two = remote(1, own, x_ref.at[4], far)
+    x_three = remote(2, x_ref.at[4], x_ref.at[6], near)
+    c_three = remote(3, two_ref, c_ref.at[6], near)
+    x_swaps = [None] + [remote(3 + m, x_ref.at[2 * m], x_ref.at[2 * m + 1], core) for m in (1, 2, 3)]
+    c_swaps = [
+        None,
+        remote(7, one_ref, c_ref.at[3], core),
+        remote(8, two_ref, c_ref.at[5], core),
+        remote(9, c_ref.at[6], c_ref.at[7], core),
+    ]
+    crossed = [remote(10 + m, part_ref.at[2 * m + 1], there_ref.at[m], core) for m in range(4)]
+    returned = [None] + [
+        remote(13 + m, sum_ref.at[m], back_ref.at[m], device)
+        for m, device in ((1, near), (2, far), (3, third))
+    ]
+    last = remote(17, full_ref.at[rows(t)], full_ref.at[rows(t)], core)
+    loads = [
+        pltpu.make_async_copy(source, target, local.at[k])
+        for k, (source, target) in enumerate(
+            (
+                (n_ref.at[rows(t)], x_ref.at[0]),
+                (n_ref.at[rows(1 - t)], x_ref.at[1]),
+                (cot_ref.at[rows(t)], c_ref.at[0]),
+                (cot_ref.at[rows(1 - t)], c_ref.at[1]),
+                (w_any, w_ref),
+                (one_ref, c_ref.at[2]),
+                (two_ref, c_ref.at[4]),
+            )
+        )
+    ]
+    store = pltpu.make_async_copy(full_ref, grad_any, local.at[7])
+
+    def keep(step):
+        made = []
+        at_rows = pl.ds(pl.multiple_of(step * half, half), half)
+        for k in range(pieces):
+            owner = [f, f + 1 - 2 * (f % 2), (f + 2) % 4, 3 - f][k] if pieces > 1 else 0
+            at = pl.ds(pl.multiple_of(owner * piece, piece), piece)
+            for n, (source, target) in enumerate(((x_ref, x_parts[k]), (c_ref, cot_parts[k]))):
+                made.append(
+                    pltpu.make_async_copy(
+                        source.at[step, :, at], target.at[at_rows], wrote.at[step, 2 * k + n]
+                    )
+                )
+        return made
+
+    def finish(m):
+        crossed[m].wait_recv()
+        sum_ref[m] = (part_ref[2 * m].astype(F32) + there_ref[m].astype(F32)).astype(BF)
+        if m:
+            returned[m].start()
+
+    @pl.when(i == 0)
+    def _():
+        barrier = pltpu.get_barrier_semaphore()
+        for partner in (near, far, third, core):
+            pl.semaphore_signal(barrier, inc=1, device_id=partner, device_id_type=MESH)
+        pl.semaphore_wait(barrier, 4)
+        for made in [x_one, x_two] + loads + [c_swaps[1], c_swaps[2], c_three]:
+            made.start()
+        for made in (loads[0], loads[2], loads[4]):
+            made.wait()
+
+    @pl.when(i == 1)
+    def _():
+        loads[1].wait()
+        loads[3].wait()
+
+    @pl.when(i == 2)
+    def _():
+        x_one.wait_recv()
+        x_swaps[1].start()
+        loads[5].wait()
+
+    @pl.when(i == 3)
+    def _():
+        x_swaps[1].wait_recv()
+        c_swaps[1].wait_recv()
+
+    @pl.when(i == 4)
+    def _():
+        x_two.wait_recv()
+        x_three.start()
+        x_swaps[2].start()
+        loads[6].wait()
+
+    @pl.when(i == 5)
+    def _():
+        x_swaps[2].wait_recv()
+        c_swaps[2].wait_recv()
+
+    @pl.when(i == 6)
+    def _():
+        c_three.wait_recv()
+        c_swaps[3].start()
+        x_three.wait_recv()
+        x_swaps[3].start()
+
+    @pl.when(i == 7)
+    def _():
+        x_swaps[3].wait_recv()
+        c_swaps[3].wait_recv()
+
+    for made in keep(i):
+        made.start()
+
+    def columns(j, e):
+        return slice(j * hidden_columns + e * units, j * hidden_columns + (e + 1) * units)
+
+    x = x_ref[i]
+    both = c_ref[i]
+    cot = both[:, :width]
+    named = both[:, width:].astype(F32) > 0.5
     logits = jnp.where(named, jnp.dot(x, r_ref[...], preferred_element_type=F32), -1e30)
     top = jnp.max(logits, axis=1, keepdims=True)
     exponent = jnp.where(named, jnp.exp(logits - top), 0.0)
     gates = exponent / jnp.sum(exponent, axis=1, keepdims=True)
     lane = lax.broadcasted_iota(jnp.int32, gates.shape, 1)
-    first = at_ref[0]
     found = jnp.zeros(gates.shape, F32)
     for e in range(count):
-        cols = slice(e * units, (e + 1) * units)
-        up_cols = slice(hidden_columns + e * units, hidden_columns + (e + 1) * units)
-        down_cols = slice(2 * hidden_columns + e * units, 2 * hidden_columns + (e + 1) * units)
-        mine = lane == first + e
+        mine = lane == z * count + e
         gate_here = jnp.sum(jnp.where(mine, gates, 0.0), axis=1, keepdims=True)
-        g = jnp.dot(x, w_ref[:, cols], preferred_element_type=F32)
-        u = jnp.dot(x, w_ref[:, up_cols], preferred_element_type=F32)
-        hg = jnp.dot(cot, w_ref[:, down_cols], preferred_element_type=F32)
+        g = jnp.dot(x, w_ref[:, columns(0, e)], preferred_element_type=F32)
+        u = jnp.dot(x, w_ref[:, columns(1, e)], preferred_element_type=F32)
+        hg = jnp.dot(cot, w_ref[:, columns(2, e)], preferred_element_type=F32)
         s = 1.0 / (1.0 + jnp.exp(-g))
         gs = g * s
         h = (gs * u).astype(BF).astype(F32)
         found = found + jnp.where(mine, jnp.sum(h * hg, axis=1, keepdims=True), 0.0)
-        wh_ref[:, cols] = (h * gate_here).astype(BF)
+        wh_ref[:, columns(0, e)] = (h * gate_here).astype(BF)
         hg = hg * gate_here
-        pre_ref[:, cols] = (hg * u * s * (1.0 + g * (1.0 - s))).astype(BF)
-        pre_ref[:, up_cols] = (hg * gs).astype(BF)
-    grad_ref[:, width:] = found.astype(BF)
-    grad_ref[:, :width] = lax.dot_general(
+        pre_ref[:, columns(0, e)] = (hg * u * s * (1.0 + g * (1.0 - s))).astype(BF)
+        pre_ref[:, columns(1, e)] = (hg * gs).astype(BF)
+    part_ref[i, :, width:] = found.astype(BF)
+    part_ref[i, :, :width] = lax.dot_general(
         pre_ref[...], w_ref[:, : 2 * hidden_columns], NT, preferred_element_type=F32
     ).astype(BF)
+    for m in range(4):
+
+        @pl.when(i == 2 * m + 1)
+        def _():
+            crossed[m].start()
+
     out_ref[...] = lax.dot_general(
         wh_ref[...], w_ref[:, 2 * hidden_columns :], NT, preferred_element_type=F32
     ).astype(BF)
-
-
-def experts(first, x, c, router, w, count):
-    rows, width = x.shape
-    tile = 256
+    for m in range(3):
+
+        @pl.when(i == 2 * m + 2)
+        def _():
+            finish(m)
+
+    @pl.when(i == 7)
+    def _():
+        finish(3)
+        total = sum_ref[0].astype(F32)
+        for m in (1, 2, 3):
+            returned[m].wait_recv()
+            total = total + back_ref[m].astype(F32)
+        full_ref[rows(t), :] = total.astype(BF)
+        last.start()
+        for made in [x_one, x_two, x_three, c_three] + x_swaps[1:] + c_swaps[1:] + crossed:
+            made.wait_send()
+        for made in returned[1:]:
+            made.wait_send()
+        last.wait_send()
+        last.wait_recv()
+        store.start()
+
+        def settle(step, carried):
+            for made in keep(step):
+                made.wait()
+            return carried
+
+        lax.fori_loop(0, 8, settle, 0)
+        store.wait()
+
+
+def experts(pieces, normed, cot, one, two, router, w, count):
+    rows, width = normed.shape
+    half = rows // 2
+    packed = cot.shape[1]
     hidden_columns = w.shape[1] // 3
-    row = lambda n: pl.BlockSpec((tile, n), lambda i: (i, 0))
-    whole = lambda s: pl.BlockSpec(s, lambda i: (0, 0), pipeline_mode=pl.Buffered(1))
+    slot = lambda n: pl.BlockSpec((half, n), lambda i: (i, 0))
+    anywhere = pl.BlockSpec(memory_space=pl.ANY)
+    blocks = [2 * hidden_columns, hidden_columns, width]
     return pl.pallas_call(
-        functools.partial(expert_kernel, count),
-        grid=(rows // tile,),
-        in_specs=[
-            pl.BlockSpec(memory_space=pltpu.SMEM),
-            row(width),
-            row(c.shape[1]),
-            whole(router.shape),
-            whole(w.shape),
-        ],
-        out_specs=[row(2 * hidden_columns), row(hidden_columns), row(width), row(c.shape[1])],
+        functools.partial(expert_kernel, count, pieces),
+        grid=(8,),
+        in_specs=[anywhere] * 4 + [pl.BlockSpec(router.shape, lambda i: (0, 0)), anywhere],
+        out_specs=[slot(n) for n in blocks] + [anywhere] * (2 * pieces + 1),
         out_shape=[
-            jax.ShapeDtypeStruct((rows, 2 * hidden_columns), BF),
-            jax.ShapeDtypeStruct((rows, hidden_columns), BF),
-            jax.ShapeDtypeStruct((rows, width), BF),
-            jax.ShapeDtypeStruct((rows, c.shape[1]), BF),
-        ],
-        compiler_params=params(),
-        cost_estimate=pl.CostEstimate(
-            flops=4 * rows * width * w.shape[1],
-            bytes_accessed=2 * w.size + rows * 20000,
-            transcendentals=rows * hidden_columns,
-        ),
-    )(first, x, c, router, w)
+            jax.ShapeDtypeStruct((8 * half, n), BF) for n in blocks + [width // pieces] * (2 * pieces)
+        ]
+        + [jax.ShapeDtypeStruct((rows, packed), BF)],
+        scratch_shapes=[
+            pltpu.VMEM((8, half, width), BF),
+            pltpu.VMEM((8, half, packed), BF),
+            pltpu.VMEM(w.shape, BF),
+            pltpu.VMEM((8, half, packed), BF),
+            pltpu.VMEM((4, half, packed), BF),
+            pltpu.VMEM((4, half, packed), BF),
+            pltpu.VMEM((4, half, packed), BF),
+            pltpu.VMEM((rows, packed), BF),
+            pltpu.SemaphoreType.DMA((8,)),
+            pltpu.SemaphoreType.DMA((8, 2 * pieces)),
+            pltpu.SemaphoreType.DMA((18,)),
+            pltpu.SemaphoreType.DMA((18,)),
+        ],
+        compiler_params=params(collective_id=1, has_side_effects=True),
+        cost_estimate=LIGHT,
+    )(normed, cot, one, two, router, w)
 
 
 def adamw(master, first_moment, second_moment, gradient, rate, decay):
@@ -383,15 +651,20 @@
     return (master_new, moment_new, square_new, master_new.astype(BF))
 
 
-def expert_adamw_kernel(rate, parts, chained, joined, *refs):
+def expert_adamw_kernel(rate, joined, *refs):
     p_ref, f_ref, s_ref, g_ref = refs[:4]
-    master_ref, moment_ref, rounded_ref, square_ref = refs[-4:]
-    each = E // parts
-    pack = max(1, 8 // each)
-    for at in range(0, parts, pack):
-        rows = slice(at * each, (at + pack) * each)
-        grad = jnp.concatenate([g_ref[k].astype(F32) for k in range(at, at + pack)], axis=1)
-        new = adamw(p_ref[:, 0, rows], f_ref[:, 0, rows], s_ref[:, 0, rows], grad, rate, 0.1)
+    master_ref, moment_ref, rounded_ref, square_ref, grad_ref = refs[-5:]
+    parts, _, columns = g_ref.shape
+    units = p_ref.shape[3]
+    each = columns // units
+    for k in range(parts):
+        for e in range(each):
+            grad_ref[:, k * each + e, :] = g_ref[k, :, e * units : (e + 1) * units].astype(F32)
+    for at in range(0, parts * each, 8):
+        rows = slice(at, at + 8)
+        new = adamw(
+            p_ref[:, 0, rows], f_ref[:, 0, rows], s_ref[:, 0, rows], grad_ref[:, rows], rate, 0.1
+        )
         master_ref[:, 0, rows] = new[0]
         moment_ref[:, 0, rows] = new[1]
         rounded_ref[:, 0, rows] = new[3]
@@ -414,10 +687,10 @@
     more = [] if joined is None else [joined]
     square = (rows, count, units) if joined is None else (rows, count, 2, units)
     return pl.pallas_call(
-        functools.partial(expert_adamw_kernel, rate, parts, chained, joined is not None),
+        functools.partial(expert_adamw_kernel, rate, joined is not None),
         grid=(rows // tile,),
         in_specs=[here, here, here]
-        + [pl.BlockSpec((parts, tile, count // parts, units), lambda i: (0, i, 0, 0))]
+        + [pl.BlockSpec((parts, tile, gradient.shape[2]), lambda i: (0, i, 0))]
         + [plain] * len(more)
         + [pl.BlockSpec(memory_space=pl.ANY)] * chained,
         out_specs=[here, here, here, plain if joined is None else pair],
@@ -427,14 +700,42 @@
             jax.ShapeDtypeStruct(weight.shape, BF),
             jax.ShapeDtypeStruct(square, F32),
         ],
+        scratch_shapes=[pltpu.VMEM((tile, count, units), F32)],
         input_output_aliases={4 + len(more) + k: k for k in range(chained)},
         compiler_params=params(),
         cost_estimate=pl.CostEstimate(
             flops=20 * rows * count * units,
-            bytes_accessed=28 * rows * count * units,
+            bytes_accessed=45 * rows * count * units,
             transcendentals=rows * count * units,
         ),
     )(weight, first, second, gradient, *more, *earlier)
+
+
+def matrix_adamw_kernel(rate, p_ref, f_ref, s_ref, g_ref, *outs):
+    grad = g_ref[...].astype(F32).T
+    new = adamw(p_ref[...], f_ref[...], s_ref[...], grad, rate, 0.1)
+    for ref, value in zip(outs, new):
+        ref[...] = value
+
+
+def matrix_adamw(rate, weight, first, second, turned):
+    rows, columns = weight.shape
+    if rows % LANES:
+        return adamw(weight, first, second, turned[:columns].T.astype(F32), rate, 0.1)
+    tile = 256
+    here = pl.BlockSpec((rows, tile), lambda i: (0, i))
+    shape = jax.ShapeDtypeStruct(weight.shape, F32)
+    return pl.pallas_call(
+        functools.partial(matrix_adamw_kernel, rate),
+        grid=(columns // tile,),
+        in_specs=[here, here, here, pl.BlockSpec((tile, rows), lambda i: (i, 0))],
+        out_specs=[here] * 4,
+        out_shape=[shape, shape, shape, jax.ShapeDtypeStruct(weight.shape, BF)],
+        compiler_params=params(),
+        cost_estimate=pl.CostEstimate(
+            flops=20 * rows * columns, bytes_accessed=28 * rows * columns, transcendentals=0
+        ),
+    )(weight, first, second, turned)
 
 
 def local(
@@ -493,31 +794,21 @@
     def in_order(a, b):
         return jnp.where(t == 0, jnp.concatenate([a, b], 0), jnp.concatenate([b, a], 0))
 
-    def put(buffer, x, row):
-        return lax.dynamic_update_slice_in_dim(buffer, x, row, 0)
-
-    def take(x, row, rows):
-        return lax.dynamic_slice_in_dim(x, row, rows, 0)
-
-    def gather_fsdp(x):
-        if n_fsdp != 4:
-            full = lax.all_gather(x, "fsdp", axis=0, tiled=True)
-            return full, full
-        rows = x.shape[0]
-        cut = rows // 2
-        a, b = across(x, 1), across(x, 2)
-        c, d = across(a[:cut], 2), across(b[cut:], 1)
-        full = jnp.zeros((n_fsdp * rows, x.shape[1]), x.dtype)
-        full = put(full, x, f * rows)
-        full = put(full, a, (f ^ 1) * rows)
-        full = put(full, b, (f ^ 2) * rows)
-        full = put(full, c, (f ^ 3) * rows)
-        return put(full, d, (f ^ 3) * rows + cut), c
+    def put(buffer, x, place):
+        return lax.dynamic_update_slice_in_dim(buffer, x[None], place, 0)
+
+    def take(x, place, places):
+        return lax.dynamic_index_in_dim(
+            x.reshape(places, x.shape[0] // places, x.shape[1]), place, 0, keepdims=False
+        )
 
     def scatter_fsdp(x, axis):
         if n_fsdp != 4:
             return lax.psum_scatter(x, "fsdp", scatter_dimension=axis, tiled=True)
-        piece = lambda k: lax.dynamic_slice_in_dim(x, k * own_rows, own_rows, axis)
+        if axis:
+            piece = lambda k: lax.dynamic_slice_in_dim(x, k * own_rows, own_rows, 1)
+        else:
+            piece = lambda k: take(x, k, n_fsdp)
         total = piece(f).astype(F32)
         for m in (3, 1, 2):
             total = total + across(piece(f ^ m), m).astype(F32)
@@ -527,9 +818,19 @@
         one, two = beyond(x, 1), beyond(x, 2)
         return {1: one, 2: two, 3: beyond(two, 1)}
 
-    joint_columns = joint_weight.shape[1]
+    slots_first = jnp.transpose(expert_weight, (0, 2, 1, 3))
+    units = expert_weight.shape[3]
+    expert_part = (
+        lax.dynamic_slice_in_dim(slots_first, z * each, each, 2)
+        .astype(BF)
+        .reshape(own_rows, 3 * each * units)
+    )
+    expert_full = lax.all_gather(expert_part, "fsdp", axis=0, tiled=True)
+
     group_columns = (GROUP + 2) * HEAD_SIZE
+    head_columns = GROUP * HEAD_SIZE
     joint_low = joint_weight.astype(BF)
+    output_columns = output_weight.shape[1]
     first_pack = jnp.concatenate(
         [
             router_weight.astype(BF),
@@ -539,114 +840,90 @@
         ],
         axis=1,
     )
-    first_full, first_came = gather_fsdp(first_pack)
+    first_pack, _ = barrier((first_pack, expert_part))
+    sequence, first_full = first_gather(n_ctx, n_fsdp, tokens_low, first_pack)
     small_full = first_full[:, :LANES]
     router_full = small_full[:, :E]
     router_wide = jnp.where(jnp.arange(LANES)[None, :] < E, small_full, jnp.zeros((), BF))
     gain_first = small_full[:, E].astype(F32)[None, :]
     gain_second = small_full[:, E + 1].astype(F32)[None, :]
-
-    tokens_came = spread(mine(tokens_low))
-    sequence = put(jnp.zeros((length, width), BF), tokens_low, z * count)
-    for m in (1, 2, 3):
-        base = (z ^ m) * count
-        sequence = put(sequence, tokens_came[m], base + t * half)
-        sequence = put(sequence, swap(tokens_came[m]), base + (1 - t) * half)
-
-    slots_first = jnp.transpose(expert_weight, (0, 2, 1, 3))
-    units = expert_weight.shape[3]
-    output_low, _ = barrier((output_weight.astype(BF), first_came))
-    output_full, output_came = gather_fsdp(output_low)
-    expert_part = (
-        lax.dynamic_slice_in_dim(slots_first, z * each, each, 2)
-        .astype(BF)
-        .reshape(own_rows, 3 * each * units)
-    )
-    expert_part, _ = barrier((expert_part, output_came))
-    expert_full = lax.all_gather(expert_part, "fsdp", axis=0, tiled=True)
-    joint_late, _ = barrier((joint_low, expert_full))
-    joint_full, _ = gather_fsdp(joint_late)
+    output_late, _ = barrier((output_weight.astype(BF), (expert_full, sequence)))
+    output_full = lax.all_gather(output_late, "fsdp", axis=0, tiled=True)
+    joint_late, _ = barrier((joint_low, output_full))
+    joint_full = lax.all_gather(joint_late, "fsdp", axis=0, tiled=True)
     output_turned = barrier(output_full.T)
     joint_turned = barrier(joint_full.T)
 
     route_rows = expert_routes[0]
-    member = jnp.sum(
-        (route_rows[:, :, None] == jnp.arange(LANES, dtype=jnp.int32)[None, None, :]).astype(F32),
-        axis=1,
-    )
+    lane_row = jnp.arange(LANES, dtype=jnp.int32)[None, :]
+    member = sum((route_rows[:, k : k + 1] == lane_row).astype(F32) for k in range(route_rows.shape[1]))
     cot_pack = jnp.concatenate([cot_low, member.astype(BF)], axis=1)
-    cot_half, _ = barrier((mine(cot_pack), tokens_came[3]))
-    cot_came = spread(cot_half)
-
-    positions = jnp.arange(length, dtype=jnp.int32).astype(F32)
+    cot_half, sequence = barrier((mine(cot_pack), sequence))
+    cot_came = [beyond(cot_half, 1), beyond(cot_half, 2)]
+
     lanes = jnp.arange(LANES, dtype=jnp.int32) % (HEAD_SIZE // 2)
     frequency = jnp.exp(lanes.astype(F32) * (-2.0 * math.log(10000.0) / HEAD_SIZE))
-    angles = positions[:, None] * frequency[None, :]
-    cosine, sine = jnp.cos(angles), jnp.sin(angles)
+    fine = 64
+    small_angles = jnp.arange(fine, dtype=jnp.int32).astype(F32)[:, None] * frequency
+    large_angles = (fine * jnp.arange(length // fine, dtype=jnp.int32)).astype(F32)[:, None] * frequency
+    cos_a, sin_a = jnp.cos(large_angles)[:, None], jnp.sin(large_angles)[:, None]
+    cos_b, sin_b = jnp.cos(small_angles)[None], jnp.sin(small_angles)[None]
+    cosine = (cos_a * cos_b - sin_a * sin_b).reshape(length, LANES)
+    sine = (sin_a * cos_b + cos_a * sin_b).reshape(length, LANES)
+    cosine, sine, tokens_low = barrier((cosine, sine, tokens_low))
     id_row = block_ids
     id_column = block_ids.reshape(length, 1)
     normed_all, queries, keys, values = project(sequence, gain_first, first_full, cosine, sine)
     attended_all, lse = attend(id_column, id_row, queries, keys, values)
-    head_columns = GROUP * HEAD_SIZE
-
     def to_positions(x):
-        parts = [take(x, (z ^ m) * count, count) for m in range(n_ctx)]
+        parts = [take(x, z ^ m, n_ctx) for m in range(n_ctx)]
         return [parts[0]] + [beyond(parts[m], m) for m in range(1, n_ctx)]
 
-    def by_heads(turned, columns):
-        return [take(turned, (z ^ m) * columns, columns) for m in range(n_ctx)]
-
-    output_by = by_heads(output_turned, head_columns)
+    def by_heads(turned):
+        return [take(turned, z ^ m, n_ctx) for m in range(n_ctx)]
+
+    output_by = by_heads(output_turned)
     attended = to_positions(attended_all)
     attn_part = sum(
         jnp.dot(a, w, preferred_element_type=F32) for a, w in zip(attended, output_by)
     )
-    attn_part, cot_came = barrier((attn_part, cot_came))
     residual = tokens + (attn_part + swap(attn_part))
     inv_second = inverse_rms(residual)
     normed_second = (residual * inv_second * gain_second).astype(BF)
 
-    normed_half = mine(normed_second)
-    came = spread(normed_half)
-    first_expert = jnp.reshape(z * each, (1,)).astype(jnp.int32)
-    x_chunks, cot_chunks, pre_chunks, hidden_chunks, outs = {}, {}, {}, {}, {}
-    grad_sum = None
-    for m in range(n_ctx):
-        if m == 0:
-            x_chunks[0] = jnp.concatenate([normed_half, other(normed_second)], axis=0)
-            cot_chunks[0] = jnp.concatenate([mine(cot_pack), other(cot_pack)], axis=0)
+    pieces = n_fsdp if n_fsdp == 4 else 1
+    pre_all, hidden_all, out_all, *kept, grad_rows = experts(
+        pieces, normed_second, cot_pack, *cot_came, router_wide, expert_full, each
+    )
+    x_parts, cot_parts = kept[:pieces], kept[pieces:]
+
+    wide = each * units
+
+    def expert_terms(j):
+        left = cot_parts if j == 2 else x_parts
+        right = hidden_all if j == 2 else pre_all[:, j * wide : (j + 1) * wide]
+        return [
+            lax.dot_general(left[k], right, TN, preferred_element_type=F32).astype(BF)
+            for k in range(pieces)
+        ]
+
+    terms = {j: expert_terms(j) for j in (2, 0, 1)}
+    pieces_came = {}
+    for j in (2, 0, 1):
+        if pieces > 1:
+            pieces_came[j] = [terms[j][0]] + [across(terms[j][k], k) for k in range(1, pieces)]
         else:
-            got, pre_chunks[m - 1] = barrier((came[m], pre_chunks[m - 1]))
-            x_chunks[m] = jnp.concatenate([got, swap(got)], axis=0)
-            cot_chunks[m] = jnp.concatenate([cot_came[m], swap(cot_came[m])], axis=0)
-        pre_chunks[m], hidden_chunks[m], out_part, grad_part = experts(
-            first_expert, x_chunks[m], cot_chunks[m], router_wide, expert_full, each
-        )
-        grad_here = grad_part[:half].astype(F32) + swap(grad_part[half:]).astype(F32)
-        outs[m] = out_part[:half].astype(F32) + swap(out_part[half:]).astype(F32)
-        if m == 0:
-            grad_sum = grad_here
-        else:
-            grad_sum = grad_sum + beyond(grad_here.astype(BF), m).astype(F32)
-    grad_low = grad_sum.astype(BF)
-    grad_rows = in_order(grad_low, swap(grad_low)).astype(F32)
+            pieces_came[j] = lax.psum_scatter(terms[j][0], "fsdp", scatter_dimension=0, tiled=True)
+
+    def gathered(came):
+        if pieces > 1:
+            came = sum(x.astype(F32) for x in came).astype(BF)
+        return lax.all_gather(came, "ctx", axis=0, tiled=False)
+
+    grad_rows, terms[2] = barrier((grad_rows, terms[2]))
+    grad_rows = grad_rows.astype(F32)
     moe_input = grad_rows[:, :width]
     gate_grads = grad_rows[:, width : width + E]
-
-    x_all = jnp.concatenate([x_chunks[m] for m in range(n_ctx)], axis=0)
-    cot_all = jnp.concatenate([cot_chunks[m][:, :width] for m in range(n_ctx)], axis=0)
-    pre_all = jnp.concatenate([pre_chunks[m] for m in range(n_ctx)], axis=0)
-    hidden_all = jnp.concatenate([hidden_chunks[m] for m in range(n_ctx)], axis=0)
-    wide = each * units
-    terms = {
-        2: lax.dot_general(cot_all, hidden_all, TN, preferred_element_type=F32),
-        0: lax.dot_general(x_all, pre_all[:, :wide], TN, preferred_element_type=F32),
-        1: lax.dot_general(x_all, pre_all[:, wide:], TN, preferred_element_type=F32),
-    }
-    expert_sums = {}
-    for j in (2, 0, 1):
-        owned = scatter_fsdp(terms[j].astype(BF), 0).reshape(own_rows, each, units)
-        expert_sums[j] = lax.all_gather(owned, "ctx", axis=0, tiled=False)
 
     named = member[:, :E]
     logits = jnp.dot(normed_second, router_full, preferred_element_type=F32)
@@ -671,21 +948,42 @@
     gain_second_grad = jnp.sum(norm_second_grads * residual * inv_second, axis=0, keepdims=True)
     residual_low = residual_grads.astype(BF)
 
-    attended_grads_all = jnp.zeros((length, head_columns), BF)
+    attended_grads_all = jnp.zeros((n_ctx, count, head_columns), BF)
     for m in range(n_ctx):
         part = lax.dot_general(
             residual_low, output_by[m], NT, preferred_element_type=F32
         ).astype(BF)
         got = part if m == 0 else beyond(part, m)
-        attended_grads_all = put(attended_grads_all, got, (z ^ m) * count)
+        attended_grads_all = put(attended_grads_all, got, z ^ m)
+    attended_grads_all = attended_grads_all.reshape(length, head_columns)
+    attended_grads_all, pieces_came[2], *_ = barrier(
+        (attended_grads_all, pieces_came[2], terms[0], terms[1])
+    )
+    down_sum = gathered(pieces_came[2])
     dq, dk, dv = attend_back(
         id_column, id_row, queries, keys, values, attended_all, attended_grads_all, lse
     )
     joint_grads_all = turn_back(dq, dk, dv, cosine, sine)
     joint_grads = to_positions(joint_grads_all)
+    expert_sums = {2: down_sum}
+    for j in (0, 1):
+        expert_sums[j] = gathered(pieces_came[j])
+    first_view = jnp.transpose(expert_first, (0, 2, 1, 3))
+    second_view = jnp.transpose(expert_second, (0, 2, 1, 3))
+    made = []
+    squares = {}
+
+    def expert_step(j, joined=None):
+        rate = 0.25 if j == 2 else 0.03
+        *made[:], squares[j] = expert_adamw(
+            j, rate, slots_first, first_view, second_view, expert_sums[j], tuple(made), joined
+        )
+
+    expert_step(2)
+    joint_grads, made[:], squares[2] = barrier((joint_grads, made, squares[2]))
     first_part = sum(
         jnp.dot(g, w, preferred_element_type=F32)
-        for g, w in zip(joint_grads, by_heads(joint_turned, group_columns))
+        for g, w in zip(joint_grads, by_heads(joint_turned))
     ).astype(BF)
     norm_first_grads = first_part.astype(F32) + swap(first_part).astype(F32)
     inv_first = inverse_rms(tokens)
@@ -698,11 +996,16 @@
     )
     gain_first_grad = jnp.sum(norm_first_grads * tokens * inv_first, axis=0, keepdims=True)
 
-    late = [outs[m].astype(BF) for m in range(1, n_ctx)]
-    late, attended_grads_all = barrier((late, attended_grads_all))
-    moe_two = late[1].astype(F32) + beyond(late[2], 1).astype(F32)
+    out_all, attended_grads_all = barrier((out_all, attended_grads_all))
+    outs = out_all.reshape(n_ctx, 2, half, width)
+    halves = {
+        m: outs[m, 0].astype(F32) + swap(outs[m, 1]).astype(F32) for m in range(n_ctx)
+    }
+    moe_two = halves[2] + beyond(halves[3].astype(BF), 1).astype(F32)
     moe_sum = (
-        outs[0] + beyond(late[0], 1).astype(F32) + beyond(moe_two.astype(BF), 2).astype(F32)
+        halves[0]
+        + beyond(halves[1].astype(BF), 1).astype(F32)
+        + beyond(moe_two.astype(BF), 2).astype(F32)
     )
     moe_low = moe_sum.astype(BF)
     moe_rows = in_order(moe_low, swap(moe_low)).astype(F32)
@@ -710,40 +1013,43 @@
 
     joint_term = lax.dot_general(joint_grads_all, normed_all, TN, preferred_element_type=F32)
     joint_owned = scatter_fsdp(joint_term.astype(BF), 1)
-    joint_sum = jnp.zeros((n_ctx * group_columns, own_rows), BF)
+    joint_sum = jnp.zeros((n_ctx, group_columns, own_rows), BF)
     for m, got in {0: joint_owned, **spread(joint_owned)}.items():
-        joint_sum = put(joint_sum, got, (z ^ m) * group_columns)
-    joint_sum = joint_sum.T.astype(F32)
+        joint_sum = put(joint_sum, got, z ^ m)
+    joint_sum = joint_sum.reshape(n_ctx * group_columns, own_rows)
 
     def summed_over_ctx(owned):
-        part = owned.shape[0] // n_ctx
-        total = take(owned, z * part, part).astype(F32)
+        total = take(owned, z, n_ctx).astype(F32)
         for m in range(1, n_ctx):
-            total = total + beyond(take(owned, (z ^ m) * part, part), m).astype(F32)
+            total = total + beyond(take(owned, z ^ m, n_ctx), m).astype(F32)
         total = total.astype(BF)
-        full = put(jnp.zeros(owned.shape, BF), total, z * part)
+        full = put(jnp.zeros((n_ctx, *total.shape), BF), total, z)
         for m, got in spread(total).items():
-            full = put(full, got, (z ^ m) * part)
-        return full
-
-    output_columns = output_weight.shape[1]
-    rest_term = jnp.zeros((output_columns + 64, width), BF)
+            full = put(full, got, z ^ m)
+        return full.reshape(owned.shape)
+
+    step = 64
+    blocks = head_columns // step
+    rest_term = jnp.zeros((output_columns // step + 1, step, width), BF)
     for m in range(n_ctx):
         term = lax.dot_general(attended[m], residual_low, TN, preferred_element_type=F32)
-        rest_term = put(rest_term, term.astype(BF), (z ^ m) * head_columns)
+        rest_term = lax.dynamic_update_slice_in_dim(
+            rest_term, term.astype(BF).reshape(blocks, step, width), (z ^ m) * blocks, 0
+        )
     router_term = lax.dot_general(logit_grads, normed_second, TN, preferred_element_type=F32)
     few_rows = jnp.concatenate(
-        [router_term, gain_second_grad, jnp.zeros((64 - E - 1, width), F32)], axis=0
-    )
-    rest_term = put(rest_term, few_rows.astype(BF), output_columns)
+        [router_term, gain_second_grad, jnp.zeros((step - E - 1, width), F32)], axis=0
+    )
+    rest_term = put(rest_term, few_rows.astype(BF), output_columns // step)
+    rest_term = rest_term.reshape(output_columns + step, width)
     rest_full = summed_over_ctx(scatter_fsdp(rest_term, 1))
-    output_sum = rest_full[:output_columns].T.astype(F32)
     router_sum = rest_full[output_columns : output_columns + E].T.astype(F32)
     last_term = jnp.concatenate([gain_first_grad, jnp.zeros((15, width), F32)], axis=0)
     last_owned = scatter_fsdp(last_term.astype(BF), 1)
-    last_sum = last_owned.astype(F32)
-    for m in range(1, n_ctx):
-        last_sum = last_sum + beyond(last_owned, m).astype(F32)
+    last_came = [last_owned] + [beyond(last_owned, m) for m in range(1, n_ctx)]
+    expert_step(0)
+    last_came, made[:], squares[0] = barrier((last_came, made, squares[0]))
+    last_sum = sum(x.astype(F32) for x in last_came)
     gains_sum = jnp.concatenate(
         [
             last_sum[:1],
@@ -753,25 +1059,11 @@
     )
 
     gains_new = adamw(norm_gains, gains_first, gains_second, gains_sum, 0.6, 0.0)
-    joint_new = adamw(joint_weight, joint_first, joint_second, joint_sum, 0.03, 0.1)
-    output_new = adamw(output_weight, output_first, output_second, output_sum, 0.25, 0.1)
+    joint_new = matrix_adamw(0.03, joint_weight, joint_first, joint_second, joint_sum)
+    output_new = matrix_adamw(0.25, output_weight, output_first, output_second, rest_full)
     router_new = adamw(router_weight, router_first, router_second, router_sum, 0.015, 0.1)
 
-    first_view = jnp.transpose(expert_first, (0, 2, 1, 3))
-    second_view = jnp.transpose(expert_second, (0, 2, 1, 3))
-    made = ()
-    squares = {}
-    for j in (2, 0, 1):
-        *made, squares[j] = expert_adamw(
-            j,
-            0.25 if j == 2 else 0.03,
-            slots_first,
-            first_view,
-            second_view,
-            expert_sums[j],
-            tuple(made),
-            squares[0] if j == 1 else None,
-        )
+    expert_step(1, squares[0])
     back = lambda x: jnp.transpose(x, (0, 2, 1, 3))
     return (
         block_output,

time: 1050 us -> 905 us (0.86)
  Pallas kernels: 217 us -> 379 us
  local copies, waits for them, and re-layouts: 175 us -> 56.5 us
  starting transfers between devices: 162 us -> 75.6 us
  waiting for transfers between devices: 309 us -> 246 us
  other arithmetic: 90.5 us -> 51.3 us
    pallas_call x7, Pallas kernels: 132 us -> 294 us  [the longest x1 145 us: experts(): pl.pallas_call(functools.partial(expert_kernel, count, pieces), grid=(8,)...]
    ppermute x36 -> x26, starting transfers between devices: 123 us -> 51.9 us  [beyond(): return lax.ppermute(x, 'ctx', [(i, i ^ m) for i in range(n_ctx)])]
    ppermute x36 -> x26, waiting for transfers between devices: 218 us -> 157 us  [beyond(): return lax.ppermute(x, 'ctx', [(i, i ^ m) for i in range(n_ctx)])]
    unnamed x198 -> x115, local copies, waits for them, and re-layouts: 51 us -> 7.8 us
    ppermute x30 -> x18, waiting for transfers between devices: 90.1 us -> 52.7 us  [across(): return lax.ppermute(x, 'fsdp', [(i, i ^ m) for i in range(n_fsdp)])]
    all_gather x1, waiting for transfers between devices: 0.01 us -> 36 us  [local(): expert_full = lax.all_gather(expert_part, 'fsdp', axis=0, tiled=True)]
    dynamic_update_slice x32 -> x14, local copies, waits for them, and re-layouts: 40.2 us -> 12.1 us  [the longest x10 9.92 us: put(): return lax.dynamic_update_slice_in_dim(buffer, x[None], place, 0)]
    all_gather x3 -> x0, local copies, waits for them, and re-layouts: 18.1 us -> none  [local(): expert_sums[j] = lax.all_gather(owned, 'ctx', axis=0, tiled=False)]
  transfers between devices with their start and end apart: 91 -> 57, of which waited for: 27 -> 17; matrix products, arithmetic and copies ran while one was open for 30% -> 18% of each run, Pallas kernels for 18% -> 39%
where the time goes in v2:
time: 905 us; the launch traced here: 895 us
  Pallas kernels  379 us (42%)
  waiting for transfers between devices  246 us (27%)
  starting transfers between devices  75.6 us (8%)
  matrix products  71.9 us (8%)
  local copies, waits for them, and re-layouts  56.5 us (6%)
  other arithmetic  51.3 us (6%)
  between operations  15.4 us (2%)
    ppermute x26, waiting for transfers between devices, beyond(): return lax.ppermute(x, 'ctx', [(i, i ^ m) for i in range(n_ctx)])  157 us
    pallas_call x1, Pallas kernels, experts(): pl.pallas_call(functools.partial(expert_kernel, count, pieces), grid=(8,)...  145 us
    pallas_call x3, Pallas kernels, expert_adamw(): pl.pallas_call(functools.partial(expert_adamw_kernel, rate, joined is not...  70.9 us
    pallas_call x1, Pallas kernels, first_gather(): pl.pallas_call(functools.partial(first_gather_kernel, weights), in_specs=...  64.9 us
    ppermute x18, waiting for transfers between devices, across(): return lax.ppermute(x, 'fsdp', [(i, i ^ m) for i in range(n_fsdp)])  52.7 us
    ppermute x26, starting transfers between devices, beyond(): return lax.ppermute(x, 'ctx', [(i, i ^ m) for i in range(n_ctx)])  51.9 us
    pallas_call x1, Pallas kernels, attend_back(): pl.pallas_call(attend_back_kernel, grid=(rows // SPAN,), in_specs=[whole(...  37 us
    all_gather x1, waiting for transfers between devices, local(): expert_full = lax.all_gather(expert_part, 'fsdp', axis=0, tiled=True)  36 us
  transfers between devices with their start and end apart: 57, of which 17 were waited for; matrix products, arithmetic and copies ran while one was open for 18% of the time, Pallas kernels for 39%

profile of v2, /device:TPU:0, one launch (start us, length us, event | category | flops | bytes accessed | tf_op | source)
XLA Modules:
  0.0 895.4 jit_solution(6965993972523933711)
XLA Ops:
  7.2 4.6 fusion.28
  11.8 2.9 reshape.362
  15.8 2.3 copy.58
  19.4 64.9 %shard_map.362 = (bf16[2048,1536]{1,0:T(8,128)(2,1)}, bf16[1536,448]{1,0:T(8,128)(2,1)}) custom-call(bf16[512,1536]{1,0:T(8,128)(2,1)} %bitcast.229, bf16[384,448]{1,0:T(8,128)(2,1)} %pad_maximum_fusion.1.pack_ref), custom_call_target="tpu_custom_call" | custom-call | flops 1000000000 | bytes 1000000 | tf_op jit(solution)/shard_map/pallas_call | solution.py:123
  84.4 36.0 %all-gather.10.cloned.1.call-done.w_any = bf16[1536,3072]{1,0:T(8,128)(2,1)} async-done(((bf16[384,3072]{1,0:T(8,128)(2,1)}), bf16[1536,3072]{1,0:T(8,128)(2,1)}) %all-gather.10.cloned.1.call-update) | async-done | bytes 9437200 | tf_op jit(solution)/shard_map/all_gather | solution.py:828
  126.6 10.2 %shard_map.363 = (bf16[2048,1536]{1,0:T(8,128)(2,1)}, bf16[3,2048,64]{2,1,0:T(8,128)(2,1)}, bf16[2048,64]{1,0:T(8,128)(2,1)}, bf16[2048,64]{1,0:T(8,128)(2,1)}) custom-call(bf16[2048,1536]{1,0:T(8,128)(2,1)} %get-tuple-element.98.x_ref, f32[1,1536]{1,0:T(1,128)} %reshape.377.gain_ref, bf16[1536,448]{1,0:T(8,128)(2,1)} %get-tuple-element.99.w_ref, ...), custom_call_target="tpu_custom_call" | custom-call | flops 1000000000 | bytes 1000000 | tf_op jit(solution)/shard_map/pallas_call | solution.py:169
  136.7 31.9 %shard_map.364 = (bf16[2048,192]{1,0:T(8,128)(2,1)}, f32[3,1,2048]{2,1,0:T(1,128)}) custom-call(s32[2048,1]{1,0:T(8,128)} %copy.57.idc_ref, s32[1,2048]{1,0:T(1,128)} %idr_ref.3, bf16[3,2048,64]{2,1,0:T(8,128)(2,1)} %get-tuple-element.102.q_ref, bf16[2048,64]{1,0:T(8,128)(2,1)} %get-tuple-element.103.k_ref, bf16[2048,64]{1,0:T(8,128)(2,1)} %get-tuple-element.104.v_ref), custom_call_target="tpu_custom_call" | custom-call | flops 1000000000 | bytes 1000000 | tf_op jit(solution)/shard_map/pallas_call | solution.py:260
  171.3 2.4 collective-permute-start.1
  176.1 6.6 collective-permute-done
  183.4 7.7 collective-permute-done.2
  192.7 2.3 fusion
  195.0 6.3 collective-permute-start.5
  204.7 4.7 multiply_reduce_fusion.2
  211.8 27.8 %collective-permute-done.5.two_ref = bf16[256,1664]{1,0:T(8,128)(2,1)} collective-permute-done((bf16[256,1664]{1,0:T(8,128)(2,1)}, bf16[256,1664]{1,0:T(8,128)(2,1)}, u32[]{:S(2)}, u32[]{:S(2)}) %collective-permute-start.5) | collective-permute-done | bytes 852000 | tf_op jit(solution)/shard_map/ppermute | solution.py:780
  239.6 144.9 %shard_map.365 = (bf16[2048,2048]{1,0:T(8,128)(2,1)}, bf16[2048,1024]{1,0:T(8,128)(2,1)}, bf16[2048,1536]{1,0:T(8,128)(2,1)}, bf16[2048,384]{1,0:T(8,128)(2,1)},...) custom-call(bf16[512,1536]{1,0:T(8,128)(2,1)} %copy-done.3, ...), custom_call_target="tpu_custom_call" | custom-call | flops 1000000000 | bytes 1000000 | tf_op jit(solution)/shard_map/pallas_call | solution.py:618
  384.6 5.5 convolution_convert_fusion.9
  390.1 2.7 convolution_convert_fusion.8
  392.8 2.7 convolution_convert_fusion.7
  395.5 2.7 convolution_convert_fusion.6
  402.8 2.9 multiply_reduce_fusion
  405.7 2.6 fusion.135
  408.9 15.3 %collective-permute-start.6 = (bf16[512,192]{0,1:T(8,128)(2,1)S(1)}, bf16[512,192]{0,1:T(8,128)(2,1)S(1)}, u32[]{:S(2)}, u32[]{:S(2)}) collective-permute-start(bf16[512,192]{0,1:T(8,128)(2,1)S(1)} %convolution_convert_fusion.12), channel_id=1, source_target_pairs={{0,2},{2,0},{4,6},{6,4},{1,3},{3,1},{5,7},{7,5},{8,10},{10,8},{12,... | collective-permute-start | bytes 589832 | tf_op jit(solution)/shard_map/ppermute | solution.py:780
  425.6 2.7 fusion.50
  428.3 2.7 fusion.38
  431.0 2.9 fusion.53
  433.9 2.7 fusion.41
  436.6 2.7 fusion.56
  439.3 2.7 fusion.44
  442.0 2.7 fusion.59
  444.7 2.7 fusion.47
  449.3 2.4 collective-permute-start.8
  456.9 7.9 collective-permute-done.7
  472.5 3.4 add_convert_fusion.3
  484.8 12.9 %collective-permute-done.32 = bf16[384,1024]{1,0:T(8,128)(2,1)S(1)} collective-permute-done((bf16[384,1024]{1,0:T(8,128)(2,1)}, bf16[384,1024]{1,0:T(8,128)(2,1)S(1)}, u32[]{:S(2)}, u32[]{:S(2)}) %collective-permute-start.32) | collective-permute-done | bytes 786464 | tf_op jit(solution)/shard_map/ppermute | solution.py:786
  497.7 15.1 %collective-permute-done.31 = bf16[384,1024]{1,0:T(8,128)(2,1)S(1)} collective-permute-done((bf16[384,1024]{1,0:T(8,128)(2,1)}, bf16[384,1024]{1,0:T(8,128)(2,1)S(1)}, u32[]{:S(2)}, u32[]{:S(2)}) %collective-permute-start.31) | collective-permute-done | bytes 786464 | tf_op jit(solution)/shard_map/ppermute | solution.py:786
  529.1 12.2 %collective-permute-done.33 = bf16[832,384]{1,0:T(8,128)(2,1)} collective-permute-done((bf16[832,384]{1,0:T(8,128)(2,1)}, bf16[832,384]{1,0:T(8,128)(2,1)}, u32[]{:S(2)}, u32[]{:S(2)}) %collective-permute-start.33) | collective-permute-done | bytes 639008 | tf_op jit(solution)/shard_map/ppermute | solution.py:786
  542.6 12.4 %collective-permute-done.35 = bf16[832,384]{1,0:T(8,128)(2,1)} collective-permute-done((bf16[832,384]{1,0:T(8,128)(2,1)}, bf16[832,384]{1,0:T(8,128)(2,1)}, u32[]{:S(2)}, u32[]{:S(2)}) %collective-permute-start.35) | collective-permute-done | bytes 639008 | tf_op jit(solution)/shard_map/ppermute | solution.py:786
  558.7 3.0 collective-permute-start.36
  563.1 3.6 slice_bitcast_fusion.6
  566.7 37.0 %shard_map.366 = (f32[3,2048,64]{2,1,0:T(8,128)}, f32[2048,64]{1,0:T(8,128)}, f32[2048,64]{1,0:T(8,128)}) custom-call(s32[2048,1]{1,0:T(8,128)} %copy.57.idc_ref, s32[1,2048]{1,0:T(1,128)} %idr_ref.3, bf16[3,2048,64]{2,1,0:T(8,128)(2,1)} %get-tuple-element.102.q_ref, bf16[2048,64]{1,0:T(8,128)(2,1)} %get-tuple-element.103.k_ref, ...), custom_call_target="tpu_custom_call" | custom-call | flops 1000000000 | bytes 1000000 | tf_op jit(solution)/shard_map/pallas_call | solution.py:347
  603.8 5.6 shard_map.367
  609.3 6.5 convolution_convert_fusion
  620.1 2.5 dynamic-slice_bitcast_fusion
  629.5 2.3 collective-permute-start.39
  631.9 3.1 fusion.34
  635.0 11.9 %collective-permute-done.39 = bf16[208,384]{1,0:T(8,128)(2,1)S(1)} collective-permute-done((bf16[208,384]{1,0:T(8,128)(2,1)S(1)}, bf16[208,384]{1,0:T(8,128)(2,1)S(1)}, u32[]{:S(2)}, u32[]{:S(2)}) %collective-permute-start.39) | collective-permute-done | bytes 159776 | tf_op jit(solution)/shard_map/ppermute | solution.py:780
  646.9 3.5 collective-permute-done.40
  652.9 2.3 collective-permute-start.21
  659.0 66.0 %collective-permute-done.41 = bf16[208,384]{1,0:T(8,128)(2,1)S(1)} collective-permute-done((bf16[208,384]{1,0:T(8,128)(2,1)S(1)}, bf16[208,384]{1,0:T(8,128)(2,1)S(1)}, u32[]{:S(2)}, u32[]{:S(2)}) %collective-permute-start.41) | collective-permute-done | bytes 159776 | tf_op jit(solution)/shard_map/ppermute | solution.py:780
  727.8 2.3 fusion.33
  730.1 6.3 copy.65
  736.4 22.3 %shard_map.368 = (f32[384,3,16,256]{3,2,1,0:T(8,128)}, f32[384,3,16,256]{3,2,1,0:T(8,128)}, bf16[384,3,16,256]{3,2,1,0:T(8,128)(2,1)}, f32[384,16,256]{2,1,0:T(8,128)}) custom-call(f32[384,3,16,256]{3,2,1,0:T(8,128)} %bitcast.213, f32[384,3,16,256]{3,2,1,0:T(8,128)} %bitcast.216, f32[384,3,16,256]{3,2,1,0:T(8,128)} %bitcast.219, bf16[4,384,1024]{2,1,0:T(8,128)(2,1)} %bitcast.249), custom_call_target="tpu_custom_call" | custom-call | flops 31457280 | bytes 70778880 | tf_op jit(solution)/shard_map/pallas_call | solution.py:689
  762.0 2.4 fusion.67
  771.4 5.4 shard_map.371
  781.6 16.3 %collective-permute-done.14 = bf16[256,1536]{1,0:T(8,128)(2,1)S(1)} collective-permute-done((bf16[256,1536]{1,0:T(8,128)(2,1)S(1)}, bf16[256,1536]{1,0:T(8,128)(2,1)S(1)}, u32[]{:S(2)}, u32[]{:S(2)}) %collective-permute-start.14) | collective-permute-done | bytes 786464 | tf_op jit(solution)/shard_map/ppermute | solution.py:780
  798.7 8.1 collective-permute-done.18
  810.6 8.2 shard_map.370
  818.8 3.1 fusion.9
  821.9 2.6 collective-permute-start.24
  825.5 3.1 fusion.30
  828.6 22.1 %shard_map.369 = (f32[384,3,16,256]{3,2,1,0:T(8,128)}, f32[384,3,16,256]{3,2,1,0:T(8,128)}, bf16[384,3,16,256]{3,2,1,0:T(8,128)(2,1)}, f32[384,16,256]{2,1,0:T(8,128)}) custom-call(f32[384,3,16,256]{3,2,1,0:T(8,128)} %bitcast.214, f32[384,3,16,256]{3,2,1,0:T(8,128)} %bitcast.217, ...), custom_call_target="tpu_custom_call", output_to_operand_aliasing={{0}: (4, {}), {1}: (5, {}), {2}: (6, {})} | custom-call | flops 31457280 | bytes 70778880 | tf_op jit(solution)/shard_map/pallas_call | solution.py:689
  850.7 2.6 collective-permute-start.29
  855.2 5.6 fusion.6
  861.4 26.6 %shard_map.372 = (f32[384,3,16,256]{3,2,1,0:T(8,128)}, f32[384,3,16,256]{3,2,1,0:T(8,128)}, bf16[384,3,16,256]{3,2,1,0:T(8,128)(2,1)}, f32[384,16,2,256]{3,2,1,0:T(2,128)}) custom-call(f32[384,3,16,256]{3,2,1,0:T(8,128)} %bitcast.215, f32[384,3,16,256]{3,2,1,0:T(8,128)} %bitcast.218, ...), custom_call_target="tpu_custom_call", output_to_operand_aliasing={{0}: (5, {}), {1}: (6, {}), {2}: (7, {})} | custom-call | flops 31457280 | bytes 70778880 | tf_op jit(solution)/shard_map/pallas_call | solution.py:689
  (302 shorter events, 118.0 us)
Async XLA Ops:
  7.2 113.2 %all-gather.10.cloned.1.call-start = ((), (), s32[]{:S(2)}) async-start(), calls=%async_computation | async-start | bytes 11796480 | tf_op jit(solution)/shard_map/all_gather | solution.py:828
  14.8 159.5 %all-gather.12.cloned.1.call-start = ((), (), s32[]{:S(2)}) async-start(), calls=%async_computation.1 | async-start | bytes 2949120 | tf_op jit(solution)/shard_map/all_gather | solution.py:851
  18.3 66.1 %copy-start.14 = (bf16[384,1280]{1,0:T(8,128)(2,1)}, bf16[384,1280]{1,0:T(8,128)(2,1)S(1)}, u32[]{:S(2)}) copy-start(bf16[384,1280]{1,0:T(8,128)(2,1)S(1)} %convert_element_type.414) | copy-start | bytes 2949124
  19.4 101.0 %copy-start.37 = (s32[1,2048]{1,0:T(1,128)S(1)}, s32[1,2048]{1,0:T(1,128)}, u32[]{:S(2)}) copy-start(s32[1,2048]{1,0:T(1,128)} %idr_ref.3) | copy-start | bytes 24580
  84.3 39.5 %copy-start.41 = (s32[1,512,8]{1,2,0:T(8,128)S(1)}, s32[1,512,8]{1,2,0:T(8,128)}, u32[]{:S(2)}) copy-start(s32[1,512,8]{1,2,0:T(8,128)} %param.22) | copy-start | bytes 49156
  84.4 40.1 %copy-start.7 = (bf16[1,512,1536]{2,1,0:T(8,128)(2,1)S(1)}, bf16[1,512,1536]{2,1,0:T(8,128)(2,1)}, u32[]{:S(2)}) copy-start(bf16[1,512,1536]{2,1,0:T(8,128)(2,1)} %param.20) | copy-start | bytes 4718596
  120.4 609.7 %all-gather.14.cloned.1.call-start = ((), (), s32[]{:S(2)}) async-start(), calls=%async_computation.2 | async-start | bytes 4915200 | tf_op jit(solution)/shard_map/all_gather | solution.py:853
  169.8 12.9 %collective-permute-start = (bf16[512,192]{1,0:T(8,128)(2,1)S(1)}, bf16[512,192]{1,0:T(8,128)(2,1)S(1)}, u32[]{:S(2)}, u32[]{:S(2)}) collective-permute-start(bf16[512,192]{1,0:T(8,128)(2,1)S(1)} %get-tuple-element.207), channel_id=1, source_target_pairs={{0,2},{2,0},{4,6},{6,4},{1,3},{3,1},{5,7},{7,5},{8,10},{10,8},{12,... | collective-permute-start | bytes 589832 | tf_op jit(solution)/shard_map/ppermute | solution.py:780
  171.3 21.4 %collective-permute-start.1 = (bf16[512,192]{1,0:T(8,128)(2,1)S(1)}, bf16[512,192]{1,0:T(8,128)(2,1)S(1)}, u32[]{:S(2)}, u32[]{:S(2)}) collective-permute-start(bf16[512,192]{1,0:T(8,128)(2,1)S(1)} %get-tuple-element.205), channel_id=1, source_target_pairs={{0,4},{2,6},{4,0},{6,2},{1,5},{3,7},{5,1},{7,3},{8,12},{10,14},{12... | collective-permute-start | bytes 589832 | tf_op jit(solution)/shard_map/ppermute | solution.py:780
  173.7 17.3 %collective-permute-start.2 = (bf16[512,192]{1,0:T(8,128)(2,1)S(1)}, bf16[512,192]{1,0:T(8,128)(2,1)S(1)}, u32[]{:S(2)}, u32[]{:S(2)}) collective-permute-start(bf16[512,192]{1,0:T(8,128)(2,1)S(1)} %get-tuple-element.206), channel_id=1, source_target_pairs={{0,6},{2,4},{4,2},{6,0},{1,7},{3,5},{5,3},{7,1},{8,14},{10,12},{12... | collective-permute-start | bytes 589832 | tf_op jit(solution)/shard_map/ppermute | solution.py:780
  195.0 9.7 %collective-permute-start.3 = (f32[512,1536]{1,0:T(8,128)}, f32[512,1536]{1,0:T(8,128)}, u32[]{:S(2)}, u32[]{:S(2)}) collective-permute-start(f32[512,1536]{1,0:T(8,128)} %fusion), channel_id=1, source_target_pairs={{0,1},{1,0},{2,3},{3,2},{4,5},{5,4},{6,7},{7,6},{8,9},{9,8},{10,11... | collective-permute-start | bytes 9437192 | tf_op jit(solution)/shard_map/ppermute | solution.py:783
  195.0 44.6 %collective-permute-start.5 = (bf16[256,1664]{1,0:T(8,128)(2,1)}, bf16[256,1664]{1,0:T(8,128)(2,1)}, u32[]{:S(2)}, u32[]{:S(2)}) collective-permute-start(bf16[256,1664]{1,0:T(8,128)(2,1)} %fusion.74), channel_id=1, source_target_pairs={{0,4},{2,6},{4,0},{6,2},{1,5},{3,7},{5,1},{7,3},{8,12},{10,14},{12... | collective-permute-start | bytes 2555912 | tf_op jit(solution)/shard_map/ppermute | solution.py:780
  201.3 38.3 %collective-permute-start.4 = (bf16[256,1664]{1,0:T(8,128)(2,1)}, bf16[256,1664]{1,0:T(8,128)(2,1)}, u32[]{:S(2)}, u32[]{:S(2)}) collective-permute-start(bf16[256,1664]{1,0:T(8,128)(2,1)} %fusion.74), channel_id=1, source_target_pairs={{0,2},{2,0},{4,6},{6,4},{1,3},{3,1},{5,7},{7,5},{8,10},{10,8},{12,... | collective-permute-start | bytes 2555912 | tf_op jit(solution)/shard_map/ppermute | solution.py:780
  204.4 532.0 %all-gather.16.cloned.1.call-start = ((), (), s32[]{:S(2)}) async-start(), calls=%async_computation.3 | async-start | bytes 3932160 | tf_op jit(solution)/shard_map/all_gather | solution.py:921
  398.2 74.2 %collective-permute-start.11 = (bf16[384,1024]{1,0:T(8,128)(2,1)}, bf16[384,1024]{1,0:T(8,128)(2,1)}, u32[]{:S(2)}, u32[]{:S(2)}) collective-permute-start(bf16[384,1024]{1,0:T(8,128)(2,1)} %convolution_convert_fusion.6), channel_id=1, source_target_pairs={{0,24},{8,16},{16,8},{24,0},{1,25},{9,17},{17,9},{25,1},{2,26},{10... | collective-permute-start | bytes 2359304 | tf_op jit(solution)/shard_map/ppermute | solution.py:786
  399.9 72.6 %collective-permute-start.10 = (bf16[384,1024]{1,0:T(8,128)(2,1)}, bf16[384,1024]{1,0:T(8,128)(2,1)}, u32[]{:S(2)}, u32[]{:S(2)}) collective-permute-start(bf16[384,1024]{1,0:T(8,128)(2,1)} %convolution_convert_fusion.7), channel_id=1, source_target_pairs={{0,16},{8,24},{16,0},{24,8},{1,17},{9,25},{17,1},{25,9},{2,18},{10... | collective-permute-start | bytes 2359304 | tf_op jit(solution)/shard_map/ppermute | solution.py:786
  401.2 71.3 %collective-permute-start.9 = (bf16[384,1024]{1,0:T(8,128)(2,1)}, bf16[384,1024]{1,0:T(8,128)(2,1)}, u32[]{:S(2)}, u32[]{:S(2)}) collective-permute-start(bf16[384,1024]{1,0:T(8,128)(2,1)} %convolution_convert_fusion.8), channel_id=1, source_target_pairs={{0,8},{8,0},{16,24},{24,16},{1,9},{9,1},{17,25},{25,17},{2,10},{10... | collective-permute-start | bytes 2359304 | tf_op jit(solution)/shard_map/ppermute | solution.py:786
  408.2 43.4 %copy-start = (bf16[512,1536]{1,0:T(8,128)(2,1)}, bf16[512,1536]{1,0:T(8,128)(2,1)S(1)}, u32[]{:S(2)}) copy-start(bf16[512,1536]{1,0:T(8,128)(2,1)S(1)} %get-tuple-element.187) | copy-start | bytes 4718596
  408.9 40.4 %collective-permute-start.6 = (bf16[512,192]{0,1:T(8,128)(2,1)S(1)}, bf16[512,192]{0,1:T(8,128)(2,1)S(1)}, u32[]{:S(2)}, u32[]{:S(2)}) collective-permute-start(bf16[512,192]{0,1:T(8,128)(2,1)S(1)} %convolution_convert_fusion.12), channel_id=1, source_target_pairs={{0,2},{2,0},{4,6},{6,4},{1,3},{3,1},{5,7},{7,5},{8,10},{10,8},{12,... | collective-permute-start | bytes 589832 | tf_op jit(solution)/shard_map/ppermute | solution.py:780
  448.8 16.1 %collective-permute-start.7 = (bf16[512,192]{0,1:T(8,128)(2,1)}, bf16[512,192]{0,1:T(8,128)(2,1)}, u32[]{:S(2)}, u32[]{:S(2)}) collective-permute-start(bf16[512,192]{0,1:T(8,128)(2,1)} %convolution_convert_fusion.11), channel_id=1, source_target_pairs={{0,4},{2,6},{4,0},{6,2},{1,5},{3,7},{5,1},{7,3},{8,12},{10,14},{12... | collective-permute-start | bytes 589832 | tf_op jit(solution)/shard_map/ppermute | solution.py:780
  449.3 17.3 %collective-permute-start.8 = (bf16[512,192]{0,1:T(8,128)(2,1)}, bf16[512,192]{0,1:T(8,128)(2,1)}, u32[]{:S(2)}, u32[]{:S(2)}) collective-permute-start(bf16[512,192]{0,1:T(8,128)(2,1)} %convolution_convert_fusion.10), channel_id=1, source_target_pairs={{0,6},{2,4},{4,2},{6,0},{1,7},{3,5},{5,3},{7,1},{8,14},{10,12},{12... | collective-permute-start | bytes 589832 | tf_op jit(solution)/shard_map/ppermute | solution.py:780
  475.9 352.8 %all-gather.18.cloned.1.call-start = ((), (), s32[]{:S(2)}) async-start(), calls=%async_computation.4 | async-start | bytes 3932160 | tf_op jit(solution)/shard_map/all_gather | solution.py:921
  476.0 21.7 %collective-permute-start.32 = (bf16[384,1024]{1,0:T(8,128)(2,1)}, bf16[384,1024]{1,0:T(8,128)(2,1)S(1)}, u32[]{:S(2)}, u32[]{:S(2)}) collective-permute-start(bf16[384,1024]{1,0:T(8,128)(2,1)} %fusion.47), channel_id=1, source_target_pairs={{0,24},{8,16},{16,8},{24,0},{1,25},{9,17},{17,9},{25,1},{2,26},{10... | collective-permute-start | bytes 2359304 | tf_op jit(solution)/shard_map/ppermute | solution.py:786
  477.7 35.0 %collective-permute-start.31 = (bf16[384,1024]{1,0:T(8,128)(2,1)}, bf16[384,1024]{1,0:T(8,128)(2,1)S(1)}, u32[]{:S(2)}, u32[]{:S(2)}) collective-permute-start(bf16[384,1024]{1,0:T(8,128)(2,1)} %fusion.44), channel_id=1, source_target_pairs={{0,16},{8,24},{16,0},{24,8},{1,17},{9,25},{17,1},{25,9},{2,18},{10... | collective-permute-start | bytes 2359304 | tf_op jit(solution)/shard_map/ppermute | solution.py:786
  479.0 33.9 %collective-permute-start.30 = (bf16[384,1024]{1,0:T(8,128)(2,1)}, bf16[384,1024]{1,0:T(8,128)(2,1)S(1)}, u32[]{:S(2)}, u32[]{:S(2)}) collective-permute-start(bf16[384,1024]{1,0:T(8,128)(2,1)} %fusion.41), channel_id=1, source_target_pairs={{0,8},{8,0},{16,24},{24,16},{1,9},{9,1},{17,25},{25,17},{2,10},{10... | collective-permute-start | bytes 2359304 | tf_op jit(solution)/shard_map/ppermute | solution.py:786
  481.8 31.0 %copy-start.29 = (bf16[384,1024]{1,0:T(8,128)(2,1)S(1)}, bf16[384,1024]{1,0:T(8,128)(2,1)}, u32[]{:S(2)}) copy-start(bf16[384,1024]{1,0:T(8,128)(2,1)} %fusion.38) | copy-start | bytes 2359300
  484.8 32.0 %copy-start.40 = (bf16[1536]{0:T(1024)(128)(2,1)S(1)}, bf16[1536]{0:T(1024)(128)(2,1)}, u32[]{:S(2)}) copy-start(bf16[1536]{0:T(1024)(128)(2,1)} %get-tuple-element.169) | copy-start | bytes 9220
  514.5 347.0 %all-gather.20.cloned.1.call-start = ((), (), s32[]{:S(2)}) async-start(), calls=%async_computation.5 | async-start | bytes 3932160 | tf_op jit(solution)/shard_map/all_gather | solution.py:921
  522.8 18.5 %collective-permute-start.33 = (bf16[832,384]{1,0:T(8,128)(2,1)}, bf16[832,384]{1,0:T(8,128)(2,1)}, u32[]{:S(2)}, u32[]{:S(2)}) collective-permute-start(bf16[832,384]{1,0:T(8,128)(2,1)} %get-tuple-element.197), channel_id=1, source_target_pairs={{0,24},{8,16},{16,8},{24,0},{1,25},{9,17},{17,9},{25,1},{2,26},{10... | collective-permute-start | bytes 1916936 | tf_op jit(solution)/shard_map/ppermute | solution.py:786
  524.3 30.7 %collective-permute-start.35 = (bf16[832,384]{1,0:T(8,128)(2,1)}, bf16[832,384]{1,0:T(8,128)(2,1)}, u32[]{:S(2)}, u32[]{:S(2)}) collective-permute-start(bf16[832,384]{1,0:T(8,128)(2,1)} %get-tuple-element.198), channel_id=1, source_target_pairs={{0,16},{8,24},{16,0},{24,8},{1,17},{9,25},{17,1},{25,9},{2,18},{10... | collective-permute-start | bytes 1916936 | tf_op jit(solution)/shard_map/ppermute | solution.py:786
  525.6 29.4 %collective-permute-start.34 = (bf16[832,384]{1,0:T(8,128)(2,1)}, bf16[832,384]{1,0:T(8,128)(2,1)}, u32[]{:S(2)}, u32[]{:S(2)}) collective-permute-start(bf16[832,384]{1,0:T(8,128)(2,1)} %get-tuple-element.199), channel_id=1, source_target_pairs={{0,8},{8,0},{16,24},{24,16},{1,9},{9,1},{17,25},{25,17},{2,10},{10... | collective-permute-start | bytes 1916936 | tf_op jit(solution)/shard_map/ppermute | solution.py:786
  526.3 89.6 %collective-permute-start.50 = (bf16[384,1024]{1,0:T(8,128)(2,1)}, bf16[384,1024]{1,0:T(8,128)(2,1)S(1)}, u32[]{:S(2)}, u32[]{:S(2)}) collective-permute-start(bf16[384,1024]{1,0:T(8,128)(2,1)} %fusion.59), channel_id=1, source_target_pairs={{0,24},{8,16},{16,8},{24,0},{1,25},{9,17},{17,9},{25,1},{2,26},{10... | collective-permute-start | bytes 2359304 | tf_op jit(solution)/shard_map/ppermute | solution.py:786
  527.8 88.0 %collective-permute-start.49 = (bf16[384,1024]{1,0:T(8,128)(2,1)}, bf16[384,1024]{1,0:T(8,128)(2,1)S(1)}, u32[]{:S(2)}, u32[]{:S(2)}) collective-permute-start(bf16[384,1024]{1,0:T(8,128)(2,1)} %fusion.56), channel_id=1, source_target_pairs={{0,16},{8,24},{16,0},{24,8},{1,17},{9,25},{17,1},{25,9},{2,18},{10... | collective-permute-start | bytes 2359304 | tf_op jit(solution)/shard_map/ppermute | solution.py:786
  541.3 74.6 %collective-permute-start.48 = (bf16[384,1024]{1,0:T(8,128)(2,1)}, bf16[384,1024]{1,0:T(8,128)(2,1)S(1)}, u32[]{:S(2)}, u32[]{:S(2)}) collective-permute-start(bf16[384,1024]{1,0:T(8,128)(2,1)} %fusion.53), channel_id=1, source_target_pairs={{0,8},{8,0},{16,24},{24,16},{1,9},{9,1},{17,25},{25,17},{2,10},{10... | collective-permute-start | bytes 2359304 | tf_op jit(solution)/shard_map/ppermute | solution.py:786
  558.7 63.9 %collective-permute-start.36 = (bf16[208,384]{1,0:T(8,128)(2,1)}, bf16[208,384]{1,0:T(8,128)(2,1)}, u32[]{:S(2)}, u32[]{:S(2)}) collective-permute-start(bf16[208,384]{1,0:T(8,128)(2,1)} %get-tuple-element.211), channel_id=1, source_target_pairs={{0,2},{2,0},{4,6},{6,4},{1,3},{3,1},{5,7},{7,5},{8,10},{10,8},{12,... | collective-permute-start | bytes 479240 | tf_op jit(solution)/shard_map/ppermute | solution.py:780
  561.7 62.5 %collective-permute-start.38 = (bf16[208,384]{1,0:T(8,128)(2,1)}, bf16[208,384]{1,0:T(8,128)(2,1)}, u32[]{:S(2)}, u32[]{:S(2)}) collective-permute-start(bf16[208,384]{1,0:T(8,128)(2,1)} %get-tuple-element.212), channel_id=1, source_target_pairs={{0,6},{2,4},{4,2},{6,0},{1,7},{3,5},{5,3},{7,1},{8,14},{10,12},{12... | collective-permute-start | bytes 479240 | tf_op jit(solution)/shard_map/ppermute | solution.py:780
  615.8 9.6 %collective-permute-start.37 = (bf16[208,384]{1,0:T(8,128)(2,1)}, bf16[208,384]{1,0:T(8,128)(2,1)}, u32[]{:S(2)}, u32[]{:S(2)}) collective-permute-start(bf16[208,384]{1,0:T(8,128)(2,1)} %get-tuple-element.213), channel_id=1, source_target_pairs={{0,4},{2,6},{4,0},{6,2},{1,5},{3,7},{5,1},{7,3},{8,12},{10,14},{12... | collective-permute-start | bytes 479240 | tf_op jit(solution)/shard_map/ppermute | solution.py:780
  615.8 13.7 %collective-permute-start.16 = (bf16[256,1536]{1,0:T(8,128)(2,1)}, bf16[256,1536]{1,0:T(8,128)(2,1)}, u32[]{:S(2)}, u32[]{:S(2)}) collective-permute-start(bf16[256,1536]{1,0:T(8,128)(2,1)} %get-tuple-element.192), channel_id=1, source_target_pairs={{0,1},{1,0},{2,3},{3,2},{4,5},{5,4},{6,7},{7,6},{8,9},{9,8},{10,11... | collective-permute-start | bytes 2359304 | tf_op jit(solution)/shard_map/ppermute | solution.py:783
  615.9 15.9 %collective-permute-start.13 = (bf16[256,1536]{1,0:T(8,128)(2,1)}, bf16[256,1536]{1,0:T(8,128)(2,1)}, u32[]{:S(2)}, u32[]{:S(2)}) collective-permute-start(bf16[256,1536]{1,0:T(8,128)(2,1)} %get-tuple-element.194), channel_id=1, source_target_pairs={{0,1},{1,0},{2,3},{3,2},{4,5},{5,4},{6,7},{7,6},{8,9},{9,8},{10,11... | collective-permute-start | bytes 2359304 | tf_op jit(solution)/shard_map/ppermute | solution.py:783
  622.5 29.2 %collective-permute-start.42 = (bf16[320,384]{1,0:T(8,128)(2,1)S(1)}, bf16[320,384]{1,0:T(8,128)(2,1)S(1)}, u32[]{:S(2)}, u32[]{:S(2)}) collective-permute-start(bf16[320,384]{1,0:T(8,128)(2,1)S(1)} %copy-done.33), channel_id=1, source_target_pairs={{0,24},{8,16},{16,8},{24,0},{1,25},{9,17},{17,9},{25,1},{2,26},{10... | collective-permute-start | bytes 737288 | tf_op jit(solution)/shard_map/ppermute | solution.py:786
  624.2 28.8 %collective-permute-start.44 = (bf16[320,384]{1,0:T(8,128)(2,1)S(1)}, bf16[320,384]{1,0:T(8,128)(2,1)S(1)}, u32[]{:S(2)}, u32[]{:S(2)}) collective-permute-start(bf16[320,384]{1,0:T(8,128)(2,1)S(1)} %copy-done.32), channel_id=1, source_target_pairs={{0,16},{8,24},{16,0},{24,8},{1,17},{9,25},{17,1},{25,9},{2,18},{10... | collective-permute-start | bytes 737288 | tf_op jit(solution)/shard_map/ppermute | solution.py:786
  625.5 29.8 %collective-permute-start.43 = (bf16[320,384]{1,0:T(8,128)(2,1)S(1)}, bf16[320,384]{1,0:T(8,128)(2,1)S(1)}, u32[]{:S(2)}, u32[]{:S(2)}) collective-permute-start(bf16[320,384]{1,0:T(8,128)(2,1)S(1)} %copy-done.31), channel_id=1, source_target_pairs={{0,8},{8,0},{16,24},{24,16},{1,9},{9,1},{17,25},{25,17},{2,10},{10... | collective-permute-start | bytes 737288 | tf_op jit(solution)/shard_map/ppermute | solution.py:786
  629.5 17.4 %collective-permute-start.39 = (bf16[208,384]{1,0:T(8,128)(2,1)S(1)}, bf16[208,384]{1,0:T(8,128)(2,1)S(1)}, u32[]{:S(2)}, u32[]{:S(2)}) collective-permute-start(bf16[208,384]{1,0:T(8,128)(2,1)S(1)} %get-tuple-element.186), channel_id=1, source_target_pairs={{0,2},{2,0},{4,6},{6,4},{1,3},{3,1},{5,7},{7,5},{8,10},{10,8},{12,... | collective-permute-start | bytes 479240 | tf_op jit(solution)/shard_map/ppermute | solution.py:780
  631.8 18.6 %collective-permute-start.40 = (bf16[208,384]{1,0:T(8,128)(2,1)S(1)}, bf16[208,384]{1,0:T(8,128)(2,1)S(1)}, u32[]{:S(2)}, u32[]{:S(2)}) collective-permute-start(bf16[208,384]{1,0:T(8,128)(2,1)S(1)} %get-tuple-element.186), channel_id=1, source_target_pairs={{0,4},{2,6},{4,0},{6,2},{1,5},{3,7},{5,1},{7,3},{8,12},{10,14},{12... | collective-permute-start | bytes 479240 | tf_op jit(solution)/shard_map/ppermute | solution.py:780
  646.9 79.1 %collective-permute-start.15 = (bf16[256,1536]{1,0:T(8,128)(2,1)S(1)}, bf16[256,1536]{1,0:T(8,128)(2,1)S(1)}, u32[]{:S(2)}, u32[]{:S(2)}) collective-permute-start(bf16[256,1536]{1,0:T(8,128)(2,1)S(1)} %copy-done.25), channel_id=1, source_target_pairs={{0,1},{1,0},{2,3},{3,2},{4,5},{5,4},{6,7},{7,6},{8,9},{9,8},{10,11... | collective-permute-start | bytes 2359304 | tf_op jit(solution)/shard_map/ppermute | solution.py:783
  650.4 75.6 %collective-permute-start.17 = (bf16[256,1536]{1,0:T(8,128)(2,1)S(1)}, bf16[256,1536]{1,0:T(8,128)(2,1)S(1)}, u32[]{:S(2)}, u32[]{:S(2)}) collective-permute-start(bf16[256,1536]{1,0:T(8,128)(2,1)S(1)} %get-tuple-element.196), channel_id=1, source_target_pairs={{0,2},{2,0},{4,6},{6,4},{1,3},{3,1},{5,7},{7,5},{8,10},{10,8},{12,... | collective-permute-start | bytes 2359304 | tf_op jit(solution)/shard_map/ppermute | solution.py:780
  651.8 106.9 %collective-permute-start.22 = (bf16[512,320]{1,0:T(8,128)(2,1)}, bf16[512,320]{1,0:T(8,128)(2,1)}, u32[]{:S(2)}, u32[]{:S(2)}) collective-permute-start(bf16[512,320]{1,0:T(8,128)(2,1)} %get-tuple-element.201), channel_id=1, source_target_pairs={{0,6},{2,4},{4,2},{6,0},{1,7},{3,5},{5,3},{7,1},{8,14},{10,12},{12... | collective-permute-start | bytes 983048 | tf_op jit(solution)/shard_map/ppermute | solution.py:780
  652.9 107.6 %collective-permute-start.21 = (bf16[512,320]{1,0:T(8,128)(2,1)}, bf16[512,320]{1,0:T(8,128)(2,1)}, u32[]{:S(2)}, u32[]{:S(2)}) collective-permute-start(bf16[512,320]{1,0:T(8,128)(2,1)} %get-tuple-element.202), channel_id=1, source_target_pairs={{0,4},{2,6},{4,0},{6,2},{1,5},{3,7},{5,1},{7,3},{8,12},{10,14},{12... | collective-permute-start | bytes 983048 | tf_op jit(solution)/shard_map/ppermute | solution.py:780
  655.3 69.8 %collective-permute-start.41 = (bf16[208,384]{1,0:T(8,128)(2,1)S(1)}, bf16[208,384]{1,0:T(8,128)(2,1)S(1)}, u32[]{:S(2)}, u32[]{:S(2)}) collective-permute-start(bf16[208,384]{1,0:T(8,128)(2,1)S(1)} %collective-permute-done.40), channel_id=1, source_target_pairs={{0,2},{2,0},{4,6},{6,4},{1,3},{3,1},{5,7},{7,5},{8,10},{10,8},{12,... | collective-permute-start | bytes 479240 | tf_op jit(solution)/shard_map/ppermute | solution.py:780
  725.0 36.7 %collective-permute-start.20 = (bf16[512,320]{1,0:T(8,128)(2,1)}, bf16[512,320]{1,0:T(8,128)(2,1)}, u32[]{:S(2)}, u32[]{:S(2)}) collective-permute-start(bf16[512,320]{1,0:T(8,128)(2,1)} %get-tuple-element.203), channel_id=1, source_target_pairs={{0,2},{2,0},{4,6},{6,4},{1,3},{3,1},{5,7},{7,5},{8,10},{10,8},{12,... | collective-permute-start | bytes 983048 | tf_op jit(solution)/shard_map/ppermute | solution.py:780
  726.0 55.6 %collective-permute-start.12 = (bf16[256,1536]{1,0:T(8,128)(2,1)}, bf16[256,1536]{1,0:T(8,128)(2,1)}, u32[]{:S(2)}, u32[]{:S(2)}) collective-permute-start(bf16[256,1536]{1,0:T(8,128)(2,1)} %get-tuple-element.191), channel_id=1, source_target_pairs={{0,1},{1,0},{2,3},{3,2},{4,5},{5,4},{6,7},{7,6},{8,9},{9,8},{10,11... | collective-permute-start | bytes 2359304 | tf_op jit(solution)/shard_map/ppermute | solution.py:783
  726.0 44.6 %collective-permute-start.45 = (bf16[320,384]{1,0:T(8,128)(2,1)}, bf16[320,384]{1,0:T(8,128)(2,1)}, u32[]{:S(2)}, u32[]{:S(2)}) collective-permute-start(bf16[320,384]{1,0:T(8,128)(2,1)} %get-tuple-element.180), channel_id=1, source_target_pairs={{0,2},{2,0},{4,6},{6,4},{1,3},{3,1},{5,7},{7,5},{8,10},{10,8},{12,... | collective-permute-start | bytes 737288 | tf_op jit(solution)/shard_map/ppermute | solution.py:780
  758.7 19.5 %collective-permute-start.46 = (bf16[320,384]{1,0:T(8,128)(2,1)}, bf16[320,384]{1,0:T(8,128)(2,1)S(1)}, u32[]{:S(2)}, u32[]{:S(2)}) collective-permute-start(bf16[320,384]{1,0:T(8,128)(2,1)} %get-tuple-element.180), channel_id=1, source_target_pairs={{0,4},{2,6},{4,0},{6,2},{1,5},{3,7},{5,1},{7,3},{8,12},{10,14},{12... | collective-permute-start | bytes 737288 | tf_op jit(solution)/shard_map/ppermute | solution.py:780
  760.6 37.3 %collective-permute-start.14 = (bf16[256,1536]{1,0:T(8,128)(2,1)S(1)}, bf16[256,1536]{1,0:T(8,128)(2,1)S(1)}, u32[]{:S(2)}, u32[]{:S(2)}) collective-permute-start(bf16[256,1536]{1,0:T(8,128)(2,1)S(1)} %copy-done.26), channel_id=1, source_target_pairs={{0,2},{2,0},{4,6},{6,4},{1,3},{3,1},{5,7},{7,5},{8,10},{10,8},{12,... | collective-permute-start | bytes 2359304 | tf_op jit(solution)/shard_map/ppermute | solution.py:780
  761.7 45.1 %collective-permute-start.18 = (bf16[256,1536]{1,0:T(8,128)(2,1)S(1)}, bf16[256,1536]{1,0:T(8,128)(2,1)}, u32[]{:S(2)}, u32[]{:S(2)}) collective-permute-start(bf16[256,1536]{1,0:T(8,128)(2,1)S(1)} %copy-done.27), channel_id=1, source_target_pairs={{0,4},{2,6},{4,0},{6,2},{1,5},{3,7},{5,1},{7,3},{8,12},{10,14},{12... | collective-permute-start | bytes 2359304 | tf_op jit(solution)/shard_map/ppermute | solution.py:780
  770.6 48.2 %collective-permute-start.23 = (bf16[512,1536]{1,0:T(8,128)(2,1)}, bf16[512,1536]{1,0:T(8,128)(2,1)}, u32[]{:S(2)}, u32[]{:S(2)}) collective-permute-start(bf16[512,1536]{1,0:T(8,128)(2,1)} %fusion.10), channel_id=1, source_target_pairs={{0,1},{1,0},{2,3},{3,2},{4,5},{5,4},{6,7},{7,6},{8,9},{9,8},{10,11... | collective-permute-start | bytes 4718600 | tf_op jit(solution)/shard_map/ppermute | solution.py:783
  778.2 31.7 %collective-permute-start.47 = (bf16[320,384]{1,0:T(8,128)(2,1)S(1)}, bf16[320,384]{1,0:T(8,128)(2,1)S(1)}, u32[]{:S(2)}, u32[]{:S(2)}) collective-permute-start(bf16[320,384]{1,0:T(8,128)(2,1)S(1)} %collective-permute-done.46), channel_id=1, source_target_pairs={{0,2},{2,0},{4,6},{6,4},{1,3},{3,1},{5,7},{7,5},{8,10},{10,8},{12,... | collective-permute-start | bytes 737288 | tf_op jit(solution)/shard_map/ppermute | solution.py:780
  809.1 16.4 %collective-permute-start.19 = (bf16[256,1536]{1,0:T(8,128)(2,1)S(1)}, bf16[256,1536]{1,0:T(8,128)(2,1)}, u32[]{:S(2)}, u32[]{:S(2)}) collective-permute-start(bf16[256,1536]{1,0:T(8,128)(2,1)S(1)} %fusion.37), channel_id=1, source_target_pairs={{0,1},{1,0},{2,3},{3,2},{4,5},{5,4},{6,7},{7,6},{8,9},{9,8},{10,11... | collective-permute-start | bytes 2359304 | tf_op jit(solution)/shard_map/ppermute | solution.py:783
  821.9 28.7 %collective-permute-start.24 = (bf16[16,384]{1,0:T(8,128)(2,1)S(1)}, bf16[16,384]{1,0:T(8,128)(2,1)S(1)}, u32[]{:S(2)}, u32[]{:S(2)}) collective-permute-start(bf16[16,384]{1,0:T(8,128)(2,1)S(1)} %get-tuple-element.226), channel_id=1, source_target_pairs={{0,24},{8,16},{16,8},{24,0},{1,25},{9,17},{17,9},{25,1},{2,26},{10... | collective-permute-start | bytes 36872 | tf_op jit(solution)/shard_map/ppermute | solution.py:786
  824.5 26.2 %collective-permute-start.25 = (bf16[16,384]{1,0:T(8,128)(2,1)S(1)}, bf16[16,384]{1,0:T(8,128)(2,1)S(1)}, u32[]{:S(2)}, u32[]{:S(2)}) collective-permute-start(bf16[16,384]{1,0:T(8,128)(2,1)S(1)} %get-tuple-element.227), channel_id=1, source_target_pairs={{0,8},{8,0},{16,24},{24,16},{1,9},{9,1},{17,25},{25,17},{2,10},{10... | collective-permute-start | bytes 36872 | tf_op jit(solution)/shard_map/ppermute | solution.py:786
  825.2 25.5 %collective-permute-start.26 = (bf16[16,384]{1,0:T(8,128)(2,1)S(1)}, bf16[16,384]{1,0:T(8,128)(2,1)S(1)}, u32[]{:S(2)}, u32[]{:S(2)}) collective-permute-start(bf16[16,384]{1,0:T(8,128)(2,1)S(1)} %get-tuple-element.228), channel_id=1, source_target_pairs={{0,16},{8,24},{16,0},{24,8},{1,17},{9,25},{17,1},{25,9},{2,18},{10... | collective-permute-start | bytes 36872 | tf_op jit(solution)/shard_map/ppermute | solution.py:786
  850.7 10.1 %collective-permute-start.29 = (bf16[16,384]{1,0:T(8,128)(2,1)S(1)}, bf16[16,384]{1,0:T(8,128)(2,1)S(1)}, u32[]{:S(2)}, u32[]{:S(2)}) collective-permute-start(bf16[16,384]{1,0:T(8,128)(2,1)S(1)} %add_convert_fusion.6), channel_id=1, source_target_pairs={{0,6},{2,4},{4,2},{6,0},{1,7},{3,5},{5,3},{7,1},{8,14},{10,12},{12... | collective-permute-start | bytes 36872 | tf_op jit(solution)/shard_map/ppermute | solution.py:780
  853.3 7.5 collective-permute-start.28
  853.3 7.5 collective-permute-start.27
  (50 other events, 341.2 us)
Sparse Core Ops, SparseCore 0:
  14.9 105.4 all-gather.9
  122.8 37.3 all-gather.11
  204.6 49.3 all-gather.13
  476.0 62.9 all-gather.15
  540.4 68.8 all-gather.17
  620.1 102.3 all-gather.19

commit v3 on v2

--- a/solution.py
+++ b/solution.py
@@ -201,9 +201,84 @@
     )
 
 
-def attend_kernel(idc_ref, idr_ref, q_ref, k_ref, v_ref, o_ref, lse_ref, s_ref, m_ref, l_ref, a_ref):
+def attend_kernel(weights, *refs):
+    idc_ref, idr_ref, q_ref, k_ref, v_ref, shard_ref, o_ref, lse_ref, att_ref, full_ref = refs[:10]
+    s_ref, m_ref, l_ref, a_ref, oall_ref, local, send, recv = refs[10:]
     i = pl.program_id(0)
     blocks = pl.num_programs(0)
+    z, f = lax.axis_index("ctx"), lax.axis_index("fsdp")
+    rows = shard_ref.shape[0]
+    cut = rows // 2
+    f1, f2 = f + 1 - 2 * (f % 2), (f + 2) % 4
+    f3 = 3 - f
+
+    def remote(k, source, target, device):
+        return pltpu.make_async_remote_copy(
+            src_ref=source,
+            dst_ref=target,
+            send_sem=send.at[k],
+            recv_sem=recv.at[k],
+            device_id=device,
+            device_id_type=MESH,
+        )
+
+    def held(owner, first, size):
+        return full_ref.at[pl.ds(pl.multiple_of(owner * rows + first, 8), size)]
+
+    own_weights = pltpu.make_async_copy(shard_ref, held(f, 0, rows), local.at[1])
+    if weights:
+        one = remote(4, shard_ref, held(f, 0, rows), {"fsdp": f1})
+        two = remote(5, shard_ref, held(f, 0, rows), {"fsdp": f2})
+        on_one = remote(6, held(f1, 0, cut), held(f1, 0, cut), {"fsdp": f2})
+        on_two = remote(7, held(f2, cut, rows - cut), held(f2, cut, rows - cut), {"fsdp": f1})
+
+    def to(c):
+        return pltpu.make_async_remote_copy(
+            src_ref=oall_ref.at[pl.ds(2 * c, 2)],
+            dst_ref=att_ref.at[pl.ds(2 * z, 2)],
+            send_sem=send.at[c],
+            recv_sem=recv.at[z],
+            device_id={"ctx": c},
+            device_id_type=MESH,
+        )
+
+    def back_from(c):
+        return pltpu.make_async_remote_copy(
+            src_ref=oall_ref.at[pl.ds(2 * c, 2)],
+            dst_ref=att_ref.at[pl.ds(2 * c, 2)],
+            send_sem=send.at[c],
+            recv_sem=recv.at[c],
+            device_id={"ctx": c},
+            device_id_type=MESH,
+        )
+
+    own_rows = pltpu.make_async_copy(
+        oall_ref.at[pl.ds(2 * z, 2)], att_ref.at[pl.ds(2 * z, 2)], local.at[0]
+    )
+
+    @pl.when(i == 0)
+    def _():
+        barrier = pltpu.get_barrier_semaphore()
+        partners = [{"ctx": (z + k) % 4} for k in (1, 2, 3)]
+        if weights:
+            partners += [{"fsdp": f1}, {"fsdp": f2}]
+        for partner in partners:
+            pl.semaphore_signal(barrier, inc=1, device_id=partner, device_id_type=MESH)
+        pl.semaphore_wait(barrier, len(partners))
+        if weights:
+            one.start()
+            two.start()
+            own_weights.start()
+
+    if weights:
+
+        @pl.when(i == 6)
+        def _():
+            one.wait_recv()
+            on_one.start()
+            two.wait_recv()
+            on_two.start()
+
     q = q_ref[...].reshape(GROUP * SPAN, HEAD_SIZE)
     m_ref[...] = jnp.full(m_ref.shape, -1e30, F32)
     l_ref[...] = jnp.zeros(l_ref.shape, F32)
@@ -251,14 +326,41 @@
         part = slice(g * SPAN, (g + 1) * SPAN)
         out = a_ref[part, :] / to_column(total[:, part], eye)
         o_ref[:, g * HEAD_SIZE : (g + 1) * HEAD_SIZE] = out.astype(BF)
+        oall_ref[i, :, g * HEAD_SIZE : (g + 1) * HEAD_SIZE] = out.astype(BF)
         lse_ref[g] = lse[:, part]
-
-
-def attend(id_column, id_row, q, k, v):
+    for c in range(4):
+
+        @pl.when(jnp.logical_and(i == 2 * c + 1, z != c))
+        def _():
+            to(c).start()
+
+    @pl.when(i == 7)
+    def _():
+        own_rows.start()
+        own_rows.wait()
+        if weights:
+            on_one.wait_recv()
+            on_two.wait_recv()
+            for made in (one, two, on_one, on_two):
+                made.wait_send()
+            own_weights.wait()
+
+    for c in range(4):
+
+        @pl.when(jnp.logical_and(i == 7, z != c))
+        def _():
+            to(c).wait_send()
+            back_from(c).wait_recv()
+
+
+def attend(n_fsdp, id_column, id_row, q, k, v, shard):
     rows = k.shape[0]
+    weights = n_fsdp == 4
+    anywhere = pl.BlockSpec(memory_space=pl.ANY)
+    full_rows = shard.shape[0] * (n_fsdp if weights else 1)
     whole = lambda s: pl.BlockSpec(s, lambda i: (0,) * len(s))
     return pl.pallas_call(
-        attend_kernel,
+        functools.partial(attend_kernel, weights),
         grid=(rows // SPAN,),
         in_specs=[
             whole(id_column.shape),
@@ -266,24 +368,33 @@
             pl.BlockSpec((GROUP, SPAN, HEAD_SIZE), lambda i: (0, i, 0)),
             whole(k.shape),
             whole(v.shape),
+            anywhere,
         ],
         out_specs=[
             pl.BlockSpec((SPAN, GROUP * HEAD_SIZE), lambda i: (i, 0)),
             pl.BlockSpec((GROUP, 1, SPAN), lambda i: (0, 0, i)),
+            anywhere,
+            anywhere,
         ],
         out_shape=[
             jax.ShapeDtypeStruct((rows, GROUP * HEAD_SIZE), BF),
             jax.ShapeDtypeStruct((GROUP, 1, rows), F32),
+            jax.ShapeDtypeStruct((8, SPAN, GROUP * HEAD_SIZE), BF),
+            jax.ShapeDtypeStruct((full_rows, shard.shape[1]), BF),
         ],
         scratch_shapes=[
             pltpu.VMEM((rows, GROUP * SPAN), F32),
             pltpu.VMEM((1, GROUP * SPAN), F32),
             pltpu.VMEM((1, GROUP * SPAN), F32),
             pltpu.VMEM((GROUP * SPAN, HEAD_SIZE), F32),
-        ],
-        compiler_params=params(),
+            pltpu.VMEM((8, SPAN, GROUP * HEAD_SIZE), BF),
+            pltpu.SemaphoreType.DMA((2,)),
+            pltpu.SemaphoreType.DMA((8,)),
+            pltpu.SemaphoreType.DMA((8,)),
+        ],
+        compiler_params=params(collective_id=2, has_side_effects=True),
         cost_estimate=LIGHT,
-    )(id_column, id_row, q, k, v)
+    )(id_column, id_row, q, k, v, shard)
 
 
 def attend_back_kernel(
@@ -369,41 +480,312 @@
     )(id_column, id_row, q, k, v, o, do, lse)
 
 
-def turn_back_kernel(dq_ref, dk_ref, dv_ref, cos_ref, sin_ref, out_ref):
-    cos, sin = cos_ref[...], sin_ref[...]
-    a = jnp.concatenate([dq_ref[0], dq_ref[1]], axis=1)
-    b = jnp.concatenate([dq_ref[2], dk_ref[...]], axis=1)
-    out_ref[:, :LANES] = (a * cos + half_turn(a, True) * sin).astype(BF)
-    out_ref[:, LANES : 2 * LANES] = (b * cos + half_turn(b, True) * sin).astype(BF)
-    out_ref[:, 2 * LANES :] = dv_ref[...].astype(BF)
-
-
-def turn_back(dq, dk, dv, cos, sin):
-    rows = dk.shape[0]
-    tile = 512
-    row = lambda n: pl.BlockSpec((tile, n), lambda i: (i, 0))
+def project_out_kernel(att_ref, w_ref, tok_ref, gain_ref, res_ref, n_ref, a_ref, p_ref, o_ref, send, recv):
+    t = lax.axis_index("tp")
+    core = {"tp": 1 - t}
+    barrier = pltpu.get_barrier_semaphore()
+    pl.semaphore_signal(barrier, inc=1, device_id=core, device_id_type=MESH)
+    pl.semaphore_wait(barrier, 1)
+    columns = att_ref.shape[2]
+    sent = []
+    for side in (0, 1):
+        rows = slice(side * SPAN, (side + 1) * SPAN)
+        for c in range(4):
+            a_ref[rows, c * columns : (c + 1) * columns] = att_ref[2 * c + side]
+        p_ref[side] = lax.dot_general(a_ref[rows, :], w_ref[...], NT, preferred_element_type=F32)
+        made = pltpu.make_async_remote_copy(
+            src_ref=p_ref.at[side],
+            dst_ref=o_ref.at[side],
+            send_sem=send.at[side],
+            recv_sem=recv.at[side],
+            device_id=core,
+            device_id_type=MESH,
+        )
+        made.start()
+        sent.append(made)
+    for side in (0, 1):
+        rows = slice(side * SPAN, (side + 1) * SPAN)
+        sent[side].wait_recv()
+        residual = tok_ref[rows, :].astype(F32) + (p_ref[side] + o_ref[side])
+        res_ref[rows, :] = residual
+        n_ref[rows, :] = (residual * inverse_rms(residual) * gain_ref[...]).astype(BF)
+    for made in sent:
+        made.wait_send()
+
+
+def project_out(att, w, tokens, gain):
+    rows, width = tokens.shape
+    columns = w.shape[1]
+    return pl.pallas_call(
+        project_out_kernel,
+        in_specs=[pl.BlockSpec(memory_space=pltpu.VMEM)] * 4,
+        out_specs=[pl.BlockSpec(memory_space=pltpu.VMEM)] * 3,
+        out_shape=[
+            jax.ShapeDtypeStruct((rows, width), F32),
+            jax.ShapeDtypeStruct((rows, width), BF),
+            jax.ShapeDtypeStruct((rows, columns), BF),
+        ],
+        scratch_shapes=[
+            pltpu.VMEM((2, SPAN, width), F32),
+            pltpu.VMEM((2, SPAN, width), F32),
+            pltpu.SemaphoreType.DMA((2,)),
+            pltpu.SemaphoreType.DMA((2,)),
+        ],
+        compiler_params=params(collective_id=3, has_side_effects=True),
+        cost_estimate=LIGHT,
+    )(att, w, tokens, gain)
+
+
+def residual_back_kernel(
+    g_ref, res_ref, n_ref, c_ref, r_ref, gain_ref, w_ref, rg_ref, low_ref, lg_ref, gg_ref, all_ref, p_ref, local, send, recv
+):
+    z = lax.axis_index("ctx")
+    width = res_ref.shape[1]
+    barrier = pltpu.get_barrier_semaphore()
+    for k in (1, 2, 3):
+        pl.semaphore_signal(barrier, inc=1, device_id={"ctx": (z + k) % 4}, device_id_type=MESH)
+    pl.semaphore_wait(barrier, 3)
+    gain = gain_ref[...]
+    gain_grad = jnp.zeros(gain.shape, F32)
+    columns = p_ref.shape[3]
+
+    def to(c, side):
+        return pltpu.make_async_remote_copy(
+            src_ref=p_ref.at[side, c],
+            dst_ref=all_ref.at[2 * z + side],
+            send_sem=send.at[side, c],
+            recv_sem=recv.at[side, z],
+            device_id={"ctx": c},
+            device_id_type=MESH,
+        )
+
+    def back_from(c, side):
+        return pltpu.make_async_remote_copy(
+            src_ref=p_ref.at[side, c],
+            dst_ref=all_ref.at[2 * c + side],
+            send_sem=send.at[side, c],
+            recv_sem=recv.at[side, c],
+            device_id={"ctx": c},
+            device_id_type=MESH,
+        )
+
+    own = [
+        pltpu.make_async_copy(p_ref.at[side, z], all_ref.at[2 * z + side], local.at[side])
+        for side in (0, 1)
+    ]
+    for side in (0, 1):
+        rows = slice(side * SPAN, (side + 1) * SPAN)
+        named = c_ref[rows, width:].astype(F32) > 0.5
+        logits = jnp.dot(n_ref[rows, :], r_ref[...], preferred_element_type=F32)
+        logits = jnp.where(named, logits, -1e30)
+        exponent = jnp.where(
+            named, jnp.exp(logits - jnp.max(logits, axis=1, keepdims=True)), 0.0
+        )
+        gates = exponent / jnp.sum(exponent, axis=1, keepdims=True)
+        found = g_ref[rows, width:].astype(F32)
+        logit_grads = (gates * (found - jnp.sum(gates * found, axis=1, keepdims=True))).astype(BF)
+        lg_ref[rows, :] = logit_grads
+        grads = g_ref[rows, :width].astype(F32) + lax.dot_general(
+            logit_grads, r_ref[...], NT, preferred_element_type=F32
+        )
+        residual = res_ref[rows, :]
+        inverse = inverse_rms(residual)
+        gain_grad = gain_grad + jnp.sum(grads * residual * inverse, axis=0, keepdims=True)
+        scaled = gain * grads
+        cube = inverse * inverse * inverse / width
+        total = (
+            c_ref[rows, :width].astype(F32)
+            + inverse * scaled
+            - residual * cube * jnp.sum(scaled * residual, axis=1, keepdims=True)
+        )
+        rg_ref[rows, :] = total
+        low = total.astype(BF)
+        low_ref[rows, :] = low
+        attended = jnp.dot(low, w_ref[...], preferred_element_type=F32).astype(BF)
+        for c in range(4):
+            p_ref[side, c] = attended[:, c * columns : (c + 1) * columns]
+        for c in range(4):
+
+            @pl.when(z != c)
+            def _():
+                to(c, side).start()
+
+        own[side].start()
+    gg_ref[...] = gain_grad
+    for side in (0, 1):
+        own[side].wait()
+        for c in range(4):
+
+            @pl.when(z != c)
+            def _():
+                to(c, side).wait_send()
+                back_from(c, side).wait_recv()
+
+
+def residual_back(grad, residual, normed, cot, router, gain, w):
+    rows, width = residual.shape
+    columns = w.shape[1] // 4
+    vmem = pl.BlockSpec(memory_space=pltpu.VMEM)
+    return pl.pallas_call(
+        residual_back_kernel,
+        in_specs=[vmem] * 7,
+        out_specs=[vmem] * 4 + [pl.BlockSpec(memory_space=pl.ANY)],
+        out_shape=[
+            jax.ShapeDtypeStruct((rows, width), F32),
+            jax.ShapeDtypeStruct((rows, width), BF),
+            jax.ShapeDtypeStruct((rows, LANES), BF),
+            jax.ShapeDtypeStruct((1, width), F32),
+            jax.ShapeDtypeStruct((8, SPAN, columns), BF),
+        ],
+        scratch_shapes=[
+            pltpu.VMEM((2, 4, SPAN, columns), BF),
+            pltpu.SemaphoreType.DMA((2,)),
+            pltpu.SemaphoreType.DMA((2, 4)),
+            pltpu.SemaphoreType.DMA((2, 4)),
+        ],
+        compiler_params=params(collective_id=4, has_side_effects=True),
+        cost_estimate=LIGHT,
+    )(grad, residual, normed, cot, router, gain, w)
+
+
+def joint_back_kernel(
+    dq_ref, dk_ref, dv_ref, cos_ref, sin_ref, w_ref, tok_ref, gain_ref, rg_ref,
+    jg_ref, in_ref, gg_ref, land_ref, a_ref, p_ref, o_ref, send, recv, core_send, core_recv,
+):
+    z, t = lax.axis_index("ctx"), lax.axis_index("tp")
+    core = {"tp": 1 - t}
+    barrier = pltpu.get_barrier_semaphore()
+    for partner in [{"ctx": (z + k) % 4} for k in (1, 2, 3)] + [core]:
+        pl.semaphore_signal(barrier, inc=1, device_id=partner, device_id_type=MESH)
+    pl.semaphore_wait(barrier, 4)
+    columns = jg_ref.shape[2]
+    rows_here = jg_ref.shape[1]
+
+    def to(c):
+        return pltpu.make_async_remote_copy(
+            src_ref=jg_ref.at[c],
+            dst_ref=land_ref.at[z],
+            send_sem=send.at[c],
+            recv_sem=recv.at[z],
+            device_id={"ctx": c},
+            device_id_type=MESH,
+        )
+
+    def back_from(c):
+        return pltpu.make_async_remote_copy(
+            src_ref=jg_ref.at[c],
+            dst_ref=land_ref.at[c],
+            send_sem=send.at[c],
+            recv_sem=recv.at[c],
+            device_id={"ctx": c},
+            device_id_type=MESH,
+        )
+
+    for c in range(4):
+        rows = slice(c * rows_here, (c + 1) * rows_here)
+        cos, sin = cos_ref[rows, :], sin_ref[rows, :]
+        a = jnp.concatenate([dq_ref[0, rows, :], dq_ref[1, rows, :]], axis=1)
+        b = jnp.concatenate([dq_ref[2, rows, :], dk_ref[rows, :]], axis=1)
+        jg_ref[c, :, :LANES] = (a * cos + half_turn(a, True) * sin).astype(BF)
+        jg_ref[c, :, LANES : 2 * LANES] = (b * cos + half_turn(b, True) * sin).astype(BF)
+        jg_ref[c, :, 2 * LANES :] = dv_ref[rows, :].astype(BF)
+
+        @pl.when(z != c)
+        def _():
+            to(c).start()
+
+    for c in range(4):
+        place = slice(c * columns, (c + 1) * columns)
+
+        @pl.when(z == c)
+        def _():
+            a_ref[:, place] = jg_ref[c]
+
+        @pl.when(z != c)
+        def _():
+            back_from(c).wait_recv()
+            a_ref[:, place] = land_ref[c]
+
+    sent = []
+    for side in (0, 1):
+        rows = slice(side * SPAN, (side + 1) * SPAN)
+        p_ref[side] = lax.dot_general(
+            a_ref[rows, :], w_ref[...], NT, preferred_element_type=F32
+        ).astype(BF)
+        made = pltpu.make_async_remote_copy(
+            src_ref=p_ref.at[side],
+            dst_ref=o_ref.at[side],
+            send_sem=core_send.at[side],
+            recv_sem=core_recv.at[side],
+            device_id=core,
+            device_id_type=MESH,
+        )
+        made.start()
+        sent.append(made)
+    gain = gain_ref[...]
+    width = gain.shape[1]
+    gain_grad = jnp.zeros(gain.shape, F32)
+    for side in (0, 1):
+        rows = slice(side * SPAN, (side + 1) * SPAN)
+        sent[side].wait_recv()
+        grads = p_ref[side].astype(F32) + o_ref[side].astype(F32)
+        tokens = tok_ref[rows, :].astype(F32)
+        inverse = inverse_rms(tokens)
+        gain_grad = gain_grad + jnp.sum(grads * tokens * inverse, axis=0, keepdims=True)
+        scaled = gain * grads
+        cube = inverse * inverse * inverse / width
+        in_ref[rows, :] = (
+            rg_ref[rows, :]
+            + inverse * scaled
+            - tokens * cube * jnp.sum(scaled * tokens, axis=1, keepdims=True)
+        )
+    gg_ref[...] = gain_grad
+    for made in sent:
+        made.wait_send()
+    for c in range(4):
+
+        @pl.when(z != c)
+        def _():
+            to(c).wait_send()
+
+
+def joint_back(dq, dk, dv, cos, sin, w, tokens, gain, grads):
+    rows, width = tokens.shape
     columns = (GROUP + 2) * HEAD_SIZE
+    vmem = pl.BlockSpec(memory_space=pltpu.VMEM)
     return pl.pallas_call(
-        turn_back_kernel,
-        grid=(rows // tile,),
-        in_specs=[
-            pl.BlockSpec((GROUP, tile, HEAD_SIZE), lambda i: (0, i, 0)),
-            row(HEAD_SIZE),
-            row(HEAD_SIZE),
-            row(LANES),
-            row(LANES),
-        ],
-        out_specs=row(columns),
-        out_shape=jax.ShapeDtypeStruct((rows, columns), BF),
-        compiler_params=params(),
-    )(dq, dk, dv, cos, sin)
-
-
-def expert_kernel(count, pieces, n_ref, cot_ref, one_ref, two_ref, r_ref, w_any, *refs):
+        joint_back_kernel,
+        in_specs=[vmem] * 9,
+        out_specs=[vmem] * 3,
+        out_shape=[
+            jax.ShapeDtypeStruct((4, rows, columns), BF),
+            jax.ShapeDtypeStruct((rows, width), F32),
+            jax.ShapeDtypeStruct((1, width), F32),
+        ],
+        scratch_shapes=[
+            pltpu.VMEM((4, rows, columns), BF),
+            pltpu.VMEM((rows, 4 * columns), BF),
+            pltpu.VMEM((2, SPAN, width), BF),
+            pltpu.VMEM((2, SPAN, width), BF),
+            pltpu.SemaphoreType.DMA((4,)),
+            pltpu.SemaphoreType.DMA((4,)),
+            pltpu.SemaphoreType.DMA((2,)),
+            pltpu.SemaphoreType.DMA((2,)),
+        ],
+        compiler_params=params(collective_id=5, has_side_effects=True),
+        cost_estimate=LIGHT,
+    )(dq, dk, dv, cos, sin, w, tokens, gain, grads)
+
+
+def owner_of(f, k):
+    return [f, f + 1 - 2 * (f % 2), (f + 2) % 4, 3 - f][k]
+
+
+def expert_kernel(count, pieces, n_ref, cot_ref, one_ref, two_ref, r_ref, w_any, shard_ref, *refs):
     pre_ref, wh_ref, out_ref = refs[:3]
     x_parts, cot_parts = refs[3 : 3 + pieces], refs[3 + pieces : 3 + 2 * pieces]
-    grad_any = refs[3 + 2 * pieces]
-    x_ref, c_ref, w_ref, part_ref, there_ref, sum_ref, back_ref, full_ref = refs[4 + 2 * pieces : -4]
+    grad_any, joint_ref = refs[3 + 2 * pieces : 5 + 2 * pieces]
+    x_ref, c_ref, w_ref, part_ref, there_ref, sum_ref, back_ref, full_ref = refs[5 + 2 * pieces : -4]
     local, wrote, send, recv = refs[-4:]
     i = pl.program_id(0)
     z, t, f = lax.axis_index("ctx"), lax.axis_index("tp"), lax.axis_index("fsdp")
@@ -460,6 +842,22 @@
         )
     ]
     store = pltpu.make_async_copy(full_ref, grad_any, local.at[7])
+    carried = []
+    if pieces > 1:
+        shard_rows = shard_ref.shape[0]
+        cut = shard_rows // 2
+        f1, f2 = owner_of(f, 1), owner_of(f, 2)
+
+        def held(place, first, size):
+            return joint_ref.at[pl.ds(pl.multiple_of(place * shard_rows + first, 8), size)]
+
+        own_shard = pltpu.make_async_copy(shard_ref, held(f, 0, shard_rows), local.at[8])
+        joint_one = remote(18, shard_ref, held(f, 0, shard_rows), {"fsdp": f1})
+        joint_two = remote(19, shard_ref, held(f, 0, shard_rows), {"fsdp": f2})
+        later = shard_rows - cut
+        on_one = remote(20, held(f1, 0, cut), held(f1, 0, cut), {"fsdp": f2})
+        on_two = remote(21, held(f2, cut, later), held(f2, cut, later), {"fsdp": f1})
+        carried = [joint_one, joint_two, on_one, on_two]
 
     def keep(step):
         made = []
@@ -483,10 +881,17 @@
 
     @pl.when(i == 0)
     def _():
+        partners = [near, far, third, core]
+        if carried:
+            partners += [{"fsdp": f1}, {"fsdp": f2}]
         barrier = pltpu.get_barrier_semaphore()
-        for partner in (near, far, third, core):
+        for partner in partners:
             pl.semaphore_signal(barrier, inc=1, device_id=partner, device_id_type=MESH)
-        pl.semaphore_wait(barrier, 4)
+        pl.semaphore_wait(barrier, len(partners))
+        if carried:
+            joint_one.start()
+            joint_two.start()
+            own_shard.start()
         for made in [x_one, x_two] + loads + [c_swaps[1], c_swaps[2], c_three]:
             made.start()
         for made in (loads[0], loads[2], loads[4]):
@@ -522,10 +927,17 @@
 
     @pl.when(i == 6)
     def _():
+        finish(2)
+        x_three.wait_recv()
+        x_swaps[3].start()
         c_three.wait_recv()
         c_swaps[3].start()
-        x_three.wait_recv()
-        x_swaps[3].start()
+
+        if carried:
+            joint_one.wait_recv()
+            on_one.start()
+            joint_two.wait_recv()
+            on_two.start()
 
     @pl.when(i == 7)
     def _():
@@ -575,7 +987,7 @@
     out_ref[...] = lax.dot_general(
         wh_ref[...], w_ref[:, 2 * hidden_columns :], NT, preferred_element_type=F32
     ).astype(BF)
-    for m in range(3):
+    for m in range(2):
 
         @pl.when(i == 2 * m + 2)
         def _():
@@ -597,6 +1009,12 @@
         last.wait_send()
         last.wait_recv()
         store.start()
+        if carried:
+            on_one.wait_recv()
+            on_two.wait_recv()
+            for made in carried:
+                made.wait_send()
+            own_shard.wait()
 
         def settle(step, carried):
             for made in keep(step):
@@ -607,7 +1025,7 @@
         store.wait()
 
 
-def experts(pieces, normed, cot, one, two, router, w, count):
+def experts(pieces, normed, cot, one, two, router, w, shard, count):
     rows, width = normed.shape
     half = rows // 2
     packed = cot.shape[1]
@@ -618,12 +1036,15 @@
     return pl.pallas_call(
         functools.partial(expert_kernel, count, pieces),
         grid=(8,),
-        in_specs=[anywhere] * 4 + [pl.BlockSpec(router.shape, lambda i: (0, 0)), anywhere],
-        out_specs=[slot(n) for n in blocks] + [anywhere] * (2 * pieces + 1),
+        in_specs=[anywhere] * 4 + [pl.BlockSpec(router.shape, lambda i: (0, 0)), anywhere, anywhere],
+        out_specs=[slot(n) for n in blocks] + [anywhere] * (2 * pieces + 2),
         out_shape=[
             jax.ShapeDtypeStruct((8 * half, n), BF) for n in blocks + [width // pieces] * (2 * pieces)
         ]
-        + [jax.ShapeDtypeStruct((rows, packed), BF)],
+        + [
+            jax.ShapeDtypeStruct((rows, packed), BF),
+            jax.ShapeDtypeStruct((pieces * shard.shape[0], shard.shape[1]), BF),
+        ],
         scratch_shapes=[
             pltpu.VMEM((8, half, width), BF),
             pltpu.VMEM((8, half, packed), BF),
@@ -633,14 +1054,14 @@
             pltpu.VMEM((4, half, packed), BF),
             pltpu.VMEM((4, half, packed), BF),
             pltpu.VMEM((rows, packed), BF),
-            pltpu.SemaphoreType.DMA((8,)),
+            pltpu.SemaphoreType.DMA((9,)),
             pltpu.SemaphoreType.DMA((8, 2 * pieces)),
-            pltpu.SemaphoreType.DMA((18,)),
-            pltpu.SemaphoreType.DMA((18,)),
+            pltpu.SemaphoreType.DMA((22,)),
+            pltpu.SemaphoreType.DMA((22,)),
         ],
         compiler_params=params(collective_id=1, has_side_effects=True),
         cost_estimate=LIGHT,
-    )(normed, cot, one, two, router, w)
+    )(normed, cot, one, two, router, w, shard)
 
 
 def adamw(master, first_moment, second_moment, gradient, rate, decay):
@@ -769,8 +1190,6 @@
     count, width = tokens_low.shape
     half = count // n_tp
     length = n_ctx * count
-    tokens = tokens_low.astype(F32)
-    cotangent = cot_low.astype(F32)
     own_rows = width // n_fsdp
     each = E // n_ctx
 
@@ -796,23 +1215,23 @@
 
     def put(buffer, x, place):
         return lax.dynamic_update_slice_in_dim(buffer, x[None], place, 0)
+
+    def put_row(x, row, place):
+        return lax.dynamic_update_slice(x, row[None], (place, 0))
 
     def take(x, place, places):
         return lax.dynamic_index_in_dim(
             x.reshape(places, x.shape[0] // places, x.shape[1]), place, 0, keepdims=False
         )
 
-    def scatter_fsdp(x, axis):
+    def sent_to_owners(x):
         if n_fsdp != 4:
-            return lax.psum_scatter(x, "fsdp", scatter_dimension=axis, tiled=True)
-        if axis:
-            piece = lambda k: lax.dynamic_slice_in_dim(x, k * own_rows, own_rows, 1)
-        else:
-            piece = lambda k: take(x, k, n_fsdp)
-        total = piece(f).astype(F32)
-        for m in (3, 1, 2):
-            total = total + across(piece(f ^ m), m).astype(F32)
-        return total.astype(BF)
+            return [lax.psum_scatter(x, "fsdp", scatter_dimension=1, tiled=True)]
+        part = lambda k: lax.dynamic_slice_in_dim(x, (f ^ k) * own_rows, own_rows, 1)
+        return [part(0)] + [across(part(k), k) for k in (1, 2, 3)]
+
+    def added(came):
+        return came[0] if len(came) == 1 else sum(x.astype(F32) for x in came).astype(BF)
 
     def spread(x):
         one, two = beyond(x, 1), beyond(x, 2)
@@ -847,12 +1266,6 @@
     router_wide = jnp.where(jnp.arange(LANES)[None, :] < E, small_full, jnp.zeros((), BF))
     gain_first = small_full[:, E].astype(F32)[None, :]
     gain_second = small_full[:, E + 1].astype(F32)[None, :]
-    output_late, _ = barrier((output_weight.astype(BF), (expert_full, sequence)))
-    output_full = lax.all_gather(output_late, "fsdp", axis=0, tiled=True)
-    joint_late, _ = barrier((joint_low, output_full))
-    joint_full = lax.all_gather(joint_late, "fsdp", axis=0, tiled=True)
-    output_turned = barrier(output_full.T)
-    joint_turned = barrier(joint_full.T)
 
     route_rows = expert_routes[0]
     lane_row = jnp.arange(LANES, dtype=jnp.int32)[None, :]
@@ -874,28 +1287,29 @@
     id_row = block_ids
     id_column = block_ids.reshape(length, 1)
     normed_all, queries, keys, values = project(sequence, gain_first, first_full, cosine, sine)
-    attended_all, lse = attend(id_column, id_row, queries, keys, values)
-    def to_positions(x):
-        parts = [take(x, z ^ m, n_ctx) for m in range(n_ctx)]
-        return [parts[0]] + [beyond(parts[m], m) for m in range(1, n_ctx)]
-
-    def by_heads(turned):
-        return [take(turned, z ^ m, n_ctx) for m in range(n_ctx)]
-
-    output_by = by_heads(output_turned)
-    attended = to_positions(attended_all)
-    attn_part = sum(
-        jnp.dot(a, w, preferred_element_type=F32) for a, w in zip(attended, output_by)
-    )
-    residual = tokens + (attn_part + swap(attn_part))
-    inv_second = inverse_rms(residual)
-    normed_second = (residual * inv_second * gain_second).astype(BF)
+    output_low = output_weight.astype(BF)
+    attended_all, lse, attended_here, output_full = attend(
+        n_fsdp, id_column, id_row, queries, keys, values, output_low
+    )
+    if n_fsdp != 4:
+        output_full = lax.all_gather(output_low, "fsdp", axis=0, tiled=True)
+    residual, normed_second, attended = project_out(
+        attended_here, output_full, tokens_low, gain_second
+    )
 
     pieces = n_fsdp if n_fsdp == 4 else 1
-    pre_all, hidden_all, out_all, *kept, grad_rows = experts(
-        pieces, normed_second, cot_pack, *cot_came, router_wide, expert_full, each
-    )
+    pre_all, hidden_all, out_all, *kept, grad_rows, joint_full = experts(
+        pieces, normed_second, cot_pack, *cot_came, router_wide, expert_full, joint_low, each
+    )
+    if pieces == 1:
+        joint_full = lax.all_gather(joint_low, "fsdp", axis=0, tiled=True)
     x_parts, cot_parts = kept[:pieces], kept[pieces:]
+    outs = out_all.reshape(n_ctx, 2, half, width)
+    outs = [
+        (outs[m, 0].astype(F32) + swap(outs[m, 1]).astype(F32)).astype(BF) for m in range(n_ctx)
+    ]
+    outs, x_parts, cot_parts = barrier((outs, x_parts, cot_parts))
+    out_near = [beyond(outs[1], 1), beyond(outs[3], 1)]
 
     wide = each * units
 
@@ -913,61 +1327,56 @@
         if pieces > 1:
             pieces_came[j] = [terms[j][0]] + [across(terms[j][k], k) for k in range(1, pieces)]
         else:
-            pieces_came[j] = lax.psum_scatter(terms[j][0], "fsdp", scatter_dimension=0, tiled=True)
+            pieces_came[j] = [
+                lax.psum_scatter(terms[j][0], "fsdp", scatter_dimension=0, tiled=True)
+            ]
 
     def gathered(came):
-        if pieces > 1:
-            came = sum(x.astype(F32) for x in came).astype(BF)
-        return lax.all_gather(came, "ctx", axis=0, tiled=False)
-
-    grad_rows, terms[2] = barrier((grad_rows, terms[2]))
-    grad_rows = grad_rows.astype(F32)
-    moe_input = grad_rows[:, :width]
-    gate_grads = grad_rows[:, width : width + E]
-
-    named = member[:, :E]
-    logits = jnp.dot(normed_second, router_full, preferred_element_type=F32)
-    masked = jnp.where(named > 0.5, logits, -1e30)
-    exponent = jnp.where(
-        named > 0.5, jnp.exp(masked - jnp.max(masked, axis=1, keepdims=True)), 0.0
-    )
-    gates = exponent / jnp.sum(exponent, axis=1, keepdims=True)
-    logit_grads = (
-        gates * (gate_grads - jnp.sum(gates * gate_grads, axis=1, keepdims=True))
-    ).astype(BF)
-    norm_second_grads = moe_input + lax.dot_general(
-        logit_grads, router_full, NT, preferred_element_type=F32
-    )
-    scaled_second = gain_second * norm_second_grads
-    cube_second = inv_second * inv_second * inv_second / width
-    residual_grads = (
-        cotangent
-        + inv_second * scaled_second
-        - residual * cube_second * jnp.sum(scaled_second * residual, axis=1, keepdims=True)
-    )
-    gain_second_grad = jnp.sum(norm_second_grads * residual * inv_second, axis=0, keepdims=True)
-    residual_low = residual_grads.astype(BF)
-
-    attended_grads_all = jnp.zeros((n_ctx, count, head_columns), BF)
-    for m in range(n_ctx):
-        part = lax.dot_general(
-            residual_low, output_by[m], NT, preferred_element_type=F32
-        ).astype(BF)
-        got = part if m == 0 else beyond(part, m)
-        attended_grads_all = put(attended_grads_all, got, z ^ m)
-    attended_grads_all = attended_grads_all.reshape(length, head_columns)
-    attended_grads_all, pieces_came[2], *_ = barrier(
-        (attended_grads_all, pieces_came[2], terms[0], terms[1])
-    )
-    down_sum = gathered(pieces_came[2])
+        return lax.all_gather(added(came), "ctx", axis=0, tiled=False)
+
+    grad_rows, joint_full, terms[2], out_near = barrier(
+        (grad_rows, joint_full, terms[2], out_near)
+    )
+    out_far = beyond((outs[2].astype(F32) + out_near[1].astype(F32)).astype(BF), 2)
+    residual_grads, residual_low, logit_grads, gain_second_grad, attended_grads_all = residual_back(
+        grad_rows, residual, normed_second, cot_pack, router_wide, gain_second, output_full
+    )
+    attended_grads_all, pieces_came[2], out_far, *_ = barrier(
+        (attended_grads_all, pieces_came[2], out_far, terms[0], terms[1])
+    )
+    expert_sums = {2: gathered(pieces_came[2])}
+    step = 64
+    few_rows = jnp.concatenate([logit_grads[:, :E], jnp.zeros((count, step - E), BF)], axis=1)
+    rest_term = jnp.concatenate(
+        [
+            lax.dot_general(attended, residual_low, TN, preferred_element_type=F32).astype(BF),
+            lax.dot_general(few_rows, normed_second, TN, preferred_element_type=F32).astype(BF),
+        ],
+        axis=0,
+    )
+    rest_term = lax.dynamic_update_slice(
+        rest_term, gain_second_grad.astype(BF), (output_columns + E, 0)
+    )
+    rest_term, attended_grads_all = barrier((rest_term, attended_grads_all))
     dq, dk, dv = attend_back(
-        id_column, id_row, queries, keys, values, attended_all, attended_grads_all, lse
-    )
-    joint_grads_all = turn_back(dq, dk, dv, cosine, sine)
-    joint_grads = to_positions(joint_grads_all)
-    expert_sums = {2: down_sum}
-    for j in (0, 1):
-        expert_sums[j] = gathered(pieces_came[j])
+        id_column,
+        id_row,
+        queries,
+        keys,
+        values,
+        attended_all,
+        attended_grads_all.reshape(length, head_columns),
+        lse,
+    )
+    dq, pieces_came[0] = barrier((dq, pieces_came[0]))
+    expert_sums[0] = gathered(pieces_came[0])
+    joint_grads, input_rows, gain_first_grad = joint_back(
+        dq, dk, dv, cosine, sine, joint_full, tokens_low, gain_first, residual_grads
+    )
+    joint_grads, pieces_came[1], rest_term = barrier((joint_grads, pieces_came[1], rest_term))
+    expert_sums[1] = gathered(pieces_came[1])
+    joint_grads_all = joint_grads.reshape(length, group_columns)
+
     first_view = jnp.transpose(expert_first, (0, 2, 1, 3))
     second_view = jnp.transpose(expert_second, (0, 2, 1, 3))
     made = []
@@ -979,90 +1388,54 @@
             j, rate, slots_first, first_view, second_view, expert_sums[j], tuple(made), joined
         )
 
+    joint_term = lax.dot_general(joint_grads_all, normed_all, TN, preferred_element_type=F32)
+    joint_term = jnp.concatenate(
+        [
+            joint_term.astype(BF),
+            jnp.where(jnp.arange(16)[:, None] == 0, gain_first_grad, 0.0).astype(BF),
+            rest_term,
+        ],
+        axis=0,
+    )
+    joint_came = sent_to_owners(joint_term)
+
     expert_step(2)
-    joint_grads, made[:], squares[2] = barrier((joint_grads, made, squares[2]))
-    first_part = sum(
-        jnp.dot(g, w, preferred_element_type=F32)
-        for g, w in zip(joint_grads, by_heads(joint_turned))
+    joint_came, made[:], squares[2] = barrier((joint_came, made, squares[2]))
+    joint_owned = added(joint_came)
+    rest_owned = put_row(
+        joint_owned[group_columns + 16 :], joint_owned[group_columns], output_columns + E + 1
+    )
+    joint_owned = joint_owned[:group_columns]
+    rest_parts = [take(rest_owned, z, n_ctx)]
+    rest_parts += [beyond(take(rest_owned, z ^ m, n_ctx), m) for m in range(1, n_ctx)]
+    expert_step(0)
+    rest_parts, made[:], squares[0] = barrier((rest_parts, made, squares[0]))
+    rest_low = sum(x.astype(F32) for x in rest_parts).astype(BF)
+    both = jnp.concatenate([joint_owned, rest_low], axis=0)
+    both_all = {0: both, **spread(both)}
+    full = jnp.zeros((n_ctx, *both.shape), BF)
+    for m, got in both_all.items():
+        full = put(full, got, z ^ m)
+    joint_sum = full[:, :group_columns].reshape(n_ctx * group_columns, own_rows)
+    rest_full = full[:, group_columns:].reshape(output_columns + step, own_rows)
+    moe_low = (
+        outs[0].astype(F32) + out_near[0].astype(F32) + out_far.astype(F32)
     ).astype(BF)
-    norm_first_grads = first_part.astype(F32) + swap(first_part).astype(F32)
-    inv_first = inverse_rms(tokens)
-    scaled_first = gain_first * norm_first_grads
-    cube_first = inv_first * inv_first * inv_first / width
-    input_rows = (
-        residual_grads
-        + inv_first * scaled_first
-        - tokens * cube_first * jnp.sum(scaled_first * tokens, axis=1, keepdims=True)
-    )
-    gain_first_grad = jnp.sum(norm_first_grads * tokens * inv_first, axis=0, keepdims=True)
-
-    out_all, attended_grads_all = barrier((out_all, attended_grads_all))
-    outs = out_all.reshape(n_ctx, 2, half, width)
-    halves = {
-        m: outs[m, 0].astype(F32) + swap(outs[m, 1]).astype(F32) for m in range(n_ctx)
-    }
-    moe_two = halves[2] + beyond(halves[3].astype(BF), 1).astype(F32)
-    moe_sum = (
-        halves[0]
-        + beyond(halves[1].astype(BF), 1).astype(F32)
-        + beyond(moe_two.astype(BF), 2).astype(F32)
-    )
-    moe_low = moe_sum.astype(BF)
     moe_rows = in_order(moe_low, swap(moe_low)).astype(F32)
     block_output = (residual + moe_rows).astype(BF)[None]
-
-    joint_term = lax.dot_general(joint_grads_all, normed_all, TN, preferred_element_type=F32)
-    joint_owned = scatter_fsdp(joint_term.astype(BF), 1)
-    joint_sum = jnp.zeros((n_ctx, group_columns, own_rows), BF)
-    for m, got in {0: joint_owned, **spread(joint_owned)}.items():
-        joint_sum = put(joint_sum, got, z ^ m)
-    joint_sum = joint_sum.reshape(n_ctx * group_columns, own_rows)
-
-    def summed_over_ctx(owned):
-        total = take(owned, z, n_ctx).astype(F32)
-        for m in range(1, n_ctx):
-            total = total + beyond(take(owned, z ^ m, n_ctx), m).astype(F32)
-        total = total.astype(BF)
-        full = put(jnp.zeros((n_ctx, *total.shape), BF), total, z)
-        for m, got in spread(total).items():
-            full = put(full, got, z ^ m)
-        return full.reshape(owned.shape)
-
-    step = 64
-    blocks = head_columns // step
-    rest_term = jnp.zeros((output_columns // step + 1, step, width), BF)
-    for m in range(n_ctx):
-        term = lax.dot_general(attended[m], residual_low, TN, preferred_element_type=F32)
-        rest_term = lax.dynamic_update_slice_in_dim(
-            rest_term, term.astype(BF).reshape(blocks, step, width), (z ^ m) * blocks, 0
-        )
-    router_term = lax.dot_general(logit_grads, normed_second, TN, preferred_element_type=F32)
-    few_rows = jnp.concatenate(
-        [router_term, gain_second_grad, jnp.zeros((step - E - 1, width), F32)], axis=0
-    )
-    rest_term = put(rest_term, few_rows.astype(BF), output_columns // step)
-    rest_term = rest_term.reshape(output_columns + step, width)
-    rest_full = summed_over_ctx(scatter_fsdp(rest_term, 1))
     router_sum = rest_full[output_columns : output_columns + E].T.astype(F32)
-    last_term = jnp.concatenate([gain_first_grad, jnp.zeros((15, width), F32)], axis=0)
-    last_owned = scatter_fsdp(last_term.astype(BF), 1)
-    last_came = [last_owned] + [beyond(last_owned, m) for m in range(1, n_ctx)]
-    expert_step(0)
-    last_came, made[:], squares[0] = barrier((last_came, made, squares[0]))
-    last_sum = sum(x.astype(F32) for x in last_came)
-    gains_sum = jnp.concatenate(
-        [
-            last_sum[:1],
-            rest_full[output_columns + E : output_columns + E + 1].astype(F32),
-        ],
-        axis=0,
-    )
+    gains_sum = jnp.stack(
+        [rest_full[output_columns + E + 1], rest_full[output_columns + E]]
+    ).astype(F32)
 
     gains_new = adamw(norm_gains, gains_first, gains_second, gains_sum, 0.6, 0.0)
     joint_new = matrix_adamw(0.03, joint_weight, joint_first, joint_second, joint_sum)
     output_new = matrix_adamw(0.25, output_weight, output_first, output_second, rest_full)
     router_new = adamw(router_weight, router_first, router_second, router_sum, 0.015, 0.1)
 
+    expert_sums[1], block_output, joint_new, output_new = barrier(
+        (expert_sums[1], block_output, joint_new, output_new)
+    )
     expert_step(1, squares[0])
     back = lambda x: jnp.transpose(x, (0, 2, 1, 3))
     return (

time: 905 us -> 775 us (0.86)
  waiting for transfers between devices: 246 us -> 98.1 us
  Pallas kernels: 379 us -> 502 us
  local copies, waits for them, and re-layouts: 56.5 us -> 24.7 us
  matrix products: 71.9 us -> 41.6 us
  starting transfers between devices: 75.6 us -> 52.1 us
  other arithmetic: 51.3 us -> 32.9 us
    pallas_call x2 -> x4, Pallas kernels: 37.5 us -> 156 us  [the longest x1 51.9 us: residual_back(): pl.pallas_call(residual_back_kernel, in_specs=[vmem] * 7, out_specs=[vmem...]
    ppermute x26 -> x11, waiting for transfers between devices: 157 us -> 78.9 us  [beyond(): return lax.ppermute(x, 'ctx', [(i, i ^ m) for i in range(n_ctx)])]
    ppermute x18 -> x12, waiting for transfers between devices: 52.7 us -> 14.6 us  [across(): return lax.ppermute(x, 'fsdp', [(i, i ^ m) for i in range(n_fsdp)])]
    all_gather x1, waiting for transfers between devices: 36 us -> 0.01 us  [local(): expert_full = lax.all_gather(expert_part, 'fsdp', axis=0, tiled=True)]
    dot_general x19 -> x2, matrix products: 30 us -> 1.83 us  [the longest x1 1.42 us: local(): lax.dot_general(attended, residual_low, TN, preferred_element_type=F32)]
    ppermute x26 -> x11, starting transfers between devices: 51.9 us -> 36.1 us  [beyond(): return lax.ppermute(x, 'ctx', [(i, i ^ m) for i in range(n_ctx)])]
    dynamic_update_slice x10 -> x3, local copies, waits for them, and re-layouts: 9.92 us -> 0.2 us  [put(): return lax.dynamic_update_slice_in_dim(buffer, x[None], place, 0)]
    ppermute x18 -> x12, starting transfers between devices: 22.4 us -> 14.1 us  [across(): return lax.ppermute(x, 'fsdp', [(i, i ^ m) for i in range(n_fsdp)])]
  transfers between devices with their start and end apart: 57 -> 32, of which waited for: 17 -> 10; matrix products, arithmetic and copies ran while one was open for 18% -> 7% of each run, Pallas kernels for 39% -> 43%
where the time goes in v3:
time: 775 us; the launch traced here: 766 us
  Pallas kernels  502 us (65%)
  waiting for transfers between devices  98.1 us (13%)
  starting transfers between devices  52.1 us (7%)
  matrix products  41.6 us (5%)
  other arithmetic  32.9 us (4%)
  local copies, waits for them, and re-layouts  24.7 us (3%)
  between operations  14.9 us (2%)
    pallas_call x1, Pallas kernels, experts(): pl.pallas_call(functools.partial(expert_kernel, count, pieces), grid=(8,)...  149 us
    ppermute x11, waiting for transfers between devices, beyond(): return lax.ppermute(x, 'ctx', [(i, i ^ m) for i in range(n_ctx)])  78.9 us
    pallas_call x3, Pallas kernels, expert_adamw(): pl.pallas_call(functools.partial(expert_adamw_kernel, rate, joined is not...  70.9 us
    pallas_call x1, Pallas kernels, first_gather(): pl.pallas_call(functools.partial(first_gather_kernel, weights), in_specs=...  64.9 us
    pallas_call x1, Pallas kernels, residual_back(): pl.pallas_call(residual_back_kernel, in_specs=[vmem] * 7, out_specs=[vmem...  51.9 us
    pallas_call x1, Pallas kernels, joint_back(): pl.pallas_call(joint_back_kernel, in_specs=[vmem] * 9, out_specs=[vmem] *...  47 us
    pallas_call x1, Pallas kernels, attend(): pl.pallas_call(functools.partial(attend_kernel, weights), grid=(rows // S...  45.3 us
    pallas_call x1, Pallas kernels, attend_back(): pl.pallas_call(attend_back_kernel, grid=(rows // SPAN,), in_specs=[whole(...  37.2 us
  transfers between devices with their start and end apart: 32, of which 10 were waited for; matrix products, arithmetic and copies ran while one was open for 7% of the time, Pallas kernels for 43%

profile of v3, /device:TPU:0, one launch (start us, length us, event | category | flops | bytes accessed | tf_op | source)
XLA Modules:
  0.0 766.2 jit_solution(11141217544852832990)
XLA Ops:
  7.2 4.6 fusion.16
  11.8 2.9 reshape.255
  17.6 64.9 %shard_map.362 = (bf16[2048,1536]{1,0:T(8,128)(2,1)}, bf16[1536,448]{1,0:T(8,128)(2,1)}) custom-call(bf16[512,1536]{1,0:T(8,128)(2,1)} %bitcast.123, bf16[384,448]{1,0:T(8,128)(2,1)} %pad_maximum_fusion.4.pack_ref), custom_call_target="tpu_custom_call" | custom-call | flops 1000000000 | bytes 1000000 | tf_op jit(solution)/shard_map/pallas_call | solution.py:123
  84.3 1.6 collective-permute-start.1
  85.9 1.5 collective-permute-start
  88.3 1.3 copy.53.refs_0_.idc_ref
  90.0 1.6 multiply_add_fusion
  92.8 9.9 %shard_map.363 = (bf16[2048,1536]{1,0:T(8,128)(2,1)}, bf16[3,2048,64]{2,1,0:T(8,128)(2,1)}, bf16[2048,64]{1,0:T(8,128)(2,1)}, bf16[2048,64]{1,0:T(8,128)(2,1)}) custom-call(bf16[2048,1536]{1,0:T(8,128)(2,1)} %get-tuple-element.149.x_ref, f32[1,1536]{1,0:T(1,128)} %reshape.262.gain_ref, bf16[1536,448]{1,0:T(8,128)(2,1)} %get-tuple-element.150.w_ref, ...), custom_call_target="tpu_custom_call" | custom-call | flops 1000000000 | bytes 1000000 | tf_op jit(solution)/shard_map/pallas_call | solution.py:169
  102.7 45.3 %shard_map.364 = (bf16[2048,192]{1,0:T(8,128)(2,1)}, f32[3,1,2048]{2,1,0:T(1,128)}, bf16[8,256,192]{2,1,0:T(8,128)(2,1)}, bf16[1536,768]{1,0:T(8,128)(2,1)}) custom-call(s32[2048,1]{1,0:T(8,128)} %copy.53.refs_0_.idc_ref, s32[1,2048]{1,0:T(1,128)} %idr_ref.1, bf16[3,2048,64]{2,1,0:T(8,128)(2,1)} %get-tuple-element.153.refs_2_.q_ref, ...), custom_call_target="tpu_custom_call" | custom-call | flops 1000000000 | bytes 1000000 | tf_op jit(solution)/shard_map/pallas_call | solution.py:362
  148.6 12.0 %shard_map.365 = (f32[512,1536]{1,0:T(8,128)}, bf16[512,1536]{1,0:T(8,128)(2,1)}, bf16[512,768]{1,0:T(8,128)(2,1)}) custom-call(bf16[8,256,192]{2,1,0:T(8,128)(2,1)} %get-tuple-element.157.att_ref, bf16[1536,768]{1,0:T(8,128)(2,1)} %get-tuple-element.158.w_ref, bf16[512,1536]{1,0:T(8,128)(2,1)} %bitcast.124, f32[1,1536]{1,0:T(1,128)} %reshape.263.gain_ref), custom_call_target="tpu_custom_call" | custom-call | flops 1000000000 | bytes 1000000 | tf_op jit(solution)/shard_map/pallas_call | solution.py:519
  160.6 1.3 pad_maximum_fusion.2.cot_ref.c_ref
  161.9 1.8 slice_select_fusion.r_ref
  163.7 149.0 %shard_map.366 = (bf16[2048,2048]{1,0:T(8,128)(2,1)}, bf16[2048,1024]{1,0:T(8,128)(2,1)}, bf16[2048,1536]{1,0:T(8,128)(2,1)}, bf16[2048,384]{1,0:T(8,128)(2,1)},...) custom-call(bf16[512,1536]{1,0:T(8,128)(2,1)} %get-tuple-element.161, ...), custom_call_target="tpu_custom_call" | custom-call | flops 1000000000 | bytes 1000000 | tf_op jit(solution)/shard_map/pallas_call | solution.py:1036
  312.7 2.2 slice_bitcast_fusion
  316.0 1.3 collective-permute-done.5
  321.7 4.2 fusion.34
  325.9 2.7 fusion.22
  328.6 2.7 fusion.37
  331.3 2.7 fusion.25
  334.0 1.8 convolution_convert_fusion.6
  335.9 2.7 convolution_convert_fusion.5
  338.6 2.7 convolution_convert_fusion.4
  341.3 2.7 fusion.40
  344.0 15.1 %collective-permute-start.6 = (bf16[256,1536]{1,0:T(8,128)(2,1)S(1)}, bf16[256,1536]{1,0:T(8,128)(2,1)S(1)}, u32[]{:S(2)}, u32[]{:S(2)}) collective-permute-start(bf16[256,1536]{1,0:T(8,128)(2,1)S(1)} %get-tuple-element.179), channel_id=1, source_target_pairs={{0,2},{2,0},{4,6},{6,4},{1,3},{3,1},{5,7},{7,5},{8,10},{10,8},{12,... | collective-permute-start | bytes 2359304 | tf_op jit(solution)/shard_map/ppermute | solution.py:1199
  359.1 2.9 convolution_convert_fusion.3
  362.0 1.4 collective-permute-start.10
  364.0 1.5 collective-permute-start.8
  365.5 2.7 fusion.28
  368.2 9.2 %collective-permute-done.6 = bf16[256,1536]{1,0:T(8,128)(2,1)S(1)} collective-permute-done((bf16[256,1536]{1,0:T(8,128)(2,1)S(1)}, bf16[256,1536]{1,0:T(8,128)(2,1)S(1)}, u32[]{:S(2)}, u32[]{:S(2)}) %collective-permute-start.6) | collective-permute-done | bytes 786464 | tf_op jit(solution)/shard_map/ppermute | solution.py:1199
  377.4 16.4 %collective-permute-done.7 = bf16[256,1536]{1,0:T(8,128)(2,1)S(1)} collective-permute-done((bf16[256,1536]{1,0:T(8,128)(2,1)S(1)}, bf16[256,1536]{1,0:T(8,128)(2,1)S(1)}, u32[]{:S(2)}, u32[]{:S(2)}) %collective-permute-start.7) | collective-permute-done | bytes 786464 | tf_op jit(solution)/shard_map/ppermute | solution.py:1199
  394.0 2.7 collective-permute-start.11
  396.7 2.7 fusion.43
  399.4 2.8 fusion.31
  402.2 51.9 %shard_map.367 = (f32[512,1536]{1,0:T(8,128)}, bf16[512,1536]{1,0:T(8,128)(2,1)}, bf16[512,128]{1,0:T(8,128)(2,1)}, f32[1,1536]{1,0:T(1,128)}, bf16[8,256,192]{2,1,0:T(8,128)(2,1)}) custom-call(bf16[512,1664]{1,0:T(8,128)(2,1)} %get-tuple-element.181.g_ref, f32[512,1536]{1,0:T(8,128)} %get-tuple-element.182.res_ref, ...), custom_call_target="tpu_custom_call" | custom-call | flops 1000000000 | bytes 1000000 | tf_op jit(solution)/shard_map/pallas_call | solution.py:629
  456.2 3.2 add_convert_fusion.3
  459.7 1.5 collective-permute-start.14
  461.8 1.5 collective-permute-start.12
  463.7 1.4 convolution_convert_fusion
  465.4 37.2 %shard_map.368 = (f32[3,2048,64]{2,1,0:T(8,128)}, f32[2048,64]{1,0:T(8,128)}, f32[2048,64]{1,0:T(8,128)}) custom-call(s32[2048,1]{1,0:T(8,128)} %copy.53.refs_0_.idc_ref, s32[1,2048]{1,0:T(1,128)} %idr_ref.1, bf16[3,2048,64]{2,1,0:T(8,128)(2,1)} %get-tuple-element.153.refs_2_.q_ref, bf16[2048,64]{1,0:T(8,128)(2,1)} %get-tuple-element.154.refs_3_.k_ref, ...), custom_call_target="tpu_custom_call" | custom-call | flops 1000000000 | bytes 1000000 | tf_op jit(solution)/shard_map/pallas_call | solution.py:458
  502.7 3.1 add_convert_fusion.2
  505.9 1.4 collective-permute-start.17
  507.8 1.6 collective-permute-start.15
  509.4 47.0 %shard_map.369 = (bf16[4,512,320]{2,1,0:T(8,128)(2,1)}, f32[512,1536]{1,0:T(8,128)}, f32[1,1536]{1,0:T(1,128)}) custom-call(f32[3,2048,64]{2,1,0:T(8,128)} %get-tuple-element.198.dq_ref, f32[2048,64]{1,0:T(8,128)} %get-tuple-element.199.dk_ref, f32[2048,64]{1,0:T(8,128)} %get-tuple-element.200.dv_ref, f32[2048,128]{1,0:T(8,128)} %bitcast.122, ...), custom_call_target="tpu_custom_call" | custom-call | flops 1000000000 | bytes 1000000 | tf_op jit(solution)/shard_map/pallas_call | solution.py:756
  556.5 3.1 add_convert_fusion.5
  559.6 6.4 convolution_convert_fusion.1
  566.2 1.3 pad_maximum_fusion
  567.5 1.6 constant_dynamic-slice_fusion
  569.1 2.6 collective-permute-start.21
  572.6 2.6 add_convert_fusion.4
  575.7 22.0 %shard_map.370 = (f32[384,3,16,256]{3,2,1,0:T(8,128)}, f32[384,3,16,256]{3,2,1,0:T(8,128)}, bf16[384,3,16,256]{3,2,1,0:T(8,128)(2,1)}, f32[384,16,256]{2,1,0:T(8,128)}) custom-call(f32[384,3,16,256]{3,2,1,0:T(8,128)} %bitcast.107, f32[384,3,16,256]{3,2,1,0:T(8,128)} %bitcast.110, f32[384,3,16,256]{3,2,1,0:T(8,128)} %bitcast.113, bf16[4,384,1024]{2,1,0:T(8,128)(2,1)} %bitcast.132), custom_call_target="tpu_custom_call" | custom-call | flops 31457280 | bytes 70778880 | tf_op jit(solution)/shard_map/pallas_call | solution.py:1110
  597.7 14.5 %collective-permute-done.20 = bf16[1168,384]{1,0:T(8,128)(2,1)S(1)} collective-permute-done((bf16[1168,384]{1,0:T(8,128)(2,1)}, bf16[1168,384]{1,0:T(8,128)(2,1)S(1)}, u32[]{:S(2)}, u32[]{:S(2)}) %collective-permute-start.20) | collective-permute-done | bytes 897056 | tf_op jit(solution)/shard_map/ppermute | solution.py:1205
  613.1 1.9 add_convert_fusion.1
  616.3 13.8 %collective-permute-start.24 = (bf16[208,384]{1,0:T(8,128)(2,1)}, bf16[208,384]{1,0:T(8,128)(2,1)}, u32[]{:S(2)}, u32[]{:S(2)}) collective-permute-start(bf16[208,384]{1,0:T(8,128)(2,1)} %get-tuple-element.295), channel_id=1, source_target_pairs={{0,6},{2,4},{4,2},{6,0},{1,7},{3,5},{5,3},{7,1},{8,14},{10,12},{12... | collective-permute-start | bytes 479240 | tf_op jit(solution)/shard_map/ppermute | solution.py:1199
  630.8 22.1 %shard_map.371 = (f32[384,3,16,256]{3,2,1,0:T(8,128)}, f32[384,3,16,256]{3,2,1,0:T(8,128)}, bf16[384,3,16,256]{3,2,1,0:T(8,128)(2,1)}, f32[384,16,256]{2,1,0:T(8,128)}) custom-call(f32[384,3,16,256]{3,2,1,0:T(8,128)} %bitcast.108, f32[384,3,16,256]{3,2,1,0:T(8,128)} %bitcast.111, ...), custom_call_target="tpu_custom_call", output_to_operand_aliasing={{0}: (4, {}), {1}: (5, {}), {2}: (6, {})} | custom-call | flops 31457280 | bytes 70778880 | tf_op jit(solution)/shard_map/pallas_call | solution.py:1110
  652.9 8.8 %collective-permute-done.23 = bf16[208,384]{1,0:T(8,128)(2,1)} collective-permute-done((bf16[208,384]{1,0:T(8,128)(2,1)}, bf16[208,384]{1,0:T(8,128)(2,1)}, u32[]{:S(2)}, u32[]{:S(2)}) %collective-permute-start.23) | collective-permute-done | bytes 159776 | tf_op jit(solution)/shard_map/ppermute | solution.py:1199
  661.7 1.2 add_convert_fusion.7
  663.7 3.8 fusion.17
  667.8 33.8 %collective-permute-done.26 = bf16[528,384]{1,0:T(8,128)(2,1)S(1)} collective-permute-done((bf16[528,384]{1,0:T(8,128)(2,1)S(1)}, bf16[528,384]{1,0:T(8,128)(2,1)S(1)}, u32[]{:S(2)}, u32[]{:S(2)}) %collective-permute-start.26) | collective-permute-done | bytes 405536 | tf_op jit(solution)/shard_map/ppermute | solution.py:1199
  701.7 10.6 %collective-permute-done.27 = bf16[528,384]{1,0:T(8,128)(2,1)S(1)} collective-permute-done((bf16[528,384]{1,0:T(8,128)(2,1)S(1)}, bf16[528,384]{1,0:T(8,128)(2,1)S(1)}, u32[]{:S(2)}, u32[]{:S(2)}) %collective-permute-start.27) | collective-permute-done | bytes 405536 | tf_op jit(solution)/shard_map/ppermute | solution.py:1199
  714.4 5.4 shard_map.373
  719.8 8.1 %shard_map.372 = (f32[384,1280]{1,0:T(8,128)}, f32[384,1280]{1,0:T(8,128)}, f32[384,1280]{1,0:T(8,128)}, bf16[384,1280]{1,0:T(8,128)(2,1)}) custom-call(f32[384,1280]{1,0:T(8,128)} %p_ref.2, f32[384,1280]{1,0:T(8,128)} %f_ref.2, f32[384,1280]{1,0:T(8,128)} %s_ref.2, bf16[1280,384]{1,0:T(8,128)(2,1)} %bitcast.130), custom_call_target="tpu_custom_call" | custom-call | flops 9830400 | bytes 13762560 | tf_op jit(solution)/shard_map/pallas_call | solution.py:1149
  728.7 1.3 fusion.59
  730.7 26.8 %shard_map.374 = (f32[384,3,16,256]{3,2,1,0:T(8,128)}, f32[384,3,16,256]{3,2,1,0:T(8,128)}, bf16[384,3,16,256]{3,2,1,0:T(8,128)(2,1)}, f32[384,16,2,256]{3,2,1,0:T(2,128)}) custom-call(f32[384,3,16,256]{3,2,1,0:T(8,128)} %bitcast.109, f32[384,3,16,256]{3,2,1,0:T(8,128)} %bitcast.112, ...), custom_call_target="tpu_custom_call", output_to_operand_aliasing={{0}: (5, {}), {1}: (6, {}), {2}: (7, {})} | custom-call | flops 31457280 | bytes 70778880 | tf_op jit(solution)/shard_map/pallas_call | solution.py:1110
  757.5 1.7 copy.67
  (177 shorter events, 27.0 us)
Async XLA Ops:
  7.2 156.5 %all-gather.8.cloned.1.call-start = ((), (), s32[]{:S(2)}) async-start(), calls=%async_computation | async-start | bytes 11796480 | tf_op jit(solution)/shard_map/all_gather | solution.py:1247
  14.8 560.9 %all-gather.12.cloned.1.call-start = ((), (), s32[]{:S(2)}) async-start(), calls=%async_computation.2 | async-start | bytes 3932160 | tf_op jit(solution)/shard_map/all_gather | solution.py:1335
  16.4 66.1 %copy-start.5 = (bf16[384,1280]{1,0:T(8,128)(2,1)}, bf16[384,1280]{1,0:T(8,128)(2,1)S(1)}, u32[]{:S(2)}) copy-start(bf16[384,1280]{1,0:T(8,128)(2,1)S(1)} %convert_element_type.329.shard_ref) | copy-start | bytes 2949124
  17.6 64.9 %copy-start.22 = (s32[1,512,8]{1,2,0:T(8,128)S(1)}, s32[1,512,8]{1,2,0:T(8,128)}, u32[]{:S(2)}) copy-start(s32[1,512,8]{1,2,0:T(8,128)} %param.22) | copy-start | bytes 49156
  17.6 65.7 %copy-start.4 = (bf16[1,512,1536]{2,1,0:T(8,128)(2,1)S(1)}, bf16[1,512,1536]{2,1,0:T(8,128)(2,1)}, u32[]{:S(2)}) copy-start(bf16[1,512,1536]{2,1,0:T(8,128)(2,1)} %param.20) | copy-start | bytes 4718596
  82.5 4.9 copy-start.7
  83.3 5.0 copy-start.19
  84.3 79.4 %collective-permute-start.1 = (bf16[256,1664]{1,0:T(8,128)(2,1)}, bf16[256,1664]{1,0:T(8,128)(2,1)}, u32[]{:S(2)}, u32[]{:S(2)}) collective-permute-start(bf16[256,1664]{1,0:T(8,128)(2,1)} %fusion.46), channel_id=1, source_target_pairs={{0,4},{2,6},{4,0},{6,2},{1,5},{3,7},{5,1},{7,3},{8,12},{10,14},{12... | collective-permute-start | bytes 2555912 | tf_op jit(solution)/shard_map/ppermute | solution.py:1199
  85.9 77.8 %collective-permute-start = (bf16[256,1664]{1,0:T(8,128)(2,1)}, bf16[256,1664]{1,0:T(8,128)(2,1)}, u32[]{:S(2)}, u32[]{:S(2)}) collective-permute-start(bf16[256,1664]{1,0:T(8,128)(2,1)} %fusion.46), channel_id=1, source_target_pairs={{0,2},{2,0},{4,6},{6,4},{1,3},{3,1},{5,7},{7,5},{8,10},{10,8},{12,... | collective-permute-start | bytes 2555912 | tf_op jit(solution)/shard_map/ppermute | solution.py:1199
  88.3 3.3 copy-start.6
  312.7 7.9 %copy-start.3 = (bf16[2048,1536]{1,0:T(8,128)(2,1)S(1)}, bf16[2048,1536]{1,0:T(8,128)(2,1)}, u32[]{:S(2)}) copy-start(bf16[2048,1536]{1,0:T(8,128)(2,1)} %get-tuple-element.165) | copy-start | bytes 18874372
  314.9 2.4 collective-permute-start.5
  315.4 3.0 collective-permute-start.4
  315.5 4.0 collective-permute-start.3
  315.9 5.8 copy-start.29
  315.9 4.8 collective-permute-start.2
  321.6 4.3 copy-start.38
  325.9 2.7 copy-start.37
  331.3 2.7 copy-start.36
  335.9 2.7 copy-start.34
  338.6 2.7 copy-start.32
  341.3 17.8 %copy-start.33 = (bf16[2048,384]{1,0:T(8,128)(2,1)S(1)}, bf16[2048,384]{1,0:T(8,128)(2,1)}, u32[]{:S(2)}) copy-start(bf16[2048,384]{1,0:T(8,128)(2,1)} %get-tuple-element.178) | copy-start | bytes 4718596
  344.0 33.4 %collective-permute-start.6 = (bf16[256,1536]{1,0:T(8,128)(2,1)S(1)}, bf16[256,1536]{1,0:T(8,128)(2,1)S(1)}, u32[]{:S(2)}, u32[]{:S(2)}) collective-permute-start(bf16[256,1536]{1,0:T(8,128)(2,1)S(1)} %get-tuple-element.179), channel_id=1, source_target_pairs={{0,2},{2,0},{4,6},{6,4},{1,3},{3,1},{5,7},{7,5},{8,10},{10,8},{12,... | collective-permute-start | bytes 2359304 | tf_op jit(solution)/shard_map/ppermute | solution.py:1199
  359.1 34.7 %collective-permute-start.7 = (bf16[256,1536]{1,0:T(8,128)(2,1)S(1)}, bf16[256,1536]{1,0:T(8,128)(2,1)S(1)}, u32[]{:S(2)}, u32[]{:S(2)}) collective-permute-start(bf16[256,1536]{1,0:T(8,128)(2,1)S(1)} %get-tuple-element.180), channel_id=1, source_target_pairs={{0,2},{2,0},{4,6},{6,4},{1,3},{3,1},{5,7},{7,5},{8,10},{10,8},{12,... | collective-permute-start | bytes 2359304 | tf_op jit(solution)/shard_map/ppermute | solution.py:1199
  362.0 92.1 %collective-permute-start.10 = (bf16[384,1024]{1,0:T(8,128)(2,1)}, bf16[384,1024]{1,0:T(8,128)(2,1)S(1)}, u32[]{:S(2)}, u32[]{:S(2)}) collective-permute-start(bf16[384,1024]{1,0:T(8,128)(2,1)} %convolution_convert_fusion.3), channel_id=1, source_target_pairs={{0,24},{8,16},{16,8},{24,0},{1,25},{9,17},{17,9},{25,1},{2,26},{10... | collective-permute-start | bytes 2359304 | tf_op jit(solution)/shard_map/ppermute | solution.py:1205
  363.5 90.7 %collective-permute-start.9 = (bf16[384,1024]{1,0:T(8,128)(2,1)}, bf16[384,1024]{1,0:T(8,128)(2,1)S(1)}, u32[]{:S(2)}, u32[]{:S(2)}) collective-permute-start(bf16[384,1024]{1,0:T(8,128)(2,1)} %convolution_convert_fusion.4), channel_id=1, source_target_pairs={{0,16},{8,24},{16,0},{24,8},{1,17},{9,25},{17,1},{25,9},{2,18},{10... | collective-permute-start | bytes 2359304 | tf_op jit(solution)/shard_map/ppermute | solution.py:1205
  364.0 90.1 %collective-permute-start.8 = (bf16[384,1024]{1,0:T(8,128)(2,1)}, bf16[384,1024]{1,0:T(8,128)(2,1)}, u32[]{:S(2)}, u32[]{:S(2)}) collective-permute-start(bf16[384,1024]{1,0:T(8,128)(2,1)} %convolution_convert_fusion.5), channel_id=1, source_target_pairs={{0,8},{8,0},{16,24},{24,16},{1,9},{9,1},{17,25},{25,17},{2,10},{10... | collective-permute-start | bytes 2359304 | tf_op jit(solution)/shard_map/ppermute | solution.py:1205
  368.2 28.5 %copy-start.31 = (bf16[2048,384]{1,0:T(8,128)(2,1)S(1)}, bf16[2048,384]{1,0:T(8,128)(2,1)}, u32[]{:S(2)}) copy-start(bf16[2048,384]{1,0:T(8,128)(2,1)} %get-tuple-element.193) | copy-start | bytes 4718596
  377.4 22.0 %copy-start.10 = (bf16[256,1536]{1,0:T(8,128)(2,1)}, bf16[256,1536]{1,0:T(8,128)(2,1)S(1)}, u32[]{:S(2)}) copy-start(bf16[256,1536]{1,0:T(8,128)(2,1)S(1)} %collective-permute-done.6) | copy-start | bytes 2359300
  394.0 60.2 %collective-permute-start.11 = (bf16[256,1536]{1,0:T(8,128)(2,1)S(1)}, bf16[256,1536]{1,0:T(8,128)(2,1)S(1)}, u32[]{:S(2)}, u32[]{:S(2)}) collective-permute-start(bf16[256,1536]{1,0:T(8,128)(2,1)S(1)} %add_convert_fusion.6), channel_id=1, source_target_pairs={{0,4},{2,6},{4,0},{6,2},{1,5},{3,7},{5,1},{7,3},{8,12},{10,14},{12... | collective-permute-start | bytes 2359304 | tf_op jit(solution)/shard_map/ppermute | solution.py:1199
  456.2 7.1 copy-start
  456.2 7.1 copy-start.17
  456.2 7.1 copy-start.28
  459.4 4.3 copy-start.24
  459.4 4.3 copy-start.40
  459.4 171.3 %all-gather.14.cloned.1.call-start = ((), (), s32[]{:S(2)}) async-start(), calls=%async_computation.3 | async-start | bytes 3932160 | tf_op jit(solution)/shard_map/all_gather | solution.py:1335
  459.7 4.0 copy-start.39
  459.7 43.0 %collective-permute-start.14 = (bf16[384,1024]{1,0:T(8,128)(2,1)}, bf16[384,1024]{1,0:T(8,128)(2,1)}, u32[]{:S(2)}, u32[]{:S(2)}) collective-permute-start(bf16[384,1024]{1,0:T(8,128)(2,1)} %fusion.31), channel_id=1, source_target_pairs={{0,24},{8,16},{16,8},{24,0},{1,25},{9,17},{17,9},{25,1},{2,26},{10... | collective-permute-start | bytes 2359304 | tf_op jit(solution)/shard_map/ppermute | solution.py:1205
  461.2 41.4 %collective-permute-start.13 = (bf16[384,1024]{1,0:T(8,128)(2,1)}, bf16[384,1024]{1,0:T(8,128)(2,1)}, u32[]{:S(2)}, u32[]{:S(2)}) collective-permute-start(bf16[384,1024]{1,0:T(8,128)(2,1)} %fusion.28), channel_id=1, source_target_pairs={{0,16},{8,24},{16,0},{24,8},{1,17},{9,25},{17,1},{25,9},{2,18},{10... | collective-permute-start | bytes 2359304 | tf_op jit(solution)/shard_map/ppermute | solution.py:1205
  461.8 40.9 %collective-permute-start.12 = (bf16[384,1024]{1,0:T(8,128)(2,1)}, bf16[384,1024]{1,0:T(8,128)(2,1)}, u32[]{:S(2)}, u32[]{:S(2)}) collective-permute-start(bf16[384,1024]{1,0:T(8,128)(2,1)} %fusion.25), channel_id=1, source_target_pairs={{0,8},{8,0},{16,24},{24,16},{1,9},{9,1},{17,25},{25,17},{2,10},{10... | collective-permute-start | bytes 2359304 | tf_op jit(solution)/shard_map/ppermute | solution.py:1205
  465.4 37.3 %copy-start.13 = (bf16[384,1024]{1,0:T(8,128)(2,1)S(1)}, bf16[384,1024]{1,0:T(8,128)(2,1)}, u32[]{:S(2)}) copy-start(bf16[384,1024]{1,0:T(8,128)(2,1)} %fusion.22) | copy-start | bytes 2359300
  505.8 222.9 %all-gather.10.cloned.1.call-start = ((), (), s32[]{:S(2)}) async-start(), calls=%async_computation.1 | async-start | bytes 3932160 | tf_op jit(solution)/shard_map/all_gather | solution.py:1335
  505.9 50.6 %collective-permute-start.17 = (bf16[384,1024]{1,0:T(8,128)(2,1)}, bf16[384,1024]{1,0:T(8,128)(2,1)}, u32[]{:S(2)}, u32[]{:S(2)}) collective-permute-start(bf16[384,1024]{1,0:T(8,128)(2,1)} %fusion.43), channel_id=1, source_target_pairs={{0,24},{8,16},{16,8},{24,0},{1,25},{9,17},{17,9},{25,1},{2,26},{10... | collective-permute-start | bytes 2359304 | tf_op jit(solution)/shard_map/ppermute | solution.py:1205
  507.2 49.2 %collective-permute-start.16 = (bf16[384,1024]{1,0:T(8,128)(2,1)}, bf16[384,1024]{1,0:T(8,128)(2,1)}, u32[]{:S(2)}, u32[]{:S(2)}) collective-permute-start(bf16[384,1024]{1,0:T(8,128)(2,1)} %fusion.40), channel_id=1, source_target_pairs={{0,16},{8,24},{16,0},{24,8},{1,17},{9,25},{17,1},{25,9},{2,18},{10... | collective-permute-start | bytes 2359304 | tf_op jit(solution)/shard_map/ppermute | solution.py:1205
  507.8 48.7 %collective-permute-start.15 = (bf16[384,1024]{1,0:T(8,128)(2,1)}, bf16[384,1024]{1,0:T(8,128)(2,1)}, u32[]{:S(2)}, u32[]{:S(2)}) collective-permute-start(bf16[384,1024]{1,0:T(8,128)(2,1)} %fusion.37), channel_id=1, source_target_pairs={{0,8},{8,0},{16,24},{24,16},{1,9},{9,1},{17,25},{25,17},{2,10},{10... | collective-permute-start | bytes 2359304 | tf_op jit(solution)/shard_map/ppermute | solution.py:1205
  509.4 47.0 %copy-start.12 = (bf16[384,1024]{1,0:T(8,128)(2,1)S(1)}, bf16[384,1024]{1,0:T(8,128)(2,1)}, u32[]{:S(2)}) copy-start(bf16[384,1024]{1,0:T(8,128)(2,1)} %fusion.34) | copy-start | bytes 2359300
  559.6 6.5 copy-start.25
  569.1 28.6 %collective-permute-start.21 = (bf16[1168,384]{1,0:T(8,128)(2,1)}, bf16[1168,384]{1,0:T(8,128)(2,1)S(1)}, u32[]{:S(2)}, u32[]{:S(2)}) collective-permute-start(bf16[1168,384]{1,0:T(8,128)(2,1)} %get-tuple-element.289), channel_id=1, source_target_pairs={{0,24},{8,16},{16,8},{24,0},{1,25},{9,17},{17,9},{25,1},{2,26},{10... | collective-permute-start | bytes 2691080 | tf_op jit(solution)/shard_map/ppermute | solution.py:1205
  571.7 40.6 %collective-permute-start.20 = (bf16[1168,384]{1,0:T(8,128)(2,1)}, bf16[1168,384]{1,0:T(8,128)(2,1)S(1)}, u32[]{:S(2)}, u32[]{:S(2)}) collective-permute-start(bf16[1168,384]{1,0:T(8,128)(2,1)} %get-tuple-element.290), channel_id=1, source_target_pairs={{0,16},{8,24},{16,0},{24,8},{1,17},{9,25},{17,1},{25,9},{2,18},{10... | collective-permute-start | bytes 2691080 | tf_op jit(solution)/shard_map/ppermute | solution.py:1205
  572.0 40.2 %collective-permute-start.19 = (bf16[1168,384]{1,0:T(8,128)(2,1)}, bf16[1168,384]{1,0:T(8,128)(2,1)}, u32[]{:S(2)}, u32[]{:S(2)}) collective-permute-start(bf16[1168,384]{1,0:T(8,128)(2,1)} %get-tuple-element.291), channel_id=1, source_target_pairs={{0,8},{8,0},{16,24},{24,16},{1,9},{9,1},{17,25},{25,17},{2,10},{10... | collective-permute-start | bytes 2691080 | tf_op jit(solution)/shard_map/ppermute | solution.py:1205
  575.2 88.6 %collective-permute-start.18 = (bf16[256,1536]{1,0:T(8,128)(2,1)}, bf16[256,1536]{1,0:T(8,128)(2,1)}, u32[]{:S(2)}, u32[]{:S(2)}) collective-permute-start(bf16[256,1536]{1,0:T(8,128)(2,1)} %add_convert_fusion.4), channel_id=1, source_target_pairs={{0,1},{1,0},{2,3},{3,2},{4,5},{5,4},{6,7},{7,6},{8,9},{9,8},{10,11... | collective-permute-start | bytes 2359304 | tf_op jit(solution)/shard_map/ppermute | solution.py:1202
  616.3 36.5 %collective-permute-start.24 = (bf16[208,384]{1,0:T(8,128)(2,1)}, bf16[208,384]{1,0:T(8,128)(2,1)}, u32[]{:S(2)}, u32[]{:S(2)}) collective-permute-start(bf16[208,384]{1,0:T(8,128)(2,1)} %get-tuple-element.295), channel_id=1, source_target_pairs={{0,6},{2,4},{4,2},{6,0},{1,7},{3,5},{5,3},{7,1},{8,14},{10,12},{12... | collective-permute-start | bytes 479240 | tf_op jit(solution)/shard_map/ppermute | solution.py:1199
  630.1 31.6 %collective-permute-start.23 = (bf16[208,384]{1,0:T(8,128)(2,1)}, bf16[208,384]{1,0:T(8,128)(2,1)}, u32[]{:S(2)}, u32[]{:S(2)}) collective-permute-start(bf16[208,384]{1,0:T(8,128)(2,1)} %get-tuple-element.296), channel_id=1, source_target_pairs={{0,4},{2,6},{4,0},{6,2},{1,5},{3,7},{5,1},{7,3},{8,12},{10,14},{12... | collective-permute-start | bytes 479240 | tf_op jit(solution)/shard_map/ppermute | solution.py:1199
  630.1 31.6 %collective-permute-start.22 = (bf16[208,384]{1,0:T(8,128)(2,1)}, bf16[208,384]{1,0:T(8,128)(2,1)}, u32[]{:S(2)}, u32[]{:S(2)}) collective-permute-start(bf16[208,384]{1,0:T(8,128)(2,1)} %get-tuple-element.297), channel_id=1, source_target_pairs={{0,2},{2,0},{4,6},{6,4},{1,3},{3,1},{5,7},{7,5},{8,10},{10,8},{12,... | collective-permute-start | bytes 479240 | tf_op jit(solution)/shard_map/ppermute | solution.py:1199
  630.8 30.9 %copy-start.16 = (bf16[208,384]{1,0:T(8,128)(2,1)S(1)}, bf16[208,384]{1,0:T(8,128)(2,1)}, u32[]{:S(2)}) copy-start(bf16[208,384]{1,0:T(8,128)(2,1)} %get-tuple-element.239) | copy-start | bytes 479236
  630.8 33.0 %copy-start.1 = (f32[512,1536]{1,0:T(8,128)S(1)}, f32[512,1536]{1,0:T(8,128)}, u32[]{:S(2)}) copy-start(f32[512,1536]{1,0:T(8,128)} %get-tuple-element.182.res_ref) | copy-start | bytes 9437188
  662.9 38.6 %collective-permute-start.25 = (bf16[528,384]{1,0:T(8,128)(2,1)S(1)}, bf16[528,384]{1,0:T(8,128)(2,1)S(1)}, u32[]{:S(2)}, u32[]{:S(2)}) collective-permute-start(bf16[528,384]{1,0:T(8,128)(2,1)S(1)} %pad_maximum_fusion.3), channel_id=1, source_target_pairs={{0,2},{2,0},{4,6},{6,4},{1,3},{3,1},{5,7},{7,5},{8,10},{10,8},{12,... | collective-permute-start | bytes 1216520 | tf_op jit(solution)/shard_map/ppermute | solution.py:1199
  663.0 38.6 %collective-permute-start.26 = (bf16[528,384]{1,0:T(8,128)(2,1)S(1)}, bf16[528,384]{1,0:T(8,128)(2,1)S(1)}, u32[]{:S(2)}, u32[]{:S(2)}) collective-permute-start(bf16[528,384]{1,0:T(8,128)(2,1)S(1)} %pad_maximum_fusion.3), channel_id=1, source_target_pairs={{0,4},{2,6},{4,0},{6,2},{1,5},{3,7},{5,1},{7,3},{8,12},{10,14},{12... | collective-permute-start | bytes 1216520 | tf_op jit(solution)/shard_map/ppermute | solution.py:1199
  701.5 10.8 %collective-permute-start.27 = (bf16[528,384]{1,0:T(8,128)(2,1)S(1)}, bf16[528,384]{1,0:T(8,128)(2,1)S(1)}, u32[]{:S(2)}, u32[]{:S(2)}) collective-permute-start(bf16[528,384]{1,0:T(8,128)(2,1)S(1)} %collective-permute-done.26), channel_id=1, source_target_pairs={{0,2},{2,0},{4,6},{6,4},{1,3},{3,1},{5,7},{7,5},{8,10},{10,8},{12,... | collective-permute-start | bytes 1216520 | tf_op jit(solution)/shard_map/ppermute | solution.py:1199
  719.8 8.9 %copy-start.20 = (f32[384,16]{0,1:T(8,128)S(1)}, f32[384,16]{0,1:T(8,128)}, u32[]{:S(2)}) copy-start(f32[384,16]{0,1:T(8,128)} %param.33) | copy-start | bytes 73732
  719.8 8.9 %copy-start.21 = (f32[384,16]{0,1:T(8,128)S(1)}, f32[384,16]{0,1:T(8,128)}, u32[]{:S(2)}) copy-start(f32[384,16]{0,1:T(8,128)} %param.34) | copy-start | bytes 73732
  719.8 10.3 %copy-start.26 = (f32[2,384]{1,0:T(2,128)S(1)}, f32[2,384]{1,0:T(2,128)}, u32[]{:S(2)}) copy-start(f32[2,384]{1,0:T(2,128)} %param.24) | copy-start | bytes 9220
  719.8 10.3 %copy-start.27 = (f32[2,384]{1,0:T(2,128)S(1)}, f32[2,384]{1,0:T(2,128)}, u32[]{:S(2)}) copy-start(f32[2,384]{1,0:T(2,128)} %param.25) | copy-start | bytes 9220
  730.7 26.8 %copy-start.8 = (f32[512,1536]{1,0:T(8,128)S(1)}, f32[512,1536]{1,0:T(8,128)}, u32[]{:S(2)}) copy-start(f32[512,1536]{1,0:T(8,128)} %get-tuple-element.252) | copy-start | bytes 9437188
  (9 other events, 11.4 us)
Sparse Core Ops, SparseCore 0:
  14.9 114.3 all-gather.7
  459.5 84.0 all-gather.11
  545.8 62.7 all-gather.13
  610.6 92.8 all-gather.9

commit v4 on v3

--- a/solution.py
+++ b/solution.py
@@ -782,10 +782,11 @@
 
 
 def expert_kernel(count, pieces, n_ref, cot_ref, one_ref, two_ref, r_ref, w_any, shard_ref, *refs):
-    pre_ref, wh_ref, out_ref = refs[:3]
-    x_parts, cot_parts = refs[3 : 3 + pieces], refs[3 + pieces : 3 + 2 * pieces]
-    grad_any, joint_ref = refs[3 + 2 * pieces : 5 + 2 * pieces]
-    x_ref, c_ref, w_ref, part_ref, there_ref, sum_ref, back_ref, full_ref = refs[5 + 2 * pieces : -4]
+    pre_ref, wh_ref = refs[:2]
+    x_parts, cot_parts = refs[2 : 2 + pieces], refs[2 + pieces : 2 + 2 * pieces]
+    grad_any, joint_ref, out_any, far_any = refs[2 + 2 * pieces : 6 + 2 * pieces]
+    x_ref, c_ref, w_ref, part_ref, there_ref, back_ref, full_ref = refs[6 + 2 * pieces : -7]
+    out_ref, out_there, out_near = refs[-7:-4]
     local, wrote, send, recv = refs[-4:]
     i = pl.program_id(0)
     z, t, f = lax.axis_index("ctx"), lax.axis_index("tp"), lax.axis_index("fsdp")
@@ -823,8 +824,16 @@
     ]
     crossed = [remote(10 + m, part_ref.at[2 * m + 1], there_ref.at[m], core) for m in range(4)]
     returned = [None] + [
-        remote(13 + m, sum_ref.at[m], back_ref.at[m], device)
+        remote(13 + m, part_ref.at[2 * m], back_ref.at[m], device)
         for m, device in ((1, near), (2, far), (3, third))
+    ]
+    out_crossed = [
+        remote(22 + m, out_ref.at[2 * m + 1], out_there.at[m], core) for m in range(4)
+    ]
+    out_sent = [remote(26 + n, out_ref.at[4 * n + 2], out_near.at[n], near) for n in (0, 1)]
+    out_stores = [
+        pltpu.make_async_copy(out_ref.at[0], out_any, local.at[9]),
+        pltpu.make_async_copy(out_ref.at[4], far_any, local.at[10]),
     ]
     last = remote(17, full_ref.at[rows(t)], full_ref.at[rows(t)], core)
     loads = [
@@ -875,9 +884,15 @@
 
     def finish(m):
         crossed[m].wait_recv()
-        sum_ref[m] = (part_ref[2 * m].astype(F32) + there_ref[m].astype(F32)).astype(BF)
+        part_ref[2 * m] = (part_ref[2 * m].astype(F32) + there_ref[m].astype(F32)).astype(BF)
         if m:
             returned[m].start()
+
+    def finish_out(m):
+        out_crossed[m].wait_recv()
+        out_ref[2 * m] = (out_ref[2 * m].astype(F32) + out_there[m].astype(F32)).astype(BF)
+        if m % 2:
+            out_sent[m // 2].start()
 
     @pl.when(i == 0)
     def _():
@@ -984,24 +999,44 @@
         def _():
             crossed[m].start()
 
-    out_ref[...] = lax.dot_general(
+    out_ref[i] = lax.dot_general(
         wh_ref[...], w_ref[:, 2 * hidden_columns :], NT, preferred_element_type=F32
     ).astype(BF)
+    for m in range(4):
+
+        @pl.when(i == 2 * m + 1)
+        def _():
+            out_crossed[m].start()
+
     for m in range(2):
 
         @pl.when(i == 2 * m + 2)
         def _():
             finish(m)
 
+    @pl.when(i == 6)
+    def _():
+        finish_out(1)
+
     @pl.when(i == 7)
     def _():
         finish(3)
-        total = sum_ref[0].astype(F32)
+        for m in (3, 0, 2):
+            finish_out(m)
+        total = part_ref[0].astype(F32)
         for m in (1, 2, 3):
             returned[m].wait_recv()
             total = total + back_ref[m].astype(F32)
         full_ref[rows(t), :] = total.astype(BF)
         last.start()
+        for n in (0, 1):
+            out_sent[n].wait_recv()
+            out_ref[4 * n] = (out_ref[4 * n].astype(F32) + out_near[n].astype(F32)).astype(BF)
+            out_stores[n].start()
+        for made in out_crossed + out_sent:
+            made.wait_send()
+        for made in out_stores:
+            made.wait()
         for made in [x_one, x_two, x_three, c_three] + x_swaps[1:] + c_swaps[1:] + crossed:
             made.wait_send()
         for made in returned[1:]:
@@ -1032,18 +1067,20 @@
     hidden_columns = w.shape[1] // 3
     slot = lambda n: pl.BlockSpec((half, n), lambda i: (i, 0))
     anywhere = pl.BlockSpec(memory_space=pl.ANY)
-    blocks = [2 * hidden_columns, hidden_columns, width]
+    blocks = [2 * hidden_columns, hidden_columns]
     return pl.pallas_call(
         functools.partial(expert_kernel, count, pieces),
         grid=(8,),
         in_specs=[anywhere] * 4 + [pl.BlockSpec(router.shape, lambda i: (0, 0)), anywhere, anywhere],
-        out_specs=[slot(n) for n in blocks] + [anywhere] * (2 * pieces + 2),
+        out_specs=[slot(n) for n in blocks] + [anywhere] * (2 * pieces + 4),
         out_shape=[
             jax.ShapeDtypeStruct((8 * half, n), BF) for n in blocks + [width // pieces] * (2 * pieces)
         ]
         + [
             jax.ShapeDtypeStruct((rows, packed), BF),
             jax.ShapeDtypeStruct((pieces * shard.shape[0], shard.shape[1]), BF),
+            jax.ShapeDtypeStruct((half, width), BF),
+            jax.ShapeDtypeStruct((half, width), BF),
         ],
         scratch_shapes=[
             pltpu.VMEM((8, half, width), BF),
@@ -1052,12 +1089,14 @@
             pltpu.VMEM((8, half, packed), BF),
             pltpu.VMEM((4, half, packed), BF),
             pltpu.VMEM((4, half, packed), BF),
-            pltpu.VMEM((4, half, packed), BF),
             pltpu.VMEM((rows, packed), BF),
-            pltpu.SemaphoreType.DMA((9,)),
+            pltpu.VMEM((8, half, width), BF),
+            pltpu.VMEM((4, half, width), BF),
+            pltpu.VMEM((2, half, width), BF),
+            pltpu.SemaphoreType.DMA((11,)),
             pltpu.SemaphoreType.DMA((8, 2 * pieces)),
-            pltpu.SemaphoreType.DMA((22,)),
-            pltpu.SemaphoreType.DMA((22,)),
+            pltpu.SemaphoreType.DMA((28,)),
+            pltpu.SemaphoreType.DMA((28,)),
         ],
         compiler_params=params(collective_id=1, has_side_effects=True),
         cost_estimate=LIGHT,
@@ -1298,18 +1337,12 @@
     )
 
     pieces = n_fsdp if n_fsdp == 4 else 1
-    pre_all, hidden_all, out_all, *kept, grad_rows, joint_full = experts(
+    pre_all, hidden_all, *kept, grad_rows, joint_full, out_here, out_two = experts(
         pieces, normed_second, cot_pack, *cot_came, router_wide, expert_full, joint_low, each
     )
     if pieces == 1:
         joint_full = lax.all_gather(joint_low, "fsdp", axis=0, tiled=True)
     x_parts, cot_parts = kept[:pieces], kept[pieces:]
-    outs = out_all.reshape(n_ctx, 2, half, width)
-    outs = [
-        (outs[m, 0].astype(F32) + swap(outs[m, 1]).astype(F32)).astype(BF) for m in range(n_ctx)
-    ]
-    outs, x_parts, cot_parts = barrier((outs, x_parts, cot_parts))
-    out_near = [beyond(outs[1], 1), beyond(outs[3], 1)]
 
     wide = each * units
 
@@ -1334,15 +1367,12 @@
     def gathered(came):
         return lax.all_gather(added(came), "ctx", axis=0, tiled=False)
 
-    grad_rows, joint_full, terms[2], out_near = barrier(
-        (grad_rows, joint_full, terms[2], out_near)
-    )
-    out_far = beyond((outs[2].astype(F32) + out_near[1].astype(F32)).astype(BF), 2)
+    grad_rows, terms[2] = barrier((grad_rows, terms[2]))
     residual_grads, residual_low, logit_grads, gain_second_grad, attended_grads_all = residual_back(
         grad_rows, residual, normed_second, cot_pack, router_wide, gain_second, output_full
     )
-    attended_grads_all, pieces_came[2], out_far, *_ = barrier(
-        (attended_grads_all, pieces_came[2], out_far, terms[0], terms[1])
+    attended_grads_all, pieces_came[2], *_ = barrier(
+        (attended_grads_all, pieces_came[2], terms[0], terms[1])
     )
     expert_sums = {2: gathered(pieces_came[2])}
     step = 64
@@ -1373,7 +1403,10 @@
     joint_grads, input_rows, gain_first_grad = joint_back(
         dq, dk, dv, cosine, sine, joint_full, tokens_low, gain_first, residual_grads
     )
-    joint_grads, pieces_came[1], rest_term = barrier((joint_grads, pieces_came[1], rest_term))
+    joint_grads, pieces_came[1], rest_term, out_two = barrier(
+        (joint_grads, pieces_came[1], rest_term, out_two)
+    )
+    out_far = beyond(out_two, 2)
     expert_sums[1] = gathered(pieces_came[1])
     joint_grads_all = joint_grads.reshape(length, group_columns)
 
@@ -1413,14 +1446,14 @@
     rest_low = sum(x.astype(F32) for x in rest_parts).astype(BF)
     both = jnp.concatenate([joint_owned, rest_low], axis=0)
     both_all = {0: both, **spread(both)}
+    expert_step(1, squares[0])
+    both_all, out_far, made[:] = barrier((both_all, out_far, made))
     full = jnp.zeros((n_ctx, *both.shape), BF)
     for m, got in both_all.items():
         full = put(full, got, z ^ m)
     joint_sum = full[:, :group_columns].reshape(n_ctx * group_columns, own_rows)
     rest_full = full[:, group_columns:].reshape(output_columns + step, own_rows)
-    moe_low = (
-        outs[0].astype(F32) + out_near[0].astype(F32) + out_far.astype(F32)
-    ).astype(BF)
+    moe_low = (out_here.astype(F32) + out_far.astype(F32)).astype(BF)
     moe_rows = in_order(moe_low, swap(moe_low)).astype(F32)
     block_output = (residual + moe_rows).astype(BF)[None]
     router_sum = rest_full[output_columns : output_columns + E].T.astype(F32)
@@ -1433,10 +1466,6 @@
     output_new = matrix_adamw(0.25, output_weight, output_first, output_second, rest_full)
     router_new = adamw(router_weight, router_first, router_second, router_sum, 0.015, 0.1)
 
-    expert_sums[1], block_output, joint_new, output_new = barrier(
-        (expert_sums[1], block_output, joint_new, output_new)
-    )
-    expert_step(1, squares[0])
     back = lambda x: jnp.transpose(x, (0, 2, 1, 3))
     return (
         block_output,

time: 775 us -> 748 us (0.965)
  waiting for transfers between devices: 98.1 us -> 76.8 us
  Pallas kernels: 502 us -> 513 us
  other arithmetic: 32.9 us -> 23.8 us
    pallas_call x1, Pallas kernels: 149 us -> 180 us  [experts(): pl.pallas_call(functools.partial(expert_kernel, count, pieces), grid=(8,)...]
    ppermute x11 -> x9, waiting for transfers between devices: 78.9 us -> 51.4 us  [beyond(): return lax.ppermute(x, 'ctx', [(i, i ^ m) for i in range(n_ctx)])]
    pallas_call x1, Pallas kernels: 51.9 us -> 32.8 us  [residual_back(): pl.pallas_call(residual_back_kernel, in_specs=[vmem] * 7, out_specs=[vmem...]
    ppermute x11 -> x9, starting transfers between devices: 36.1 us -> 32.2 us  [beyond(): return lax.ppermute(x, 'ctx', [(i, i ^ m) for i in range(n_ctx)])]
  transfers between devices with their start and end apart: 32 -> 26, of which waited for: 10 -> 3; matrix products, arithmetic and copies ran while one was open for 7% -> 6% of each run, Pallas kernels for 43% -> 45%
where the time goes in v4:
time: 748 us; the launch traced here: 740 us
  Pallas kernels  513 us (69%)
  waiting for transfers between devices  76.8 us (10%)
  starting transfers between devices  46.5 us (6%)
  matrix products  43.1 us (6%)
  other arithmetic  23.8 us (3%)
  local copies, waits for them, and re-layouts  21.3 us (3%)
  between operations  14.9 us (2%)
    pallas_call x1, Pallas kernels, experts(): pl.pallas_call(functools.partial(expert_kernel, count, pieces), grid=(8,)...  180 us
    pallas_call x3, Pallas kernels, expert_adamw(): pl.pallas_call(functools.partial(expert_adamw_kernel, rate, joined is not...  70.8 us
    pallas_call x1, Pallas kernels, first_gather(): pl.pallas_call(functools.partial(first_gather_kernel, weights), in_specs=...  64.9 us
    ppermute x9, waiting for transfers between devices, beyond(): return lax.ppermute(x, 'ctx', [(i, i ^ m) for i in range(n_ctx)])  51.4 us
    pallas_call x1, Pallas kernels, joint_back(): pl.pallas_call(joint_back_kernel, in_specs=[vmem] * 9, out_specs=[vmem] *...  46 us
    pallas_call x1, Pallas kernels, attend(): pl.pallas_call(functools.partial(attend_kernel, weights), grid=(rows // S...  45.3 us
    pallas_call x1, Pallas kernels, attend_back(): pl.pallas_call(attend_back_kernel, grid=(rows // SPAN,), in_specs=[whole(...  37.5 us
    dot_general x12, matrix products, expert_terms(): lax.dot_general(left[k], right, TN, preferred_element_type=F32).astype(BF)  35.8 us
  transfers between devices with their start and end apart: 26, of which 3 were waited for; matrix products, arithmetic and copies ran while one was open for 6% of the time, Pallas kernels for 45%

profile of v4, /device:TPU:0, one launch (start us, length us, event | category | flops | bytes accessed | tf_op | source)
XLA Modules:
  0.0 739.7 jit_solution(10615360511582648295)
XLA Ops:
  7.2 4.6 fusion.16
  11.8 2.9 reshape.244
  14.9 1.4 copy-done.2
  17.0 0.9 pad_maximum_fusion.4.pack_ref
  17.9 64.9 %shard_map.362 = (bf16[2048,1536]{1,0:T(8,128)(2,1)}, bf16[1536,448]{1,0:T(8,128)(2,1)}) custom-call(bf16[512,1536]{1,0:T(8,128)(2,1)} %bitcast.94, bf16[384,448]{1,0:T(8,128)(2,1)} %pad_maximum_fusion.4.pack_ref), custom_call_target="tpu_custom_call" | custom-call | flops 1000000000 | bytes 1000000 | tf_op jit(solution)/shard_map/pallas_call | solution.py:123
  83.7 1.0 fusion.42
  84.6 1.6 collective-permute-start
  86.2 1.5 collective-permute-start.1
  89.2 1.6 multiply_add_fusion
  90.9 1.3 copy.52.refs_0_.idc_ref
  93.1 9.9 %shard_map.363 = (bf16[2048,1536]{1,0:T(8,128)(2,1)}, bf16[3,2048,64]{2,1,0:T(8,128)(2,1)}, bf16[2048,64]{1,0:T(8,128)(2,1)}, bf16[2048,64]{1,0:T(8,128)(2,1)}) custom-call(bf16[2048,1536]{1,0:T(8,128)(2,1)} %get-tuple-element.133.x_ref, f32[1,1536]{1,0:T(1,128)} %reshape.250.gain_ref, bf16[1536,448]{1,0:T(8,128)(2,1)} %get-tuple-element.134.w_ref, ...), custom_call_target="tpu_custom_call" | custom-call | flops 1000000000 | bytes 1000000 | tf_op jit(solution)/shard_map/pallas_call | solution.py:169
  103.0 45.3 %shard_map.364 = (bf16[2048,192]{1,0:T(8,128)(2,1)}, f32[3,1,2048]{2,1,0:T(1,128)}, bf16[8,256,192]{2,1,0:T(8,128)(2,1)}, bf16[1536,768]{1,0:T(8,128)(2,1)}) custom-call(s32[2048,1]{1,0:T(8,128)} %copy.52.refs_0_.idc_ref, s32[1,2048]{1,0:T(1,128)} %idr_ref.1, bf16[3,2048,64]{2,1,0:T(8,128)(2,1)} %get-tuple-element.137.refs_2_.q_ref, ...), custom_call_target="tpu_custom_call" | custom-call | flops 1000000000 | bytes 1000000 | tf_op jit(solution)/shard_map/pallas_call | solution.py:362
  148.9 11.9 %shard_map.365 = (f32[512,1536]{1,0:T(8,128)}, bf16[512,1536]{1,0:T(8,128)(2,1)}, bf16[512,768]{1,0:T(8,128)(2,1)}) custom-call(bf16[8,256,192]{2,1,0:T(8,128)(2,1)} %get-tuple-element.140.att_ref, bf16[1536,768]{1,0:T(8,128)(2,1)} %get-tuple-element.141.w_ref, bf16[512,1536]{1,0:T(8,128)(2,1)} %bitcast.95, f32[1,1536]{1,0:T(1,128)} %reshape.251.gain_ref), custom_call_target="tpu_custom_call" | custom-call | flops 1000000000 | bytes 1000000 | tf_op jit(solution)/shard_map/pallas_call | solution.py:519
  160.8 1.3 pad_maximum_fusion.2.cot_ref.c_ref
  162.2 1.8 slice_select_fusion.r_ref
  164.0 180.4 %shard_map.366 = (bf16[2048,2048]{1,0:T(8,128)(2,1)}, bf16[2048,1024]{1,0:T(8,128)(2,1)}, bf16[2048,384]{1,0:T(8,128)(2,1)}, bf16[2048,384]{1,0:T(8,128)(2,1)}, ...) custom-call(bf16[512,1536]{1,0:T(8,128)(2,1)} %get-tuple-element.144, ...), custom_call_target="tpu_custom_call" | custom-call | flops 1000000000 | bytes 1000000 | tf_op jit(solution)/shard_map/pallas_call | solution.py:1071
  344.4 5.5 fusion.39
  349.9 2.7 fusion.27
  352.6 2.7 fusion.36
  355.3 2.7 fusion.24
  358.0 2.7 fusion.33
  360.7 2.7 fusion.21
  363.4 1.8 fusion.30
  366.1 2.7 convolution_convert_fusion.3
  368.8 2.7 convolution_convert_fusion.4
  371.5 2.9 convolution_convert_fusion.5
  374.4 1.5 collective-permute-start.4
  375.9 1.4 collective-permute-start.3
  377.9 1.8 convolution_convert_fusion.6
  379.7 32.8 %shard_map.367 = (f32[512,1536]{1,0:T(8,128)}, bf16[512,1536]{1,0:T(8,128)(2,1)}, bf16[512,128]{1,0:T(8,128)(2,1)}, f32[1,1536]{1,0:T(1,128)}, bf16[8,256,192]{2,1,0:T(8,128)(2,1)}) custom-call(bf16[512,1664]{1,0:T(8,128)(2,1)} %get-tuple-element.155.g_ref, f32[512,1536]{1,0:T(8,128)} %get-tuple-element.143.res_ref, ...), custom_call_target="tpu_custom_call" | custom-call | flops 1000000000 | bytes 1000000 | tf_op jit(solution)/shard_map/pallas_call | solution.py:629
  412.5 4.9 fusion.18
  417.4 1.5 add_convert_fusion.5
  419.0 1.5 collective-permute-start.7
  420.6 1.4 collective-permute-start.6
  423.1 1.4 convolution_convert_fusion
  424.8 37.5 %shard_map.368 = (f32[3,2048,64]{2,1,0:T(8,128)}, f32[2048,64]{1,0:T(8,128)}, f32[2048,64]{1,0:T(8,128)}) custom-call(s32[2048,1]{1,0:T(8,128)} %copy.52.refs_0_.idc_ref, s32[1,2048]{1,0:T(1,128)} %idr_ref.1, bf16[3,2048,64]{2,1,0:T(8,128)(2,1)} %get-tuple-element.137.refs_2_.q_ref, bf16[2048,64]{1,0:T(8,128)(2,1)} %get-tuple-element.138.refs_3_.k_ref, ...), custom_call_target="tpu_custom_call" | custom-call | flops 1000000000 | bytes 1000000 | tf_op jit(solution)/shard_map/pallas_call | solution.py:458
  462.3 3.1 add_convert_fusion.4
  465.5 1.3 collective-permute-start.10
  466.8 1.6 collective-permute-start.9
  469.1 46.0 %shard_map.369 = (bf16[4,512,320]{2,1,0:T(8,128)(2,1)}, f32[512,1536]{1,0:T(8,128)}, f32[1,1536]{1,0:T(1,128)}) custom-call(f32[3,2048,64]{2,1,0:T(8,128)} %get-tuple-element.169.dq_ref, f32[2048,64]{1,0:T(8,128)} %get-tuple-element.170.dk_ref, f32[2048,64]{1,0:T(8,128)} %get-tuple-element.171.dv_ref, f32[2048,128]{1,0:T(8,128)} %bitcast.93, ...), custom_call_target="tpu_custom_call" | custom-call | flops 1000000000 | bytes 1000000 | tf_op jit(solution)/shard_map/pallas_call | solution.py:756
  515.1 3.1 add_convert_fusion.3
  518.4 5.5 convolution_convert_fusion.1
  524.4 1.6 constant_dynamic-slice_fusion
  526.0 1.5 collective-permute-start.11
  527.5 1.5 collective-permute-start.12
  529.5 22.0 %shard_map.370 = (f32[384,3,16,256]{3,2,1,0:T(8,128)}, f32[384,3,16,256]{3,2,1,0:T(8,128)}, bf16[384,3,16,256]{3,2,1,0:T(8,128)(2,1)}, f32[384,16,256]{2,1,0:T(8,128)}) custom-call(f32[384,3,16,256]{3,2,1,0:T(8,128)} %bitcast.78, f32[384,3,16,256]{3,2,1,0:T(8,128)} %bitcast.81, f32[384,3,16,256]{3,2,1,0:T(8,128)} %bitcast.84, bf16[4,384,1024]{2,1,0:T(8,128)(2,1)} %bitcast.101), custom_call_target="tpu_custom_call" | custom-call | flops 31457280 | bytes 70778880 | tf_op jit(solution)/shard_map/pallas_call | solution.py:1149
  551.5 18.0 %collective-permute-done.12 = bf16[1168,384]{1,0:T(8,128)(2,1)S(1)} collective-permute-done((bf16[1168,384]{1,0:T(8,128)(2,1)}, bf16[1168,384]{1,0:T(8,128)(2,1)S(1)}, u32[]{:S(2)}, u32[]{:S(2)}) %collective-permute-start.12) | collective-permute-done | bytes 897056 | tf_op jit(solution)/shard_map/ppermute | solution.py:1244
  569.5 0.9 copy-done.8
  570.4 2.0 add_convert_fusion.1
  572.6 11.9 %collective-permute-start.14 = (bf16[208,384]{1,0:T(8,128)(2,1)S(1)}, bf16[208,384]{1,0:T(8,128)(2,1)S(1)}, u32[]{:S(2)}, u32[]{:S(2)}) collective-permute-start(bf16[208,384]{1,0:T(8,128)(2,1)S(1)} %get-tuple-element.257), channel_id=1, source_target_pairs={{0,2},{2,0},{4,6},{6,4},{1,3},{3,1},{5,7},{7,5},{8,10},{10,8},{12,... | collective-permute-start | bytes 479240 | tf_op jit(solution)/shard_map/ppermute | solution.py:1238
  584.5 3.7 collective-permute-start.15
  588.3 22.1 %shard_map.371 = (f32[384,3,16,256]{3,2,1,0:T(8,128)}, f32[384,3,16,256]{3,2,1,0:T(8,128)}, bf16[384,3,16,256]{3,2,1,0:T(8,128)(2,1)}, f32[384,16,256]{2,1,0:T(8,128)}) custom-call(f32[384,3,16,256]{3,2,1,0:T(8,128)} %bitcast.79, f32[384,3,16,256]{3,2,1,0:T(8,128)} %bitcast.82, ...), custom_call_target="tpu_custom_call", output_to_operand_aliasing={{0}: (4, {}), {1}: (5, {}), {2}: (6, {})} | custom-call | flops 31457280 | bytes 70778880 | tf_op jit(solution)/shard_map/pallas_call | solution.py:1149
  610.5 12.3 %collective-permute-start.18 = (bf16[528,384]{1,0:T(8,128)(2,1)S(1)}, bf16[528,384]{1,0:T(8,128)(2,1)S(1)}, u32[]{:S(2)}, u32[]{:S(2)}) collective-permute-start(bf16[528,384]{1,0:T(8,128)(2,1)S(1)} %pad_maximum_fusion.3), channel_id=1, source_target_pairs={{0,4},{2,6},{4,0},{6,2},{1,5},{3,7},{5,1},{7,3},{8,12},{10,14},{12... | collective-permute-start | bytes 1216520 | tf_op jit(solution)/shard_map/ppermute | solution.py:1238
  622.9 1.1 collective-permute-start.17
  624.0 51.4 %collective-permute-done.18 = bf16[528,384]{1,0:T(8,128)(2,1)S(1)} collective-permute-done((bf16[528,384]{1,0:T(8,128)(2,1)S(1)}, bf16[528,384]{1,0:T(8,128)(2,1)S(1)}, u32[]{:S(2)}, u32[]{:S(2)}) %collective-permute-start.18) | collective-permute-done | bytes 405536 | tf_op jit(solution)/shard_map/ppermute | solution.py:1238
  675.4 7.2 all-gather.14.cloned.1.call-done
  682.7 26.7 %shard_map.372 = (f32[384,3,16,256]{3,2,1,0:T(8,128)}, f32[384,3,16,256]{3,2,1,0:T(8,128)}, bf16[384,3,16,256]{3,2,1,0:T(8,128)(2,1)}, f32[384,16,2,256]{3,2,1,0:T(2,128)}) custom-call(f32[384,3,16,256]{3,2,1,0:T(8,128)} %bitcast.80, f32[384,3,16,256]{3,2,1,0:T(8,128)} %bitcast.83, ...), custom_call_target="tpu_custom_call", output_to_operand_aliasing={{0}: (5, {}), {1}: (6, {}), {2}: (7, {})} | custom-call | flops 31457280 | bytes 70778880 | tf_op jit(solution)/shard_map/pallas_call | solution.py:1149
  710.1 1.0 slice.105
  711.2 0.9 slice.102
  712.1 5.4 shard_map.374
  717.5 8.3 %shard_map.373 = (f32[384,1280]{1,0:T(8,128)}, f32[384,1280]{1,0:T(8,128)}, f32[384,1280]{1,0:T(8,128)}, bf16[384,1280]{1,0:T(8,128)(2,1)}) custom-call(f32[384,1280]{1,0:T(8,128)} %p_ref.2, f32[384,1280]{1,0:T(8,128)} %f_ref.2, f32[384,1280]{1,0:T(8,128)} %s_ref.2, bf16[1280,384]{1,0:T(8,128)(2,1)} %bitcast.99), custom_call_target="tpu_custom_call" | custom-call | flops 9830400 | bytes 13762560 | tf_op jit(solution)/shard_map/pallas_call | solution.py:1188
  727.2 1.4 fusion.55
  728.6 1.8 fusion.17
  731.0 1.7 copy.67
  (156 shorter events, 12.5 us)
Async XLA Ops:
  7.2 156.8 %all-gather.8.cloned.1.call-start = ((), (), s32[]{:S(2)}) async-start(), calls=%async_computation | async-start | bytes 11796480 | tf_op jit(solution)/shard_map/all_gather | solution.py:1286
  14.8 1.5 copy-start.2
  14.8 1.6 copy-start.12
  14.8 1.8 copy-start.18
  14.8 514.7 %all-gather.10.cloned.1.call-start = ((), (), s32[]{:S(2)}) async-start(), calls=%async_computation.1 | async-start | bytes 3932160 | tf_op jit(solution)/shard_map/all_gather | solution.py:1368
  16.4 66.4 %copy-start.4 = (bf16[384,1280]{1,0:T(8,128)(2,1)}, bf16[384,1280]{1,0:T(8,128)(2,1)S(1)}, u32[]{:S(2)}) copy-start(bf16[384,1280]{1,0:T(8,128)(2,1)S(1)} %convert_element_type.269.shard_ref) | copy-start | bytes 2949124
  17.9 64.9 %copy-start.17 = (s32[1,512,8]{1,2,0:T(8,128)S(1)}, s32[1,512,8]{1,2,0:T(8,128)}, u32[]{:S(2)}) copy-start(s32[1,512,8]{1,2,0:T(8,128)} %param.22) | copy-start | bytes 49156
  17.9 65.7 %copy-start.3 = (bf16[1,512,1536]{2,1,0:T(8,128)(2,1)S(1)}, bf16[1,512,1536]{2,1,0:T(8,128)(2,1)}, u32[]{:S(2)}) copy-start(bf16[1,512,1536]{2,1,0:T(8,128)(2,1)} %param.20) | copy-start | bytes 4718596
  82.8 4.9 copy-start.5
  84.6 6.2 copy-start.14
  84.6 79.3 %collective-permute-start = (bf16[256,1664]{1,0:T(8,128)(2,1)}, bf16[256,1664]{1,0:T(8,128)(2,1)}, u32[]{:S(2)}, u32[]{:S(2)}) collective-permute-start(bf16[256,1664]{1,0:T(8,128)(2,1)} %fusion.42), channel_id=1, source_target_pairs={{0,2},{2,0},{4,6},{6,4},{1,3},{3,1},{5,7},{7,5},{8,10},{10,8},{12,... | collective-permute-start | bytes 2555912 | tf_op jit(solution)/shard_map/ppermute | solution.py:1238
  86.2 77.7 %collective-permute-start.1 = (bf16[256,1664]{1,0:T(8,128)(2,1)}, bf16[256,1664]{1,0:T(8,128)(2,1)}, u32[]{:S(2)}, u32[]{:S(2)}) collective-permute-start(bf16[256,1664]{1,0:T(8,128)(2,1)} %fusion.42), channel_id=1, source_target_pairs={{0,4},{2,6},{4,0},{6,2},{1,5},{3,7},{5,1},{7,3},{8,12},{10,14},{12... | collective-permute-start | bytes 2555912 | tf_op jit(solution)/shard_map/ppermute | solution.py:1238
  88.3 4.0 copy-start.6
  344.4 5.5 copy-start.25
  344.4 5.5 copy-start.35
  349.9 2.7 copy-start.34
  355.3 2.7 copy-start.33
  360.7 2.7 copy-start.28
  363.4 2.2 copy-start.26
  363.4 2.7 copy-start.32
  366.1 2.7 copy-start.31
  368.8 2.7 copy-start.30
  371.5 6.4 copy-start.29
  374.4 43.0 %collective-permute-start.4 = (bf16[384,1024]{1,0:T(8,128)(2,1)}, bf16[384,1024]{1,0:T(8,128)(2,1)S(1)}, u32[]{:S(2)}, u32[]{:S(2)}) collective-permute-start(bf16[384,1024]{1,0:T(8,128)(2,1)} %convolution_convert_fusion.3), channel_id=1, source_target_pairs={{0,24},{8,16},{16,8},{24,0},{1,25},{9,17},{17,9},{25,1},{2,26},{10... | collective-permute-start | bytes 2359304 | tf_op jit(solution)/shard_map/ppermute | solution.py:1244
  375.9 41.6 %collective-permute-start.3 = (bf16[384,1024]{1,0:T(8,128)(2,1)}, bf16[384,1024]{1,0:T(8,128)(2,1)S(1)}, u32[]{:S(2)}, u32[]{:S(2)}) collective-permute-start(bf16[384,1024]{1,0:T(8,128)(2,1)} %convolution_convert_fusion.4), channel_id=1, source_target_pairs={{0,16},{8,24},{16,0},{24,8},{1,17},{9,25},{17,1},{25,9},{2,18},{10... | collective-permute-start | bytes 2359304 | tf_op jit(solution)/shard_map/ppermute | solution.py:1244
  377.3 40.1 %collective-permute-start.2 = (bf16[384,1024]{1,0:T(8,128)(2,1)}, bf16[384,1024]{1,0:T(8,128)(2,1)S(1)}, u32[]{:S(2)}, u32[]{:S(2)}) collective-permute-start(bf16[384,1024]{1,0:T(8,128)(2,1)} %convolution_convert_fusion.5), channel_id=1, source_target_pairs={{0,8},{8,0},{16,24},{24,16},{1,9},{9,1},{17,25},{25,17},{2,10},{10... | collective-permute-start | bytes 2359304 | tf_op jit(solution)/shard_map/ppermute | solution.py:1244
  417.4 5.2 copy-start
  417.4 5.2 copy-start.11
  417.4 5.2 copy-start.24
  419.0 4.1 copy-start.20
  419.0 4.1 copy-start.37
  419.0 169.3 %all-gather.12.cloned.1.call-start = ((), (), s32[]{:S(2)}) async-start(), calls=%async_computation.2 | async-start | bytes 3932160 | tf_op jit(solution)/shard_map/all_gather | solution.py:1368
  419.0 4.0 copy-start.27
  419.0 43.2 %collective-permute-start.7 = (bf16[384,1024]{1,0:T(8,128)(2,1)}, bf16[384,1024]{1,0:T(8,128)(2,1)}, u32[]{:S(2)}, u32[]{:S(2)}) collective-permute-start(bf16[384,1024]{1,0:T(8,128)(2,1)} %fusion.27), channel_id=1, source_target_pairs={{0,24},{8,16},{16,8},{24,0},{1,25},{9,17},{17,9},{25,1},{2,26},{10... | collective-permute-start | bytes 2359304 | tf_op jit(solution)/shard_map/ppermute | solution.py:1244
  420.6 41.7 %collective-permute-start.6 = (bf16[384,1024]{1,0:T(8,128)(2,1)}, bf16[384,1024]{1,0:T(8,128)(2,1)}, u32[]{:S(2)}, u32[]{:S(2)}) collective-permute-start(bf16[384,1024]{1,0:T(8,128)(2,1)} %fusion.24), channel_id=1, source_target_pairs={{0,16},{8,24},{16,0},{24,8},{1,17},{9,25},{17,1},{25,9},{2,18},{10... | collective-permute-start | bytes 2359304 | tf_op jit(solution)/shard_map/ppermute | solution.py:1244
  422.0 40.3 %collective-permute-start.5 = (bf16[384,1024]{1,0:T(8,128)(2,1)}, bf16[384,1024]{1,0:T(8,128)(2,1)}, u32[]{:S(2)}, u32[]{:S(2)}) collective-permute-start(bf16[384,1024]{1,0:T(8,128)(2,1)} %fusion.21), channel_id=1, source_target_pairs={{0,8},{8,0},{16,24},{24,16},{1,9},{9,1},{17,25},{25,17},{2,10},{10... | collective-permute-start | bytes 2359304 | tf_op jit(solution)/shard_map/ppermute | solution.py:1244
  424.8 37.5 %copy-start.10 = (bf16[384,1024]{1,0:T(8,128)(2,1)S(1)}, bf16[384,1024]{1,0:T(8,128)(2,1)}, u32[]{:S(2)}) copy-start(bf16[384,1024]{1,0:T(8,128)(2,1)} %fusion.18) | copy-start | bytes 2359300
  465.5 217.2 %all-gather.14.cloned.1.call-start = ((), (), s32[]{:S(2)}) async-start(), calls=%async_computation.3 | async-start | bytes 3932160 | tf_op jit(solution)/shard_map/all_gather | solution.py:1368
  465.5 49.5 %collective-permute-start.10 = (bf16[384,1024]{1,0:T(8,128)(2,1)}, bf16[384,1024]{1,0:T(8,128)(2,1)}, u32[]{:S(2)}, u32[]{:S(2)}) collective-permute-start(bf16[384,1024]{1,0:T(8,128)(2,1)} %fusion.39), channel_id=1, source_target_pairs={{0,24},{8,16},{16,8},{24,0},{1,25},{9,17},{17,9},{25,1},{2,26},{10... | collective-permute-start | bytes 2359304 | tf_op jit(solution)/shard_map/ppermute | solution.py:1244
  466.8 48.2 %collective-permute-start.9 = (bf16[384,1024]{1,0:T(8,128)(2,1)}, bf16[384,1024]{1,0:T(8,128)(2,1)}, u32[]{:S(2)}, u32[]{:S(2)}) collective-permute-start(bf16[384,1024]{1,0:T(8,128)(2,1)} %fusion.36), channel_id=1, source_target_pairs={{0,16},{8,24},{16,0},{24,8},{1,17},{9,25},{17,1},{25,9},{2,18},{10... | collective-permute-start | bytes 2359304 | tf_op jit(solution)/shard_map/ppermute | solution.py:1244
  468.5 46.6 %collective-permute-start.8 = (bf16[384,1024]{1,0:T(8,128)(2,1)}, bf16[384,1024]{1,0:T(8,128)(2,1)}, u32[]{:S(2)}, u32[]{:S(2)}) collective-permute-start(bf16[384,1024]{1,0:T(8,128)(2,1)} %fusion.33), channel_id=1, source_target_pairs={{0,8},{8,0},{16,24},{24,16},{1,9},{9,1},{17,25},{25,17},{2,10},{10... | collective-permute-start | bytes 2359304 | tf_op jit(solution)/shard_map/ppermute | solution.py:1244
  515.1 3.1 copy-start.21
  526.0 25.5 %collective-permute-start.11 = (bf16[1168,384]{1,0:T(8,128)(2,1)}, bf16[1168,384]{1,0:T(8,128)(2,1)S(1)}, u32[]{:S(2)}, u32[]{:S(2)}) collective-permute-start(bf16[1168,384]{1,0:T(8,128)(2,1)} %get-tuple-element.251), channel_id=1, source_target_pairs={{0,8},{8,0},{16,24},{24,16},{1,9},{9,1},{17,25},{25,17},{2,10},{10... | collective-permute-start | bytes 2691080 | tf_op jit(solution)/shard_map/ppermute | solution.py:1244
  527.5 42.0 %collective-permute-start.12 = (bf16[1168,384]{1,0:T(8,128)(2,1)}, bf16[1168,384]{1,0:T(8,128)(2,1)S(1)}, u32[]{:S(2)}, u32[]{:S(2)}) collective-permute-start(bf16[1168,384]{1,0:T(8,128)(2,1)} %get-tuple-element.250), channel_id=1, source_target_pairs={{0,16},{8,24},{16,0},{24,8},{1,17},{9,25},{17,1},{25,9},{2,18},{10... | collective-permute-start | bytes 2691080 | tf_op jit(solution)/shard_map/ppermute | solution.py:1244
  528.9 40.6 %collective-permute-start.13 = (bf16[1168,384]{1,0:T(8,128)(2,1)}, bf16[1168,384]{1,0:T(8,128)(2,1)}, u32[]{:S(2)}, u32[]{:S(2)}) collective-permute-start(bf16[1168,384]{1,0:T(8,128)(2,1)} %get-tuple-element.249), channel_id=1, source_target_pairs={{0,24},{8,16},{16,8},{24,0},{1,25},{9,17},{17,9},{25,1},{2,26},{10... | collective-permute-start | bytes 2691080 | tf_op jit(solution)/shard_map/ppermute | solution.py:1244
  569.5 0.9 copy-start.8
  572.6 37.7 %collective-permute-start.14 = (bf16[208,384]{1,0:T(8,128)(2,1)S(1)}, bf16[208,384]{1,0:T(8,128)(2,1)S(1)}, u32[]{:S(2)}, u32[]{:S(2)}) collective-permute-start(bf16[208,384]{1,0:T(8,128)(2,1)S(1)} %get-tuple-element.257), channel_id=1, source_target_pairs={{0,2},{2,0},{4,6},{6,4},{1,3},{3,1},{5,7},{7,5},{8,10},{10,8},{12,... | collective-permute-start | bytes 479240 | tf_op jit(solution)/shard_map/ppermute | solution.py:1238
  584.5 25.8 %collective-permute-start.15 = (bf16[208,384]{1,0:T(8,128)(2,1)S(1)}, bf16[208,384]{1,0:T(8,128)(2,1)S(1)}, u32[]{:S(2)}, u32[]{:S(2)}) collective-permute-start(bf16[208,384]{1,0:T(8,128)(2,1)S(1)} %get-tuple-element.256), channel_id=1, source_target_pairs={{0,4},{2,6},{4,0},{6,2},{1,5},{3,7},{5,1},{7,3},{8,12},{10,14},{12... | collective-permute-start | bytes 479240 | tf_op jit(solution)/shard_map/ppermute | solution.py:1238
  588.2 22.1 %collective-permute-start.16 = (bf16[208,384]{1,0:T(8,128)(2,1)S(1)}, bf16[208,384]{1,0:T(8,128)(2,1)S(1)}, u32[]{:S(2)}, u32[]{:S(2)}) collective-permute-start(bf16[208,384]{1,0:T(8,128)(2,1)S(1)} %get-tuple-element.255), channel_id=1, source_target_pairs={{0,6},{2,4},{4,2},{6,0},{1,7},{3,5},{5,3},{7,1},{8,14},{10,12},{12... | collective-permute-start | bytes 479240 | tf_op jit(solution)/shard_map/ppermute | solution.py:1238
  588.3 34.5 %copy-start.36 = (bf16[256,1536]{1,0:T(8,128)(2,1)S(1)}, bf16[256,1536]{1,0:T(8,128)(2,1)}, u32[]{:S(2)}) copy-start(bf16[256,1536]{1,0:T(8,128)(2,1)} %get-tuple-element.208) | copy-start | bytes 2359300
  610.5 64.9 %collective-permute-start.18 = (bf16[528,384]{1,0:T(8,128)(2,1)S(1)}, bf16[528,384]{1,0:T(8,128)(2,1)S(1)}, u32[]{:S(2)}, u32[]{:S(2)}) collective-permute-start(bf16[528,384]{1,0:T(8,128)(2,1)S(1)} %pad_maximum_fusion.3), channel_id=1, source_target_pairs={{0,4},{2,6},{4,0},{6,2},{1,5},{3,7},{5,1},{7,3},{8,12},{10,14},{12... | collective-permute-start | bytes 1216520 | tf_op jit(solution)/shard_map/ppermute | solution.py:1238
  622.8 86.6 %collective-permute-start.20 = (bf16[256,1536]{1,0:T(8,128)(2,1)S(1)}, bf16[256,1536]{1,0:T(8,128)(2,1)S(1)}, u32[]{:S(2)}, u32[]{:S(2)}) collective-permute-start(bf16[256,1536]{1,0:T(8,128)(2,1)S(1)} %copy-done.36), channel_id=1, source_target_pairs={{0,4},{2,6},{4,0},{6,2},{1,5},{3,7},{5,1},{7,3},{8,12},{10,14},{12... | collective-permute-start | bytes 2359304 | tf_op jit(solution)/shard_map/ppermute | solution.py:1238
  622.9 86.5 %collective-permute-start.17 = (bf16[528,384]{1,0:T(8,128)(2,1)S(1)}, bf16[528,384]{1,0:T(8,128)(2,1)S(1)}, u32[]{:S(2)}, u32[]{:S(2)}) collective-permute-start(bf16[528,384]{1,0:T(8,128)(2,1)S(1)} %pad_maximum_fusion.3), channel_id=1, source_target_pairs={{0,2},{2,0},{4,6},{6,4},{1,3},{3,1},{5,7},{7,5},{8,10},{10,8},{12,... | collective-permute-start | bytes 1216520 | tf_op jit(solution)/shard_map/ppermute | solution.py:1238
  675.4 34.0 %collective-permute-start.19 = (bf16[528,384]{1,0:T(8,128)(2,1)S(1)}, bf16[528,384]{1,0:T(8,128)(2,1)S(1)}, u32[]{:S(2)}, u32[]{:S(2)}) collective-permute-start(bf16[528,384]{1,0:T(8,128)(2,1)S(1)} %collective-permute-done.18), channel_id=1, source_target_pairs={{0,2},{2,0},{4,6},{6,4},{1,3},{3,1},{5,7},{7,5},{8,10},{10,8},{12,... | collective-permute-start | bytes 1216520 | tf_op jit(solution)/shard_map/ppermute | solution.py:1238
  682.6 26.7 %copy-start.9 = (bf16[256,1536]{1,0:T(8,128)(2,1)S(1)}, bf16[256,1536]{1,0:T(8,128)(2,1)}, u32[]{:S(2)}) copy-start(bf16[256,1536]{1,0:T(8,128)(2,1)} %get-tuple-element.146) | copy-start | bytes 2359300
  709.6 19.0 %collective-permute-start.21 = (bf16[256,1536]{1,0:T(8,128)(2,1)S(1)}, bf16[256,1536]{1,0:T(8,128)(2,1)S(1)}, u32[]{:S(2)}, u32[]{:S(2)}) collective-permute-start(bf16[256,1536]{1,0:T(8,128)(2,1)S(1)} %add_convert_fusion.2), channel_id=1, source_target_pairs={{0,1},{1,0},{2,3},{3,2},{4,5},{5,4},{6,7},{7,6},{8,9},{9,8},{10,11... | collective-permute-start | bytes 2359304 | tf_op jit(solution)/shard_map/ppermute | solution.py:1241
  717.5 9.1 %copy-start.19 = (f32[2,384]{1,0:T(2,128)S(1)}, f32[2,384]{1,0:T(2,128)}, u32[]{:S(2)}) copy-start(f32[2,384]{1,0:T(2,128)} %param.23) | copy-start | bytes 9220
  717.5 9.1 %copy-start.22 = (f32[2,384]{1,0:T(2,128)S(1)}, f32[2,384]{1,0:T(2,128)}, u32[]{:S(2)}) copy-start(f32[2,384]{1,0:T(2,128)} %param.24) | copy-start | bytes 9220
  717.5 9.1 %copy-start.23 = (f32[2,384]{1,0:T(2,128)S(1)}, f32[2,384]{1,0:T(2,128)}, u32[]{:S(2)}) copy-start(f32[2,384]{1,0:T(2,128)} %param.25) | copy-start | bytes 9220
  717.5 9.7 %copy-start.13 = (f32[384,16]{0,1:T(8,128)S(1)}, f32[384,16]{0,1:T(8,128)}, u32[]{:S(2)}) copy-start(f32[384,16]{0,1:T(8,128)} %param.32) | copy-start | bytes 73732
  717.5 9.7 %copy-start.15 = (f32[384,16]{0,1:T(8,128)S(1)}, f32[384,16]{0,1:T(8,128)}, u32[]{:S(2)}) copy-start(f32[384,16]{0,1:T(8,128)} %param.33) | copy-start | bytes 73732
  717.5 9.7 %copy-start.16 = (f32[384,16]{0,1:T(8,128)S(1)}, f32[384,16]{0,1:T(8,128)}, u32[]{:S(2)}) copy-start(f32[384,16]{0,1:T(8,128)} %param.34) | copy-start | bytes 73732
  717.5 11.0 %copy-start.1 = (f32[512,1536]{1,0:T(8,128)S(1)}, f32[512,1536]{1,0:T(8,128)}, u32[]{:S(2)}) copy-start(f32[512,1536]{1,0:T(8,128)} %get-tuple-element.143.res_ref) | copy-start | bytes 9437188
  728.6 2.5 copy-start.7
Sparse Core Ops, SparseCore 0:
  14.9 114.6 all-gather.7
  419.1 82.6 all-gather.9
  503.9 63.1 all-gather.11
  569.2 113.4 all-gather.13

commit v5 on v4

--- a/solution.py
+++ b/solution.py
@@ -1138,7 +1138,7 @@
 def expert_adamw(slot, rate, weight, first, second, gradient, earlier, joined=None):
     rows, _, count, units = weight.shape
     parts = gradient.shape[0]
-    tile = next(t for t in (32, 16, 8) if rows % t == 0)
+    tile = next(t for t in (64, 16, 8) if rows % t == 0)
     here = pl.BlockSpec((tile, 1, count, units), lambda i: (i, slot, 0, 0))
     plain = pl.BlockSpec((tile, count, units), lambda i: (i, 0, 0))
     pair = pl.BlockSpec((tile, count, 2, units), lambda i: (i, 0, 0, 0))

time: 748 us -> 746 us (level)
  transfers between devices with their start and end apart: 26 -> 26, of which waited for: 3 -> 4; matrix products, arithmetic and copies ran while one was open for 6% -> 6% of each run, Pallas kernels for 45% -> 44%
where the time goes in v5:
time: 746 us; the launch traced here: 738 us
  Pallas kernels  508 us (68%)
  waiting for transfers between devices  79.3 us (11%)
  starting transfers between devices  47.3 us (6%)
  matrix products  43.1 us (6%)
  other arithmetic  23.8 us (3%)
  local copies, waits for them, and re-layouts  21.3 us (3%)
  between operations  14.9 us (2%)
    pallas_call x1, Pallas kernels, experts(): pl.pallas_call(functools.partial(expert_kernel, count, pieces), grid=(8,)...  180 us
    pallas_call x3, Pallas kernels, expert_adamw(): pl.pallas_call(functools.partial(expert_adamw_kernel, rate, joined is not...  66 us
    pallas_call x1, Pallas kernels, first_gather(): pl.pallas_call(functools.partial(first_gather_kernel, weights), in_specs=...  64.9 us
    ppermute x9, waiting for transfers between devices, beyond(): return lax.ppermute(x, 'ctx', [(i, i ^ m) for i in range(n_ctx)])  52.3 us
    pallas_call x1, Pallas kernels, joint_back(): pl.pallas_call(joint_back_kernel, in_specs=[vmem] * 9, out_specs=[vmem] *...  46 us
    pallas_call x1, Pallas kernels, attend(): pl.pallas_call(functools.partial(attend_kernel, weights), grid=(rows // S...  45.3 us
    pallas_call x1, Pallas kernels, attend_back(): pl.pallas_call(attend_back_kernel, grid=(rows // SPAN,), in_specs=[whole(...  37.5 us
    dot_general x12, matrix products, expert_terms(): lax.dot_general(left[k], right, TN, preferred_element_type=F32).astype(BF)  35.8 us
  transfers between devices with their start and end apart: 26, of which 4 were waited for; matrix products, arithmetic and copies ran while one was open for 6% of the time, Pallas kernels for 44%

profile of v5, /device:TPU:0, one launch (start us, length us, event | category | flops | bytes accessed | tf_op | source)
XLA Modules:
  0.0 738.1 jit_solution(16338135684727270344)
XLA Ops:
  7.2 4.6 fusion.16
  11.8 2.9 reshape.244
  14.9 1.4 copy-done.2
  17.0 0.9 pad_maximum_fusion.4.pack_ref
  17.9 64.9 %shard_map.362 = (bf16[2048,1536]{1,0:T(8,128)(2,1)}, bf16[1536,448]{1,0:T(8,128)(2,1)}) custom-call(bf16[512,1536]{1,0:T(8,128)(2,1)} %bitcast.94, bf16[384,448]{1,0:T(8,128)(2,1)} %pad_maximum_fusion.4.pack_ref), custom_call_target="tpu_custom_call" | custom-call | flops 1000000000 | bytes 1000000 | tf_op jit(solution)/shard_map/pallas_call | solution.py:123
  83.7 1.0 fusion.42
  84.6 1.6 collective-permute-start
  86.2 1.5 collective-permute-start.1
  89.2 1.6 multiply_add_fusion
  90.9 1.3 copy.52.refs_0_.idc_ref
  93.1 9.9 %shard_map.363 = (bf16[2048,1536]{1,0:T(8,128)(2,1)}, bf16[3,2048,64]{2,1,0:T(8,128)(2,1)}, bf16[2048,64]{1,0:T(8,128)(2,1)}, bf16[2048,64]{1,0:T(8,128)(2,1)}) custom-call(bf16[2048,1536]{1,0:T(8,128)(2,1)} %get-tuple-element.133.x_ref, f32[1,1536]{1,0:T(1,128)} %reshape.250.gain_ref, bf16[1536,448]{1,0:T(8,128)(2,1)} %get-tuple-element.134.w_ref, ...), custom_call_target="tpu_custom_call" | custom-call | flops 1000000000 | bytes 1000000 | tf_op jit(solution)/shard_map/pallas_call | solution.py:169
  103.0 45.3 %shard_map.364 = (bf16[2048,192]{1,0:T(8,128)(2,1)}, f32[3,1,2048]{2,1,0:T(1,128)}, bf16[8,256,192]{2,1,0:T(8,128)(2,1)}, bf16[1536,768]{1,0:T(8,128)(2,1)}) custom-call(s32[2048,1]{1,0:T(8,128)} %copy.52.refs_0_.idc_ref, s32[1,2048]{1,0:T(1,128)} %idr_ref.1, bf16[3,2048,64]{2,1,0:T(8,128)(2,1)} %get-tuple-element.137.refs_2_.q_ref, ...), custom_call_target="tpu_custom_call" | custom-call | flops 1000000000 | bytes 1000000 | tf_op jit(solution)/shard_map/pallas_call | solution.py:362
  148.9 11.9 %shard_map.365 = (f32[512,1536]{1,0:T(8,128)}, bf16[512,1536]{1,0:T(8,128)(2,1)}, bf16[512,768]{1,0:T(8,128)(2,1)}) custom-call(bf16[8,256,192]{2,1,0:T(8,128)(2,1)} %get-tuple-element.140.att_ref, bf16[1536,768]{1,0:T(8,128)(2,1)} %get-tuple-element.141.w_ref, bf16[512,1536]{1,0:T(8,128)(2,1)} %bitcast.95, f32[1,1536]{1,0:T(1,128)} %reshape.251.gain_ref), custom_call_target="tpu_custom_call" | custom-call | flops 1000000000 | bytes 1000000 | tf_op jit(solution)/shard_map/pallas_call | solution.py:519
  160.8 1.3 pad_maximum_fusion.2.cot_ref.c_ref
  162.2 1.8 slice_select_fusion.r_ref
  164.0 180.4 %shard_map.366 = (bf16[2048,2048]{1,0:T(8,128)(2,1)}, bf16[2048,1024]{1,0:T(8,128)(2,1)}, bf16[2048,384]{1,0:T(8,128)(2,1)}, bf16[2048,384]{1,0:T(8,128)(2,1)}, ...) custom-call(bf16[512,1536]{1,0:T(8,128)(2,1)} %get-tuple-element.144, ...), custom_call_target="tpu_custom_call" | custom-call | flops 1000000000 | bytes 1000000 | tf_op jit(solution)/shard_map/pallas_call | solution.py:1071
  344.4 5.5 fusion.39
  349.9 2.7 fusion.27
  352.6 2.7 fusion.36
  355.3 2.7 fusion.24
  358.0 2.7 fusion.33
  360.7 2.7 fusion.21
  363.4 1.8 fusion.30
  366.1 2.7 convolution_convert_fusion.3
  368.8 2.7 convolution_convert_fusion.4
  371.5 2.9 convolution_convert_fusion.5
  374.4 1.5 collective-permute-start.4
  375.9 1.4 collective-permute-start.3
  377.9 1.8 convolution_convert_fusion.6
  379.7 32.8 %shard_map.367 = (f32[512,1536]{1,0:T(8,128)}, bf16[512,1536]{1,0:T(8,128)(2,1)}, bf16[512,128]{1,0:T(8,128)(2,1)}, f32[1,1536]{1,0:T(1,128)}, bf16[8,256,192]{2,1,0:T(8,128)(2,1)}) custom-call(bf16[512,1664]{1,0:T(8,128)(2,1)} %get-tuple-element.155.g_ref, f32[512,1536]{1,0:T(8,128)} %get-tuple-element.143.res_ref, ...), custom_call_target="tpu_custom_call" | custom-call | flops 1000000000 | bytes 1000000 | tf_op jit(solution)/shard_map/pallas_call | solution.py:629
  412.5 4.9 fusion.18
  417.4 1.5 add_convert_fusion.5
  419.0 1.5 collective-permute-start.7
  420.6 1.4 collective-permute-start.6
  423.1 1.4 convolution_convert_fusion
  424.8 37.5 %shard_map.368 = (f32[3,2048,64]{2,1,0:T(8,128)}, f32[2048,64]{1,0:T(8,128)}, f32[2048,64]{1,0:T(8,128)}) custom-call(s32[2048,1]{1,0:T(8,128)} %copy.52.refs_0_.idc_ref, s32[1,2048]{1,0:T(1,128)} %idr_ref.1, bf16[3,2048,64]{2,1,0:T(8,128)(2,1)} %get-tuple-element.137.refs_2_.q_ref, bf16[2048,64]{1,0:T(8,128)(2,1)} %get-tuple-element.138.refs_3_.k_ref, ...), custom_call_target="tpu_custom_call" | custom-call | flops 1000000000 | bytes 1000000 | tf_op jit(solution)/shard_map/pallas_call | solution.py:458
  462.3 3.1 add_convert_fusion.4
  465.5 1.3 collective-permute-start.10
  466.8 1.6 collective-permute-start.9
  469.1 46.0 %shard_map.369 = (bf16[4,512,320]{2,1,0:T(8,128)(2,1)}, f32[512,1536]{1,0:T(8,128)}, f32[1,1536]{1,0:T(1,128)}) custom-call(f32[3,2048,64]{2,1,0:T(8,128)} %get-tuple-element.169.dq_ref, f32[2048,64]{1,0:T(8,128)} %get-tuple-element.170.dk_ref, f32[2048,64]{1,0:T(8,128)} %get-tuple-element.171.dv_ref, f32[2048,128]{1,0:T(8,128)} %bitcast.93, ...), custom_call_target="tpu_custom_call" | custom-call | flops 1000000000 | bytes 1000000 | tf_op jit(solution)/shard_map/pallas_call | solution.py:756
  515.1 3.1 add_convert_fusion.3
  518.4 5.5 convolution_convert_fusion.1
  524.4 1.6 constant_dynamic-slice_fusion
  526.0 1.5 collective-permute-start.11
  527.5 1.5 collective-permute-start.12
  529.5 20.4 %shard_map.370 = (f32[384,3,16,256]{3,2,1,0:T(8,128)}, f32[384,3,16,256]{3,2,1,0:T(8,128)}, bf16[384,3,16,256]{3,2,1,0:T(8,128)(2,1)}, f32[384,16,256]{2,1,0:T(8,128)}) custom-call(f32[384,3,16,256]{3,2,1,0:T(8,128)} %bitcast.78, f32[384,3,16,256]{3,2,1,0:T(8,128)} %bitcast.81, f32[384,3,16,256]{3,2,1,0:T(8,128)} %bitcast.84, bf16[4,384,1024]{2,1,0:T(8,128)(2,1)} %bitcast.101), custom_call_target="tpu_custom_call" | custom-call | flops 31457280 | bytes 70778880 | tf_op jit(solution)/shard_map/pallas_call | solution.py:1149
  549.9 19.6 %collective-permute-done.12 = bf16[1168,384]{1,0:T(8,128)(2,1)S(1)} collective-permute-done((bf16[1168,384]{1,0:T(8,128)(2,1)}, bf16[1168,384]{1,0:T(8,128)(2,1)S(1)}, u32[]{:S(2)}, u32[]{:S(2)}) %collective-permute-start.12) | collective-permute-done | bytes 897056 | tf_op jit(solution)/shard_map/ppermute | solution.py:1244
  569.5 0.9 copy-done.8
  570.4 2.0 add_convert_fusion.1
  572.6 11.9 %collective-permute-start.14 = (bf16[208,384]{1,0:T(8,128)(2,1)S(1)}, bf16[208,384]{1,0:T(8,128)(2,1)S(1)}, u32[]{:S(2)}, u32[]{:S(2)}) collective-permute-start(bf16[208,384]{1,0:T(8,128)(2,1)S(1)} %get-tuple-element.257), channel_id=1, source_target_pairs={{0,2},{2,0},{4,6},{6,4},{1,3},{3,1},{5,7},{7,5},{8,10},{10,8},{12,... | collective-permute-start | bytes 479240 | tf_op jit(solution)/shard_map/ppermute | solution.py:1238
  584.5 3.7 collective-permute-start.15
  588.3 20.4 %shard_map.371 = (f32[384,3,16,256]{3,2,1,0:T(8,128)}, f32[384,3,16,256]{3,2,1,0:T(8,128)}, bf16[384,3,16,256]{3,2,1,0:T(8,128)(2,1)}, f32[384,16,256]{2,1,0:T(8,128)}) custom-call(f32[384,3,16,256]{3,2,1,0:T(8,128)} %bitcast.79, f32[384,3,16,256]{3,2,1,0:T(8,128)} %bitcast.82, ...), custom_call_target="tpu_custom_call", output_to_operand_aliasing={{0}: (4, {}), {1}: (5, {}), {2}: (6, {})} | custom-call | flops 31457280 | bytes 70778880 | tf_op jit(solution)/shard_map/pallas_call | solution.py:1149
  609.7 13.1 %collective-permute-start.18 = (bf16[528,384]{1,0:T(8,128)(2,1)S(1)}, bf16[528,384]{1,0:T(8,128)(2,1)S(1)}, u32[]{:S(2)}, u32[]{:S(2)}) collective-permute-start(bf16[528,384]{1,0:T(8,128)(2,1)S(1)} %pad_maximum_fusion.3), channel_id=1, source_target_pairs={{0,4},{2,6},{4,0},{6,2},{1,5},{3,7},{5,1},{7,3},{8,12},{10,14},{12... | collective-permute-start | bytes 1216520 | tf_op jit(solution)/shard_map/ppermute | solution.py:1238
  622.9 1.1 collective-permute-start.17
  624.0 51.4 %collective-permute-done.18 = bf16[528,384]{1,0:T(8,128)(2,1)S(1)} collective-permute-done((bf16[528,384]{1,0:T(8,128)(2,1)S(1)}, bf16[528,384]{1,0:T(8,128)(2,1)S(1)}, u32[]{:S(2)}, u32[]{:S(2)}) %collective-permute-start.18) | collective-permute-done | bytes 405536 | tf_op jit(solution)/shard_map/ppermute | solution.py:1238
  675.4 7.2 all-gather.14.cloned.1.call-done
  682.7 25.2 %shard_map.372 = (f32[384,3,16,256]{3,2,1,0:T(8,128)}, f32[384,3,16,256]{3,2,1,0:T(8,128)}, bf16[384,3,16,256]{3,2,1,0:T(8,128)(2,1)}, f32[384,16,2,256]{3,2,1,0:T(2,128)}) custom-call(f32[384,3,16,256]{3,2,1,0:T(8,128)} %bitcast.80, f32[384,3,16,256]{3,2,1,0:T(8,128)} %bitcast.83, ...), custom_call_target="tpu_custom_call", output_to_operand_aliasing={{0}: (5, {}), {1}: (6, {}), {2}: (7, {})} | custom-call | flops 31457280 | bytes 70778880 | tf_op jit(solution)/shard_map/pallas_call | solution.py:1149
  708.6 1.0 slice.105
  709.6 0.9 slice.102
  710.5 5.4 shard_map.374
  716.0 8.3 %shard_map.373 = (f32[384,1280]{1,0:T(8,128)}, f32[384,1280]{1,0:T(8,128)}, f32[384,1280]{1,0:T(8,128)}, bf16[384,1280]{1,0:T(8,128)(2,1)}) custom-call(f32[384,1280]{1,0:T(8,128)} %p_ref.2, f32[384,1280]{1,0:T(8,128)} %f_ref.2, f32[384,1280]{1,0:T(8,128)} %s_ref.2, bf16[1280,384]{1,0:T(8,128)(2,1)} %bitcast.99), custom_call_target="tpu_custom_call" | custom-call | flops 9830400 | bytes 13762560 | tf_op jit(solution)/shard_map/pallas_call | solution.py:1188
  725.7 1.4 fusion.55
  727.0 1.8 fusion.17
  729.5 1.7 copy.67
  (156 shorter events, 13.3 us)
Async XLA Ops:
  7.2 156.8 %all-gather.8.cloned.1.call-start = ((), (), s32[]{:S(2)}) async-start(), calls=%async_computation | async-start | bytes 11796480 | tf_op jit(solution)/shard_map/all_gather | solution.py:1286
  14.8 1.5 copy-start.2
  14.8 1.6 copy-start.12
  14.8 1.8 copy-start.18
  14.8 514.7 %all-gather.10.cloned.1.call-start = ((), (), s32[]{:S(2)}) async-start(), calls=%async_computation.1 | async-start | bytes 3932160 | tf_op jit(solution)/shard_map/all_gather | solution.py:1368
  16.4 66.4 %copy-start.4 = (bf16[384,1280]{1,0:T(8,128)(2,1)}, bf16[384,1280]{1,0:T(8,128)(2,1)S(1)}, u32[]{:S(2)}) copy-start(bf16[384,1280]{1,0:T(8,128)(2,1)S(1)} %convert_element_type.269.shard_ref) | copy-start | bytes 2949124
  17.9 64.9 %copy-start.17 = (s32[1,512,8]{1,2,0:T(8,128)S(1)}, s32[1,512,8]{1,2,0:T(8,128)}, u32[]{:S(2)}) copy-start(s32[1,512,8]{1,2,0:T(8,128)} %param.22) | copy-start | bytes 49156
  17.9 65.7 %copy-start.3 = (bf16[1,512,1536]{2,1,0:T(8,128)(2,1)S(1)}, bf16[1,512,1536]{2,1,0:T(8,128)(2,1)}, u32[]{:S(2)}) copy-start(bf16[1,512,1536]{2,1,0:T(8,128)(2,1)} %param.20) | copy-start | bytes 4718596
  82.8 4.9 copy-start.5
  84.6 6.2 copy-start.14
  84.6 79.3 %collective-permute-start = (bf16[256,1664]{1,0:T(8,128)(2,1)}, bf16[256,1664]{1,0:T(8,128)(2,1)}, u32[]{:S(2)}, u32[]{:S(2)}) collective-permute-start(bf16[256,1664]{1,0:T(8,128)(2,1)} %fusion.42), channel_id=1, source_target_pairs={{0,2},{2,0},{4,6},{6,4},{1,3},{3,1},{5,7},{7,5},{8,10},{10,8},{12,... | collective-permute-start | bytes 2555912 | tf_op jit(solution)/shard_map/ppermute | solution.py:1238
  86.2 77.7 %collective-permute-start.1 = (bf16[256,1664]{1,0:T(8,128)(2,1)}, bf16[256,1664]{1,0:T(8,128)(2,1)}, u32[]{:S(2)}, u32[]{:S(2)}) collective-permute-start(bf16[256,1664]{1,0:T(8,128)(2,1)} %fusion.42), channel_id=1, source_target_pairs={{0,4},{2,6},{4,0},{6,2},{1,5},{3,7},{5,1},{7,3},{8,12},{10,14},{12... | collective-permute-start | bytes 2555912 | tf_op jit(solution)/shard_map/ppermute | solution.py:1238
  88.3 4.0 copy-start.6
  344.4 5.5 copy-start.25
  344.4 5.5 copy-start.35
  349.9 2.7 copy-start.34
  355.3 2.7 copy-start.33
  360.7 2.7 copy-start.28
  363.4 2.2 copy-start.26
  363.4 2.7 copy-start.32
  366.1 2.7 copy-start.31
  368.8 2.7 copy-start.30
  371.5 6.4 copy-start.29
  374.4 43.0 %collective-permute-start.4 = (bf16[384,1024]{1,0:T(8,128)(2,1)}, bf16[384,1024]{1,0:T(8,128)(2,1)S(1)}, u32[]{:S(2)}, u32[]{:S(2)}) collective-permute-start(bf16[384,1024]{1,0:T(8,128)(2,1)} %convolution_convert_fusion.3), channel_id=1, source_target_pairs={{0,24},{8,16},{16,8},{24,0},{1,25},{9,17},{17,9},{25,1},{2,26},{10... | collective-permute-start | bytes 2359304 | tf_op jit(solution)/shard_map/ppermute | solution.py:1244
  375.9 41.6 %collective-permute-start.3 = (bf16[384,1024]{1,0:T(8,128)(2,1)}, bf16[384,1024]{1,0:T(8,128)(2,1)S(1)}, u32[]{:S(2)}, u32[]{:S(2)}) collective-permute-start(bf16[384,1024]{1,0:T(8,128)(2,1)} %convolution_convert_fusion.4), channel_id=1, source_target_pairs={{0,16},{8,24},{16,0},{24,8},{1,17},{9,25},{17,1},{25,9},{2,18},{10... | collective-permute-start | bytes 2359304 | tf_op jit(solution)/shard_map/ppermute | solution.py:1244
  377.3 40.1 %collective-permute-start.2 = (bf16[384,1024]{1,0:T(8,128)(2,1)}, bf16[384,1024]{1,0:T(8,128)(2,1)S(1)}, u32[]{:S(2)}, u32[]{:S(2)}) collective-permute-start(bf16[384,1024]{1,0:T(8,128)(2,1)} %convolution_convert_fusion.5), channel_id=1, source_target_pairs={{0,8},{8,0},{16,24},{24,16},{1,9},{9,1},{17,25},{25,17},{2,10},{10... | collective-permute-start | bytes 2359304 | tf_op jit(solution)/shard_map/ppermute | solution.py:1244
  417.4 5.2 copy-start
  417.4 5.2 copy-start.11
  417.4 5.2 copy-start.24
  419.0 4.1 copy-start.20
  419.0 4.1 copy-start.37
  419.0 169.3 %all-gather.12.cloned.1.call-start = ((), (), s32[]{:S(2)}) async-start(), calls=%async_computation.2 | async-start | bytes 3932160 | tf_op jit(solution)/shard_map/all_gather | solution.py:1368
  419.0 4.0 copy-start.27
  419.0 43.2 %collective-permute-start.7 = (bf16[384,1024]{1,0:T(8,128)(2,1)}, bf16[384,1024]{1,0:T(8,128)(2,1)}, u32[]{:S(2)}, u32[]{:S(2)}) collective-permute-start(bf16[384,1024]{1,0:T(8,128)(2,1)} %fusion.27), channel_id=1, source_target_pairs={{0,24},{8,16},{16,8},{24,0},{1,25},{9,17},{17,9},{25,1},{2,26},{10... | collective-permute-start | bytes 2359304 | tf_op jit(solution)/shard_map/ppermute | solution.py:1244
  420.6 41.7 %collective-permute-start.6 = (bf16[384,1024]{1,0:T(8,128)(2,1)}, bf16[384,1024]{1,0:T(8,128)(2,1)}, u32[]{:S(2)}, u32[]{:S(2)}) collective-permute-start(bf16[384,1024]{1,0:T(8,128)(2,1)} %fusion.24), channel_id=1, source_target_pairs={{0,16},{8,24},{16,0},{24,8},{1,17},{9,25},{17,1},{25,9},{2,18},{10... | collective-permute-start | bytes 2359304 | tf_op jit(solution)/shard_map/ppermute | solution.py:1244
  422.0 40.3 %collective-permute-start.5 = (bf16[384,1024]{1,0:T(8,128)(2,1)}, bf16[384,1024]{1,0:T(8,128)(2,1)}, u32[]{:S(2)}, u32[]{:S(2)}) collective-permute-start(bf16[384,1024]{1,0:T(8,128)(2,1)} %fusion.21), channel_id=1, source_target_pairs={{0,8},{8,0},{16,24},{24,16},{1,9},{9,1},{17,25},{25,17},{2,10},{10... | collective-permute-start | bytes 2359304 | tf_op jit(solution)/shard_map/ppermute | solution.py:1244
  424.8 37.5 %copy-start.10 = (bf16[384,1024]{1,0:T(8,128)(2,1)S(1)}, bf16[384,1024]{1,0:T(8,128)(2,1)}, u32[]{:S(2)}) copy-start(bf16[384,1024]{1,0:T(8,128)(2,1)} %fusion.18) | copy-start | bytes 2359300
  465.5 217.2 %all-gather.14.cloned.1.call-start = ((), (), s32[]{:S(2)}) async-start(), calls=%async_computation.3 | async-start | bytes 3932160 | tf_op jit(solution)/shard_map/all_gather | solution.py:1368
  465.5 49.5 %collective-permute-start.10 = (bf16[384,1024]{1,0:T(8,128)(2,1)}, bf16[384,1024]{1,0:T(8,128)(2,1)}, u32[]{:S(2)}, u32[]{:S(2)}) collective-permute-start(bf16[384,1024]{1,0:T(8,128)(2,1)} %fusion.39), channel_id=1, source_target_pairs={{0,24},{8,16},{16,8},{24,0},{1,25},{9,17},{17,9},{25,1},{2,26},{10... | collective-permute-start | bytes 2359304 | tf_op jit(solution)/shard_map/ppermute | solution.py:1244
  466.8 48.2 %collective-permute-start.9 = (bf16[384,1024]{1,0:T(8,128)(2,1)}, bf16[384,1024]{1,0:T(8,128)(2,1)}, u32[]{:S(2)}, u32[]{:S(2)}) collective-permute-start(bf16[384,1024]{1,0:T(8,128)(2,1)} %fusion.36), channel_id=1, source_target_pairs={{0,16},{8,24},{16,0},{24,8},{1,17},{9,25},{17,1},{25,9},{2,18},{10... | collective-permute-start | bytes 2359304 | tf_op jit(solution)/shard_map/ppermute | solution.py:1244
  468.5 46.6 %collective-permute-start.8 = (bf16[384,1024]{1,0:T(8,128)(2,1)}, bf16[384,1024]{1,0:T(8,128)(2,1)}, u32[]{:S(2)}, u32[]{:S(2)}) collective-permute-start(bf16[384,1024]{1,0:T(8,128)(2,1)} %fusion.33), channel_id=1, source_target_pairs={{0,8},{8,0},{16,24},{24,16},{1,9},{9,1},{17,25},{25,17},{2,10},{10... | collective-permute-start | bytes 2359304 | tf_op jit(solution)/shard_map/ppermute | solution.py:1244
  515.1 3.1 copy-start.21
  526.0 23.9 %collective-permute-start.11 = (bf16[1168,384]{1,0:T(8,128)(2,1)}, bf16[1168,384]{1,0:T(8,128)(2,1)S(1)}, u32[]{:S(2)}, u32[]{:S(2)}) collective-permute-start(bf16[1168,384]{1,0:T(8,128)(2,1)} %get-tuple-element.251), channel_id=1, source_target_pairs={{0,8},{8,0},{16,24},{24,16},{1,9},{9,1},{17,25},{25,17},{2,10},{10... | collective-permute-start | bytes 2691080 | tf_op jit(solution)/shard_map/ppermute | solution.py:1244
  527.5 42.0 %collective-permute-start.12 = (bf16[1168,384]{1,0:T(8,128)(2,1)}, bf16[1168,384]{1,0:T(8,128)(2,1)S(1)}, u32[]{:S(2)}, u32[]{:S(2)}) collective-permute-start(bf16[1168,384]{1,0:T(8,128)(2,1)} %get-tuple-element.250), channel_id=1, source_target_pairs={{0,16},{8,24},{16,0},{24,8},{1,17},{9,25},{17,1},{25,9},{2,18},{10... | collective-permute-start | bytes 2691080 | tf_op jit(solution)/shard_map/ppermute | solution.py:1244
  528.9 40.6 %collective-permute-start.13 = (bf16[1168,384]{1,0:T(8,128)(2,1)}, bf16[1168,384]{1,0:T(8,128)(2,1)}, u32[]{:S(2)}, u32[]{:S(2)}) collective-permute-start(bf16[1168,384]{1,0:T(8,128)(2,1)} %get-tuple-element.249), channel_id=1, source_target_pairs={{0,24},{8,16},{16,8},{24,0},{1,25},{9,17},{17,9},{25,1},{2,26},{10... | collective-permute-start | bytes 2691080 | tf_op jit(solution)/shard_map/ppermute | solution.py:1244
  569.5 0.9 copy-start.8
  572.6 36.1 %collective-permute-start.14 = (bf16[208,384]{1,0:T(8,128)(2,1)S(1)}, bf16[208,384]{1,0:T(8,128)(2,1)S(1)}, u32[]{:S(2)}, u32[]{:S(2)}) collective-permute-start(bf16[208,384]{1,0:T(8,128)(2,1)S(1)} %get-tuple-element.257), channel_id=1, source_target_pairs={{0,2},{2,0},{4,6},{6,4},{1,3},{3,1},{5,7},{7,5},{8,10},{10,8},{12,... | collective-permute-start | bytes 479240 | tf_op jit(solution)/shard_map/ppermute | solution.py:1238
  584.5 24.2 %collective-permute-start.15 = (bf16[208,384]{1,0:T(8,128)(2,1)S(1)}, bf16[208,384]{1,0:T(8,128)(2,1)S(1)}, u32[]{:S(2)}, u32[]{:S(2)}) collective-permute-start(bf16[208,384]{1,0:T(8,128)(2,1)S(1)} %get-tuple-element.256), channel_id=1, source_target_pairs={{0,4},{2,6},{4,0},{6,2},{1,5},{3,7},{5,1},{7,3},{8,12},{10,14},{12... | collective-permute-start | bytes 479240 | tf_op jit(solution)/shard_map/ppermute | solution.py:1238
  588.2 21.4 %collective-permute-start.16 = (bf16[208,384]{1,0:T(8,128)(2,1)S(1)}, bf16[208,384]{1,0:T(8,128)(2,1)S(1)}, u32[]{:S(2)}, u32[]{:S(2)}) collective-permute-start(bf16[208,384]{1,0:T(8,128)(2,1)S(1)} %get-tuple-element.255), channel_id=1, source_target_pairs={{0,6},{2,4},{4,2},{6,0},{1,7},{3,5},{5,3},{7,1},{8,14},{10,12},{12... | collective-permute-start | bytes 479240 | tf_op jit(solution)/shard_map/ppermute | solution.py:1238
  588.3 34.5 %copy-start.36 = (bf16[256,1536]{1,0:T(8,128)(2,1)S(1)}, bf16[256,1536]{1,0:T(8,128)(2,1)}, u32[]{:S(2)}) copy-start(bf16[256,1536]{1,0:T(8,128)(2,1)} %get-tuple-element.208) | copy-start | bytes 2359300
  609.7 65.7 %collective-permute-start.18 = (bf16[528,384]{1,0:T(8,128)(2,1)S(1)}, bf16[528,384]{1,0:T(8,128)(2,1)S(1)}, u32[]{:S(2)}, u32[]{:S(2)}) collective-permute-start(bf16[528,384]{1,0:T(8,128)(2,1)S(1)} %pad_maximum_fusion.3), channel_id=1, source_target_pairs={{0,4},{2,6},{4,0},{6,2},{1,5},{3,7},{5,1},{7,3},{8,12},{10,14},{12... | collective-permute-start | bytes 1216520 | tf_op jit(solution)/shard_map/ppermute | solution.py:1238
  622.8 85.0 %collective-permute-start.20 = (bf16[256,1536]{1,0:T(8,128)(2,1)S(1)}, bf16[256,1536]{1,0:T(8,128)(2,1)S(1)}, u32[]{:S(2)}, u32[]{:S(2)}) collective-permute-start(bf16[256,1536]{1,0:T(8,128)(2,1)S(1)} %copy-done.36), channel_id=1, source_target_pairs={{0,4},{2,6},{4,0},{6,2},{1,5},{3,7},{5,1},{7,3},{8,12},{10,14},{12... | collective-permute-start | bytes 2359304 | tf_op jit(solution)/shard_map/ppermute | solution.py:1238
  622.9 84.9 %collective-permute-start.17 = (bf16[528,384]{1,0:T(8,128)(2,1)S(1)}, bf16[528,384]{1,0:T(8,128)(2,1)S(1)}, u32[]{:S(2)}, u32[]{:S(2)}) collective-permute-start(bf16[528,384]{1,0:T(8,128)(2,1)S(1)} %pad_maximum_fusion.3), channel_id=1, source_target_pairs={{0,2},{2,0},{4,6},{6,4},{1,3},{3,1},{5,7},{7,5},{8,10},{10,8},{12,... | collective-permute-start | bytes 1216520 | tf_op jit(solution)/shard_map/ppermute | solution.py:1238
  675.4 32.4 %collective-permute-start.19 = (bf16[528,384]{1,0:T(8,128)(2,1)S(1)}, bf16[528,384]{1,0:T(8,128)(2,1)S(1)}, u32[]{:S(2)}, u32[]{:S(2)}) collective-permute-start(bf16[528,384]{1,0:T(8,128)(2,1)S(1)} %collective-permute-done.18), channel_id=1, source_target_pairs={{0,2},{2,0},{4,6},{6,4},{1,3},{3,1},{5,7},{7,5},{8,10},{10,8},{12,... | collective-permute-start | bytes 1216520 | tf_op jit(solution)/shard_map/ppermute | solution.py:1238
  682.6 25.2 %copy-start.9 = (bf16[256,1536]{1,0:T(8,128)(2,1)S(1)}, bf16[256,1536]{1,0:T(8,128)(2,1)}, u32[]{:S(2)}) copy-start(bf16[256,1536]{1,0:T(8,128)(2,1)} %get-tuple-element.146) | copy-start | bytes 2359300
  708.1 19.0 %collective-permute-start.21 = (bf16[256,1536]{1,0:T(8,128)(2,1)S(1)}, bf16[256,1536]{1,0:T(8,128)(2,1)S(1)}, u32[]{:S(2)}, u32[]{:S(2)}) collective-permute-start(bf16[256,1536]{1,0:T(8,128)(2,1)S(1)} %add_convert_fusion.2), channel_id=1, source_target_pairs={{0,1},{1,0},{2,3},{3,2},{4,5},{5,4},{6,7},{7,6},{8,9},{9,8},{10,11... | collective-permute-start | bytes 2359304 | tf_op jit(solution)/shard_map/ppermute | solution.py:1241
  715.9 9.1 %copy-start.19 = (f32[2,384]{1,0:T(2,128)S(1)}, f32[2,384]{1,0:T(2,128)}, u32[]{:S(2)}) copy-start(f32[2,384]{1,0:T(2,128)} %param.23) | copy-start | bytes 9220
  715.9 9.1 %copy-start.22 = (f32[2,384]{1,0:T(2,128)S(1)}, f32[2,384]{1,0:T(2,128)}, u32[]{:S(2)}) copy-start(f32[2,384]{1,0:T(2,128)} %param.24) | copy-start | bytes 9220
  716.0 9.1 %copy-start.23 = (f32[2,384]{1,0:T(2,128)S(1)}, f32[2,384]{1,0:T(2,128)}, u32[]{:S(2)}) copy-start(f32[2,384]{1,0:T(2,128)} %param.25) | copy-start | bytes 9220
  716.0 9.7 %copy-start.13 = (f32[384,16]{0,1:T(8,128)S(1)}, f32[384,16]{0,1:T(8,128)}, u32[]{:S(2)}) copy-start(f32[384,16]{0,1:T(8,128)} %param.32) | copy-start | bytes 73732
  716.0 9.7 %copy-start.15 = (f32[384,16]{0,1:T(8,128)S(1)}, f32[384,16]{0,1:T(8,128)}, u32[]{:S(2)}) copy-start(f32[384,16]{0,1:T(8,128)} %param.33) | copy-start | bytes 73732
  716.0 9.7 %copy-start.16 = (f32[384,16]{0,1:T(8,128)S(1)}, f32[384,16]{0,1:T(8,128)}, u32[]{:S(2)}) copy-start(f32[384,16]{0,1:T(8,128)} %param.34) | copy-start | bytes 73732
  716.0 11.0 %copy-start.1 = (f32[512,1536]{1,0:T(8,128)S(1)}, f32[512,1536]{1,0:T(8,128)}, u32[]{:S(2)}) copy-start(f32[512,1536]{1,0:T(8,128)} %get-tuple-element.143.res_ref) | copy-start | bytes 9437188
  727.0 2.5 copy-start.7
Sparse Core Ops, SparseCore 0:
  14.9 114.6 all-gather.7
  419.1 82.6 all-gather.9
  503.9 63.1 all-gather.11
  569.2 113.4 all-gather.13
